TPU v7x, 32 devices: a whole 2x2x4 slice. The times are simulated.
32 devices in a mesh: row: 4 (over y, x), col: 8 (over z, core).
Axes of the slice: x: 2, y: 2, z: 4, core: 2. Of those that a mesh axis runs over, the one named last changes fastest.
Arguments:
- features: bfloat16 [16384, 512], P(('row', 'col')), may hold values from -6 to 6
- tile_cols: int32 [4, 8, 16, 8], P('row', 'col'), may hold values from 0 to 31, as said below
- tile_masks: bfloat16 [4, 8, 16, 8, 128, 128], P('row', 'col'), may hold values from 0 to 1, as said below
- degree: int32 [16384], P(('row', 'col')), may hold values from 8 to 32
- owner_nodes: int32 [16384], P(('row', 'col')), may hold values from 0 to 16383, as said below
- owner_position: int32 [16384], P(('row', 'col')), may hold values from 0 to 16383, as said below
- self_weight: bfloat16 [512, 512], replicated, may hold values from -0.25 to 0.25
- neigh_weight: bfloat16 [512, 512], replicated, may hold values from -0.25 to 0.25
- cotangent: bfloat16 [16384, 512], P(('row', 'col')), may hold values from -6 to 6
Outputs:
- hidden: bfloat16 [16384, 512], P(('row', 'col'))
- grad_features: bfloat16 [16384, 512], P(('row', 'col'))
- grad_self: float32 [512, 512], replicated
- grad_neigh: float32 [512, 512], replicated
Inputs may be any that keep to these rules, and one draw needn't show every extreme that they name: `tile_cols`: in each grid cell, the 8 entries of one tile row are different tile columns. `tile_masks`: entries are 0 or 1. `owner_nodes`: A permutation of the node numbers. For any two devices, the number of nodes of the first one's block that the second one holds in the owner layout is 0 or exactly 32. `owner_position`: the inverse permutation of owner_nodes.
All inputs are finite; a program needn't handle non-finite values.
Results may differ from a plain program's by a relative error of at most 0.013.
Values may be sent and summed in bfloat16 or wider, within the bound.
No kernel may reach another device: no remote copies, remote signals or barrier semaphores. Data moves between devices by JAX's collectives and lax.ppermute only.
A program may use at most 128 MiB of HBM per device.

v0:
```python
import math

import jax
import jax.numpy as jnp
from jax import lax
from jax.sharding import PartitionSpec as P


def rank_within(group_keys, order_keys):
    same_group = group_keys[:, None] == group_keys[None, :]
    earlier = order_keys[None, :] < order_keys[:, None]
    return jnp.sum(same_group & earlier, axis=1)


def on_device(
    features,
    tile_cols,
    tile_masks,
    degree,
    owner_nodes,
    owner_position,
    self_weight,
    neigh_weight,
    cotangent,
):
    row_count = features.shape[0]
    feat_width = features.shape[1]
    row_devices = lax.axis_size("row")
    col_devices = lax.axis_size("col")
    all_devices = row_devices * col_devices
    slot_count = 2 * row_count // all_devices
    pattern = tile_masks[0, 0]
    columns = tile_cols[0, 0]
    tile_size = pattern.shape[-1]
    breadth = pattern.shape[1]
    group_rows = row_count // tile_size
    own_dest = owner_nodes // row_count
    own_flat = own_dest * slot_count + rank_within(own_dest, jnp.arange(row_count, dtype=jnp.int32))
    node_source = owner_position // row_count
    node_flat = node_source * slot_count + rank_within(node_source, owner_position)
    outbound = (
        jnp.zeros((all_devices * slot_count, feat_width), jnp.bfloat16).at[own_flat].set(features)
    )
    inbound = lax.all_to_all(outbound, ("row", "col"), split_axis=0, concat_axis=0, tiled=True)
    node_feats = inbound[node_flat]
    column_feats = lax.all_gather(node_feats, "col", axis=0, tiled=True)
    feat_tiles = column_feats.reshape(-1, tile_size, feat_width)
    tile_rows = row_count * lax.axis_size("row") // tile_size
    groups = tile_rows // group_rows
    mask_block = pattern.reshape(groups, group_rows, breadth, tile_size, tile_size)
    col_block = columns.reshape(groups, group_rows, breadth)

    def one_group(operands):
        chosen = feat_tiles[operands[1]]
        return jnp.einsum("tkij,tkjf->tif", operands[0], chosen, preferred_element_type=jnp.float32)

    products = lax.map(one_group, (mask_block, col_block))
    node_summed = lax.psum_scatter(
        products.reshape(row_count * lax.axis_size("row"), feat_width).astype(jnp.bfloat16),
        "row",
        scatter_dimension=0,
        tiled=True,
    ).astype(jnp.float32)
    outgoing = (
        jnp.zeros((all_devices * slot_count, feat_width), jnp.float32)
        .at[node_flat]
        .set(node_summed)
    )
    summed = lax.all_to_all(
        outgoing.astype(jnp.bfloat16), ("row", "col"), split_axis=0, concat_axis=0, tiled=True
    ).astype(outgoing.dtype)[own_flat]
    degrees = degree.astype(jnp.float32)[:, None]
    aggregate = (summed / degrees).astype(jnp.bfloat16)
    preact = jnp.dot(features, self_weight, preferred_element_type=jnp.float32) + jnp.dot(
        aggregate, neigh_weight, preferred_element_type=jnp.float32
    )
    hidden = jax.nn.silu(preact).astype(jnp.bfloat16)
    gate_value = jax.nn.sigmoid(preact)
    slopes = (
        cotangent.astype(jnp.float32) * gate_value * (1.0 + preact * (1.0 - gate_value))
    ).astype(jnp.bfloat16)
    along_rows = (((0,), (0,)), ((), ()))
    grad_terms = (
        lax.dot_general(features, slopes, along_rows, preferred_element_type=jnp.float32),
        lax.dot_general(aggregate, slopes, along_rows, preferred_element_type=jnp.float32),
    )
    along_cols = (((1,), (1,)), ((), ()))
    own_back = lax.dot_general(slopes, self_weight, along_cols, preferred_element_type=jnp.float32)
    spread = (
        lax.dot_general(slopes, neigh_weight, along_cols, preferred_element_type=jnp.float32)
        / degrees
    ).astype(jnp.bfloat16)
    outgoing_back = (
        jnp.zeros((all_devices * slot_count, feat_width), jnp.bfloat16).at[own_flat].set(spread)
    )
    node_spread = lax.all_to_all(
        outgoing_back, ("row", "col"), split_axis=0, concat_axis=0, tiled=True
    )[node_flat]
    grid_spread = lax.all_gather(node_spread, "row", axis=0, tiled=True)
    spread_tiles = grid_spread.reshape(-1, tile_size, feat_width)
    col_tiles = column_feats.shape[0] // tile_size
    group_total = pattern.shape[0] // group_rows

    def add_group(group_index, totals):
        mask_part = lax.dynamic_slice_in_dim(pattern, group_index * group_rows, group_rows, 0)
        col_part = lax.dynamic_slice_in_dim(columns, group_index * group_rows, group_rows, 0)
        row_part = lax.dynamic_slice_in_dim(spread_tiles, group_index * group_rows, group_rows, 0)
        pieces = jnp.einsum(
            "tkij,tif->tkjf", mask_part, row_part, preferred_element_type=jnp.float32
        )
        return totals.at[col_part.reshape(-1)].add(pieces.reshape(-1, tile_size, feat_width))

    start_zero = jnp.zeros((col_tiles, tile_size, feat_width), jnp.float32)
    back_terms = lax.fori_loop(0, group_total, add_group, start_zero).reshape(-1, feat_width)
    node_back = lax.psum_scatter(
        back_terms.astype(jnp.bfloat16), "col", scatter_dimension=0, tiled=True
    ).astype(jnp.float32)
    outgoing_sum = (
        jnp.zeros((all_devices * slot_count, feat_width), jnp.float32).at[node_flat].set(node_back)
    )
    neigh_back = lax.all_to_all(
        outgoing_sum.astype(jnp.bfloat16), ("row", "col"), split_axis=0, concat_axis=0, tiled=True
    ).astype(outgoing_sum.dtype)[own_flat]
    grad_features = (own_back + neigh_back).astype(jnp.bfloat16)
    summed_grads = lax.psum((grad_terms[0], grad_terms[1]), ("row", "col"))
    grad_scale = 1.0 / math.sqrt(row_count * all_devices)
    return (hidden, grad_features, summed_grads[0] * grad_scale, summed_grads[1] * grad_scale)


def solution(mesh):
    placed = (
        P(("row", "col"), None),
        P("row", "col", None, None),
        P("row", "col", None, None, None, None),
        P(("row", "col")),
        P(("row", "col")),
        P(("row", "col")),
        P(),
        P(),
        P(("row", "col"), None),
    )
    return jax.shard_map(
        on_device,
        mesh=mesh,
        in_specs=placed,
        out_specs=(P(("row", "col"), None), P(("row", "col"), None), P(), P()),
        check_vma=False,
    )
```

profile of v0, /device:TPU:0, one launch (start us, length us, event | category | flops | bytes accessed | tf_op | source)
XLA Modules:
  0.0 608.6 jit_solution(3043573700753177568)
XLA Ops:
  7.2 0.7 add_select_fusion
  7.9 0.3 convert_reduce_fusion
  8.2 0.7 compare_select_fusion.2
  8.9 4.0 scatter_custom_fusion.1
  12.8 7.3 %all-to-all-start = ((bf16[32,32,512]{2,1,0:T(8,128)(2,1)}), bf16[32,32,512]{2,1,0:T(8,128)(2,1)S(1)}, u32[]{:S(2)}, u32[]{:S(2)}) async-start(bf16[32,32,512]{2,1,0:T(8,128)(2,1)} %bitcast.12), calls=%async_computation | async-start | bytes 2097152 | tf_op jit(solution)/shard_map/all_to_all | solution.py:44
  20.2 0.7 add_select_fusion.1
  20.9 1.1 convert_reduce_fusion.1
  22.0 0.7 compare_select_fusion.3
  22.7 25.1 %all-to-all-done = bf16[32,32,512]{2,1,0:T(8,128)(2,1)S(1)} async-done(((bf16[32,32,512]{2,1,0:T(8,128)(2,1)}), bf16[32,32,512]{2,1,0:T(8,128)(2,1)S(1)}, u32[]{:S(2)}, u32[]{:S(2)}) %all-to-all-start) | async-done | bytes 1048608 | tf_op jit(solution)/shard_map/all_to_all | solution.py:44
  47.7 2.6 gather_fusion.1
  50.5 44.8 %all-gather.5.cloned.1.call-done = bf16[4096,512]{1,0:T(8,128)(2,1)} async-done(((bf16[512,512]{1,0:T(8,128)(2,1)}), bf16[4096,512]{1,0:T(8,128)(2,1)}) %all-gather.5.cloned.1.call-update) | async-done | bytes 4194320 | tf_op jit(solution)/shard_map/all_gather | solution.py:46
  95.3 33.3 %while.23 = (s32[]{:T(128)}, bf16[4,4,128,512]{3,2,1,0:T(8,128)(2,1)S(1)}, bf16[4,4,8,128,128]{4,3,2,1,0:T(8,128)(2,1)}, s32[4,4,8]{2,1,0:T(4,128)S(1)}, bf16[32,128,512]{2,1,0:T(8,128)(2,1)}, /*index=5*/s32[]{:T(128)}) while((s32[]{:T(128)}, bf16[4,4,128,512]{3,2,1,0:T(8,128)(2,1)S(1)}, bf16[4,4,8,128,128]{4,3,2,1,0:T(8,128)(2,1)}, ...), condition=%wide.region_4.5_spmd, body=%wide.region_3.4_spmd.sunk | while | flops 536872064 | bytes 14686033 | solution.py:57
  95.3 0.1 reshape.220
  95.4 5.0 gather_fusion
  100.4 3.2 fusion.49
  103.7 5.0 gather_fusion
  108.7 3.2 fusion.49
  112.1 5.0 gather_fusion
  117.0 3.2 fusion.49
  120.4 5.0 gather_fusion
  125.4 3.2 fusion.49
  128.6 1.3 copy-done.2
  130.0 34.0 %reduce-scatter.3.cloned.1.call-done = bf16[512,512]{1,0:T(8,128)(2,1)} async-done(((bf16[2048,512]{1,0:T(8,128)(2,1)}), bf16[512,512]{1,0:T(8,128)(2,1)}) %reduce-scatter.3.cloned.1.call-update) | async-done | bytes 524304 | tf_op jit(solution)/shard_map/reduce_scatter | solution.py:58
  164.0 3.3 scatter_custom_fusion.2
  167.3 1.1 convert_element_type.68
  168.4 4.7 all-to-all-start.1
  173.3 2.5 fusion.28
  175.7 25.0 %all-to-all-done.1 = bf16[32,32,512]{2,1,0:T(8,128)(2,1)} async-done(((bf16[32,32,512]{2,1,0:T(8,128)(2,1)}), bf16[32,32,512]{2,1,0:T(8,128)(2,1)}, u32[]{:S(2)}, u32[]{:S(2)}) %all-to-all-start.1) | async-done | bytes 1048608 | tf_op jit(solution)/shard_map/all_to_all | solution.py:69
  200.8 1.5 bitcast_convert_fusion.1
  202.3 2.3 gather_fusion.2
  204.6 3.4 multiply_convert_fusion
  208.0 0.8 copy-done.4
  208.8 0.5 fusion.11
  209.3 2.9 scatter_custom_fusion.3
  212.2 29.6 %all_to_all.42 = bf16[32,32,512]{2,1,0:T(8,128)(2,1)S(1)} all-to-all(bf16[32,32,512]{2,1,0:T(8,128)(2,1)S(1)} %bitcast.82), channel_id=1, replica_groups=mesh['row'=4,'col'=8] {'row','col'}, dimensions={0} | all-to-all | bytes 2097152 | tf_op jit(solution)/shard_map/all_to_all | solution.py:96
  241.8 2.6 gather_fusion.3
  244.5 6.4 %copy.26 = bf16[1,1,16,8,128,128]{4,5,3,2,1,0:T(8,128)(2,1)} copy(bf16[1,1,16,8,128,128]{5,4,3,2,1,0:T(8,128)(2,1)} %bitcast.78) | data formatting | bytes 8388608 | tf_op args[2]
  251.0 26.5 %all-gather.7.cloned.1.call-done = bf16[2048,512]{1,0:T(8,128)(2,1)} async-done(((bf16[512,512]{1,0:T(8,128)(2,1)}), bf16[2048,512]{1,0:T(8,128)(2,1)}) %all-gather.7.cloned.1.call-update) | async-done | bytes 2097168 | tf_op jit(solution)/shard_map/all_gather | solution.py:99
  277.5 4.3 broadcast_in_dim.18
  281.8 99.5 %while.24 = (s32[]{:T(128)}, f32[32,128,512]{2,1,0:T(8,128)}, s32[16,8]{1,0:T(8,128)S(1)}, bf16[16,8,128,128]{2,3,1,0:T(8,128)(2,1)}, bf16[16,128,512]{2,1,0:T(8...) while((s32[]{:T(128)}, f32[32,128,512]{2,1,0:T(8,128)}, s32[16,8]{1,0:T(8,128)S(1)}, ...), condition=%wide.region_10.11_spmd, body=%wide.region_8.10_spmd.sunk | while | flops 538968192 | bytes 35129368 | solution.py:114
  281.9 0.1 reshape.223
  281.9 5.8 fusion.53
  287.8 19.0 %scatter_fusion = f32[32,128,512]{2,1,0:T(8,128)} fusion(f32[32,128,512]{2,1,0:T(8,128)} %get-tuple-element.270, s32[32]{0:T(128)S(1)} %fusion.52, f32[32,128,512]{2,1,0:T(8,128)} %bitcast.71), kind=kCustom, calls=%fused_computation.5.clone.1 | custom fusion | flops 2097152 | bytes 25165952 | tf_op jit(solution)/shard_map/while/body/eval_jaxpr/scatter-add | solution.py:111
  306.8 0.1 reshape.223
  306.8 5.8 fusion.53
  312.7 19.1 %scatter_fusion = f32[32,128,512]{2,1,0:T(8,128)} fusion(f32[32,128,512]{2,1,0:T(8,128)} %get-tuple-element.270, s32[32]{0:T(128)S(1)} %fusion.52, f32[32,128,512]{2,1,0:T(8,128)} %bitcast.71), kind=kCustom, calls=%fused_computation.5.clone.1 | custom fusion | flops 2097152 | bytes 25165952 | tf_op jit(solution)/shard_map/while/body/eval_jaxpr/scatter-add | solution.py:111
  331.8 5.8 fusion.53
  337.6 18.8 %scatter_fusion = f32[32,128,512]{2,1,0:T(8,128)} fusion(f32[32,128,512]{2,1,0:T(8,128)} %get-tuple-element.270, s32[32]{0:T(128)S(1)} %fusion.52, f32[32,128,512]{2,1,0:T(8,128)} %bitcast.71), kind=kCustom, calls=%fused_computation.5.clone.1 | custom fusion | flops 2097152 | bytes 25165952 | tf_op jit(solution)/shard_map/while/body/eval_jaxpr/scatter-add | solution.py:111
  356.6 5.8 fusion.53
  362.4 18.9 %scatter_fusion = f32[32,128,512]{2,1,0:T(8,128)} fusion(f32[32,128,512]{2,1,0:T(8,128)} %get-tuple-element.270, s32[32]{0:T(128)S(1)} %fusion.52, f32[32,128,512]{2,1,0:T(8,128)} %bitcast.71), kind=kCustom, calls=%fused_computation.5.clone.1 | custom fusion | flops 2097152 | bytes 25165952 | tf_op jit(solution)/shard_map/while/body/eval_jaxpr/scatter-add | solution.py:111
  381.3 6.0 convert_element_type.77
  387.3 49.9 %reduce-scatter.5.cloned.1.call-done = bf16[512,512]{1,0:T(8,128)(2,1)} async-done(((bf16[4096,512]{1,0:T(8,128)(2,1)}), bf16[512,512]{1,0:T(8,128)(2,1)}) %reduce-scatter.5.cloned.1.call-update) | async-done | bytes 524304 | tf_op jit(solution)/shard_map/reduce_scatter | solution.py:115
  437.2 3.3 scatter_custom_fusion.4
  440.5 1.2 convert_element_type.80
  441.7 3.5 all-to-all-start.3
  445.3 2.5 convolution_bitcast_fusion.1
  447.8 1.5 fusion.27
  449.3 141.8 %all-reduce.3.cloned.1.call-done = (f32[512,512]{0,1:T(8,128)}, f32[512,512]{0,1:T(8,128)}) async-done(((f32[512,512]{0,1:T(8,128)}, f32[512,512]{0,1:T(8,128)}), (f32[512,512]{0,1:T(8,128)}, f32[512,512]{0,1:T(8,128)})) %all-reduce.3.cloned.1.call-update) | async-done | bytes 2097168 | tf_op jit(solution)/shard_map/psum | solution.py:125
  591.1 1.8 broadcast_multiply_fusion
  592.9 1.3 copy.29
  594.2 1.3 copy.30
  595.5 1.6 bitcast_convert_fusion
  597.1 2.3 gather_fusion.4
  599.4 2.7 fusion.10
  (54 shorter events, 1.0 us)
Async XLA Ops:
  7.2 197.4 %copy-start = (bf16[512,512]{1,0:T(8,128)(2,1)S(1)}, bf16[512,512]{1,0:T(8,128)(2,1)}, u32[]{:S(2)}) copy-start(bf16[512,512]{1,0:T(8,128)(2,1)} %param.20) | copy-start | bytes 1572868
  8.9 41.6 %copy-start.7 = (s32[1,1,16,8]{2,3,1,0:T(8,128)S(1)}, s32[1,1,16,8]{2,3,1,0:T(8,128)}, u32[]{:S(2)}) copy-start(s32[1,1,16,8]{2,3,1,0:T(8,128)} %param.14) | copy-start | bytes 1540
  12.8 34.9 %all-to-all-start = ((bf16[32,32,512]{2,1,0:T(8,128)(2,1)}), bf16[32,32,512]{2,1,0:T(8,128)(2,1)S(1)}, u32[]{:S(2)}, u32[]{:S(2)}) async-start(bf16[32,32,512]{2,1,0:T(8,128)(2,1)} %bitcast.12), calls=%async_computation | async-start | bytes 2097152 | tf_op jit(solution)/shard_map/all_to_all | solution.py:44
  20.1 75.2 %all-gather.5.cloned.1.call-start = ((), (), s32[]{:S(2)}) async-start(), calls=%async_computation.8 | async-start | bytes 4718592 | tf_op jit(solution)/shard_map/all_gather | solution.py:46
  50.4 113.7 %reduce-scatter.3.cloned.1.call-start = ((), (), s32[]{:S(2)}) async-start(), calls=%async_computation.6 | async-start | bytes 2621440 | tf_op jit(solution)/shard_map/reduce_scatter | solution.py:58
  128.6 1.3 copy-start.2
  130.0 43.3 %copy-start.8 = (s32[512]{0:T(512)S(1)}, s32[512]{0:T(512)}, u32[]{:S(2)}) copy-start(s32[512]{0:T(512)} %param.16) | copy-start | bytes 6148
  130.0 43.3 %copy-start.3 = (bf16[512,512]{1,0:T(8,128)(2,1)S(1)}, bf16[512,512]{1,0:T(8,128)(2,1)}, u32[]{:S(2)}) copy-start(bf16[512,512]{1,0:T(8,128)(2,1)} %param.19) | copy-start | bytes 1572868
  168.4 32.3 %all-to-all-start.1 = ((bf16[32,32,512]{2,1,0:T(8,128)(2,1)}), bf16[32,32,512]{2,1,0:T(8,128)(2,1)}, u32[]{:S(2)}, u32[]{:S(2)}) async-start(bf16[32,32,512]{2,1,0:T(8,128)(2,1)} %bitcast.81), calls=%async_computation.2 | async-start | bytes 2097152 | tf_op jit(solution)/shard_map/all_to_all | solution.py:69
  173.2 104.3 %all-gather.7.cloned.1.call-start = ((), (), s32[]{:S(2)}) async-start(), calls=%async_computation.9 | async-start | bytes 2621440 | tf_op jit(solution)/shard_map/all_gather | solution.py:99
  208.0 0.8 copy-start.4
  244.4 192.8 %reduce-scatter.5.cloned.1.call-start = ((), (), s32[]{:S(2)}) async-start(), calls=%async_computation.7 | async-start | bytes 4718592 | tf_op jit(solution)/shard_map/reduce_scatter | solution.py:115
  387.3 58.0 %copy-start.5 = (bf16[512,512]{1,0:T(8,128)(2,1)S(1)}, bf16[512,512]{1,0:T(8,128)(2,1)}, u32[]{:S(2)}) copy-start(bf16[512,512]{1,0:T(8,128)(2,1)} %copy-done.4) | copy-start | bytes 1572868
  441.7 6.1 copy-start.6
  441.7 153.8 %all-to-all-start.3 = ((bf16[32,32,512]{2,1,0:T(8,128)(2,1)}), bf16[32,32,512]{2,1,0:T(8,128)(2,1)}, u32[]{:S(2)}, u32[]{:S(2)}) async-start(bf16[32,32,512]{2,1,0:T(8,128)(2,1)} %bitcast.80), calls=%async_computation.5 | async-start | bytes 2097152 | tf_op jit(solution)/shard_map/all_to_all | solution.py:121
  445.2 145.9 %all-reduce.3.cloned.1.call-start = ((), (), s32[]{:S(2)}) async-start(), calls=%async_computation.10 | async-start | bytes 4194304 | tf_op jit(solution)/shard_map/psum | solution.py:125
  595.5 6.5 %copy-start.1 = (bf16[512,512]{1,0:T(8,128)(2,1)S(1)}, bf16[512,512]{1,0:T(8,128)(2,1)}, u32[]{:S(2)}) copy-start(bf16[512,512]{1,0:T(8,128)(2,1)} %param.20) | copy-start | bytes 1572868
Sparse Core Ops, SparseCore 0:
  50.5 44.7 all-gather.4
  130.1 33.9 reduce-scatter.2
  244.6 32.9 all-gather.6
  387.4 49.7 reduce-scatter.4
  452.8 138.2 all-reduce.2
where the time goes:
time: 610 us; the launch traced here: 609 us
  waiting for transfers between devices  347 us (57%)
  other arithmetic  99.8 us (16%)
  local copies, waits for them, and re-layouts  53 us (9%)
  matrix products  49.1 us (8%)
  blocking collectives  29.6 us (5%)
  starting transfers between devices  15.8 us (3%)
  between operations  14 us (2%)
    psum x1, waiting for transfers between devices, on_device(): summed_grads = lax.psum((grad_terms[0], grad_terms[1]), ('row', 'col'))  142 us
    scatter-add x4, other arithmetic, add_group(): totals.at[col_part.reshape(-1)]  75.8 us
    reduce_scatter x1, waiting for transfers between devices, on_device(): lax.psum_scatter(back_terms.astype(jnp.bfloat16), 'col', scatter_dimensio...  49.9 us
    all_gather x1, waiting for transfers between devices, on_device(): column_feats = lax.all_gather(node_feats, 'col', axis=0, tiled=True)  44.8 us
    reduce_scatter x1, waiting for transfers between devices, on_device(): lax.psum_scatter(products.reshape(row_count * lax.axis_size('row'), feat_...  34 us
    all_to_all x1, blocking collectives, on_device(): lax.all_to_all(outgoing_back, ('row', 'col'), split_axis=0, concat_axis=0...  29.6 us
    all_gather x1, waiting for transfers between devices, on_device(): grid_spread = lax.all_gather(node_spread, 'row', axis=0, tiled=True)  26.5 us
    all_to_all x1, waiting for transfers between devices, on_device(): lax.all_to_all(outbound, ('row', 'col'), split_axis=0, concat_axis=0, til...  25.1 us
  transfers between devices with their start and end apart: 8, of which 7 were waited for; matrix products, arithmetic and copies ran while one was open for 3% of the time, Pallas kernels for 0%

commit v1 on v0

v1 whole, which is shorter than its diff:
```python
import functools
import math

import jax
import jax.numpy as jnp
from jax import lax
from jax.experimental import pallas as pl
from jax.experimental.pallas import tpu as pltpu
from jax.sharding import PartitionSpec as P

BF = jnp.bfloat16
F32 = jnp.float32
VMEM = pl.BlockSpec(memory_space=pltpu.VMEM)
LIMIT = 56 * 1024 * 1024


def params():
    return pltpu.CompilerParams(vmem_limit_bytes=LIMIT)


def cost(flops, nbytes):
    return pl.CostEstimate(flops=int(flops), bytes_accessed=int(nbytes), transcendentals=0)


def dot(a, b, ca=1, cb=0):
    return lax.dot_general(a, b, (((ca,), (cb,)), ((), ())), preferred_element_type=F32)


def as_column(row):
    return jnp.broadcast_to(row, (128, row.shape[1])).T


def block_of(index, size):
    if size & (size - 1) == 0:
        return lax.shift_right_logical(index, size.bit_length() - 1)
    return lax.div(index, jnp.full_like(index, size))


def rank_row(group_row, order_row):
    n = group_row.shape[1]
    group_col = as_column(group_row)[:, :1]
    order_col = as_column(order_row)[:, :1]
    earlier = (group_col == group_row) & (order_col < order_row)
    return jnp.sum(jnp.where(earlier, 1.0, 0.0), axis=0, keepdims=True).astype(jnp.int32)


def slots_onehot(flat_row, slots):
    iota = lax.broadcasted_iota(jnp.int32, (slots, flat_row.shape[1]), 0)
    return jnp.where(iota == flat_row, 1.0, 0.0).astype(BF)


def entries_onehot(flat_col, slots):
    iota = lax.broadcasted_iota(jnp.int32, (flat_col.shape[0], slots), 1)
    return jnp.where(flat_col[:, :1] == iota, 1.0, 0.0).astype(BF)


def own_slots(nodes_row, cap):
    n = nodes_row.shape[1]
    dest = block_of(nodes_row, n)
    rank = rank_row(dest, lax.broadcasted_iota(jnp.int32, (1, n), 1))
    return dest, rank


def pack_kernel(cap, nodes_ref, value_ref, out_ref):
    dest, rank = own_slots(nodes_ref[...], cap)
    out_ref[...] = dot(slots_onehot(dest * cap + rank, out_ref.shape[0]), value_ref[...]).astype(BF)


def index_kernel(cap, nodes_ref, position_ref, degree_ref, cot_ref, cot_out, degree_out, own_col, node_row, node_col):
    devices, _ = degree_out.shape
    n = nodes_ref.shape[1]
    dest, rank = own_slots(nodes_ref[...], cap)
    flat = dest * cap + rank
    own_col[...] = as_column(flat)
    cot_out[...] = dot(slots_onehot(flat, cot_out.shape[0]), cot_ref[...]).astype(BF)
    by_dest = jnp.where(lax.broadcasted_iota(jnp.int32, (devices, n), 0) == dest, degree_ref[...].astype(F32), 0.0)
    by_rank = entries_onehot(as_column(rank), cap)
    degree_out[...] = dot(by_dest.astype(BF), by_rank)
    position = position_ref[...]
    source = block_of(position, n)
    place = source * cap + rank_row(source, position)
    node_row[...] = jnp.broadcast_to(place, node_row.shape)
    node_col[...] = as_column(place)


def unpack_kernel(col_ref, value_ref, out_ref):
    out_ref[...] = dot(entries_onehot(col_ref[...], value_ref.shape[0]), value_ref[...]).astype(BF)


def spmm_kernel(ways, cols_ref, group_ref, x_ref, *refs):
    masks, outs = refs[:ways], refs[ways:]
    q = pl.program_id(0)
    depth = pl.num_programs(0)
    _, breadth, tile, _ = masks[0].shape
    for s in range(ways):
        base = (group_ref[s] * depth + q) * breadth
        total = None
        for p in range(0, breadth, 2):
            width = min(2, breadth - p)
            left = jnp.concatenate([masks[s][0, p + w] for w in range(width)], axis=1)
            right = jnp.concatenate(
                [x_ref[pl.ds(pl.multiple_of(cols_ref[base + p + w] * tile, tile), tile), :] for w in range(width)], axis=0
            )
            term = dot(left, right)
            total = term if total is None else total + term
        outs[s][...] = total.astype(BF)


def spmm_back_kernel(ways, cols_ref, group_ref, *refs):
    spreads, masks, out_ref, total = refs[:ways], refs[ways : 2 * ways], refs[2 * ways], refs[2 * ways + 1]
    q = pl.program_id(0)
    depth = pl.num_programs(0)
    _, breadth, tile, _ = masks[0].shape

    @pl.when(q == 0)
    def _():
        total[...] = jnp.zeros_like(total)

    for s in range(ways):
        base = (group_ref[s] * depth + q) * breadth
        rows = spreads[s][...]
        for k in range(breadth):
            at = pl.ds(pl.multiple_of(cols_ref[base + k] * tile, tile), tile)
            total[at, :] += dot(masks[s][0, k], rows, 0, 0)

    @pl.when(q == depth - 1)
    def _():
        out_ref[...] = total[...].astype(BF)


def layer_kernel(ways, *refs):
    terms = refs[:ways]
    (x_ref, cot_ref, degree_ref, col_ref, self_ref, neigh_ref, hidden_out, slopes_out, agg_out, spread_out) = refs[ways:]
    devices, cap = degree_ref.shape
    slots = cot_ref.shape[0]
    place = col_ref[...][:, :1]
    rows = place.shape[0]
    summed = terms[0][...].astype(F32)
    for s in range(1, ways):
        summed = summed + terms[s][...].astype(F32)
    source = block_of(place, cap)
    rank = place - source * cap
    by_source = entries_onehot(source, devices)
    degrees = dot(by_source, degree_ref[...].astype(BF))
    picked = lax.broadcasted_iota(jnp.int32, (rows, cap), 1) == rank
    degrees = jnp.sum(jnp.where(picked, degrees, 0.0), axis=1, keepdims=True)
    agg = (summed / degrees).astype(BF)
    agg_out[...] = agg
    preact = dot(x_ref[...], self_ref[...]) + dot(agg, neigh_ref[...])
    gate = jax.nn.sigmoid(preact)
    hidden_out[...] = (preact * gate).astype(BF)
    cot = dot(entries_onehot(place, slots), cot_ref[...])
    slopes = (cot * gate * (1.0 + preact * (1.0 - gate))).astype(BF)
    slopes_out[...] = slopes
    spread_out[...] = (dot(slopes, neigh_ref[...], 1, 1) / degrees).astype(BF)


def terms_kernel(x_ref, agg_ref, slopes_ref, hidden_ref, self_ref, row_ref, grads_out, back_out, packed_out):
    width = x_ref.shape[1]
    slopes = slopes_ref[...]
    packed_out[...] = dot(slots_onehot(row_ref[...][:1], packed_out.shape[0]), hidden_ref[...]).astype(BF)
    grads_out[:width, :] = dot(x_ref[...], slopes, 0, 0).astype(BF)
    grads_out[width:, :] = dot(agg_ref[...], slopes, 0, 0).astype(BF)
    back_out[...] = dot(slopes, self_ref[...], 1, 1)


def join_kernel(own_ref, neigh_ref, row_ref, out_ref):
    joined = (own_ref[...] + neigh_ref[...].astype(F32)).astype(BF)
    out_ref[...] = dot(slots_onehot(row_ref[...][:1], out_ref.shape[0]), joined).astype(BF)


def on_device(
    features,
    tile_cols,
    tile_masks,
    degree,
    owner_nodes,
    owner_position,
    self_weight,
    neigh_weight,
    cotangent,
):
    rows, width = features.shape
    row_devices = lax.axis_size("row")
    col_devices = lax.axis_size("col")
    devices = row_devices * col_devices
    cap = 2 * rows // devices
    slots = devices * cap
    masks = tile_masks[0, 0]
    tile = masks.shape[-1]
    breadth = masks.shape[1]
    depth = rows // tile
    cols = tile_cols[0, 0].reshape(-1)
    me = lax.axis_index("row")
    ways = row_devices
    groups = jnp.bitwise_xor(me, jnp.arange(ways, dtype=jnp.int32)).astype(jnp.int32)
    everyone = ("row", "col")
    call = functools.partial(pl.pallas_call, compiler_params=params())

    def shape(r, c, dtype=BF):
        return jax.ShapeDtypeStruct((r, c), dtype)

    def relay(packed):
        there = packed.reshape(devices, cap, -1)
        return lax.all_to_all(there, everyone, split_axis=0, concat_axis=0, tiled=True).reshape(slots, -1)

    def across(value, s):
        return lax.ppermute(value, "row", [(i, i ^ s) for i in range(ways)])

    nodes = owner_nodes.reshape(1, rows)
    slab = rows * width
    packed = call(
        functools.partial(pack_kernel, cap),
        out_shape=shape(slots, width),
        in_specs=[VMEM] * 2,
        out_specs=VMEM,
        cost_estimate=cost(2 * slots * slab, 6 * slab),
        name="pack_features",
    )(nodes, features)
    inbound = relay(packed)
    cot_packed, degree_packed, own_col, node_row, node_col = call(
        functools.partial(index_kernel, cap),
        out_shape=(
            shape(slots, width),
            shape(devices, cap, F32),
            shape(rows, 128, jnp.int32),
            shape(8, rows, jnp.int32),
            shape(rows, 128, jnp.int32),
        ),
        in_specs=[VMEM] * 4,
        out_specs=(VMEM,) * 5,
        cost_estimate=cost(2 * slots * slab, 6 * slab),
        name="index_cotangent",
    )(nodes, owner_position.reshape(1, rows), degree.reshape(1, rows), cotangent)
    degree_in = lax.all_to_all(degree_packed, everyone, split_axis=0, concat_axis=0, tiled=True)
    cot_in = relay(cot_packed)
    x_node = call(
        unpack_kernel,
        out_shape=shape(rows, width),
        in_specs=[VMEM] * 2,
        out_specs=VMEM,
        cost_estimate=cost(2 * slots * slab, 6 * slab),
        name="unpack_features",
    )(node_col, inbound)
    x_cols = lax.all_gather(x_node, "col", axis=0, tiled=True)

    def mask_spec(s):
        return pl.BlockSpec((1, breadth, tile, tile), lambda q, c, g, s=s: (g[s] * depth + q, 0, 0, 0))

    spmm_flops = 2 * masks.size * width
    partials = call(
        functools.partial(spmm_kernel, ways),
        grid_spec=pltpu.PrefetchScalarGridSpec(
            num_scalar_prefetch=2,
            grid=(depth,),
            in_specs=[VMEM] + [mask_spec(s) for s in range(ways)],
            out_specs=[pl.BlockSpec((tile, width), lambda q, c, g: (q, 0)) for s in range(ways)],
        ),
        out_shape=[shape(rows, width) for s in range(ways)],
        cost_estimate=cost(spmm_flops, 2 * masks.size + 2 * x_cols.size + 2 * ways * slab),
        name="spmm",
    )(cols, groups, x_cols, *([masks] * ways))
    terms = [partials[0]] + [across(partials[s], s) for s in range(1, ways)]
    row_block = rows // 2

    def by_rows(c):
        return pl.BlockSpec((row_block, c), lambda i: (i, 0))

    hidden, slopes, agg, spread = call(
        functools.partial(layer_kernel, ways),
        grid=(2,),
        out_shape=(shape(rows, width),) * 4,
        in_specs=[by_rows(width)] * (ways + 1) + [VMEM] * 2 + [by_rows(128)] + [VMEM] * 2,
        out_specs=(by_rows(width),) * 4,
        cost_estimate=cost(10 * slab * width, 2 * slab * (ways + 9)),
        name="layer",
    )(*terms, x_node, cot_in, degree_in, node_col, self_weight, neigh_weight)
    spreads = [spread] + [across(spread, s) for s in range(1, ways)]
    grads, own_back, hidden_packed = call(
        terms_kernel,
        out_shape=(shape(2 * width, width), shape(rows, width, F32), shape(slots, width)),
        in_specs=[VMEM] * 6,
        out_specs=(VMEM,) * 3,
        cost_estimate=cost(10 * slab * width, 2 * slab * 11),
        name="terms",
    )(x_node, agg, slopes, hidden, self_weight, node_row)
    hidden_in = relay(hidden_packed)
    back = call(
        functools.partial(spmm_back_kernel, ways),
        grid_spec=pltpu.PrefetchScalarGridSpec(
            num_scalar_prefetch=2,
            grid=(depth,),
            in_specs=[pl.BlockSpec((tile, width), lambda q, c, g: (q, 0)) for s in range(ways)]
            + [mask_spec(s) for s in range(ways)],
            out_specs=VMEM,
            scratch_shapes=[pltpu.VMEM(x_cols.shape, F32)],
        ),
        out_shape=shape(*x_cols.shape),
        cost_estimate=cost(spmm_flops, 2 * masks.size + 2 * x_cols.size + 2 * ways * slab),
        name="spmm_back",
    )(cols, groups, *spreads, *([masks] * ways))
    neigh_back = lax.psum_scatter(back, "col", scatter_dimension=0, tiled=True)
    grad_packed = call(
        join_kernel,
        out_shape=shape(slots, width),
        in_specs=[VMEM] * 3,
        out_specs=VMEM,
        cost_estimate=cost(2 * slots * slab, 8 * slab),
        name="join_pack",
    )(own_back, neigh_back, node_row)
    grad_in = relay(grad_packed)

    def unpack_own(value):
        return call(
            unpack_kernel,
            out_shape=shape(rows, width),
            in_specs=[VMEM] * 2,
            out_specs=VMEM,
            cost_estimate=cost(2 * slots * slab, 6 * slab),
            name="unpack_owner",
        )(own_col, value)

    hidden_own = unpack_own(hidden_in)
    grad_own = unpack_own(grad_in)

    parts = grads.reshape(ways, -1, width)
    kept = lax.dynamic_index_in_dim(parts, me, 0, keepdims=False).astype(F32)
    for s in range(1, ways):
        kept = kept + across(lax.dynamic_index_in_dim(parts, groups[s], 0, keepdims=False), s).astype(F32)
    pieces = kept.astype(BF).reshape(col_devices, -1, width)
    pieces = lax.all_to_all(pieces, "col", split_axis=0, concat_axis=0, tiled=True)
    scale = 1.0 / math.sqrt(rows * devices)
    mine = (jnp.sum(pieces.astype(F32), axis=0) * scale).astype(BF)
    whole = lax.all_gather(mine, ("row", "col"), axis=0, tiled=True).astype(F32)
    return (hidden_own, grad_own, whole[:width], whole[width:])


def solution(mesh):
    placed = (
        P(("row", "col"), None),
        P("row", "col", None, None),
        P("row", "col", None, None, None, None),
        P(("row", "col")),
        P(("row", "col")),
        P(("row", "col")),
        P(),
        P(),
        P(("row", "col"), None),
    )
    return jax.shard_map(
        on_device,
        mesh=mesh,
        in_specs=placed,
        out_specs=(P(("row", "col"), None), P(("row", "col"), None), P(), P()),
        check_vma=False,
    )
```

time: 610 us -> 332 us (0.54)
  waiting for transfers between devices: 347 us -> 200 us
  other arithmetic: 99.8 us -> 2.34 us
  matrix products: 49.1 us -> 0 us
  Pallas kernels: 0 us -> 46.5 us
  local copies, waits for them, and re-layouts: 53 us -> 9.68 us
  starting transfers between devices: 15.8 us -> 26.2 us
    psum x1 -> x0, waiting for transfers between devices: 142 us -> none  [on_device(): summed_grads = lax.psum((grad_terms[0], grad_terms[1]), ('row', 'col'))]
    reduce_scatter x2 -> x1, waiting for transfers between devices: 84 us -> 6.42 us  [on_device(): neigh_back = lax.psum_scatter(back, 'col', scatter_dimension=0, tiled=True)]
    scatter-add x4 -> x0, other arithmetic: 75.8 us -> none  [add_group(): totals.at[col_part.reshape(-1)]]
    ppermute x0 -> x9, waiting for transfers between devices: none -> 54.5 us  [across(): return lax.ppermute(value, 'row', [(i, i ^ s) for i in range(ways)])]
    dot_general x14 -> x0, matrix products: 49.1 us -> none  [the longest x4 23.3 us: add_group(): jnp.einsum('tkij,tif->tkjf', mask_part, row_part, preferred_element_type=...]
    pallas_call x0 -> x10, Pallas kernels: none -> 46.5 us  [the longest x1 10.4 us: on_device(): call(functools.partial(spmm_back_kernel, ways), grid_spec=pltpu.PrefetchS...]
    gather x8 -> x0, local copies, waits for them, and re-layouts: 29.8 us -> none  [the longest x4 19.9 us: one_group(): chosen = feat_tiles[operands[1]]]
    all_gather x2, waiting for transfers between devices: 71.3 us -> 94.2 us  [the longest x1 53 us: on_device(): x_cols = lax.all_gather(x_node, 'col', axis=0, tiled=True)]
  transfers between devices with their start and end apart: 8 -> 16, of which waited for: 7 -> 12; matrix products, arithmetic and copies ran while one was open for 3% -> 2% of each run, Pallas kernels for 0% -> 7%
where the time goes in v1:
time: 332 us; the launch traced here: 331 us
  waiting for transfers between devices  200 us (60%)
  Pallas kernels  46.5 us (14%)
  blocking collectives  26.9 us (8%)
  starting transfers between devices  26.2 us (8%)
  between operations  19.7 us (6%)
  local copies, waits for them, and re-layouts  9.68 us (3%)
    ppermute x9, waiting for transfers between devices, across(): return lax.ppermute(value, 'row', [(i, i ^ s) for i in range(ways)])  54.5 us
    all_gather x1, waiting for transfers between devices, on_device(): x_cols = lax.all_gather(x_node, 'col', axis=0, tiled=True)  53 us
    all_to_all x4, waiting for transfers between devices, relay(): lax.all_to_all(there, everyone, split_axis=0, concat_axis=0, tiled=True)  44.7 us
    all_gather x1, waiting for transfers between devices, on_device(): whole = lax.all_gather(mine, ('row', 'col'), axis=0, tiled=True).astype(F32)  41.2 us
    all_to_all x1, blocking collectives, on_device(): lax.all_to_all(pieces, 'col', split_axis=0, concat_axis=0, tiled=True)  16.7 us
    all_to_all x4, starting transfers between devices, relay(): lax.all_to_all(there, everyone, split_axis=0, concat_axis=0, tiled=True)  15.5 us
    ppermute x9, starting transfers between devices, across(): return lax.ppermute(value, 'row', [(i, i ^ s) for i in range(ways)])  10.6 us
    pallas_call x1, Pallas kernels, on_device(): call(functools.partial(spmm_back_kernel, ways), grid_spec=pltpu.PrefetchS...  10.4 us
  transfers between devices with their start and end apart: 16, of which 12 were waited for; matrix products, arithmetic and copies ran while one was open for 2% of the time, Pallas kernels for 7%

profile of v1, /device:TPU:0, one launch (start us, length us, event | category | flops | bytes accessed | tf_op | source)
XLA Modules:
  0.0 331.1 jit_solution(3185873472967409000)
XLA Ops:
  7.2 3.1 pack_features.1
  10.3 7.3 %all-to-all-start = ((bf16[32,32,512]{2,1,0:T(8,128)(2,1)}), bf16[32,32,512]{2,1,0:T(8,128)(2,1)S(1)}, u32[]{:S(2)}, u32[]{:S(2)}) async-start(bf16[32,32,512]{2,1,0:T(8,128)(2,1)} %bitcast.50), calls=%async_computation | async-start | bytes 2097152 | tf_op jit(solution)/shard_map/all_to_all | solution.py:205
  17.6 0.0 all-gather.3.cloned.1.call-start
  17.6 3.4 %index_cotangent.1 = (bf16[1024,512]{1,0:T(8,128)(2,1)}, f32[32,32]{1,0:T(8,128)}, s32[512,128]{1,0:T(8,128)}, s32[8,512]{1,0:T(8,128)}, s32[512,128]{1,0:T(8,128)}) custom-call(s32[1,512]{1,0:T(1,128)} %bitcast.54, s32[1,512]{1,0:T(1,128)} %bitcast.55, s32[1,512]{1,0:T(1,128)} %bitcast.56, bf16[512,512]{1,0:T(8,128)(2,1)} %cot_ref.1), custom_call_target="tpu_custom_call" | custom-call | flops 536870912 | bytes 1572864 | tf_op jit(solution)/shard_map/index_cotangent/pallas_call | solution.py:221
  21.1 24.1 %all-to-all-done = bf16[32,32,512]{2,1,0:T(8,128)(2,1)S(1)} async-done(((bf16[32,32,512]{2,1,0:T(8,128)(2,1)}), bf16[32,32,512]{2,1,0:T(8,128)(2,1)S(1)}, u32[]{:S(2)}, u32[]{:S(2)}) %all-to-all-start) | async-done | bytes 1048608 | tf_op jit(solution)/shard_map/all_to_all | solution.py:205
  45.2 1.0 copy-done.3
  46.2 2.9 unpack_features.1.refs_4_.x_ref
  49.0 0.0 all-gather.3.cloned.1.call-update
  49.0 10.2 %all_to_all.36 = f32[32,1,32]{2,1,0:T(1,128)} all-to-all(f32[32,1,32]{2,1,0:T(1,128)} %bitcast.52), channel_id=1, replica_groups=mesh['row'=4,'col'=8] {'row','col'}, dimensions={0} | all-to-all | bytes 8192 | tf_op jit(solution)/shard_map/all_to_all | solution.py:235
  59.2 2.6 all-to-all-start.1
  61.9 0.0 reduce-scatter.2.cloned.1.call-start
  61.9 0.0 copy-done.11
  61.9 0.1 copy.15
  62.0 0.6 reshape_squeeze.3.cols_ref
  62.6 0.6 iota_xor_fusion.group_ref
  63.2 53.0 %all-gather.3.cloned.1.call-done.x_ref = bf16[4096,512]{1,0:T(8,128)(2,1)} async-done(((bf16[512,512]{1,0:T(8,128)(2,1)}), bf16[4096,512]{1,0:T(8,128)(2,1)}) %all-gather.3.cloned.1.call-update) | async-done | bytes 4194320 | tf_op jit(solution)/shard_map/all_gather | solution.py:245
  116.2 7.5 %spmm.1 = (bf16[512,512]{1,0:T(8,128)(2,1)}, bf16[512,512]{1,0:T(8,128)(2,1)}, bf16[512,512]{1,0:T(8,128)(2,1)}, bf16[512,512]{1,0:T(8,128)(2,1)}) custom-call(s32[128]{0:T(128)} %reshape_squeeze.3.cols_ref, s32[4]{0:T(128)} %iota_xor_fusion.group_ref, bf16[4096,512]{1,0:T(8,128)(2,1)} %all-gather.3.cloned.1.call-done.x_ref, ...), custom_call_target="tpu_custom_call" | custom-call | flops 2147483648 | bytes 10485760 | tf_op jit(solution)/shard_map/spmm/pallas_call | solution.py:251
  123.7 1.5 collective-permute-start
  125.2 1.5 collective-permute-start.1
  126.7 0.6 collective-permute-start.2
  127.2 0.0 all-to-all-done.1
  127.2 11.5 %collective-permute-done.refs_1_ = bf16[512,512]{1,0:T(8,128)(2,1)S(1)} collective-permute-done((bf16[512,512]{1,0:T(8,128)(2,1)}, bf16[512,512]{1,0:T(8,128)(2,1)S(1)}, u32[]{:S(2)}, u32[]{:S(2)}) %collective-permute-start) | collective-permute-done | bytes 524320 | tf_op jit(solution)/shard_map/ppermute | solution.py:208
  138.7 11.7 %collective-permute-done.1.refs_2_ = bf16[512,512]{1,0:T(8,128)(2,1)S(1)} collective-permute-done((bf16[512,512]{1,0:T(8,128)(2,1)}, bf16[512,512]{1,0:T(8,128)(2,1)S(1)}, u32[]{:S(2)}, u32[]{:S(2)}) %collective-permute-start.1) | collective-permute-done | bytes 524320 | tf_op jit(solution)/shard_map/ppermute | solution.py:208
  150.4 0.0 collective-permute-done.2.refs_3_
  150.4 0.0 copy-done
  150.5 0.8 copy-done.5
  151.3 0.2 copy-done.6
  151.5 5.7 %layer.1 = (bf16[512,512]{1,0:T(8,128)(2,1)}, bf16[512,512]{1,0:T(8,128)(2,1)}, bf16[512,512]{1,0:T(8,128)(2,1)}, bf16[512,512]{1,0:T(8,128)(2,1)}) custom-call(bf16[512,512]{1,0:T(8,128)(2,1)} %get-tuple-element.22.refs_0_, bf16[512,512]{1,0:T(8,128)(2,1)} %copy-done.4, bf16[512,512]{1,0:T(8,128)(2,1)} %copy-done.5, bf16[512,512]{1,0:T(8,128)(2,1)} %copy-done.6, ...), custom_call_target="tpu_custom_call" | custom-call | flops 1342177280 | bytes 6815744 | tf_op jit(solution)/shard_map/layer/pallas_call | solution.py:269
  157.1 1.0 collective-permute-start.3
  158.2 1.1 collective-permute-start.4
  159.2 1.5 collective-permute-start.5
  160.7 11.6 %collective-permute-done.3.refs_1_ = bf16[512,512]{1,0:T(8,128)(2,1)S(1)} collective-permute-done((bf16[512,512]{1,0:T(8,128)(2,1)}, bf16[512,512]{1,0:T(8,128)(2,1)S(1)}, u32[]{:S(2)}, u32[]{:S(2)}) %collective-permute-start.3) | collective-permute-done | bytes 524320 | tf_op jit(solution)/shard_map/ppermute | solution.py:208
  172.3 8.6 %collective-permute-done.4.refs_2_ = bf16[512,512]{1,0:T(8,128)(2,1)S(1)} collective-permute-done((bf16[512,512]{1,0:T(8,128)(2,1)}, bf16[512,512]{1,0:T(8,128)(2,1)S(1)}, u32[]{:S(2)}, u32[]{:S(2)}) %collective-permute-start.4) | collective-permute-done | bytes 524320 | tf_op jit(solution)/shard_map/ppermute | solution.py:208
  180.8 1.7 collective-permute-done.5.refs_3_
  182.6 0.8 copy-done.9
  183.4 10.4 %spmm_back.1 = bf16[4096,512]{1,0:T(8,128)(2,1)} custom-call(s32[128]{0:T(128)} %reshape_squeeze.3.cols_ref, s32[4]{0:T(128)} %iota_xor_fusion.group_ref, bf16[512,512]{1,0:T(8,128)(2,1)} %get-tuple-element.34.refs_0_, bf16[512,512]{1,0:T(8,128)(2,1)} %copy-done.7, bf16[512,512]{1,0:T(8,128)(2,1)} %copy-done.8, bf16[512,512]{1,0:T(8,128)(2,1)} %copy-done.9, ...), custom_call_target="tpu_custom_call" | custom-call | flops 2147483648 | bytes 10485760 | tf_op jit(solution)/shard_map/spmm_back/pallas_call | solution.py:288
  193.8 0.0 reduce-scatter.2.cloned.1.call-update
  193.8 0.6 copy-done.10
  194.5 0.6 fusion.4
  200.9 4.6 %terms.1 = (bf16[1024,512]{1,0:T(8,128)(2,1)}, f32[512,512]{1,0:T(8,128)}, bf16[1024,512]{1,0:T(8,128)(2,1)}) custom-call(bf16[512,512]{1,0:T(8,128)(2,1)} %unpack_features.1.refs_4_.x_ref, bf16[512,512]{1,0:T(8,128)(2,1)} %get-tuple-element.28.agg_ref, bf16[512,512]{1,0:T(8,128)(2,1)} %get-tuple-element.29.slopes_ref, ...), custom_call_target="tpu_custom_call" | custom-call | flops 1342177280 | bytes 5767168 | tf_op jit(solution)/shard_map/terms/pallas_call | solution.py:279
  205.5 1.2 dynamic-slice_bitcast_fusion.2
  206.7 2.5 collective-permute-start.8
  209.2 0.4 collective-permute-start.7
  209.6 0.6 collective-permute-start.6
  210.3 6.6 %collective-permute-done.8 = bf16[256,512]{1,0:T(8,128)(2,1)S(1)} collective-permute-done((bf16[256,512]{1,0:T(8,128)(2,1)S(1)}, bf16[256,512]{1,0:T(8,128)(2,1)S(1)}, u32[]{:S(2)}, u32[]{:S(2)}) %collective-permute-start.8) | collective-permute-done | bytes 262176 | tf_op jit(solution)/shard_map/ppermute | solution.py:208
  216.9 2.8 collective-permute-done.7
  219.7 0.0 collective-permute-done.6
  219.7 1.1 fusion.2
  220.8 16.7 %all_to_all.37 = bf16[8,32,512]{2,1,0:T(8,128)(2,1)S(1)} all-to-all(bf16[8,32,512]{2,1,0:T(8,128)(2,1)S(1)} %bitcast.44), channel_id=1, replica_groups=mesh['row'=4,'col'=8] {'col'}, dimensions={0} | all-to-all | bytes 524288 | tf_op jit(solution)/shard_map/all_to_all | solution.py:331
  237.5 2.9 all-to-all-start.3
  240.4 0.0 all-gather.5.cloned.1.call-start
  240.4 0.6 multiply_convert_fusion
  241.1 0.0 all-gather.5.cloned.1.call-update
  241.1 6.4 %reduce-scatter.2.cloned.1.call-done.neigh_ref = bf16[512,512]{1,0:T(8,128)(2,1)} async-done(((bf16[4096,512]{1,0:T(8,128)(2,1)}), bf16[512,512]{1,0:T(8,128)(2,1)}) %reduce-scatter.2.cloned.1.call-update) | async-done | bytes 524304 | tf_op jit(solution)/shard_map/reduce_scatter | solution.py:302
  247.5 3.1 join_pack.1
  250.6 20.6 %all-to-all-done.3 = bf16[32,32,512]{2,1,0:T(8,128)(2,1)S(1)} async-done(((bf16[32,32,512]{2,1,0:T(8,128)(2,1)}), bf16[32,32,512]{2,1,0:T(8,128)(2,1)S(1)}, u32[]{:S(2)}, u32[]{:S(2)}) %all-to-all-start.3) | async-done | bytes 1048608 | tf_op jit(solution)/shard_map/all_to_all | solution.py:205
  271.2 2.6 all-to-all-start.4
  273.9 0.0 copy-done.1
  273.9 2.9 unpack_owner.2
  276.7 41.2 %all-gather.5.cloned.1.call-done = bf16[1024,512]{1,0:T(8,128)(2,1)} async-done(((bf16[32,512]{1,0:T(8,128)(2,1)}), bf16[1024,512]{1,0:T(8,128)(2,1)}) %all-gather.5.cloned.1.call-update) | async-done | bytes 1048592 | tf_op jit(solution)/shard_map/all_gather | solution.py:334
  317.9 2.8 fusion.3
  320.7 0.0 all-to-all-done.4
  320.7 1.0 copy-done.2
  321.7 2.9 unpack_owner.3
  (16 shorter events, 0.1 us)
Async XLA Ops:
  10.3 51.6 %copy-start.11 = (s32[1,1,16,8]{2,3,1,0:T(8,128)S(1)}, s32[1,1,16,8]{2,3,1,0:T(8,128)}, u32[]{:S(2)}) copy-start(s32[1,1,16,8]{2,3,1,0:T(8,128)} %param.10) | copy-start | bytes 1540
  10.3 34.9 %all-to-all-start = ((bf16[32,32,512]{2,1,0:T(8,128)(2,1)}), bf16[32,32,512]{2,1,0:T(8,128)(2,1)S(1)}, u32[]{:S(2)}, u32[]{:S(2)}) async-start(bf16[32,32,512]{2,1,0:T(8,128)(2,1)} %bitcast.50), calls=%async_computation | async-start | bytes 2097152 | tf_op jit(solution)/shard_map/all_to_all | solution.py:205
  17.6 98.6 %all-gather.3.cloned.1.call-start = ((), (), s32[]{:S(2)}) async-start(), calls=%async_computation.7 | async-start | bytes 4718592 | tf_op jit(solution)/shard_map/all_gather | solution.py:245
  45.2 1.0 copy-start.3
  59.2 68.0 %all-to-all-start.1 = ((bf16[32,32,512]{2,1,0:T(8,128)(2,1)}), bf16[32,32,512]{2,1,0:T(8,128)(2,1)S(1)}, u32[]{:S(2)}, u32[]{:S(2)}) async-start(bf16[32,32,512]{2,1,0:T(8,128)(2,1)} %bitcast.46), calls=%async_computation.1 | async-start | bytes 2097152 | tf_op jit(solution)/shard_map/all_to_all | solution.py:205
  61.9 185.6 %reduce-scatter.2.cloned.1.call-start = ((), (), s32[]{:S(2)}) async-start(), calls=%async_computation.8 | async-start | bytes 4718592 | tf_op jit(solution)/shard_map/reduce_scatter | solution.py:302
  123.7 15.0 %collective-permute-start = (bf16[512,512]{1,0:T(8,128)(2,1)}, bf16[512,512]{1,0:T(8,128)(2,1)S(1)}, u32[]{:S(2)}, u32[]{:S(2)}) collective-permute-start(bf16[512,512]{1,0:T(8,128)(2,1)} %get-tuple-element.23), channel_id=1, source_target_pairs={{0,8},{8,0},{16,24},{24,16},{1,9},{9,1},{17,25},{25,17},{2,10},{10... | collective-permute-start | bytes 1572872 | tf_op jit(solution)/shard_map/ppermute | solution.py:208
  125.2 25.2 %collective-permute-start.1 = (bf16[512,512]{1,0:T(8,128)(2,1)}, bf16[512,512]{1,0:T(8,128)(2,1)S(1)}, u32[]{:S(2)}, u32[]{:S(2)}) collective-permute-start(bf16[512,512]{1,0:T(8,128)(2,1)} %get-tuple-element.24), channel_id=1, source_target_pairs={{0,16},{8,24},{16,0},{24,8},{1,17},{9,25},{17,1},{25,9},{2,18},{10... | collective-permute-start | bytes 1572872 | tf_op jit(solution)/shard_map/ppermute | solution.py:208
  126.7 23.8 %collective-permute-start.2 = (bf16[512,512]{1,0:T(8,128)(2,1)}, bf16[512,512]{1,0:T(8,128)(2,1)S(1)}, u32[]{:S(2)}, u32[]{:S(2)}) collective-permute-start(bf16[512,512]{1,0:T(8,128)(2,1)} %get-tuple-element.25), channel_id=1, source_target_pairs={{0,24},{8,16},{16,8},{24,0},{1,25},{9,17},{17,9},{25,1},{2,26},{10... | collective-permute-start | bytes 1572872 | tf_op jit(solution)/shard_map/ppermute | solution.py:208
  127.2 23.2 %copy-start = (bf16[32,32,512]{2,1,0:T(8,128)(2,1)}, bf16[32,32,512]{2,1,0:T(8,128)(2,1)S(1)}, u32[]{:S(2)}) copy-start(bf16[32,32,512]{2,1,0:T(8,128)(2,1)S(1)} %all-to-all-done.1) | copy-start | bytes 3145732
  138.7 11.7 %copy-start.4 = (bf16[512,512]{1,0:T(8,128)(2,1)}, bf16[512,512]{1,0:T(8,128)(2,1)S(1)}, u32[]{:S(2)}) copy-start(bf16[512,512]{1,0:T(8,128)(2,1)S(1)} %collective-permute-done.refs_1_) | copy-start | bytes 1572868
  150.4 0.8 copy-start.5
  150.4 1.0 copy-start.6
  157.1 15.1 %collective-permute-start.3 = (bf16[512,512]{1,0:T(8,128)(2,1)}, bf16[512,512]{1,0:T(8,128)(2,1)S(1)}, u32[]{:S(2)}, u32[]{:S(2)}) collective-permute-start(bf16[512,512]{1,0:T(8,128)(2,1)} %get-tuple-element.34.refs_0_), channel_id=1, source_target_pairs={{0,8},{8,0},{16,24},{24,16},{1,9},{9,1},{17,25},{25,17},{2,10},{10... | collective-permute-start | bytes 1572872 | tf_op jit(solution)/shard_map/ppermute | solution.py:208
  158.2 22.7 %collective-permute-start.4 = (bf16[512,512]{1,0:T(8,128)(2,1)}, bf16[512,512]{1,0:T(8,128)(2,1)S(1)}, u32[]{:S(2)}, u32[]{:S(2)}) collective-permute-start(bf16[512,512]{1,0:T(8,128)(2,1)} %get-tuple-element.34.refs_0_), channel_id=1, source_target_pairs={{0,16},{8,24},{16,0},{24,8},{1,17},{9,25},{17,1},{25,9},{2,18},{10... | collective-permute-start | bytes 1572872 | tf_op jit(solution)/shard_map/ppermute | solution.py:208
  159.2 23.3 %collective-permute-start.5 = (bf16[512,512]{1,0:T(8,128)(2,1)}, bf16[512,512]{1,0:T(8,128)(2,1)S(1)}, u32[]{:S(2)}, u32[]{:S(2)}) collective-permute-start(bf16[512,512]{1,0:T(8,128)(2,1)} %get-tuple-element.34.refs_0_), channel_id=1, source_target_pairs={{0,24},{8,16},{16,8},{24,0},{1,25},{9,17},{17,9},{25,1},{2,26},{10... | collective-permute-start | bytes 1572872 | tf_op jit(solution)/shard_map/ppermute | solution.py:208
  172.3 10.3 %copy-start.7 = (bf16[512,512]{1,0:T(8,128)(2,1)}, bf16[512,512]{1,0:T(8,128)(2,1)S(1)}, u32[]{:S(2)}) copy-start(bf16[512,512]{1,0:T(8,128)(2,1)S(1)} %collective-permute-done.3.refs_1_) | copy-start | bytes 1572868
  180.8 1.7 copy-start.8
  182.6 0.8 copy-start.9
  193.8 0.7 copy-start.10
  206.7 10.2 %collective-permute-start.8 = (bf16[256,512]{1,0:T(8,128)(2,1)S(1)}, bf16[256,512]{1,0:T(8,128)(2,1)S(1)}, u32[]{:S(2)}, u32[]{:S(2)}) collective-permute-start(bf16[256,512]{1,0:T(8,128)(2,1)S(1)} %get-tuple-element.39), channel_id=1, source_target_pairs={{0,24},{8,16},{16,8},{24,0},{1,25},{9,17},{17,9},{25,1},{2,26},{10... | collective-permute-start | bytes 786440 | tf_op jit(solution)/shard_map/ppermute | solution.py:208
  209.2 10.4 %collective-permute-start.7 = (bf16[256,512]{1,0:T(8,128)(2,1)S(1)}, bf16[256,512]{1,0:T(8,128)(2,1)S(1)}, u32[]{:S(2)}, u32[]{:S(2)}) collective-permute-start(bf16[256,512]{1,0:T(8,128)(2,1)S(1)} %get-tuple-element.40), channel_id=1, source_target_pairs={{0,16},{8,24},{16,0},{24,8},{1,17},{9,25},{17,1},{25,9},{2,18},{10... | collective-permute-start | bytes 786440 | tf_op jit(solution)/shard_map/ppermute | solution.py:208
  209.6 10.0 %collective-permute-start.6 = (bf16[256,512]{1,0:T(8,128)(2,1)S(1)}, bf16[256,512]{1,0:T(8,128)(2,1)S(1)}, u32[]{:S(2)}, u32[]{:S(2)}) collective-permute-start(bf16[256,512]{1,0:T(8,128)(2,1)S(1)} %get-tuple-element.38), channel_id=1, source_target_pairs={{0,8},{8,0},{16,24},{24,16},{1,9},{9,1},{17,25},{25,17},{2,10},{10... | collective-permute-start | bytes 786440 | tf_op jit(solution)/shard_map/ppermute | solution.py:208
  237.5 33.7 %all-to-all-start.3 = ((bf16[32,32,512]{2,1,0:T(8,128)(2,1)}), bf16[32,32,512]{2,1,0:T(8,128)(2,1)S(1)}, u32[]{:S(2)}, u32[]{:S(2)}) async-start(bf16[32,32,512]{2,1,0:T(8,128)(2,1)} %bitcast.45), calls=%async_computation.3 | async-start | bytes 2097152 | tf_op jit(solution)/shard_map/all_to_all | solution.py:205
  240.4 77.5 %all-gather.5.cloned.1.call-start = ((), (), s32[]{:S(2)}) async-start(), calls=%async_computation.9 | async-start | bytes 1081344 | tf_op jit(solution)/shard_map/all_gather | solution.py:334
  271.2 2.7 copy-start.1
  271.2 49.5 %all-to-all-start.4 = ((bf16[32,32,512]{2,1,0:T(8,128)(2,1)}), bf16[32,32,512]{2,1,0:T(8,128)(2,1)S(1)}, u32[]{:S(2)}, u32[]{:S(2)}) async-start(bf16[32,32,512]{2,1,0:T(8,128)(2,1)} %bitcast.41), calls=%async_computation.5 | async-start | bytes 2097152 | tf_op jit(solution)/shard_map/all_to_all | solution.py:205
  320.7 1.0 copy-start.2
Sparse Core Ops, SparseCore 0:
  49.2 67.0 all-gather.2
  193.9 53.5 reduce-scatter.1
  251.1 66.7 all-gather.4

commit v2 on v1

--- a/solution.py
+++ b/solution.py
@@ -66,16 +66,15 @@
     out_ref[...] = dot(slots_onehot(dest * cap + rank, out_ref.shape[0]), value_ref[...]).astype(BF)
 
 
-def index_kernel(cap, nodes_ref, position_ref, degree_ref, cot_ref, cot_out, degree_out, own_col, node_row, node_col):
-    devices, _ = degree_out.shape
+def index_kernel(cap, nodes_ref, position_ref, degree_ref, cot_ref, cot_out, own_col, node_row, node_col):
     n = nodes_ref.shape[1]
+    width = cot_ref.shape[1]
     dest, rank = own_slots(nodes_ref[...], cap)
     flat = dest * cap + rank
     own_col[...] = as_column(flat)
-    cot_out[...] = dot(slots_onehot(flat, cot_out.shape[0]), cot_ref[...]).astype(BF)
-    by_dest = jnp.where(lax.broadcasted_iota(jnp.int32, (devices, n), 0) == dest, degree_ref[...].astype(F32), 0.0)
-    by_rank = entries_onehot(as_column(rank), cap)
-    degree_out[...] = dot(by_dest.astype(BF), by_rank)
+    packing = slots_onehot(flat, cot_out.shape[0])
+    cot_out[:, :width] = dot(packing, cot_ref[...]).astype(BF)
+    cot_out[:, width:] = dot(packing, as_column(degree_ref[...].astype(F32)).astype(BF)).astype(BF)
     position = position_ref[...]
     source = block_of(position, n)
     place = source * cap + rank_row(source, position)
@@ -87,23 +86,21 @@
     out_ref[...] = dot(entries_onehot(col_ref[...], value_ref.shape[0]), value_ref[...]).astype(BF)
 
 
-def spmm_kernel(ways, cols_ref, group_ref, x_ref, *refs):
-    masks, outs = refs[:ways], refs[ways:]
+def spmm_kernel(way, cols_ref, group_ref, x_ref, masks_ref, out_ref):
     q = pl.program_id(0)
     depth = pl.num_programs(0)
-    _, breadth, tile, _ = masks[0].shape
-    for s in range(ways):
-        base = (group_ref[s] * depth + q) * breadth
-        total = None
-        for p in range(0, breadth, 2):
-            width = min(2, breadth - p)
-            left = jnp.concatenate([masks[s][0, p + w] for w in range(width)], axis=1)
-            right = jnp.concatenate(
-                [x_ref[pl.ds(pl.multiple_of(cols_ref[base + p + w] * tile, tile), tile), :] for w in range(width)], axis=0
-            )
-            term = dot(left, right)
-            total = term if total is None else total + term
-        outs[s][...] = total.astype(BF)
+    _, breadth, tile, _ = masks_ref.shape
+    base = (group_ref[way] * depth + q) * breadth
+    total = None
+    for p in range(0, breadth, 2):
+        width = min(2, breadth - p)
+        left = jnp.concatenate([masks_ref[0, p + w] for w in range(width)], axis=1)
+        right = jnp.concatenate(
+            [x_ref[pl.ds(pl.multiple_of(cols_ref[base + p + w] * tile, tile), tile), :] for w in range(width)], axis=0
+        )
+        term = dot(left, right)
+        total = term if total is None else total + term
+    out_ref[...] = total.astype(BF)
 
 
 def spmm_back_kernel(ways, cols_ref, group_ref, *refs):
@@ -130,27 +127,19 @@
 
 def layer_kernel(ways, *refs):
     terms = refs[:ways]
-    (x_ref, cot_ref, degree_ref, col_ref, self_ref, neigh_ref, hidden_out, slopes_out, agg_out, spread_out) = refs[ways:]
-    devices, cap = degree_ref.shape
-    slots = cot_ref.shape[0]
-    place = col_ref[...][:, :1]
-    rows = place.shape[0]
+    (x_ref, cot_ref, col_ref, self_ref, neigh_ref, hidden_out, slopes_out, agg_out, spread_out) = refs[ways:]
+    width = x_ref.shape[1]
     summed = terms[0][...].astype(F32)
     for s in range(1, ways):
         summed = summed + terms[s][...].astype(F32)
-    source = block_of(place, cap)
-    rank = place - source * cap
-    by_source = entries_onehot(source, devices)
-    degrees = dot(by_source, degree_ref[...].astype(BF))
-    picked = lax.broadcasted_iota(jnp.int32, (rows, cap), 1) == rank
-    degrees = jnp.sum(jnp.where(picked, degrees, 0.0), axis=1, keepdims=True)
+    cot = dot(entries_onehot(col_ref[...], cot_ref.shape[0]), cot_ref[...])
+    degrees = cot[:, width : width + 1]
     agg = (summed / degrees).astype(BF)
     agg_out[...] = agg
     preact = dot(x_ref[...], self_ref[...]) + dot(agg, neigh_ref[...])
     gate = jax.nn.sigmoid(preact)
     hidden_out[...] = (preact * gate).astype(BF)
-    cot = dot(entries_onehot(place, slots), cot_ref[...])
-    slopes = (cot * gate * (1.0 + preact * (1.0 - gate))).astype(BF)
+    slopes = (cot[:, :width] * gate * (1.0 + preact * (1.0 - gate))).astype(BF)
     slopes_out[...] = slopes
     spread_out[...] = (dot(slopes, neigh_ref[...], 1, 1) / degrees).astype(BF)
 
@@ -218,22 +207,19 @@
         name="pack_features",
     )(nodes, features)
     inbound = relay(packed)
-    cot_packed, degree_packed, own_col, node_row, node_col = call(
+    cot_packed, own_col, node_row, node_col = call(
         functools.partial(index_kernel, cap),
         out_shape=(
-            shape(slots, width),
-            shape(devices, cap, F32),
+            shape(slots, width + 128),
             shape(rows, 128, jnp.int32),
             shape(8, rows, jnp.int32),
             shape(rows, 128, jnp.int32),
         ),
         in_specs=[VMEM] * 4,
-        out_specs=(VMEM,) * 5,
+        out_specs=(VMEM,) * 4,
         cost_estimate=cost(2 * slots * slab, 6 * slab),
         name="index_cotangent",
     )(nodes, owner_position.reshape(1, rows), degree.reshape(1, rows), cotangent)
-    degree_in = lax.all_to_all(degree_packed, everyone, split_axis=0, concat_axis=0, tiled=True)
-    cot_in = relay(cot_packed)
     x_node = call(
         unpack_kernel,
         out_shape=shape(rows, width),
@@ -243,24 +229,29 @@
         name="unpack_features",
     )(node_col, inbound)
     x_cols = lax.all_gather(x_node, "col", axis=0, tiled=True)
+    x_cols, cot_packed = lax.optimization_barrier((x_cols, cot_packed))
+    cot_in = relay(cot_packed)
 
     def mask_spec(s):
         return pl.BlockSpec((1, breadth, tile, tile), lambda q, c, g, s=s: (g[s] * depth + q, 0, 0, 0))
 
     spmm_flops = 2 * masks.size * width
-    partials = call(
-        functools.partial(spmm_kernel, ways),
-        grid_spec=pltpu.PrefetchScalarGridSpec(
-            num_scalar_prefetch=2,
-            grid=(depth,),
-            in_specs=[VMEM] + [mask_spec(s) for s in range(ways)],
-            out_specs=[pl.BlockSpec((tile, width), lambda q, c, g: (q, 0)) for s in range(ways)],
-        ),
-        out_shape=[shape(rows, width) for s in range(ways)],
-        cost_estimate=cost(spmm_flops, 2 * masks.size + 2 * x_cols.size + 2 * ways * slab),
-        name="spmm",
-    )(cols, groups, x_cols, *([masks] * ways))
-    terms = [partials[0]] + [across(partials[s], s) for s in range(1, ways)]
+    def spmm(way):
+        partial = call(
+            functools.partial(spmm_kernel, way),
+            grid_spec=pltpu.PrefetchScalarGridSpec(
+                num_scalar_prefetch=2,
+                grid=(depth,),
+                in_specs=[VMEM, mask_spec(way)],
+                out_specs=pl.BlockSpec((tile, width), lambda q, c, g: (q, 0)),
+            ),
+            out_shape=shape(rows, width),
+            cost_estimate=cost(spmm_flops // ways, 2 * masks.size // ways + 2 * x_cols.size + 2 * slab),
+            name="spmm_%d" % way,
+        )(cols, groups, x_cols, masks)
+        return across(partial, way) if way else partial
+
+    terms = [spmm(way) for way in range(ways - 1, -1, -1)]
     row_block = rows // 2
 
     def by_rows(c):
@@ -270,12 +261,11 @@
         functools.partial(layer_kernel, ways),
         grid=(2,),
         out_shape=(shape(rows, width),) * 4,
-        in_specs=[by_rows(width)] * (ways + 1) + [VMEM] * 2 + [by_rows(128)] + [VMEM] * 2,
+        in_specs=[by_rows(width)] * (ways + 1) + [VMEM, by_rows(128)] + [VMEM] * 2,
         out_specs=(by_rows(width),) * 4,
         cost_estimate=cost(10 * slab * width, 2 * slab * (ways + 9)),
         name="layer",
-    )(*terms, x_node, cot_in, degree_in, node_col, self_weight, neigh_weight)
-    spreads = [spread] + [across(spread, s) for s in range(1, ways)]
+    )(*terms, x_node, cot_in, node_col, self_weight, neigh_weight)
     grads, own_back, hidden_packed = call(
         terms_kernel,
         out_shape=(shape(2 * width, width), shape(rows, width, F32), shape(slots, width)),
@@ -285,6 +275,8 @@
         name="terms",
     )(x_node, agg, slopes, hidden, self_weight, node_row)
     hidden_in = relay(hidden_packed)
+    spreads = [spread] + [across(spread, s) for s in range(1, ways)]
+    *spreads, own_back = lax.optimization_barrier((*spreads, own_back))
     back = call(
         functools.partial(spmm_back_kernel, ways),
         grid_spec=pltpu.PrefetchScalarGridSpec(
@@ -299,6 +291,7 @@
         cost_estimate=cost(spmm_flops, 2 * masks.size + 2 * x_cols.size + 2 * ways * slab),
         name="spmm_back",
     )(cols, groups, *spreads, *([masks] * ways))
+    back, grads, hidden_in = lax.optimization_barrier((back, grads, hidden_in))
     neigh_back = lax.psum_scatter(back, "col", scatter_dimension=0, tiled=True)
     grad_packed = call(
         join_kernel,
@@ -323,15 +316,24 @@
     hidden_own = unpack_own(hidden_in)
     grad_own = unpack_own(grad_in)
 
+    place = lax.axis_index("col")
+    others = jnp.bitwise_xor(place, jnp.arange(col_devices, dtype=jnp.int32)).astype(jnp.int32)
+
+    def along(value, s):
+        return lax.ppermute(value, "col", [(i, i ^ s) for i in range(col_devices)])
+
+    def pick(value, at):
+        return lax.dynamic_index_in_dim(value, at, 0, keepdims=False)
+
     parts = grads.reshape(ways, -1, width)
-    kept = lax.dynamic_index_in_dim(parts, me, 0, keepdims=False).astype(F32)
-    for s in range(1, ways):
-        kept = kept + across(lax.dynamic_index_in_dim(parts, groups[s], 0, keepdims=False), s).astype(F32)
+    kept = [pick(parts, me)] + [across(pick(parts, groups[s]), s) for s in range(1, ways)]
+    kept = sum(term.astype(F32) for term in kept)
     pieces = kept.astype(BF).reshape(col_devices, -1, width)
-    pieces = lax.all_to_all(pieces, "col", split_axis=0, concat_axis=0, tiled=True)
+    mine = [pick(pieces, place)] + [along(pick(pieces, others[s]), s) for s in range(1, col_devices)]
     scale = 1.0 / math.sqrt(rows * devices)
-    mine = (jnp.sum(pieces.astype(F32), axis=0) * scale).astype(BF)
-    whole = lax.all_gather(mine, ("row", "col"), axis=0, tiled=True).astype(F32)
+    mine = (sum(term.astype(F32) for term in mine) * scale).astype(BF)
+    in_row = jnp.stack([mine] + [along(mine, s) for s in range(1, col_devices)])[others].reshape(-1, width)
+    whole = jnp.stack([in_row] + [across(in_row, s) for s in range(1, ways)])[groups].reshape(-1, width).astype(F32)
     return (hidden_own, grad_own, whole[:width], whole[width:])
 
 

time: 332 us -> 330 us (level)
  waiting for transfers between devices: 200 us -> 166 us
  blocking collectives: 26.9 us -> 0 us
  starting transfers between devices: 26.2 us -> 52.5 us
  Pallas kernels: 46.5 us -> 63.2 us
  between operations: 19.7 us -> 33.2 us
    all_gather x1 -> x0, waiting for transfers between devices: 41.2 us -> none  [on_device(): whole = lax.all_gather(mine, ('row', 'col'), axis=0, tiled=True).astype(F32)]
    all_to_all x2 -> x0, blocking collectives: 26.9 us -> none  [the longest x1 16.7 us: on_device(): lax.all_to_all(pieces, 'col', split_axis=0, concat_axis=0, tiled=True)]
    ppermute x0 -> x14, waiting for transfers between devices: none -> 24.2 us  [along(): return lax.ppermute(value, 'col', [(i, i ^ s) for i in range(col_devices)])]
    all_to_all x4, waiting for transfers between devices: 44.7 us -> 23.9 us  [relay(): lax.all_to_all(there, everyone, split_axis=0, concat_axis=0, tiled=True)]
    ppermute x0 -> x14, starting transfers between devices: none -> 19.1 us  [along(): return lax.ppermute(value, 'col', [(i, i ^ s) for i in range(col_devices)])]
    pallas_call x2 -> x5, Pallas kernels: 11 us -> 27.3 us  [the longest x4 23.7 us: spmm(): call(functools.partial(spmm_kernel, way), grid_spec=pltpu.PrefetchScalarG...]
    ppermute x9 -> x12, waiting for transfers between devices: 54.5 us -> 63.7 us  [across(): return lax.ppermute(value, 'row', [(i, i ^ s) for i in range(ways)])]
    all_gather x1, waiting for transfers between devices: 53 us -> 44.9 us  [on_device(): x_cols = lax.all_gather(x_node, 'col', axis=0, tiled=True)]
  transfers between devices with their start and end apart: 16 -> 32, of which waited for: 12 -> 14; matrix products, arithmetic and copies ran while one was open for 2% -> 2% of each run, Pallas kernels for 7% -> 13%
where the time goes in v2:
time: 330 us; the launch traced here: 327 us
  waiting for transfers between devices  166 us (50%)
  Pallas kernels  63.2 us (19%)
  starting transfers between devices  52.5 us (16%)
  between operations  33.2 us (10%)
  local copies, waits for them, and re-layouts  9.58 us (3%)
    ppermute x12, waiting for transfers between devices, across(): return lax.ppermute(value, 'row', [(i, i ^ s) for i in range(ways)])  63.7 us
    all_gather x1, waiting for transfers between devices, on_device(): x_cols = lax.all_gather(x_node, 'col', axis=0, tiled=True)  44.9 us
    ppermute x14, waiting for transfers between devices, along(): return lax.ppermute(value, 'col', [(i, i ^ s) for i in range(col_devices)])  24.2 us
    all_to_all x4, waiting for transfers between devices, relay(): lax.all_to_all(there, everyone, split_axis=0, concat_axis=0, tiled=True)  23.9 us
    pallas_call x4, Pallas kernels, spmm(): call(functools.partial(spmm_kernel, way), grid_spec=pltpu.PrefetchScalarG...  23.7 us
    ppermute x14, starting transfers between devices, along(): return lax.ppermute(value, 'col', [(i, i ^ s) for i in range(col_devices)])  19.1 us
    all_to_all x4, starting transfers between devices, relay(): lax.all_to_all(there, everyone, split_axis=0, concat_axis=0, tiled=True)  19 us
    ppermute x12, starting transfers between devices, across(): return lax.ppermute(value, 'row', [(i, i ^ s) for i in range(ways)])  14.1 us
  transfers between devices with their start and end apart: 32, of which 14 were waited for; matrix products, arithmetic and copies ran while one was open for 2% of the time, Pallas kernels for 13%

profile of v2, /device:TPU:0, one launch (start us, length us, event | category | flops | bytes accessed | tf_op | source)
XLA Modules:
  0.0 326.6 jit_solution(11439430416319014550)
XLA Ops:
  7.2 3.1 pack_features.1
  10.3 7.3 %all-to-all-start = ((bf16[32,32,512]{2,1,0:T(8,128)(2,1)}), bf16[32,32,512]{2,1,0:T(8,128)(2,1)S(1)}, u32[]{:S(2)}, u32[]{:S(2)}) async-start(bf16[32,32,512]{2,1,0:T(8,128)(2,1)} %bitcast.99), calls=%async_computation | async-start | bytes 2097152 | tf_op jit(solution)/shard_map/all_to_all | solution.py:194
  17.7 3.7 %index_cotangent.1 = (bf16[1024,640]{1,0:T(8,128)(2,1)}, s32[512,128]{1,0:T(8,128)}, s32[8,512]{1,0:T(8,128)}, s32[512,128]{1,0:T(8,128)}) custom-call(s32[1,512]{1,0:T(1,128)} %bitcast.110, s32[1,512]{1,0:T(1,128)} %bitcast.111, s32[1,512]{1,0:T(1,128)} %bitcast.112, bf16[512,512]{1,0:T(8,128)(2,1)} %cot_ref.1), custom_call_target="tpu_custom_call" | custom-call | flops 536870912 | bytes 1572864 | tf_op jit(solution)/shard_map/index_cotangent/pallas_call | solution.py:210
  21.3 23.9 %all-to-all-done = bf16[32,32,512]{2,1,0:T(8,128)(2,1)S(1)} async-done(((bf16[32,32,512]{2,1,0:T(8,128)(2,1)}), bf16[32,32,512]{2,1,0:T(8,128)(2,1)S(1)}, u32[]{:S(2)}, u32[]{:S(2)}) %all-to-all-start) | async-done | bytes 1048608 | tf_op jit(solution)/shard_map/all_to_all | solution.py:194
  45.2 1.0 copy-done.4
  46.2 2.9 unpack_features.1.refs_4_.x_ref
  49.0 44.9 %all-gather.2.cloned.1.call-done.x_ref = bf16[4096,512]{1,0:T(8,128)(2,1)} async-done(((bf16[512,512]{1,0:T(8,128)(2,1)}), bf16[4096,512]{1,0:T(8,128)(2,1)}) %all-gather.2.cloned.1.call-update) | async-done | bytes 4194320 | tf_op jit(solution)/shard_map/all_gather | solution.py:231
  94.0 3.3 %all-to-all-start.1 = ((bf16[32,32,640]{2,1,0:T(8,128)(2,1)}), bf16[32,32,640]{2,1,0:T(8,128)(2,1)S(1)}, u32[]{:S(2)}, u32[]{:S(2)}) async-start(bf16[32,32,640]{2,1,0:T(8,128)(2,1)} %bitcast.90), calls=%async_computation.1 | async-start | bytes 2621440 | tf_op jit(solution)/shard_map/all_to_all | solution.py:194
  97.4 0.6 reshape_squeeze.3.cols_ref
  98.0 0.6 iota_xor_fusion.1.group_ref
  98.6 5.9 %spmm_3.1 = bf16[512,512]{1,0:T(8,128)(2,1)} custom-call(s32[128]{0:T(128)} %reshape_squeeze.3.cols_ref, s32[4]{0:T(128)} %iota_xor_fusion.1.group_ref, bf16[4096,512]{1,0:T(8,128)(2,1)} %all-gather.2.cloned.1.call-done.x_ref, bf16[16,8,128,128]{3,2,1,0:T(8,128)(2,1)} %bitcast.80), custom_call_target="tpu_custom_call" | custom-call | flops 536870912 | bytes 5767168 | tf_op jit(solution)/shard_map/spmm_3/pallas_call | solution.py:240
  104.5 5.9 %spmm_2.1 = bf16[512,512]{1,0:T(8,128)(2,1)} custom-call(s32[128]{0:T(128)} %reshape_squeeze.3.cols_ref, s32[4]{0:T(128)} %iota_xor_fusion.1.group_ref, bf16[4096,512]{1,0:T(8,128)(2,1)} %all-gather.2.cloned.1.call-done.x_ref, bf16[16,8,128,128]{3,2,1,0:T(8,128)(2,1)} %bitcast.81), custom_call_target="tpu_custom_call" | custom-call | flops 536870912 | bytes 5767168 | tf_op jit(solution)/shard_map/spmm_2/pallas_call | solution.py:240
  110.3 6.0 %spmm_1.1 = bf16[512,512]{1,0:T(8,128)(2,1)} custom-call(s32[128]{0:T(128)} %reshape_squeeze.3.cols_ref, s32[4]{0:T(128)} %iota_xor_fusion.1.group_ref, bf16[4096,512]{1,0:T(8,128)(2,1)} %all-gather.2.cloned.1.call-done.x_ref, bf16[16,8,128,128]{3,2,1,0:T(8,128)(2,1)} %bitcast.82), custom_call_target="tpu_custom_call" | custom-call | flops 536870912 | bytes 5767168 | tf_op jit(solution)/shard_map/spmm_1/pallas_call | solution.py:240
  116.3 2.7 collective-permute-start
  119.0 0.6 collective-permute-start.1
  119.8 5.9 %spmm_0.1.refs_3_ = bf16[512,512]{1,0:T(8,128)(2,1)} custom-call(s32[128]{0:T(128)} %reshape_squeeze.3.cols_ref, s32[4]{0:T(128)} %iota_xor_fusion.1.group_ref, bf16[4096,512]{1,0:T(8,128)(2,1)} %all-gather.2.cloned.1.call-done.x_ref, bf16[16,8,128,128]{3,2,1,0:T(8,128)(2,1)} %bitcast.83), custom_call_target="tpu_custom_call" | custom-call | flops 536870912 | bytes 5767168 | tf_op jit(solution)/shard_map/spmm_0/pallas_call | solution.py:240
  125.7 9.5 %collective-permute-done.refs_0_ = bf16[512,512]{1,0:T(8,128)(2,1)S(1)} collective-permute-done((bf16[512,512]{1,0:T(8,128)(2,1)S(1)}, bf16[512,512]{1,0:T(8,128)(2,1)S(1)}, u32[]{:S(2)}, u32[]{:S(2)}) %collective-permute-start) | collective-permute-done | bytes 524320 | tf_op jit(solution)/shard_map/ppermute | solution.py:197
  135.3 10.2 %collective-permute-done.1.refs_1_ = bf16[512,512]{1,0:T(8,128)(2,1)S(1)} collective-permute-done((bf16[512,512]{1,0:T(8,128)(2,1)S(1)}, bf16[512,512]{1,0:T(8,128)(2,1)S(1)}, u32[]{:S(2)}, u32[]{:S(2)}) %collective-permute-start.1) | collective-permute-done | bytes 524320 | tf_op jit(solution)/shard_map/ppermute | solution.py:197
  145.7 0.6 copy-done.7
  146.9 5.9 %layer.1 = (bf16[512,512]{1,0:T(8,128)(2,1)}, bf16[512,512]{1,0:T(8,128)(2,1)}, bf16[512,512]{1,0:T(8,128)(2,1)}, bf16[512,512]{1,0:T(8,128)(2,1)}) custom-call(bf16[512,512]{1,0:T(8,128)(2,1)} %copy-done.6, bf16[512,512]{1,0:T(8,128)(2,1)} %copy-done.7, bf16[512,512]{1,0:T(8,128)(2,1)} %copy-done.8, bf16[512,512]{1,0:T(8,128)(2,1)} %spmm_0.1.refs_3_, ...), custom_call_target="tpu_custom_call" | custom-call | flops 1342177280 | bytes 6815744 | tf_op jit(solution)/shard_map/layer/pallas_call | solution.py:260
  152.8 4.7 %terms.1 = (bf16[1024,512]{1,0:T(8,128)(2,1)}, f32[512,512]{1,0:T(8,128)}, bf16[1024,512]{1,0:T(8,128)(2,1)}) custom-call(bf16[512,512]{1,0:T(8,128)(2,1)} %unpack_features.1.refs_4_.x_ref, bf16[512,512]{1,0:T(8,128)(2,1)} %get-tuple-element.31.agg_ref, bf16[512,512]{1,0:T(8,128)(2,1)} %get-tuple-element.32.slopes_ref, ...), custom_call_target="tpu_custom_call" | custom-call | flops 1342177280 | bytes 5767168 | tf_op jit(solution)/shard_map/terms/pallas_call | solution.py:269
  157.5 4.1 %all-to-all-start.2 = ((bf16[32,32,512]{2,1,0:T(8,128)(2,1)}), bf16[32,32,512]{2,1,0:T(8,128)(2,1)S(1)}, u32[]{:S(2)}, u32[]{:S(2)}) async-start(bf16[32,32,512]{2,1,0:T(8,128)(2,1)} %bitcast.97), calls=%async_computation.2 | async-start | bytes 2097152 | tf_op jit(solution)/shard_map/all_to_all | solution.py:194
  161.8 1.8 collective-permute-start.3
  163.6 1.5 collective-permute-start.4
  165.4 21.0 %collective-permute-done.3.refs_1_ = bf16[512,512]{1,0:T(8,128)(2,1)S(1)} collective-permute-done((bf16[512,512]{1,0:T(8,128)(2,1)S(1)}, bf16[512,512]{1,0:T(8,128)(2,1)S(1)}, u32[]{:S(2)}, u32[]{:S(2)}) %collective-permute-start.3) | collective-permute-done | bytes 524320 | tf_op jit(solution)/shard_map/ppermute | solution.py:197
  186.4 12.8 %collective-permute-done.5.refs_3_ = bf16[512,512]{1,0:T(8,128)(2,1)S(1)} collective-permute-done((bf16[512,512]{1,0:T(8,128)(2,1)S(1)}, bf16[512,512]{1,0:T(8,128)(2,1)S(1)}, u32[]{:S(2)}, u32[]{:S(2)}) %collective-permute-start.5) | collective-permute-done | bytes 524320 | tf_op jit(solution)/shard_map/ppermute | solution.py:197
  199.2 0.8 copy-done.13
  200.0 10.4 %spmm_back.1 = bf16[4096,512]{1,0:T(8,128)(2,1)} custom-call(s32[128]{0:T(128)} %reshape_squeeze.3.cols_ref, s32[4]{0:T(128)} %iota_xor_fusion.1.group_ref, bf16[512,512]{1,0:T(8,128)(2,1)} %get-tuple-element.36.refs_0_, bf16[512,512]{1,0:T(8,128)(2,1)} %copy-done.9, bf16[512,512]{1,0:T(8,128)(2,1)} %copy-done.11, bf16[512,512]{1,0:T(8,128)(2,1)} %copy-done.13, ...), custom_call_target="tpu_custom_call" | custom-call | flops 2147483648 | bytes 10485760 | tf_op jit(solution)/shard_map/spmm_back/pallas_call | solution.py:280
  210.5 0.6 copy-done.14
  211.1 0.6 fusion.16
  217.7 1.7 collective-permute-start.7
  219.4 1.5 collective-permute-start.6
  220.9 0.7 fusion.15
  234.9 1.1 fusion.2
  236.1 1.8 collective-permute-start.15
  237.9 1.4 collective-permute-start.14
  239.3 0.5 collective-permute-start.13
  239.8 2.5 collective-permute-start.12
  242.3 0.5 collective-permute-start.11
  242.8 0.9 collective-permute-start.10
  243.7 1.0 collective-permute-done.14
  244.7 0.6 collective-permute-start.9
  245.3 3.4 %collective-permute-done.13 = bf16[32,512]{1,0:T(8,128)(2,1)S(1)} collective-permute-done((bf16[32,512]{1,0:T(8,128)(2,1)S(1)}, bf16[32,512]{1,0:T(8,128)(2,1)S(1)}, u32[]{:S(2)}, u32[]{:S(2)}) %collective-permute-start.13) | collective-permute-done | bytes 32800 | tf_op jit(solution)/shard_map/ppermute | solution.py:323
  248.8 1.4 collective-permute-done.12
  250.8 1.4 collective-permute-start.18
  252.2 1.6 collective-permute-start.19
  253.8 1.1 collective-permute-start.20
  254.9 2.7 collective-permute-start.21
  257.7 9.6 %reduce-scatter.2.cloned.1.call-done.neigh_ref = bf16[512,512]{1,0:T(8,128)(2,1)} async-done(((bf16[4096,512]{1,0:T(8,128)(2,1)}), bf16[512,512]{1,0:T(8,128)(2,1)}) %reduce-scatter.2.cloned.1.call-update) | async-done | bytes 524304 | tf_op jit(solution)/shard_map/reduce_scatter | solution.py:295
  267.3 3.2 join_pack.1
  270.4 4.3 %all-to-all-start.3 = ((bf16[32,32,512]{2,1,0:T(8,128)(2,1)}), bf16[32,32,512]{2,1,0:T(8,128)(2,1)S(1)}, u32[]{:S(2)}, u32[]{:S(2)}) async-start(bf16[32,32,512]{2,1,0:T(8,128)(2,1)} %bitcast.89), calls=%async_computation.4 | async-start | bytes 2097152 | tf_op jit(solution)/shard_map/all_to_all | solution.py:194
  274.8 3.4 %collective-permute-start.22 = (bf16[32,512]{1,0:T(8,128)(2,1)S(1)}, bf16[32,512]{1,0:T(8,128)(2,1)S(1)}, u32[]{:S(2)}, u32[]{:S(2)}) collective-permute-start(bf16[32,512]{1,0:T(8,128)(2,1)S(1)} %get-tuple-element.47), channel_id=1, source_target_pairs={{0,7},{1,6},{2,5},{3,4},{4,3},{5,2},{6,1},{7,0},{8,15},{9,14},{10,... | collective-permute-start | bytes 98312 | tf_op jit(solution)/shard_map/ppermute | solution.py:323
  278.3 18.3 %collective-permute-done.22 = bf16[32,512]{1,0:T(8,128)(2,1)S(1)} collective-permute-done((bf16[32,512]{1,0:T(8,128)(2,1)S(1)}, bf16[32,512]{1,0:T(8,128)(2,1)S(1)}, u32[]{:S(2)}, u32[]{:S(2)}) %collective-permute-start.22) | collective-permute-done | bytes 32800 | tf_op jit(solution)/shard_map/ppermute | solution.py:323
  296.6 0.6 gather_fusion
  297.2 2.5 collective-permute-start.25
  299.6 0.5 collective-permute-start.24
  300.2 0.5 collective-permute-start.23
  300.7 2.9 unpack_owner.2
  303.6 4.7 %collective-permute-done.25 = bf16[256,512]{1,0:T(8,128)(2,1)S(1)} collective-permute-done((bf16[256,512]{1,0:T(8,128)(2,1)S(1)}, bf16[256,512]{1,0:T(8,128)(2,1)S(1)}, u32[]{:S(2)}, u32[]{:S(2)}) %collective-permute-start.25) | collective-permute-done | bytes 262176 | tf_op jit(solution)/shard_map/ppermute | solution.py:197
  308.3 5.2 %collective-permute-done.24 = bf16[256,512]{1,0:T(8,128)(2,1)S(1)} collective-permute-done((bf16[256,512]{1,0:T(8,128)(2,1)S(1)}, bf16[256,512]{1,0:T(8,128)(2,1)S(1)}, u32[]{:S(2)}, u32[]{:S(2)}) %collective-permute-start.24) | collective-permute-done | bytes 262176 | tf_op jit(solution)/shard_map/ppermute | solution.py:197
  313.7 0.6 gather_fusion.1
  314.3 1.6 fusion.14
  315.9 1.0 copy-done.3
  316.9 2.9 unpack_owner.3
  (72 shorter events, 3.1 us)
Async XLA Ops:
  10.3 87.0 %copy-start.15 = (s32[1,1,16,8]{2,3,1,0:T(8,128)S(1)}, s32[1,1,16,8]{2,3,1,0:T(8,128)}, u32[]{:S(2)}) copy-start(s32[1,1,16,8]{2,3,1,0:T(8,128)} %param.10) | copy-start | bytes 1540
  10.3 34.9 %all-to-all-start = ((bf16[32,32,512]{2,1,0:T(8,128)(2,1)}), bf16[32,32,512]{2,1,0:T(8,128)(2,1)S(1)}, u32[]{:S(2)}, u32[]{:S(2)}) async-start(bf16[32,32,512]{2,1,0:T(8,128)(2,1)} %bitcast.99), calls=%async_computation | async-start | bytes 2097152 | tf_op jit(solution)/shard_map/all_to_all | solution.py:194
  17.6 76.4 %all-gather.2.cloned.1.call-start = ((), (), s32[]{:S(2)}) async-start(), calls=%async_computation.5 | async-start | bytes 4718592 | tf_op jit(solution)/shard_map/all_gather | solution.py:231
  45.2 1.0 copy-start.4
  94.0 51.7 %all-to-all-start.1 = ((bf16[32,32,640]{2,1,0:T(8,128)(2,1)}), bf16[32,32,640]{2,1,0:T(8,128)(2,1)S(1)}, u32[]{:S(2)}, u32[]{:S(2)}) async-start(bf16[32,32,640]{2,1,0:T(8,128)(2,1)} %bitcast.90), calls=%async_computation.1 | async-start | bytes 2621440 | tf_op jit(solution)/shard_map/all_to_all | solution.py:194
  110.3 6.0 %copy-start.12 = (bf16[512,512]{1,0:T(8,128)(2,1)S(1)}, bf16[512,512]{1,0:T(8,128)(2,1)}, u32[]{:S(2)}) copy-start(bf16[512,512]{1,0:T(8,128)(2,1)} %spmm_3.1) | copy-start | bytes 1572868
  110.3 8.7 %copy-start.10 = (bf16[512,512]{1,0:T(8,128)(2,1)S(1)}, bf16[512,512]{1,0:T(8,128)(2,1)}, u32[]{:S(2)}) copy-start(bf16[512,512]{1,0:T(8,128)(2,1)} %spmm_2.1) | copy-start | bytes 1572868
  116.3 18.9 %collective-permute-start = (bf16[512,512]{1,0:T(8,128)(2,1)S(1)}, bf16[512,512]{1,0:T(8,128)(2,1)S(1)}, u32[]{:S(2)}, u32[]{:S(2)}) collective-permute-start(bf16[512,512]{1,0:T(8,128)(2,1)S(1)} %copy-done.12), channel_id=1, source_target_pairs={{0,24},{8,16},{16,8},{24,0},{1,25},{9,17},{17,9},{25,1},{2,26},{10... | collective-permute-start | bytes 1572872 | tf_op jit(solution)/shard_map/ppermute | solution.py:197
  119.0 26.5 %collective-permute-start.1 = (bf16[512,512]{1,0:T(8,128)(2,1)S(1)}, bf16[512,512]{1,0:T(8,128)(2,1)S(1)}, u32[]{:S(2)}, u32[]{:S(2)}) collective-permute-start(bf16[512,512]{1,0:T(8,128)(2,1)S(1)} %copy-done.10), channel_id=1, source_target_pairs={{0,16},{8,24},{16,0},{24,8},{1,17},{9,25},{17,1},{25,9},{2,18},{10... | collective-permute-start | bytes 1572872 | tf_op jit(solution)/shard_map/ppermute | solution.py:197
  119.6 26.1 %collective-permute-start.2 = (bf16[512,512]{1,0:T(8,128)(2,1)}, bf16[512,512]{1,0:T(8,128)(2,1)S(1)}, u32[]{:S(2)}, u32[]{:S(2)}) collective-permute-start(bf16[512,512]{1,0:T(8,128)(2,1)} %spmm_1.1), channel_id=1, source_target_pairs={{0,8},{8,0},{16,24},{24,16},{1,9},{9,1},{17,25},{25,17},{2,10},{10... | collective-permute-start | bytes 1572872 | tf_op jit(solution)/shard_map/ppermute | solution.py:197
  135.3 10.4 %copy-start.6 = (bf16[512,512]{1,0:T(8,128)(2,1)}, bf16[512,512]{1,0:T(8,128)(2,1)S(1)}, u32[]{:S(2)}) copy-start(bf16[512,512]{1,0:T(8,128)(2,1)S(1)} %collective-permute-done.refs_0_) | copy-start | bytes 1572868
  145.5 0.8 copy-start.7
  145.7 0.8 copy-start.8
  145.7 1.3 copy-start
  152.8 9.0 %copy-start.5 = (bf16[512,512]{1,0:T(8,128)(2,1)S(1)}, bf16[512,512]{1,0:T(8,128)(2,1)}, u32[]{:S(2)}) copy-start(bf16[512,512]{1,0:T(8,128)(2,1)} %get-tuple-element.36.refs_0_) | copy-start | bytes 1572868
  157.5 53.0 %all-to-all-start.2 = ((bf16[32,32,512]{2,1,0:T(8,128)(2,1)}), bf16[32,32,512]{2,1,0:T(8,128)(2,1)S(1)}, u32[]{:S(2)}, u32[]{:S(2)}) async-start(bf16[32,32,512]{2,1,0:T(8,128)(2,1)} %bitcast.97), calls=%async_computation.2 | async-start | bytes 2097152 | tf_op jit(solution)/shard_map/all_to_all | solution.py:194
  161.6 105.7 %reduce-scatter.2.cloned.1.call-start = ((), (), s32[]{:S(2)}) async-start(), calls=%async_computation.6 | async-start | bytes 4718592 | tf_op jit(solution)/shard_map/reduce_scatter | solution.py:295
  161.8 24.6 %collective-permute-start.3 = (bf16[512,512]{1,0:T(8,128)(2,1)S(1)}, bf16[512,512]{1,0:T(8,128)(2,1)S(1)}, u32[]{:S(2)}, u32[]{:S(2)}) collective-permute-start(bf16[512,512]{1,0:T(8,128)(2,1)S(1)} %copy-done.5), channel_id=1, source_target_pairs={{0,8},{8,0},{16,24},{24,16},{1,9},{9,1},{17,25},{25,17},{2,10},{10... | collective-permute-start | bytes 1572872 | tf_op jit(solution)/shard_map/ppermute | solution.py:197
  163.6 22.7 %collective-permute-start.4 = (bf16[512,512]{1,0:T(8,128)(2,1)S(1)}, bf16[512,512]{1,0:T(8,128)(2,1)S(1)}, u32[]{:S(2)}, u32[]{:S(2)}) collective-permute-start(bf16[512,512]{1,0:T(8,128)(2,1)S(1)} %copy-done.5), channel_id=1, source_target_pairs={{0,16},{8,24},{16,0},{24,8},{1,17},{9,25},{17,1},{25,9},{2,18},{10... | collective-permute-start | bytes 1572872 | tf_op jit(solution)/shard_map/ppermute | solution.py:197
  165.1 34.1 %collective-permute-start.5 = (bf16[512,512]{1,0:T(8,128)(2,1)S(1)}, bf16[512,512]{1,0:T(8,128)(2,1)S(1)}, u32[]{:S(2)}, u32[]{:S(2)}) collective-permute-start(bf16[512,512]{1,0:T(8,128)(2,1)S(1)} %copy-done.5), channel_id=1, source_target_pairs={{0,24},{8,16},{16,8},{24,0},{1,25},{9,17},{17,9},{25,1},{2,26},{10... | collective-permute-start | bytes 1572872 | tf_op jit(solution)/shard_map/ppermute | solution.py:197
  186.4 12.9 %copy-start.9 = (bf16[512,512]{1,0:T(8,128)(2,1)}, bf16[512,512]{1,0:T(8,128)(2,1)S(1)}, u32[]{:S(2)}) copy-start(bf16[512,512]{1,0:T(8,128)(2,1)S(1)} %collective-permute-done.3.refs_1_) | copy-start | bytes 1572868
  186.4 12.9 %copy-start.11 = (bf16[512,512]{1,0:T(8,128)(2,1)}, bf16[512,512]{1,0:T(8,128)(2,1)S(1)}, u32[]{:S(2)}) copy-start(bf16[512,512]{1,0:T(8,128)(2,1)S(1)} %collective-permute-done.4.refs_2_) | copy-start | bytes 1572868
  199.2 0.8 copy-start.13
  210.5 0.7 copy-start.14
  210.5 6.8 %copy-start.1 = (bf16[1024,512]{1,0:T(8,128)(2,1)S(1)}, bf16[1024,512]{1,0:T(8,128)(2,1)}, u32[]{:S(2)}) copy-start(bf16[1024,512]{1,0:T(8,128)(2,1)} %get-tuple-element.45) | copy-start | bytes 3145732
  210.5 59.9 %copy-start.2 = (bf16[32,32,512]{2,1,0:T(8,128)(2,1)}, bf16[32,32,512]{2,1,0:T(8,128)(2,1)S(1)}, u32[]{:S(2)}) copy-start(bf16[32,32,512]{2,1,0:T(8,128)(2,1)S(1)} %all-to-all-done.2) | copy-start | bytes 3145732
  217.3 17.6 %collective-permute-start.8 = (bf16[256,512]{1,0:T(8,128)(2,1)S(1)}, bf16[256,512]{1,0:T(8,128)(2,1)S(1)}, u32[]{:S(2)}, u32[]{:S(2)}) collective-permute-start(bf16[256,512]{1,0:T(8,128)(2,1)S(1)} %get-tuple-element.51), channel_id=1, source_target_pairs={{0,24},{8,16},{16,8},{24,0},{1,25},{9,17},{17,9},{25,1},{2,26},{10... | collective-permute-start | bytes 786440 | tf_op jit(solution)/shard_map/ppermute | solution.py:197
  217.7 17.2 %collective-permute-start.7 = (bf16[256,512]{1,0:T(8,128)(2,1)S(1)}, bf16[256,512]{1,0:T(8,128)(2,1)S(1)}, u32[]{:S(2)}, u32[]{:S(2)}) collective-permute-start(bf16[256,512]{1,0:T(8,128)(2,1)S(1)} %get-tuple-element.52), channel_id=1, source_target_pairs={{0,16},{8,24},{16,0},{24,8},{1,17},{9,25},{17,1},{25,9},{2,18},{10... | collective-permute-start | bytes 786440 | tf_op jit(solution)/shard_map/ppermute | solution.py:197
  219.4 15.5 %collective-permute-start.6 = (bf16[256,512]{1,0:T(8,128)(2,1)S(1)}, bf16[256,512]{1,0:T(8,128)(2,1)}, u32[]{:S(2)}, u32[]{:S(2)}) collective-permute-start(bf16[256,512]{1,0:T(8,128)(2,1)S(1)} %get-tuple-element.50), channel_id=1, source_target_pairs={{0,8},{8,0},{16,24},{24,16},{1,9},{9,1},{17,25},{25,17},{2,10},{10... | collective-permute-start | bytes 786440 | tf_op jit(solution)/shard_map/ppermute | solution.py:197
  236.1 6.7 %collective-permute-start.15 = (bf16[32,512]{1,0:T(8,128)(2,1)S(1)}, bf16[32,512]{1,0:T(8,128)(2,1)S(1)}, u32[]{:S(2)}, u32[]{:S(2)}) collective-permute-start(bf16[32,512]{1,0:T(8,128)(2,1)S(1)} %get-tuple-element.54), channel_id=1, source_target_pairs={{0,7},{1,6},{2,5},{3,4},{4,3},{5,2},{6,1},{7,0},{8,15},{9,14},{10,... | collective-permute-start | bytes 98312 | tf_op jit(solution)/shard_map/ppermute | solution.py:323
  237.9 6.8 %collective-permute-start.14 = (bf16[32,512]{1,0:T(8,128)(2,1)S(1)}, bf16[32,512]{1,0:T(8,128)(2,1)S(1)}, u32[]{:S(2)}, u32[]{:S(2)}) collective-permute-start(bf16[32,512]{1,0:T(8,128)(2,1)S(1)} %get-tuple-element.55), channel_id=1, source_target_pairs={{0,6},{1,7},{2,4},{3,5},{4,2},{5,3},{6,0},{7,1},{8,14},{9,15},{10,... | collective-permute-start | bytes 98312 | tf_op jit(solution)/shard_map/ppermute | solution.py:323
  239.3 9.5 %collective-permute-start.13 = (bf16[32,512]{1,0:T(8,128)(2,1)S(1)}, bf16[32,512]{1,0:T(8,128)(2,1)S(1)}, u32[]{:S(2)}, u32[]{:S(2)}) collective-permute-start(bf16[32,512]{1,0:T(8,128)(2,1)S(1)} %get-tuple-element.56), channel_id=1, source_target_pairs={{0,5},{1,4},{2,7},{3,6},{4,1},{5,0},{6,3},{7,2},{8,13},{9,12},{10,... | collective-permute-start | bytes 98312 | tf_op jit(solution)/shard_map/ppermute | solution.py:323
  239.8 10.4 %collective-permute-start.12 = (bf16[32,512]{1,0:T(8,128)(2,1)S(1)}, bf16[32,512]{1,0:T(8,128)(2,1)S(1)}, u32[]{:S(2)}, u32[]{:S(2)}) collective-permute-start(bf16[32,512]{1,0:T(8,128)(2,1)S(1)} %get-tuple-element.57), channel_id=1, source_target_pairs={{0,4},{1,5},{2,6},{3,7},{4,0},{5,1},{6,2},{7,3},{8,12},{9,13},{10,... | collective-permute-start | bytes 98312 | tf_op jit(solution)/shard_map/ppermute | solution.py:323
  242.3 7.9 %collective-permute-start.11 = (bf16[32,512]{1,0:T(8,128)(2,1)S(1)}, bf16[32,512]{1,0:T(8,128)(2,1)S(1)}, u32[]{:S(2)}, u32[]{:S(2)}) collective-permute-start(bf16[32,512]{1,0:T(8,128)(2,1)S(1)} %get-tuple-element.58), channel_id=1, source_target_pairs={{0,3},{1,2},{2,1},{3,0},{4,7},{5,6},{6,5},{7,4},{8,11},{9,10},{10,... | collective-permute-start | bytes 98312 | tf_op jit(solution)/shard_map/ppermute | solution.py:323
  242.8 7.4 %collective-permute-start.10 = (bf16[32,512]{1,0:T(8,128)(2,1)S(1)}, bf16[32,512]{1,0:T(8,128)(2,1)S(1)}, u32[]{:S(2)}, u32[]{:S(2)}) collective-permute-start(bf16[32,512]{1,0:T(8,128)(2,1)S(1)} %get-tuple-element.59), channel_id=1, source_target_pairs={{0,2},{1,3},{2,0},{3,1},{4,6},{5,7},{6,4},{7,5},{8,10},{9,11},{10,... | collective-permute-start | bytes 98312 | tf_op jit(solution)/shard_map/ppermute | solution.py:323
  244.7 5.5 %collective-permute-start.9 = (bf16[32,512]{1,0:T(8,128)(2,1)S(1)}, bf16[32,512]{1,0:T(8,128)(2,1)S(1)}, u32[]{:S(2)}, u32[]{:S(2)}) collective-permute-start(bf16[32,512]{1,0:T(8,128)(2,1)S(1)} %get-tuple-element.53), channel_id=1, source_target_pairs={{0,1},{1,0},{2,3},{3,2},{4,5},{5,4},{6,7},{7,6},{8,9},{9,8},{10,11... | collective-permute-start | bytes 98312 | tf_op jit(solution)/shard_map/ppermute | solution.py:323
  250.3 4.7 %collective-permute-start.16 = (bf16[32,512]{1,0:T(8,128)(2,1)S(1)}, bf16[32,512]{1,0:T(8,128)(2,1)S(1)}, u32[]{:S(2)}, u32[]{:S(2)}) collective-permute-start(bf16[32,512]{1,0:T(8,128)(2,1)S(1)} %get-tuple-element.47), channel_id=1, source_target_pairs={{0,1},{1,0},{2,3},{3,2},{4,5},{5,4},{6,7},{7,6},{8,9},{9,8},{10,11... | collective-permute-start | bytes 98312 | tf_op jit(solution)/shard_map/ppermute | solution.py:323
  250.6 24.2 %collective-permute-start.17 = (bf16[32,512]{1,0:T(8,128)(2,1)S(1)}, bf16[32,512]{1,0:T(8,128)(2,1)S(1)}, u32[]{:S(2)}, u32[]{:S(2)}) collective-permute-start(bf16[32,512]{1,0:T(8,128)(2,1)S(1)} %get-tuple-element.47), channel_id=1, source_target_pairs={{0,2},{1,3},{2,0},{3,1},{4,6},{5,7},{6,4},{7,5},{8,10},{9,11},{10,... | collective-permute-start | bytes 98312 | tf_op jit(solution)/shard_map/ppermute | solution.py:323
  250.8 27.4 %collective-permute-start.18 = (bf16[32,512]{1,0:T(8,128)(2,1)S(1)}, bf16[32,512]{1,0:T(8,128)(2,1)S(1)}, u32[]{:S(2)}, u32[]{:S(2)}) collective-permute-start(bf16[32,512]{1,0:T(8,128)(2,1)S(1)} %get-tuple-element.47), channel_id=1, source_target_pairs={{0,3},{1,2},{2,1},{3,0},{4,7},{5,6},{6,5},{7,4},{8,11},{9,10},{10,... | collective-permute-start | bytes 98312 | tf_op jit(solution)/shard_map/ppermute | solution.py:323
  252.2 26.0 %collective-permute-start.19 = (bf16[32,512]{1,0:T(8,128)(2,1)S(1)}, bf16[32,512]{1,0:T(8,128)(2,1)S(1)}, u32[]{:S(2)}, u32[]{:S(2)}) collective-permute-start(bf16[32,512]{1,0:T(8,128)(2,1)S(1)} %get-tuple-element.47), channel_id=1, source_target_pairs={{0,4},{1,5},{2,6},{3,7},{4,0},{5,1},{6,2},{7,3},{8,12},{9,13},{10,... | collective-permute-start | bytes 98312 | tf_op jit(solution)/shard_map/ppermute | solution.py:323
  253.8 24.4 %collective-permute-start.20 = (bf16[32,512]{1,0:T(8,128)(2,1)S(1)}, bf16[32,512]{1,0:T(8,128)(2,1)S(1)}, u32[]{:S(2)}, u32[]{:S(2)}) collective-permute-start(bf16[32,512]{1,0:T(8,128)(2,1)S(1)} %get-tuple-element.47), channel_id=1, source_target_pairs={{0,5},{1,4},{2,7},{3,6},{4,1},{5,0},{6,3},{7,2},{8,13},{9,12},{10,... | collective-permute-start | bytes 98312 | tf_op jit(solution)/shard_map/ppermute | solution.py:323
  254.9 23.3 %collective-permute-start.21 = (bf16[32,512]{1,0:T(8,128)(2,1)S(1)}, bf16[32,512]{1,0:T(8,128)(2,1)S(1)}, u32[]{:S(2)}, u32[]{:S(2)}) collective-permute-start(bf16[32,512]{1,0:T(8,128)(2,1)S(1)} %get-tuple-element.47), channel_id=1, source_target_pairs={{0,6},{1,7},{2,4},{3,5},{4,2},{5,3},{6,0},{7,1},{8,14},{9,15},{10,... | collective-permute-start | bytes 98312 | tf_op jit(solution)/shard_map/ppermute | solution.py:323
  270.4 45.5 %all-to-all-start.3 = ((bf16[32,32,512]{2,1,0:T(8,128)(2,1)}), bf16[32,32,512]{2,1,0:T(8,128)(2,1)S(1)}, u32[]{:S(2)}, u32[]{:S(2)}) async-start(bf16[32,32,512]{2,1,0:T(8,128)(2,1)} %bitcast.89), calls=%async_computation.4 | async-start | bytes 2097152 | tf_op jit(solution)/shard_map/all_to_all | solution.py:194
  274.8 21.8 %collective-permute-start.22 = (bf16[32,512]{1,0:T(8,128)(2,1)S(1)}, bf16[32,512]{1,0:T(8,128)(2,1)S(1)}, u32[]{:S(2)}, u32[]{:S(2)}) collective-permute-start(bf16[32,512]{1,0:T(8,128)(2,1)S(1)} %get-tuple-element.47), channel_id=1, source_target_pairs={{0,7},{1,6},{2,5},{3,4},{4,3},{5,2},{6,1},{7,0},{8,15},{9,14},{10,... | collective-permute-start | bytes 98312 | tf_op jit(solution)/shard_map/ppermute | solution.py:323
  297.2 11.1 %collective-permute-start.25 = (bf16[256,512]{1,0:T(8,128)(2,1)S(1)}, bf16[256,512]{1,0:T(8,128)(2,1)S(1)}, u32[]{:S(2)}, u32[]{:S(2)}) collective-permute-start(bf16[256,512]{1,0:T(8,128)(2,1)S(1)} %bitcast.102), channel_id=1, source_target_pairs={{0,24},{8,16},{16,8},{24,0},{1,25},{9,17},{17,9},{25,1},{2,26},{10... | collective-permute-start | bytes 786440 | tf_op jit(solution)/shard_map/ppermute | solution.py:197
  299.6 13.9 %collective-permute-start.24 = (bf16[256,512]{1,0:T(8,128)(2,1)S(1)}, bf16[256,512]{1,0:T(8,128)(2,1)S(1)}, u32[]{:S(2)}, u32[]{:S(2)}) collective-permute-start(bf16[256,512]{1,0:T(8,128)(2,1)S(1)} %bitcast.103), channel_id=1, source_target_pairs={{0,16},{8,24},{16,0},{24,8},{1,17},{9,25},{17,1},{25,9},{2,18},{10... | collective-permute-start | bytes 786440 | tf_op jit(solution)/shard_map/ppermute | solution.py:197
  300.2 13.4 %collective-permute-start.23 = (bf16[256,512]{1,0:T(8,128)(2,1)S(1)}, bf16[256,512]{1,0:T(8,128)(2,1)S(1)}, u32[]{:S(2)}, u32[]{:S(2)}) collective-permute-start(bf16[256,512]{1,0:T(8,128)(2,1)S(1)} %bitcast.104), channel_id=1, source_target_pairs={{0,8},{8,0},{16,24},{24,16},{1,9},{9,1},{17,25},{25,17},{2,10},{10... | collective-permute-start | bytes 786440 | tf_op jit(solution)/shard_map/ppermute | solution.py:197
  315.9 1.0 copy-start.3
Sparse Core Ops, SparseCore 0:
  49.2 44.7 all-gather.1
  210.6 56.5 reduce-scatter.1

commit v3 on v1

--- a/solution.py
+++ b/solution.py
@@ -66,32 +66,54 @@
     out_ref[...] = dot(slots_onehot(dest * cap + rank, out_ref.shape[0]), value_ref[...]).astype(BF)
 
 
-def index_kernel(cap, nodes_ref, position_ref, degree_ref, cot_ref, cot_out, degree_out, own_col, node_row, node_col):
-    devices, _ = degree_out.shape
+def index_kernel(
+    cap, ways, nodes_ref, position_ref, degree_ref, cot_ref, cot_out, own_col, node_row, node_col, turned_row, turned_col
+):
     n = nodes_ref.shape[1]
+    width = cot_ref.shape[1]
     dest, rank = own_slots(nodes_ref[...], cap)
     flat = dest * cap + rank
     own_col[...] = as_column(flat)
-    cot_out[...] = dot(slots_onehot(flat, cot_out.shape[0]), cot_ref[...]).astype(BF)
-    by_dest = jnp.where(lax.broadcasted_iota(jnp.int32, (devices, n), 0) == dest, degree_ref[...].astype(F32), 0.0)
-    by_rank = entries_onehot(as_column(rank), cap)
-    degree_out[...] = dot(by_dest.astype(BF), by_rank)
+    packing = slots_onehot(flat, cot_out.shape[0])
+    cot_out[:, :width] = dot(packing, cot_ref[...]).astype(BF)
+    cot_out[:, width:] = dot(packing, as_column(degree_ref[...].astype(F32)).astype(BF)).astype(BF)
     position = position_ref[...]
     source = block_of(position, n)
-    place = source * cap + rank_row(source, position)
+    rank = rank_row(source, position)
+    place = source * cap + rank
     node_row[...] = jnp.broadcast_to(place, node_row.shape)
     node_col[...] = as_column(place)
+    across = cot_out.shape[0] // (cap * ways)
+    down = block_of(source, across)
+    turned = ((source - down * across) * ways + down) * cap + rank
+    turned_row[...] = jnp.broadcast_to(turned, turned_row.shape)
+    turned_col[...] = as_column(turned)
 
 
 def unpack_kernel(col_ref, value_ref, out_ref):
     out_ref[...] = dot(entries_onehot(col_ref[...], value_ref.shape[0]), value_ref[...]).astype(BF)
 
 
-def spmm_kernel(ways, cols_ref, group_ref, x_ref, *refs):
-    masks, outs = refs[:ways], refs[ways:]
+def spmm_kernel(ways, cols_ref, group_ref, x_hbm, *refs):
+    masks, outs = refs[:ways], refs[ways : 2 * ways]
+    x_ref, sems = refs[2 * ways :]
     q = pl.program_id(0)
     depth = pl.num_programs(0)
     _, breadth, tile, _ = masks[0].shape
+
+    @pl.when(q == 0)
+    def _():
+        count = sems.shape[0]
+        share = x_ref.shape[0] // count
+        copies = [
+            pltpu.make_async_copy(x_hbm.at[pl.ds(i * share, share)], x_ref.at[pl.ds(i * share, share)], sems.at[i])
+            for i in range(count)
+        ]
+        for copy in copies:
+            copy.start()
+        for copy in copies:
+            copy.wait()
+
     for s in range(ways):
         base = (group_ref[s] * depth + q) * breadth
         total = None
@@ -130,38 +152,36 @@
 
 def layer_kernel(ways, *refs):
     terms = refs[:ways]
-    (x_ref, cot_ref, degree_ref, col_ref, self_ref, neigh_ref, hidden_out, slopes_out, agg_out, spread_out) = refs[ways:]
-    devices, cap = degree_ref.shape
-    slots = cot_ref.shape[0]
-    place = col_ref[...][:, :1]
-    rows = place.shape[0]
+    (x_ref, cot_ref, col_ref, row_ref, self_ref, neigh_ref, packed_out, slopes_out, agg_out, spread_out) = refs[ways:]
+    width = x_ref.shape[1]
     summed = terms[0][...].astype(F32)
     for s in range(1, ways):
         summed = summed + terms[s][...].astype(F32)
-    source = block_of(place, cap)
-    rank = place - source * cap
-    by_source = entries_onehot(source, devices)
-    degrees = dot(by_source, degree_ref[...].astype(BF))
-    picked = lax.broadcasted_iota(jnp.int32, (rows, cap), 1) == rank
-    degrees = jnp.sum(jnp.where(picked, degrees, 0.0), axis=1, keepdims=True)
+    cot = dot(entries_onehot(col_ref[...], cot_ref.shape[0]), cot_ref[...])
+    degrees = cot[:, width : width + 1]
     agg = (summed / degrees).astype(BF)
     agg_out[...] = agg
     preact = dot(x_ref[...], self_ref[...]) + dot(agg, neigh_ref[...])
     gate = jax.nn.sigmoid(preact)
-    hidden_out[...] = (preact * gate).astype(BF)
-    cot = dot(entries_onehot(place, slots), cot_ref[...])
-    slopes = (cot * gate * (1.0 + preact * (1.0 - gate))).astype(BF)
+    hidden = (preact * gate).astype(BF)
+    slopes = (cot[:, :width] * gate * (1.0 + preact * (1.0 - gate))).astype(BF)
     slopes_out[...] = slopes
     spread_out[...] = (dot(slopes, neigh_ref[...], 1, 1) / degrees).astype(BF)
-
-
-def terms_kernel(x_ref, agg_ref, slopes_ref, hidden_ref, self_ref, row_ref, grads_out, back_out, packed_out):
+    packed_out[...] = dot(slots_onehot(row_ref[...][:1], packed_out.shape[0]), hidden).astype(BF)
+
+
+def terms_kernel(x_ref, agg_ref, slopes_ref, self_ref, grads_out, back_out):
     width = x_ref.shape[1]
     slopes = slopes_ref[...]
-    packed_out[...] = dot(slots_onehot(row_ref[...][:1], packed_out.shape[0]), hidden_ref[...]).astype(BF)
     grads_out[:width, :] = dot(x_ref[...], slopes, 0, 0).astype(BF)
     grads_out[width:, :] = dot(agg_ref[...], slopes, 0, 0).astype(BF)
     back_out[...] = dot(slopes, self_ref[...], 1, 1)
+
+
+def place_kernel(index_ref, *refs):
+    out_ref = refs[-1]
+    for s, part in enumerate(refs[:-1]):
+        out_ref[index_ref[s]] = part[...].astype(out_ref.dtype)
 
 
 def join_kernel(own_ref, neigh_ref, row_ref, out_ref):
@@ -204,6 +224,17 @@
         there = packed.reshape(devices, cap, -1)
         return lax.all_to_all(there, everyone, split_axis=0, concat_axis=0, tiled=True).reshape(slots, -1)
 
+    def row_phase(packed):
+        there = packed.reshape(row_devices, col_devices * cap, -1)
+        return lax.all_to_all(there, "row", split_axis=0, concat_axis=0, tiled=True).reshape(slots, -1)
+
+    def col_phase(packed):
+        there = packed.reshape(col_devices, row_devices * cap, -1)
+        return lax.all_to_all(there, "col", split_axis=0, concat_axis=0, tiled=True).reshape(slots, -1)
+
+    def turn(packed, first, second):
+        return packed.reshape(first, second, cap, -1).transpose(1, 0, 2, 3).reshape(slots, -1)
+
     def across(value, s):
         return lax.ppermute(value, "row", [(i, i ^ s) for i in range(ways)])
 
@@ -218,22 +249,21 @@
         name="pack_features",
     )(nodes, features)
     inbound = relay(packed)
-    cot_packed, degree_packed, own_col, node_row, node_col = call(
-        functools.partial(index_kernel, cap),
+    cot_packed, own_col, node_row, node_col, turned_row, turned_col = call(
+        functools.partial(index_kernel, cap, ways),
         out_shape=(
-            shape(slots, width),
-            shape(devices, cap, F32),
+            shape(slots, width + 128),
+            shape(rows, 128, jnp.int32),
+            shape(8, rows, jnp.int32),
             shape(rows, 128, jnp.int32),
             shape(8, rows, jnp.int32),
             shape(rows, 128, jnp.int32),
         ),
         in_specs=[VMEM] * 4,
-        out_specs=(VMEM,) * 5,
+        out_specs=(VMEM,) * 6,
         cost_estimate=cost(2 * slots * slab, 6 * slab),
         name="index_cotangent",
     )(nodes, owner_position.reshape(1, rows), degree.reshape(1, rows), cotangent)
-    degree_in = lax.all_to_all(degree_packed, everyone, split_axis=0, concat_axis=0, tiled=True)
-    cot_in = relay(cot_packed)
     x_node = call(
         unpack_kernel,
         out_shape=shape(rows, width),
@@ -242,49 +272,56 @@
         cost_estimate=cost(2 * slots * slab, 6 * slab),
         name="unpack_features",
     )(node_col, inbound)
+    cot_packed, x_node, cols, groups = lax.optimization_barrier((cot_packed, x_node, cols, groups))
     x_cols = lax.all_gather(x_node, "col", axis=0, tiled=True)
+    cot_mid = turn(row_phase(cot_packed), row_devices, col_devices)
+    x_cols, cot_mid = lax.optimization_barrier((x_cols, cot_mid))
+    cot_in = col_phase(cot_mid)
 
     def mask_spec(s):
         return pl.BlockSpec((1, breadth, tile, tile), lambda q, c, g, s=s: (g[s] * depth + q, 0, 0, 0))
 
     spmm_flops = 2 * masks.size * width
+    copies = 8
     partials = call(
         functools.partial(spmm_kernel, ways),
         grid_spec=pltpu.PrefetchScalarGridSpec(
             num_scalar_prefetch=2,
             grid=(depth,),
-            in_specs=[VMEM] + [mask_spec(s) for s in range(ways)],
+            in_specs=[pl.BlockSpec(memory_space=pl.ANY)] + [mask_spec(s) for s in range(ways)],
             out_specs=[pl.BlockSpec((tile, width), lambda q, c, g: (q, 0)) for s in range(ways)],
+            scratch_shapes=[pltpu.VMEM(x_cols.shape, BF), pltpu.SemaphoreType.DMA((copies,))],
         ),
         out_shape=[shape(rows, width) for s in range(ways)],
         cost_estimate=cost(spmm_flops, 2 * masks.size + 2 * x_cols.size + 2 * ways * slab),
         name="spmm",
     )(cols, groups, x_cols, *([masks] * ways))
     terms = [partials[0]] + [across(partials[s], s) for s in range(1, ways)]
-    row_block = rows // 2
-
-    def by_rows(c):
-        return pl.BlockSpec((row_block, c), lambda i: (i, 0))
-
-    hidden, slopes, agg, spread = call(
+    hidden_packed, slopes, agg, spread = call(
         functools.partial(layer_kernel, ways),
-        grid=(2,),
-        out_shape=(shape(rows, width),) * 4,
-        in_specs=[by_rows(width)] * (ways + 1) + [VMEM] * 2 + [by_rows(128)] + [VMEM] * 2,
-        out_specs=(by_rows(width),) * 4,
+        out_shape=(shape(slots, width),) + (shape(rows, width),) * 3,
+        in_specs=[VMEM] * (ways + 6),
+        out_specs=(VMEM,) * 4,
         cost_estimate=cost(10 * slab * width, 2 * slab * (ways + 9)),
         name="layer",
-    )(*terms, x_node, cot_in, degree_in, node_col, self_weight, neigh_weight)
+    )(*terms, x_node, cot_in, turned_col, turned_row, self_weight, neigh_weight)
     spreads = [spread] + [across(spread, s) for s in range(1, ways)]
-    grads, own_back, hidden_packed = call(
+    hidden_mid = col_phase(hidden_packed)
+    grads, own_back = call(
         terms_kernel,
-        out_shape=(shape(2 * width, width), shape(rows, width, F32), shape(slots, width)),
-        in_specs=[VMEM] * 6,
-        out_specs=(VMEM,) * 3,
-        cost_estimate=cost(10 * slab * width, 2 * slab * 11),
+        out_shape=(shape(2 * width, width), shape(rows, width, F32)),
+        in_specs=[VMEM] * 4,
+        out_specs=(VMEM,) * 2,
+        cost_estimate=cost(6 * slab * width, 2 * slab * 9),
         name="terms",
-    )(x_node, agg, slopes, hidden, self_weight, node_row)
-    hidden_in = relay(hidden_packed)
+    )(x_node, agg, slopes, self_weight)
+    *spreads, own_back, grads = lax.optimization_barrier((*spreads, own_back, grads))
+    parts = grads.reshape(ways, -1, width)
+
+    def pick(value, at):
+        return lax.dynamic_index_in_dim(value, at, 0, keepdims=False)
+
+    kept = [pick(parts, me)] + [across(pick(parts, groups[s]), s) for s in range(1, ways)]
     back = call(
         functools.partial(spmm_back_kernel, ways),
         grid_spec=pltpu.PrefetchScalarGridSpec(
@@ -299,7 +336,34 @@
         cost_estimate=cost(spmm_flops, 2 * masks.size + 2 * x_cols.size + 2 * ways * slab),
         name="spmm_back",
     )(cols, groups, *spreads, *([masks] * ways))
+    back, hidden_mid, *kept = lax.optimization_barrier((back, hidden_mid, *kept))
     neigh_back = lax.psum_scatter(back, "col", scatter_dimension=0, tiled=True)
+    hidden_in = row_phase(turn(hidden_mid, col_devices, row_devices))
+    place = lax.axis_index("col")
+    others = jnp.bitwise_xor(place, jnp.arange(col_devices, dtype=jnp.int32)).astype(jnp.int32)
+
+    def along(value, s):
+        return lax.ppermute(value, "col", [(i, i ^ s) for i in range(col_devices)])
+
+    def in_place(index, arrays, dtype):
+        count, (r, c) = len(arrays), arrays[0].shape
+        return call(
+            place_kernel,
+            in_specs=[pl.BlockSpec(memory_space=pltpu.SMEM)] + [VMEM] * count,
+            out_specs=VMEM,
+            out_shape=jax.ShapeDtypeStruct((count, r, c), dtype),
+            cost_estimate=cost(0, 6 * count * r * c),
+            name="in_place",
+        )(index, *arrays).reshape(count * r, c)
+
+    kept = sum(term.astype(F32) for term in kept)
+    pieces = kept.astype(BF).reshape(col_devices, -1, width)
+    mine = [pick(pieces, place)] + [along(pick(pieces, others[s]), s) for s in range(1, col_devices)]
+    scale = 1.0 / math.sqrt(rows * devices)
+    mine = (sum(term.astype(F32) for term in mine) * scale).astype(BF)
+    in_row = in_place(others, [mine] + [along(mine, s) for s in range(1, col_devices)], BF)
+    whole = in_place(groups, [in_row] + [across(in_row, s) for s in range(1, ways)], F32)
+    own_back, whole = lax.optimization_barrier((own_back, whole))
     grad_packed = call(
         join_kernel,
         out_shape=shape(slots, width),
@@ -322,16 +386,6 @@
 
     hidden_own = unpack_own(hidden_in)
     grad_own = unpack_own(grad_in)
-
-    parts = grads.reshape(ways, -1, width)
-    kept = lax.dynamic_index_in_dim(parts, me, 0, keepdims=False).astype(F32)
-    for s in range(1, ways):
-        kept = kept + across(lax.dynamic_index_in_dim(parts, groups[s], 0, keepdims=False), s).astype(F32)
-    pieces = kept.astype(BF).reshape(col_devices, -1, width)
-    pieces = lax.all_to_all(pieces, "col", split_axis=0, concat_axis=0, tiled=True)
-    scale = 1.0 / math.sqrt(rows * devices)
-    mine = (jnp.sum(pieces.astype(F32), axis=0) * scale).astype(BF)
-    whole = lax.all_gather(mine, ("row", "col"), axis=0, tiled=True).astype(F32)
     return (hidden_own, grad_own, whole[:width], whole[width:])
 
 

time: 332 us -> 309 us (0.931)
  waiting for transfers between devices: 200 us -> 129 us
  starting transfers between devices: 26.2 us -> 57.8 us
  between operations: 19.7 us -> 33.8 us
  blocking collectives: 26.9 us -> 19.5 us
  Pallas kernels: 46.5 us -> 52.4 us
  local copies, waits for them, and re-layouts: 9.68 us -> 13.3 us
    all_gather x1 -> x0, waiting for transfers between devices: 41.2 us -> none  [on_device(): whole = lax.all_gather(mine, ('row', 'col'), axis=0, tiled=True).astype(F32)]
    all_gather x1, waiting for transfers between devices: 53 us -> 24.2 us  [on_device(): x_cols = lax.all_gather(x_node, 'col', axis=0, tiled=True)]
    ppermute x0 -> x14, starting transfers between devices: none -> 17.4 us  [along(): return lax.ppermute(value, 'col', [(i, i ^ s) for i in range(col_devices)])]
    all_to_all x0 -> x3, starting transfers between devices: none -> 12.2 us  [the longest x2 8.48 us: col_phase(): lax.all_to_all(there, 'col', split_axis=0, concat_axis=0, tiled=True)]
    ppermute x0 -> x14, waiting for transfers between devices: none -> 10.6 us  [along(): return lax.ppermute(value, 'col', [(i, i ^ s) for i in range(col_devices)])]
    all_to_all x2 -> x1, blocking collectives: 26.9 us -> 19.5 us  [row_phase(): lax.all_to_all(there, 'row', split_axis=0, concat_axis=0, tiled=True)]
    reduce_scatter x1, waiting for transfers between devices: 6.42 us -> 0.01 us  [on_device(): neigh_back = lax.psum_scatter(back, 'col', scatter_dimension=0, tiled=True)]
    ppermute x9 -> x12, waiting for transfers between devices: 54.5 us -> 48.5 us  [across(): return lax.ppermute(value, 'row', [(i, i ^ s) for i in range(ways)])]
  transfers between devices with their start and end apart: 16 -> 33, of which waited for: 12 -> 18; matrix products, arithmetic and copies ran while one was open for 2% -> 3% of each run, Pallas kernels for 7% -> 12%
where the time goes in v3:
time: 309 us; the launch traced here: 308 us
  waiting for transfers between devices  129 us (42%)
  starting transfers between devices  57.8 us (19%)
  Pallas kernels  52.4 us (17%)
  between operations  33.8 us (11%)
  blocking collectives  19.5 us (6%)
  local copies, waits for them, and re-layouts  13.3 us (4%)
    ppermute x12, waiting for transfers between devices, across(): return lax.ppermute(value, 'row', [(i, i ^ s) for i in range(ways)])  48.5 us
    all_to_all x2, waiting for transfers between devices, relay(): lax.all_to_all(there, everyone, split_axis=0, concat_axis=0, tiled=True)  45.7 us
    all_gather x1, waiting for transfers between devices, on_device(): x_cols = lax.all_gather(x_node, 'col', axis=0, tiled=True)  24.2 us
    all_to_all x1, blocking collectives, row_phase(): lax.all_to_all(there, 'row', split_axis=0, concat_axis=0, tiled=True)  19.5 us
    ppermute x14, starting transfers between devices, along(): return lax.ppermute(value, 'col', [(i, i ^ s) for i in range(col_devices)])  17.4 us
    ppermute x12, starting transfers between devices, across(): return lax.ppermute(value, 'row', [(i, i ^ s) for i in range(ways)])  14.1 us
    all_to_all x2, starting transfers between devices, relay(): lax.all_to_all(there, everyone, split_axis=0, concat_axis=0, tiled=True)  14 us
    ppermute x14, waiting for transfers between devices, along(): return lax.ppermute(value, 'col', [(i, i ^ s) for i in range(col_devices)])  10.6 us
  transfers between devices with their start and end apart: 33, of which 18 were waited for; matrix products, arithmetic and copies ran while one was open for 3% of the time, Pallas kernels for 12%

profile of v3, /device:TPU:0, one launch (start us, length us, event | category | flops | bytes accessed | tf_op | source)
XLA Modules:
  0.0 307.6 jit_solution(13595419843525950664)
XLA Ops:
  7.2 3.1 %pack_features.1 = bf16[1024,512]{1,0:T(8,128)(2,1)} custom-call(s32[1,512]{1,0:T(1,128)} %bitcast.88, bf16[512,512]{1,0:T(8,128)(2,1)} %value_ref.1), custom_call_target="tpu_custom_call" | custom-call | flops 536870912 | bytes 1572864 | tf_op jit(solution)/shard_map/pack_features/pallas_call | solution.py:243
  10.3 7.3 %all-to-all-start = ((bf16[32,32,512]{2,1,0:T(8,128)(2,1)}), bf16[32,32,512]{2,1,0:T(8,128)(2,1)S(1)}, u32[]{:S(2)}, u32[]{:S(2)}) async-start(bf16[32,32,512]{2,1,0:T(8,128)(2,1)} %bitcast.83), calls=%async_computation | async-start | bytes 2097152 | tf_op jit(solution)/shard_map/all_to_all | solution.py:225
  17.7 0.7 reshape_squeeze.3.cols_ref
  18.4 3.7 %index_cotangent.1 = (bf16[1024,640]{1,0:T(8,128)(2,1)}, s32[512,128]{1,0:T(8,128)}, s32[8,512]{1,0:T(8,128)}, s32[512,128]{1,0:T(8,128)}, s32[8,512]{1,0:T(8,128)}, /*index=5*/s32[512,128]{1,0:T(8,128)}) custom-call(s32[1,512]{1,0:T(1,128)} %bitcast.89, s32[1,512]{1,0:T(1,128)} %bitcast.90, s32[1,512]{1,0:T(1,128)} %bitcast.91, bf16[512,512]{1,0:T(8,128)(2,1)} %cot_ref.1), custom_call_target="tpu_custom_call" | custom-call | flops 536870912 | bytes 1572864 | tf_op jit(solution)/shard_map/index_cotangent/pallas_call | solution.py:252
  22.7 22.5 %all-to-all-done = bf16[32,32,512]{2,1,0:T(8,128)(2,1)S(1)} async-done(((bf16[32,32,512]{2,1,0:T(8,128)(2,1)}), bf16[32,32,512]{2,1,0:T(8,128)(2,1)S(1)}, u32[]{:S(2)}, u32[]{:S(2)}) %all-to-all-start) | async-done | bytes 1048608 | tf_op jit(solution)/shard_map/all_to_all | solution.py:225
  45.2 1.0 copy-done.4
  46.2 2.9 unpack_features.1.refs_4_.x_ref
  49.1 19.5 %all_to_all.30 = bf16[4,256,640]{2,1,0:T(8,128)(2,1)S(1)} all-to-all(bf16[4,256,640]{2,1,0:T(8,128)(2,1)S(1)} %bitcast.76), channel_id=1, replica_groups=mesh['row'=4,'col'=8] {'row'}, dimensions={0} | all-to-all | bytes 2621440 | tf_op jit(solution)/shard_map/all_to_all | solution.py:229
  68.6 1.2 copy.18
  69.8 24.2 %all-gather.2.cloned.1.call-done.x_hbm = bf16[4096,512]{1,0:T(8,128)(2,1)} async-done(((bf16[512,512]{1,0:T(8,128)(2,1)}), bf16[4096,512]{1,0:T(8,128)(2,1)}) %all-gather.2.cloned.1.call-update) | async-done | bytes 4194320 | tf_op jit(solution)/shard_map/all_gather | solution.py:276
  94.0 3.6 %all-to-all-start.2 = ((bf16[8,128,640]{2,1,0:T(8,128)(2,1)}), bf16[8,128,640]{2,1,0:T(8,128)(2,1)S(1)}, u32[]{:S(2)}, u32[]{:S(2)}) async-start(bf16[8,128,640]{2,1,0:T(8,128)(2,1)} %bitcast.10), calls=%async_computation.2 | async-start | bytes 2621440 | tf_op jit(solution)/shard_map/all_to_all | solution.py:233
  97.6 8.4 %spmm.1 = (bf16[512,512]{1,0:T(8,128)(2,1)}, bf16[512,512]{1,0:T(8,128)(2,1)}, bf16[512,512]{1,0:T(8,128)(2,1)}, bf16[512,512]{1,0:T(8,128)(2,1)}) custom-call(s32[128]{0:T(128)} %reshape_squeeze.3.cols_ref, s32[4]{0:T(128)} %iota_xor_fusion.1.group_ref.index_ref, bf16[4096,512]{1,0:T(8,128)(2,1)} %all-gather.2.cloned.1.call-done.x_hbm, ...), custom_call_target="tpu_custom_call" | custom-call | flops 2147483648 | bytes 10485760 | tf_op jit(solution)/shard_map/spmm/pallas_call | solution.py:286
  106.0 1.6 collective-permute-start
  107.6 1.5 collective-permute-start.1
  109.6 11.5 %collective-permute-done.refs_1_ = bf16[512,512]{1,0:T(8,128)(2,1)S(1)} collective-permute-done((bf16[512,512]{1,0:T(8,128)(2,1)}, bf16[512,512]{1,0:T(8,128)(2,1)S(1)}, u32[]{:S(2)}, u32[]{:S(2)}) %collective-permute-start) | collective-permute-done | bytes 524320 | tf_op jit(solution)/shard_map/ppermute | solution.py:239
  121.0 11.9 %collective-permute-done.1.refs_2_ = bf16[512,512]{1,0:T(8,128)(2,1)S(1)} collective-permute-done((bf16[512,512]{1,0:T(8,128)(2,1)}, bf16[512,512]{1,0:T(8,128)(2,1)S(1)}, u32[]{:S(2)}, u32[]{:S(2)}) %collective-permute-start.1) | collective-permute-done | bytes 524320 | tf_op jit(solution)/shard_map/ppermute | solution.py:239
  133.0 0.8 copy-done.10
  134.4 6.9 %layer.1 = (bf16[1024,512]{1,0:T(8,128)(2,1)}, bf16[512,512]{1,0:T(8,128)(2,1)}, bf16[512,512]{1,0:T(8,128)(2,1)}, bf16[512,512]{1,0:T(8,128)(2,1)}) custom-call(bf16[512,512]{1,0:T(8,128)(2,1)} %get-tuple-element.48.refs_0_, bf16[512,512]{1,0:T(8,128)(2,1)} %copy-done.9, bf16[512,512]{1,0:T(8,128)(2,1)} %copy-done.10, bf16[512,512]{1,0:T(8,128)(2,1)} %copy-done.11, ...), custom_call_target="tpu_custom_call" | custom-call | flops 1342177280 | bytes 6815744 | tf_op jit(solution)/shard_map/layer/pallas_call | solution.py:300
  141.3 4.9 %all-to-all-start.3 = ((bf16[8,128,512]{2,1,0:T(8,128)(2,1)}), bf16[8,128,512]{2,1,0:T(8,128)(2,1)S(1)}, u32[]{:S(2)}, u32[]{:S(2)}) async-start(bf16[8,128,512]{2,1,0:T(8,128)(2,1)} %bitcast.81), calls=%async_computation.3 | async-start | bytes 2097152 | tf_op jit(solution)/shard_map/all_to_all | solution.py:233
  146.2 1.1 collective-permute-start.3
  147.3 1.0 collective-permute-start.4
  148.3 1.5 collective-permute-start.5
  156.3 3.6 %terms.1 = (bf16[1024,512]{1,0:T(8,128)(2,1)}, f32[512,512]{1,0:T(8,128)}) custom-call(bf16[512,512]{1,0:T(8,128)(2,1)} %unpack_features.1.refs_4_.x_ref, bf16[512,512]{1,0:T(8,128)(2,1)} %get-tuple-element.56.agg_ref, bf16[512,512]{1,0:T(8,128)(2,1)} %get-tuple-element.57.slopes_ref, bf16[512,512]{1,0:T(8,128)(2,1)} %self_ref.1), custom_call_target="tpu_custom_call" | custom-call | flops 805306368 | bytes 4718592 | tf_op jit(solution)/shard_map/terms/pallas_call | solution.py:310
  160.0 1.1 collective-permute-done.3.refs_1_
  161.0 10.1 %collective-permute-done.4.refs_2_ = bf16[512,512]{1,0:T(8,128)(2,1)S(1)} collective-permute-done((bf16[512,512]{1,0:T(8,128)(2,1)S(1)}, bf16[512,512]{1,0:T(8,128)(2,1)S(1)}, u32[]{:S(2)}, u32[]{:S(2)}) %collective-permute-start.4) | collective-permute-done | bytes 524320 | tf_op jit(solution)/shard_map/ppermute | solution.py:239
  171.1 1.6 collective-permute-done.5.refs_3_
  172.8 2.3 dynamic-slice_bitcast_fusion
  175.1 1.0 collective-permute-start.6
  176.1 1.5 collective-permute-start.7
  177.6 1.0 collective-permute-start.8
  178.6 10.4 %spmm_back.1 = bf16[4096,512]{1,0:T(8,128)(2,1)} custom-call(s32[128]{0:T(128)} %reshape_squeeze.3.cols_ref, s32[4]{0:T(128)} %iota_xor_fusion.1.group_ref.index_ref, bf16[512,512]{1,0:T(8,128)(2,1)} %get-tuple-element.60.refs_0_, bf16[512,512]{1,0:T(8,128)(2,1)} %copy-done.6, bf16[512,512]{1,0:T(8,128)(2,1)} %copy-done.7, bf16[512,512]{1,0:T(8,128)(2,1)} %copy-done.8, ...), custom_call_target="tpu_custom_call" | custom-call | flops 2147483648 | bytes 10485760 | tf_op jit(solution)/shard_map/spmm_back/pallas_call | solution.py:325
  189.8 0.7 fusion.9
  204.1 1.0 copy.19
  205.2 3.7 %all-to-all-start.4 = ((bf16[4,256,512]{2,1,0:T(8,128)(2,1)}), bf16[4,256,512]{2,1,0:T(8,128)(2,1)S(1)}, u32[]{:S(2)}, u32[]{:S(2)}) async-start(bf16[4,256,512]{2,1,0:T(8,128)(2,1)} %bitcast.24), calls=%async_computation.4 | async-start | bytes 2097152 | tf_op jit(solution)/shard_map/all_to_all | solution.py:229
  208.9 1.1 add_convert_fusion
  210.0 1.5 collective-permute-start.15
  211.6 2.0 collective-permute-start.14
  214.0 2.2 collective-permute-start.12
  216.3 0.8 collective-permute-start.11
  217.1 0.9 collective-permute-start.10
  218.2 1.4 collective-permute-start.9
  219.6 3.4 %collective-permute-done.13 = bf16[32,512]{1,0:T(8,128)(2,1)S(1)} collective-permute-done((bf16[32,512]{1,0:T(8,128)(2,1)S(1)}, bf16[32,512]{1,0:T(8,128)(2,1)S(1)}, u32[]{:S(2)}, u32[]{:S(2)}) %collective-permute-start.13) | collective-permute-done | bytes 32800 | tf_op jit(solution)/shard_map/ppermute | solution.py:346
  223.0 1.4 collective-permute-done.12
  225.0 1.4 collective-permute-start.18
  226.4 1.6 collective-permute-start.19
  228.0 1.2 collective-permute-start.20
  229.2 2.7 collective-permute-start.21
  231.9 0.8 collective-permute-start.22
  232.8 3.2 %collective-permute-done.20.refs_5_ = bf16[32,512]{1,0:T(8,128)(2,1)S(1)} collective-permute-done((bf16[32,512]{1,0:T(8,128)(2,1)S(1)}, bf16[32,512]{1,0:T(8,128)(2,1)S(1)}, u32[]{:S(2)}, u32[]{:S(2)}) %collective-permute-start.20) | collective-permute-done | bytes 32800 | tf_op jit(solution)/shard_map/ppermute | solution.py:346
  236.2 2.0 collective-permute-done.22.refs_7_
  238.9 1.6 in_place.2
  240.5 1.8 collective-permute-start.23
  242.3 1.5 collective-permute-start.24
  244.0 5.9 %collective-permute-done.23.refs_1_ = bf16[256,512]{1,0:T(8,128)(2,1)S(1)} collective-permute-done((bf16[256,512]{1,0:T(8,128)(2,1)}, bf16[256,512]{1,0:T(8,128)(2,1)S(1)}, u32[]{:S(2)}, u32[]{:S(2)}) %collective-permute-start.23) | collective-permute-done | bytes 262176 | tf_op jit(solution)/shard_map/ppermute | solution.py:239
  249.8 6.4 %collective-permute-done.24.refs_2_ = bf16[256,512]{1,0:T(8,128)(2,1)S(1)} collective-permute-done((bf16[256,512]{1,0:T(8,128)(2,1)}, bf16[256,512]{1,0:T(8,128)(2,1)S(1)}, u32[]{:S(2)}, u32[]{:S(2)}) %collective-permute-start.24) | collective-permute-done | bytes 262176 | tf_op jit(solution)/shard_map/ppermute | solution.py:239
  256.2 0.7 copy-done.15
  256.9 0.7 copy-done.16
  257.7 2.7 in_place.3
  260.4 3.3 %join_pack.1 = bf16[1024,512]{1,0:T(8,128)(2,1)} custom-call(f32[512,512]{1,0:T(8,128)} %get-tuple-element.72.own_ref, bf16[512,512]{1,0:T(8,128)(2,1)} %reduce-scatter.2.cloned.1.call-done.neigh_ref, s32[8,512]{1,0:T(8,128)} %get-tuple-element.74.row_ref), custom_call_target="tpu_custom_call" | custom-call | flops 536870912 | bytes 2097152 | tf_op jit(solution)/shard_map/join_pack/pallas_call | solution.py:367
  263.6 6.7 %all-to-all-start.5 = ((bf16[32,32,512]{2,1,0:T(8,128)(2,1)}), bf16[32,32,512]{2,1,0:T(8,128)(2,1)}, u32[]{:S(2)}, u32[]{:S(2)}) async-start(bf16[32,32,512]{2,1,0:T(8,128)(2,1)} %bitcast.75), calls=%async_computation.6 | async-start | bytes 2097152 | tf_op jit(solution)/shard_map/all_to_all | solution.py:225
  270.3 1.5 fusion.8
  271.8 2.9 unpack_owner.2
  274.7 23.2 %all-to-all-done.5 = bf16[32,32,512]{2,1,0:T(8,128)(2,1)} async-done(((bf16[32,32,512]{2,1,0:T(8,128)(2,1)}), bf16[32,32,512]{2,1,0:T(8,128)(2,1)}, u32[]{:S(2)}, u32[]{:S(2)}) %all-to-all-start.5) | async-done | bytes 1048608 | tf_op jit(solution)/shard_map/all_to_all | solution.py:225
  297.9 2.9 unpack_owner.3
  (86 shorter events, 6.1 us)
Async XLA Ops:
  7.2 10.5 %copy-start.27 = (s32[1,1,16,8]{2,3,1,0:T(8,128)S(1)}, s32[1,1,16,8]{2,3,1,0:T(8,128)}, u32[]{:S(2)}) copy-start(s32[1,1,16,8]{2,3,1,0:T(8,128)} %param.10) | copy-start | bytes 1540
  10.3 34.9 %all-to-all-start = ((bf16[32,32,512]{2,1,0:T(8,128)(2,1)}), bf16[32,32,512]{2,1,0:T(8,128)(2,1)S(1)}, u32[]{:S(2)}, u32[]{:S(2)}) async-start(bf16[32,32,512]{2,1,0:T(8,128)(2,1)} %bitcast.83), calls=%async_computation | async-start | bytes 2097152 | tf_op jit(solution)/shard_map/all_to_all | solution.py:225
  17.6 76.4 %all-gather.2.cloned.1.call-start = ((), (), s32[]{:S(2)}) async-start(), calls=%async_computation.7 | async-start | bytes 4718592 | tf_op jit(solution)/shard_map/all_gather | solution.py:276
  22.1 26.9 %copy-start.2 = (bf16[1024,640]{1,0:T(8,128)(2,1)S(1)}, bf16[1024,640]{1,0:T(8,128)(2,1)}, u32[]{:S(2)}) copy-start(bf16[1024,640]{1,0:T(8,128)(2,1)} %get-tuple-element.46) | copy-start | bytes 3932164
  45.2 1.0 copy-start.4
  94.0 38.9 %all-to-all-start.2 = ((bf16[8,128,640]{2,1,0:T(8,128)(2,1)}), bf16[8,128,640]{2,1,0:T(8,128)(2,1)S(1)}, u32[]{:S(2)}, u32[]{:S(2)}) async-start(bf16[8,128,640]{2,1,0:T(8,128)(2,1)} %bitcast.10), calls=%async_computation.2 | async-start | bytes 2621440 | tf_op jit(solution)/shard_map/all_to_all | solution.py:233
  106.0 15.0 %collective-permute-start = (bf16[512,512]{1,0:T(8,128)(2,1)}, bf16[512,512]{1,0:T(8,128)(2,1)S(1)}, u32[]{:S(2)}, u32[]{:S(2)}) collective-permute-start(bf16[512,512]{1,0:T(8,128)(2,1)} %get-tuple-element.49), channel_id=1, source_target_pairs={{0,8},{8,0},{16,24},{24,16},{1,9},{9,1},{17,25},{25,17},{2,10},{10... | collective-permute-start | bytes 1572872 | tf_op jit(solution)/shard_map/ppermute | solution.py:239
  107.6 25.4 %collective-permute-start.1 = (bf16[512,512]{1,0:T(8,128)(2,1)}, bf16[512,512]{1,0:T(8,128)(2,1)S(1)}, u32[]{:S(2)}, u32[]{:S(2)}) collective-permute-start(bf16[512,512]{1,0:T(8,128)(2,1)} %get-tuple-element.50), channel_id=1, source_target_pairs={{0,16},{8,24},{16,0},{24,8},{1,17},{9,25},{17,1},{25,9},{2,18},{10... | collective-permute-start | bytes 1572872 | tf_op jit(solution)/shard_map/ppermute | solution.py:239
  109.0 23.9 %collective-permute-start.2 = (bf16[512,512]{1,0:T(8,128)(2,1)}, bf16[512,512]{1,0:T(8,128)(2,1)S(1)}, u32[]{:S(2)}, u32[]{:S(2)}) collective-permute-start(bf16[512,512]{1,0:T(8,128)(2,1)} %get-tuple-element.51), channel_id=1, source_target_pairs={{0,24},{8,16},{16,8},{24,0},{1,25},{9,17},{17,9},{25,1},{2,26},{10... | collective-permute-start | bytes 1572872 | tf_op jit(solution)/shard_map/ppermute | solution.py:239
  121.0 11.9 %copy-start.9 = (bf16[512,512]{1,0:T(8,128)(2,1)}, bf16[512,512]{1,0:T(8,128)(2,1)S(1)}, u32[]{:S(2)}) copy-start(bf16[512,512]{1,0:T(8,128)(2,1)S(1)} %collective-permute-done.refs_1_) | copy-start | bytes 1572868
  132.9 0.8 copy-start.10
  132.9 1.0 copy-start.11
  132.9 1.4 copy-start.1
  141.3 5.0 %copy-start.5 = (bf16[512,512]{1,0:T(8,128)(2,1)S(1)}, bf16[512,512]{1,0:T(8,128)(2,1)}, u32[]{:S(2)}) copy-start(bf16[512,512]{1,0:T(8,128)(2,1)} %get-tuple-element.60.refs_0_) | copy-start | bytes 1572868
  141.3 8.5 %copy-start.26 = (s32[4]{0:T(128)S(1)}, s32[4]{0:T(128)}, u32[]{:S(2)}) copy-start(s32[4]{0:T(128)} %iota_xor_fusion.1.group_ref.index_ref) | copy-start | bytes 52
  141.3 47.8 %all-to-all-start.3 = ((bf16[8,128,512]{2,1,0:T(8,128)(2,1)}), bf16[8,128,512]{2,1,0:T(8,128)(2,1)S(1)}, u32[]{:S(2)}, u32[]{:S(2)}) async-start(bf16[8,128,512]{2,1,0:T(8,128)(2,1)} %bitcast.81), calls=%async_computation.3 | async-start | bytes 2097152 | tf_op jit(solution)/shard_map/all_to_all | solution.py:233
  146.2 114.2 %reduce-scatter.2.cloned.1.call-start = ((), (), s32[]{:S(2)}) async-start(), calls=%async_computation.8 | async-start | bytes 4718592 | tf_op jit(solution)/shard_map/reduce_scatter | solution.py:340
  146.2 14.8 %collective-permute-start.3 = (bf16[512,512]{1,0:T(8,128)(2,1)S(1)}, bf16[512,512]{1,0:T(8,128)(2,1)S(1)}, u32[]{:S(2)}, u32[]{:S(2)}) collective-permute-start(bf16[512,512]{1,0:T(8,128)(2,1)S(1)} %copy-done.5), channel_id=1, source_target_pairs={{0,8},{8,0},{16,24},{24,16},{1,9},{9,1},{17,25},{25,17},{2,10},{10... | collective-permute-start | bytes 1572872 | tf_op jit(solution)/shard_map/ppermute | solution.py:239
  147.3 23.8 %collective-permute-start.4 = (bf16[512,512]{1,0:T(8,128)(2,1)S(1)}, bf16[512,512]{1,0:T(8,128)(2,1)S(1)}, u32[]{:S(2)}, u32[]{:S(2)}) collective-permute-start(bf16[512,512]{1,0:T(8,128)(2,1)S(1)} %copy-done.5), channel_id=1, source_target_pairs={{0,16},{8,24},{16,0},{24,8},{1,17},{9,25},{17,1},{25,9},{2,18},{10... | collective-permute-start | bytes 1572872 | tf_op jit(solution)/shard_map/ppermute | solution.py:239
  148.3 24.4 %collective-permute-start.5 = (bf16[512,512]{1,0:T(8,128)(2,1)S(1)}, bf16[512,512]{1,0:T(8,128)(2,1)S(1)}, u32[]{:S(2)}, u32[]{:S(2)}) collective-permute-start(bf16[512,512]{1,0:T(8,128)(2,1)S(1)} %copy-done.5), channel_id=1, source_target_pairs={{0,24},{8,16},{16,8},{24,0},{1,25},{9,17},{17,9},{25,1},{2,26},{10... | collective-permute-start | bytes 1572872 | tf_op jit(solution)/shard_map/ppermute | solution.py:239
  161.0 17.5 %copy-start.6 = (bf16[512,512]{1,0:T(8,128)(2,1)}, bf16[512,512]{1,0:T(8,128)(2,1)S(1)}, u32[]{:S(2)}) copy-start(bf16[512,512]{1,0:T(8,128)(2,1)S(1)} %collective-permute-done.3.refs_1_) | copy-start | bytes 1572868
  171.1 7.4 %copy-start.7 = (bf16[512,512]{1,0:T(8,128)(2,1)}, bf16[512,512]{1,0:T(8,128)(2,1)S(1)}, u32[]{:S(2)}) copy-start(bf16[512,512]{1,0:T(8,128)(2,1)S(1)} %collective-permute-done.4.refs_2_) | copy-start | bytes 1572868
  172.8 5.8 %copy-start.8 = (bf16[512,512]{1,0:T(8,128)(2,1)}, bf16[512,512]{1,0:T(8,128)(2,1)S(1)}, u32[]{:S(2)}) copy-start(bf16[512,512]{1,0:T(8,128)(2,1)S(1)} %collective-permute-done.5.refs_3_) | copy-start | bytes 1572868
  175.1 13.9 %collective-permute-start.6 = (bf16[256,512]{1,0:T(8,128)(2,1)}, bf16[256,512]{1,0:T(8,128)(2,1)S(1)}, u32[]{:S(2)}, u32[]{:S(2)}) collective-permute-start(bf16[256,512]{1,0:T(8,128)(2,1)} %get-tuple-element.80), channel_id=1, source_target_pairs={{0,8},{8,0},{16,24},{24,16},{1,9},{9,1},{17,25},{25,17},{2,10},{10... | collective-permute-start | bytes 786440 | tf_op jit(solution)/shard_map/ppermute | solution.py:239
  176.1 13.0 %collective-permute-start.7 = (bf16[256,512]{1,0:T(8,128)(2,1)}, bf16[256,512]{1,0:T(8,128)(2,1)S(1)}, u32[]{:S(2)}, u32[]{:S(2)}) collective-permute-start(bf16[256,512]{1,0:T(8,128)(2,1)} %get-tuple-element.79), channel_id=1, source_target_pairs={{0,16},{8,24},{16,0},{24,8},{1,17},{9,25},{17,1},{25,9},{2,18},{10... | collective-permute-start | bytes 786440 | tf_op jit(solution)/shard_map/ppermute | solution.py:239
  177.6 11.5 %collective-permute-start.8 = (bf16[256,512]{1,0:T(8,128)(2,1)}, bf16[256,512]{1,0:T(8,128)(2,1)}, u32[]{:S(2)}, u32[]{:S(2)}) collective-permute-start(bf16[256,512]{1,0:T(8,128)(2,1)} %get-tuple-element.78), channel_id=1, source_target_pairs={{0,24},{8,16},{16,8},{24,0},{1,25},{9,17},{17,9},{25,1},{2,26},{10... | collective-permute-start | bytes 786440 | tf_op jit(solution)/shard_map/ppermute | solution.py:239
  189.1 0.7 copy-start.12
  189.8 15.4 %copy-start.18 = (s32[8]{0:T(128)}, s32[8]{0:T(128)S(1)}, u32[]{:S(2)}) copy-start(s32[8]{0:T(128)S(1)} %iota_xor_fusion.index_ref) | copy-start | bytes 100
  204.1 4.8 %copy-start.13 = (bf16[256,512]{1,0:T(8,128)(2,1)S(1)}, bf16[256,512]{1,0:T(8,128)(2,1)}, u32[]{:S(2)}) copy-start(bf16[256,512]{1,0:T(8,128)(2,1)} %copy-done.12) | copy-start | bytes 786436
  205.2 58.5 %all-to-all-start.4 = ((bf16[4,256,512]{2,1,0:T(8,128)(2,1)}), bf16[4,256,512]{2,1,0:T(8,128)(2,1)S(1)}, u32[]{:S(2)}, u32[]{:S(2)}) async-start(bf16[4,256,512]{2,1,0:T(8,128)(2,1)} %bitcast.24), calls=%async_computation.4 | async-start | bytes 2097152 | tf_op jit(solution)/shard_map/all_to_all | solution.py:229
  210.0 7.0 %collective-permute-start.15 = (bf16[32,512]{1,0:T(8,128)(2,1)S(1)}, bf16[32,512]{1,0:T(8,128)(2,1)S(1)}, u32[]{:S(2)}, u32[]{:S(2)}) collective-permute-start(bf16[32,512]{1,0:T(8,128)(2,1)S(1)} %get-tuple-element.83), channel_id=1, source_target_pairs={{0,7},{1,6},{2,5},{3,4},{4,3},{5,2},{6,1},{7,0},{8,15},{9,14},{10,... | collective-permute-start | bytes 98312 | tf_op jit(solution)/shard_map/ppermute | solution.py:346
  211.6 6.6 %collective-permute-start.14 = (bf16[32,512]{1,0:T(8,128)(2,1)S(1)}, bf16[32,512]{1,0:T(8,128)(2,1)S(1)}, u32[]{:S(2)}, u32[]{:S(2)}) collective-permute-start(bf16[32,512]{1,0:T(8,128)(2,1)S(1)} %get-tuple-element.84), channel_id=1, source_target_pairs={{0,6},{1,7},{2,4},{3,5},{4,2},{5,3},{6,0},{7,1},{8,14},{9,15},{10,... | collective-permute-start | bytes 98312 | tf_op jit(solution)/shard_map/ppermute | solution.py:346
  213.6 9.4 %collective-permute-start.13 = (bf16[32,512]{1,0:T(8,128)(2,1)S(1)}, bf16[32,512]{1,0:T(8,128)(2,1)S(1)}, u32[]{:S(2)}, u32[]{:S(2)}) collective-permute-start(bf16[32,512]{1,0:T(8,128)(2,1)S(1)} %get-tuple-element.85), channel_id=1, source_target_pairs={{0,5},{1,4},{2,7},{3,6},{4,1},{5,0},{6,3},{7,2},{8,13},{9,12},{10,... | collective-permute-start | bytes 98312 | tf_op jit(solution)/shard_map/ppermute | solution.py:346
  214.0 10.4 %collective-permute-start.12 = (bf16[32,512]{1,0:T(8,128)(2,1)S(1)}, bf16[32,512]{1,0:T(8,128)(2,1)S(1)}, u32[]{:S(2)}, u32[]{:S(2)}) collective-permute-start(bf16[32,512]{1,0:T(8,128)(2,1)S(1)} %get-tuple-element.86), channel_id=1, source_target_pairs={{0,4},{1,5},{2,6},{3,7},{4,0},{5,1},{6,2},{7,3},{8,12},{9,13},{10,... | collective-permute-start | bytes 98312 | tf_op jit(solution)/shard_map/ppermute | solution.py:346
  216.3 8.1 %collective-permute-start.11 = (bf16[32,512]{1,0:T(8,128)(2,1)S(1)}, bf16[32,512]{1,0:T(8,128)(2,1)S(1)}, u32[]{:S(2)}, u32[]{:S(2)}) collective-permute-start(bf16[32,512]{1,0:T(8,128)(2,1)S(1)} %get-tuple-element.87), channel_id=1, source_target_pairs={{0,3},{1,2},{2,1},{3,0},{4,7},{5,6},{6,5},{7,4},{8,11},{9,10},{10,... | collective-permute-start | bytes 98312 | tf_op jit(solution)/shard_map/ppermute | solution.py:346
  217.1 7.3 %collective-permute-start.10 = (bf16[32,512]{1,0:T(8,128)(2,1)S(1)}, bf16[32,512]{1,0:T(8,128)(2,1)S(1)}, u32[]{:S(2)}, u32[]{:S(2)}) collective-permute-start(bf16[32,512]{1,0:T(8,128)(2,1)S(1)} %get-tuple-element.88), channel_id=1, source_target_pairs={{0,2},{1,3},{2,0},{3,1},{4,6},{5,7},{6,4},{7,5},{8,10},{9,11},{10,... | collective-permute-start | bytes 98312 | tf_op jit(solution)/shard_map/ppermute | solution.py:346
  218.2 6.2 %collective-permute-start.9 = (bf16[32,512]{1,0:T(8,128)(2,1)S(1)}, bf16[32,512]{1,0:T(8,128)(2,1)S(1)}, u32[]{:S(2)}, u32[]{:S(2)}) collective-permute-start(bf16[32,512]{1,0:T(8,128)(2,1)S(1)} %get-tuple-element.82), channel_id=1, source_target_pairs={{0,1},{1,0},{2,3},{3,2},{4,5},{5,4},{6,7},{7,6},{8,9},{9,8},{10,11... | collective-permute-start | bytes 98312 | tf_op jit(solution)/shard_map/ppermute | solution.py:346
  224.5 13.7 %copy-start.17 = (bf16[32,512]{1,0:T(8,128)(2,1)}, bf16[32,512]{1,0:T(8,128)(2,1)S(1)}, u32[]{:S(2)}) copy-start(bf16[32,512]{1,0:T(8,128)(2,1)S(1)} %fusion.7.refs_0_) | copy-start | bytes 98308
  224.5 4.7 %collective-permute-start.16 = (bf16[32,512]{1,0:T(8,128)(2,1)S(1)}, bf16[32,512]{1,0:T(8,128)(2,1)S(1)}, u32[]{:S(2)}, u32[]{:S(2)}) collective-permute-start(bf16[32,512]{1,0:T(8,128)(2,1)S(1)} %fusion.7.refs_0_), channel_id=1, source_target_pairs={{0,1},{1,0},{2,3},{3,2},{4,5},{5,4},{6,7},{7,6},{8,9},{9,8},{10,11... | collective-permute-start | bytes 98312 | tf_op jit(solution)/shard_map/ppermute | solution.py:346
  224.8 7.1 %collective-permute-start.17 = (bf16[32,512]{1,0:T(8,128)(2,1)S(1)}, bf16[32,512]{1,0:T(8,128)(2,1)S(1)}, u32[]{:S(2)}, u32[]{:S(2)}) collective-permute-start(bf16[32,512]{1,0:T(8,128)(2,1)S(1)} %fusion.7.refs_0_), channel_id=1, source_target_pairs={{0,2},{1,3},{2,0},{3,1},{4,6},{5,7},{6,4},{7,5},{8,10},{9,11},{10,... | collective-permute-start | bytes 98312 | tf_op jit(solution)/shard_map/ppermute | solution.py:346
  225.0 7.6 %collective-permute-start.18 = (bf16[32,512]{1,0:T(8,128)(2,1)S(1)}, bf16[32,512]{1,0:T(8,128)(2,1)S(1)}, u32[]{:S(2)}, u32[]{:S(2)}) collective-permute-start(bf16[32,512]{1,0:T(8,128)(2,1)S(1)} %fusion.7.refs_0_), channel_id=1, source_target_pairs={{0,3},{1,2},{2,1},{3,0},{4,7},{5,6},{6,5},{7,4},{8,11},{9,10},{10,... | collective-permute-start | bytes 98312 | tf_op jit(solution)/shard_map/ppermute | solution.py:346
  226.4 6.4 %collective-permute-start.19 = (bf16[32,512]{1,0:T(8,128)(2,1)S(1)}, bf16[32,512]{1,0:T(8,128)(2,1)S(1)}, u32[]{:S(2)}, u32[]{:S(2)}) collective-permute-start(bf16[32,512]{1,0:T(8,128)(2,1)S(1)} %fusion.7.refs_0_), channel_id=1, source_target_pairs={{0,4},{1,5},{2,6},{3,7},{4,0},{5,1},{6,2},{7,3},{8,12},{9,13},{10,... | collective-permute-start | bytes 98312 | tf_op jit(solution)/shard_map/ppermute | solution.py:346
  228.0 7.9 %collective-permute-start.20 = (bf16[32,512]{1,0:T(8,128)(2,1)S(1)}, bf16[32,512]{1,0:T(8,128)(2,1)S(1)}, u32[]{:S(2)}, u32[]{:S(2)}) collective-permute-start(bf16[32,512]{1,0:T(8,128)(2,1)S(1)} %fusion.7.refs_0_), channel_id=1, source_target_pairs={{0,5},{1,4},{2,7},{3,6},{4,1},{5,0},{6,3},{7,2},{8,13},{9,12},{10,... | collective-permute-start | bytes 98312 | tf_op jit(solution)/shard_map/ppermute | solution.py:346
  229.2 9.0 %copy-start.19 = (bf16[32,512]{1,0:T(8,128)(2,1)}, bf16[32,512]{1,0:T(8,128)(2,1)S(1)}, u32[]{:S(2)}) copy-start(bf16[32,512]{1,0:T(8,128)(2,1)S(1)} %collective-permute-done.16.refs_1_) | copy-start | bytes 98308
  229.2 7.0 %collective-permute-start.21 = (bf16[32,512]{1,0:T(8,128)(2,1)S(1)}, bf16[32,512]{1,0:T(8,128)(2,1)S(1)}, u32[]{:S(2)}, u32[]{:S(2)}) collective-permute-start(bf16[32,512]{1,0:T(8,128)(2,1)S(1)} %fusion.7.refs_0_), channel_id=1, source_target_pairs={{0,6},{1,7},{2,4},{3,5},{4,2},{5,3},{6,0},{7,1},{8,14},{9,15},{10,... | collective-permute-start | bytes 98312 | tf_op jit(solution)/shard_map/ppermute | solution.py:346
  231.9 6.3 %copy-start.20 = (bf16[32,512]{1,0:T(8,128)(2,1)}, bf16[32,512]{1,0:T(8,128)(2,1)S(1)}, u32[]{:S(2)}) copy-start(bf16[32,512]{1,0:T(8,128)(2,1)S(1)} %collective-permute-done.17.refs_2_) | copy-start | bytes 98308
  231.9 6.3 %collective-permute-start.22 = (bf16[32,512]{1,0:T(8,128)(2,1)S(1)}, bf16[32,512]{1,0:T(8,128)(2,1)S(1)}, u32[]{:S(2)}, u32[]{:S(2)}) collective-permute-start(bf16[32,512]{1,0:T(8,128)(2,1)S(1)} %fusion.7.refs_0_), channel_id=1, source_target_pairs={{0,7},{1,6},{2,5},{3,4},{4,3},{5,2},{6,1},{7,0},{8,15},{9,14},{10,... | collective-permute-start | bytes 98312 | tf_op jit(solution)/shard_map/ppermute | solution.py:346
  232.6 5.6 %copy-start.21 = (bf16[32,512]{1,0:T(8,128)(2,1)}, bf16[32,512]{1,0:T(8,128)(2,1)S(1)}, u32[]{:S(2)}) copy-start(bf16[32,512]{1,0:T(8,128)(2,1)S(1)} %collective-permute-done.18.refs_3_) | copy-start | bytes 98308
  232.8 5.4 %copy-start.22 = (bf16[32,512]{1,0:T(8,128)(2,1)}, bf16[32,512]{1,0:T(8,128)(2,1)S(1)}, u32[]{:S(2)}) copy-start(bf16[32,512]{1,0:T(8,128)(2,1)S(1)} %collective-permute-done.19.refs_4_) | copy-start | bytes 98308
  235.9 2.3 copy-start.23
  236.2 2.0 copy-start.24
  238.2 0.6 copy-start.25
  240.5 9.3 %collective-permute-start.23 = (bf16[256,512]{1,0:T(8,128)(2,1)}, bf16[256,512]{1,0:T(8,128)(2,1)S(1)}, u32[]{:S(2)}, u32[]{:S(2)}) collective-permute-start(bf16[256,512]{1,0:T(8,128)(2,1)} %bitcast.84), channel_id=1, source_target_pairs={{0,8},{8,0},{16,24},{24,16},{1,9},{9,1},{17,25},{25,17},{2,10},{10... | collective-permute-start | bytes 786440 | tf_op jit(solution)/shard_map/ppermute | solution.py:239
  242.3 14.0 %collective-permute-start.24 = (bf16[256,512]{1,0:T(8,128)(2,1)}, bf16[256,512]{1,0:T(8,128)(2,1)S(1)}, u32[]{:S(2)}, u32[]{:S(2)}) collective-permute-start(bf16[256,512]{1,0:T(8,128)(2,1)} %bitcast.85), channel_id=1, source_target_pairs={{0,16},{8,24},{16,0},{24,8},{1,17},{9,25},{17,1},{25,9},{2,18},{10... | collective-permute-start | bytes 786440 | tf_op jit(solution)/shard_map/ppermute | solution.py:239
  243.7 12.5 %collective-permute-start.25 = (bf16[256,512]{1,0:T(8,128)(2,1)}, bf16[256,512]{1,0:T(8,128)(2,1)S(1)}, u32[]{:S(2)}, u32[]{:S(2)}) collective-permute-start(bf16[256,512]{1,0:T(8,128)(2,1)} %bitcast.86), channel_id=1, source_target_pairs={{0,24},{8,16},{16,8},{24,0},{1,25},{9,17},{17,9},{25,1},{2,26},{10... | collective-permute-start | bytes 786440 | tf_op jit(solution)/shard_map/ppermute | solution.py:239
  249.8 6.4 %copy-start.14 = (bf16[256,512]{1,0:T(8,128)(2,1)}, bf16[256,512]{1,0:T(8,128)(2,1)S(1)}, u32[]{:S(2)}) copy-start(bf16[256,512]{1,0:T(8,128)(2,1)S(1)} %collective-permute-done.23.refs_1_) | copy-start | bytes 786436
  256.2 0.7 copy-start.15
  256.9 0.7 copy-start.16
  260.4 9.9 %copy-start = (f32[4,256,512]{2,1,0:T(8,128)S(1)}, f32[4,256,512]{2,1,0:T(8,128)}, u32[]{:S(2)}) copy-start(f32[4,256,512]{2,1,0:T(8,128)} %in_place.3) | copy-start | bytes 6291460
  263.6 8.2 %copy-start.3 = (bf16[4,256,512]{2,1,0:T(8,128)(2,1)}, bf16[4,256,512]{2,1,0:T(8,128)(2,1)S(1)}, u32[]{:S(2)}) copy-start(bf16[4,256,512]{2,1,0:T(8,128)(2,1)S(1)} %all-to-all-done.4) | copy-start | bytes 3145732
  263.6 34.2 %all-to-all-start.5 = ((bf16[32,32,512]{2,1,0:T(8,128)(2,1)}), bf16[32,32,512]{2,1,0:T(8,128)(2,1)}, u32[]{:S(2)}, u32[]{:S(2)}) async-start(bf16[32,32,512]{2,1,0:T(8,128)(2,1)} %bitcast.75), calls=%async_computation.6 | async-start | bytes 2097152 | tf_op jit(solution)/shard_map/all_to_all | solution.py:225
Sparse Core Ops, SparseCore 0:
  49.2 44.7 all-gather.1
  189.2 59.0 reduce-scatter.1

commit v4 on v3

--- a/solution.py
+++ b/solution.py
@@ -11,11 +11,11 @@
 BF = jnp.bfloat16
 F32 = jnp.float32
 VMEM = pl.BlockSpec(memory_space=pltpu.VMEM)
-LIMIT = 56 * 1024 * 1024
-
-
-def params():
-    return pltpu.CompilerParams(vmem_limit_bytes=LIMIT)
+MIB = 1024 * 1024
+
+
+def params(mib=16):
+    return pltpu.CompilerParams(vmem_limit_bytes=int(mib * MIB))
 
 
 def cost(flops, nbytes):
@@ -128,8 +128,9 @@
         outs[s][...] = total.astype(BF)
 
 
-def spmm_back_kernel(ways, cols_ref, group_ref, *refs):
-    spreads, masks, out_ref, total = refs[:ways], refs[ways : 2 * ways], refs[2 * ways], refs[2 * ways + 1]
+def spmm_back_kernel(ways, pieces, cols_ref, group_ref, *refs):
+    given = sum(pieces)
+    spreads, masks, out_ref, total = refs[:given], refs[given : given + ways], refs[-2], refs[-1]
     q = pl.program_id(0)
     depth = pl.num_programs(0)
     _, breadth, tile, _ = masks[0].shape
@@ -138,9 +139,13 @@
     def _():
         total[...] = jnp.zeros_like(total)
 
+    at_piece = 0
     for s in range(ways):
         base = (group_ref[s] * depth + q) * breadth
-        rows = spreads[s][...]
+        rows = spreads[at_piece][...]
+        for p in range(1, pieces[s]):
+            rows = jnp.where(q * pieces[s] >= p * depth, spreads[at_piece + p][...], rows)
+        at_piece += pieces[s]
         for k in range(breadth):
             at = pl.ds(pl.multiple_of(cols_ref[base + k] * tile, tile), tile)
             total[at, :] += dot(masks[s][0, k], rows, 0, 0)
@@ -148,6 +153,14 @@
     @pl.when(q == depth - 1)
     def _():
         out_ref[...] = total[...].astype(BF)
+
+
+def pass_on_kernel(left_ref, right_ref, top_ref, bottom_ref, left_out, right_out):
+    half = top_ref.shape[0]
+    left_out[:half, :] = left_ref[:half, :]
+    left_out[half:, :] = (left_ref[half:, :].astype(F32) + bottom_ref[...].astype(F32)).astype(BF)
+    right_out[:half, :] = (right_ref[:half, :].astype(F32) + top_ref[...].astype(F32)).astype(BF)
+    right_out[half:, :] = right_ref[half:, :]
 
 
 def layer_kernel(ways, *refs):
@@ -170,18 +183,38 @@
     packed_out[...] = dot(slots_onehot(row_ref[...][:1], packed_out.shape[0]), hidden).astype(BF)
 
 
-def terms_kernel(x_ref, agg_ref, slopes_ref, self_ref, grads_out, back_out):
-    width = x_ref.shape[1]
+def terms_kernel(core_ref, x_ref, agg_ref, slopes_ref, self_ref, kept_out, sent_out, back_out):
     slopes = slopes_ref[...]
-    grads_out[:width, :] = dot(x_ref[...], slopes, 0, 0).astype(BF)
-    grads_out[width:, :] = dot(agg_ref[...], slopes, 0, 0).astype(BF)
     back_out[...] = dot(slopes, self_ref[...], 1, 1)
+    grad_self = dot(x_ref[...], slopes, 0, 0).astype(BF)
+    grad_neigh = dot(agg_ref[...], slopes, 0, 0).astype(BF)
+    first = core_ref[0] == 0
+    kept_out[...] = jnp.where(first, grad_self, grad_neigh)
+    sent_out[...] = jnp.where(first, grad_neigh, grad_self)
+
+
+def split_sum_kernel(count, scale, index_ref, *refs):
+    terms, outs, total_ref = refs[:count], refs[count:-1], refs[-1]
+    total = terms[0][...].astype(F32)
+    for term in terms[1:]:
+        total = total + term[...].astype(F32)
+    total_ref[...] = total * scale
+    size = outs[0].shape[0]
+    for s, out in enumerate(outs):
+        out[...] = total_ref[pl.ds(pl.multiple_of(index_ref[s] * size, size), size), :].astype(out.dtype)
 
 
 def place_kernel(index_ref, *refs):
     out_ref = refs[-1]
     for s, part in enumerate(refs[:-1]):
         out_ref[index_ref[s]] = part[...].astype(out_ref.dtype)
+
+
+def final_kernel(core_ref, kept_ref, came_ref, self_out, neigh_out):
+    first = core_ref[0] == 0
+    kept, came = kept_ref[...].astype(F32), came_ref[...].astype(F32)
+    self_out[...] = jnp.where(first, kept, came)
+    neigh_out[...] = jnp.where(first, came, kept)
 
 
 def join_kernel(own_ref, neigh_ref, row_ref, out_ref):
@@ -215,7 +248,14 @@
     ways = row_devices
     groups = jnp.bitwise_xor(me, jnp.arange(ways, dtype=jnp.int32)).astype(jnp.int32)
     everyone = ("row", "col")
-    call = functools.partial(pl.pallas_call, compiler_params=params())
+    place = lax.axis_index("col")
+    lines = col_devices // 2
+    core = jnp.full((1,), lax.rem(place, 2), jnp.int32)
+    others = jnp.bitwise_xor(lax.div(place, 2), jnp.arange(lines, dtype=jnp.int32)).astype(jnp.int32)
+    SMEM = pl.BlockSpec(memory_space=pltpu.SMEM)
+
+    def call(*args, mib=16, **kwargs):
+        return pl.pallas_call(*args, compiler_params=params(mib), **kwargs)
 
     def shape(r, c, dtype=BF):
         return jax.ShapeDtypeStruct((r, c), dtype)
@@ -237,6 +277,35 @@
 
     def across(value, s):
         return lax.ppermute(value, "row", [(i, i ^ s) for i in range(ways)])
+
+    def along(value, s):
+        return lax.ppermute(value, "col", [(i, i ^ (2 * s)) for i in range(col_devices)])
+
+    def swap(value):
+        return lax.ppermute(value, "col", [(i, i ^ 1) for i in range(col_devices)])
+
+    def split_sum(index, arrays, pieces, scale=1.0):
+        r, c = arrays[0].shape
+        return call(
+            functools.partial(split_sum_kernel, len(arrays), scale),
+            in_specs=[SMEM] + [VMEM] * len(arrays),
+            out_specs=[VMEM] * pieces,
+            out_shape=[shape(r // pieces, c) for _ in range(pieces)],
+            scratch_shapes=[pltpu.VMEM((r, c), F32)],
+            cost_estimate=cost(r * c * len(arrays), 2 * r * c * (len(arrays) + 1)),
+            name="split_sum",
+        )(index, *arrays)
+
+    def in_place(index, arrays):
+        count, (r, c) = len(arrays), arrays[0].shape
+        return call(
+            place_kernel,
+            in_specs=[SMEM] + [VMEM] * count,
+            out_specs=VMEM,
+            out_shape=jax.ShapeDtypeStruct((count, r, c), BF),
+            cost_estimate=cost(0, 4 * count * r * c),
+            name="in_place",
+        )(index, *arrays).reshape(count * r, c)
 
     nodes = owner_nodes.reshape(1, rows)
     slab = rows * width
@@ -272,7 +341,9 @@
         cost_estimate=cost(2 * slots * slab, 6 * slab),
         name="unpack_features",
     )(node_col, inbound)
-    cot_packed, x_node, cols, groups = lax.optimization_barrier((cot_packed, x_node, cols, groups))
+    cot_packed, x_node, cols, groups, core, others = lax.optimization_barrier(
+        (cot_packed, x_node, cols, groups, core, others)
+    )
     x_cols = lax.all_gather(x_node, "col", axis=0, tiled=True)
     cot_mid = turn(row_phase(cot_packed), row_devices, col_devices)
     x_cols, cot_mid = lax.optimization_barrier((x_cols, cot_mid))
@@ -280,6 +351,10 @@
 
     def mask_spec(s):
         return pl.BlockSpec((1, breadth, tile, tile), lambda q, c, g, s=s: (g[s] * depth + q, 0, 0, 0))
+
+    def piece_spec(p, count):
+        share = depth // count
+        return pl.BlockSpec((tile, width), lambda q, c, g: (jnp.clip(q - p * share, 0, share - 1), 0))
 
     spmm_flops = 2 * masks.size * width
     copies = 8
@@ -294,76 +369,85 @@
         ),
         out_shape=[shape(rows, width) for s in range(ways)],
         cost_estimate=cost(spmm_flops, 2 * masks.size + 2 * x_cols.size + 2 * ways * slab),
+        mib=12 + 3 * x_cols.size / MIB,
         name="spmm",
     )(cols, groups, x_cols, *([masks] * ways))
-    terms = [partials[0]] + [across(partials[s], s) for s in range(1, ways)]
+    if ways == 4:
+        half = rows // 2
+        top = across(partials[3][:half], 1)
+        bottom = across(partials[3][half:], 2)
+        left, right = call(
+            pass_on_kernel,
+            out_shape=(shape(rows, width),) * 2,
+            in_specs=[VMEM] * 4,
+            out_specs=(VMEM,) * 2,
+            cost_estimate=cost(2 * slab, 10 * slab),
+            name="pass_on",
+        )(partials[1], partials[2], top, bottom)
+        terms = [partials[0], across(left, 1), across(right, 2)]
+    else:
+        terms = [partials[0]] + [across(partials[s], s) for s in range(1, ways)]
     hidden_packed, slopes, agg, spread = call(
-        functools.partial(layer_kernel, ways),
+        functools.partial(layer_kernel, len(terms)),
         out_shape=(shape(slots, width),) + (shape(rows, width),) * 3,
-        in_specs=[VMEM] * (ways + 6),
+        in_specs=[VMEM] * (len(terms) + 6),
         out_specs=(VMEM,) * 4,
         cost_estimate=cost(10 * slab * width, 2 * slab * (ways + 9)),
+        mib=24,
         name="layer",
     )(*terms, x_node, cot_in, turned_col, turned_row, self_weight, neigh_weight)
-    spreads = [spread] + [across(spread, s) for s in range(1, ways)]
+    if ways == 4:
+        left, right = across(spread, 1), across(spread, 2)
+        left, right, hidden_packed = lax.optimization_barrier((left, right, hidden_packed))
+        spreads = [spread, left, right, across(right[:half], 1), across(left[half:], 2)]
+        pieces = (1, 1, 1, 2)
+    else:
+        spreads = [spread] + [across(spread, s) for s in range(1, ways)]
+        pieces = (1,) * ways
     hidden_mid = col_phase(hidden_packed)
-    grads, own_back = call(
+    grad_kept, grad_sent, own_back = call(
         terms_kernel,
-        out_shape=(shape(2 * width, width), shape(rows, width, F32)),
-        in_specs=[VMEM] * 4,
-        out_specs=(VMEM,) * 2,
+        out_shape=(shape(width, width), shape(width, width), shape(rows, width, F32)),
+        in_specs=[SMEM] + [VMEM] * 4,
+        out_specs=(VMEM,) * 3,
         cost_estimate=cost(6 * slab * width, 2 * slab * 9),
         name="terms",
-    )(x_node, agg, slopes, self_weight)
-    *spreads, own_back, grads = lax.optimization_barrier((*spreads, own_back, grads))
-    parts = grads.reshape(ways, -1, width)
-
-    def pick(value, at):
-        return lax.dynamic_index_in_dim(value, at, 0, keepdims=False)
-
-    kept = [pick(parts, me)] + [across(pick(parts, groups[s]), s) for s in range(1, ways)]
+    )(core, x_node, agg, slopes, self_weight)
+    *spreads, own_back, grad_kept, grad_sent = lax.optimization_barrier((*spreads, own_back, grad_kept, grad_sent))
     back = call(
-        functools.partial(spmm_back_kernel, ways),
+        functools.partial(spmm_back_kernel, ways, pieces),
         grid_spec=pltpu.PrefetchScalarGridSpec(
             num_scalar_prefetch=2,
             grid=(depth,),
-            in_specs=[pl.BlockSpec((tile, width), lambda q, c, g: (q, 0)) for s in range(ways)]
+            in_specs=[piece_spec(p, count) for count in pieces for p in range(count)]
             + [mask_spec(s) for s in range(ways)],
             out_specs=VMEM,
             scratch_shapes=[pltpu.VMEM(x_cols.shape, F32)],
         ),
         out_shape=shape(*x_cols.shape),
         cost_estimate=cost(spmm_flops, 2 * masks.size + 2 * x_cols.size + 2 * ways * slab),
+        mib=12 + 7 * x_cols.size / MIB,
         name="spmm_back",
     )(cols, groups, *spreads, *([masks] * ways))
-    back, hidden_mid, *kept = lax.optimization_barrier((back, hidden_mid, *kept))
+    back, hidden_mid, grad_sent = lax.optimization_barrier((back, hidden_mid, grad_sent))
     neigh_back = lax.psum_scatter(back, "col", scatter_dimension=0, tiled=True)
     hidden_in = row_phase(turn(hidden_mid, col_devices, row_devices))
-    place = lax.axis_index("col")
-    others = jnp.bitwise_xor(place, jnp.arange(col_devices, dtype=jnp.int32)).astype(jnp.int32)
-
-    def along(value, s):
-        return lax.ppermute(value, "col", [(i, i ^ s) for i in range(col_devices)])
-
-    def in_place(index, arrays, dtype):
-        count, (r, c) = len(arrays), arrays[0].shape
-        return call(
-            place_kernel,
-            in_specs=[pl.BlockSpec(memory_space=pltpu.SMEM)] + [VMEM] * count,
-            out_specs=VMEM,
-            out_shape=jax.ShapeDtypeStruct((count, r, c), dtype),
-            cost_estimate=cost(0, 6 * count * r * c),
-            name="in_place",
-        )(index, *arrays).reshape(count * r, c)
-
-    kept = sum(term.astype(F32) for term in kept)
-    pieces = kept.astype(BF).reshape(col_devices, -1, width)
-    mine = [pick(pieces, place)] + [along(pick(pieces, others[s]), s) for s in range(1, col_devices)]
+    pieces = split_sum(groups, [grad_kept, swap(grad_sent)], ways)
+    pieces = split_sum(others, [pieces[0]] + [across(pieces[s], s) for s in range(1, ways)], lines)
     scale = 1.0 / math.sqrt(rows * devices)
-    mine = (sum(term.astype(F32) for term in mine) * scale).astype(BF)
-    in_row = in_place(others, [mine] + [along(mine, s) for s in range(1, col_devices)], BF)
-    whole = in_place(groups, [in_row] + [across(in_row, s) for s in range(1, ways)], F32)
-    own_back, whole = lax.optimization_barrier((own_back, whole))
+    zero = jnp.zeros((1,), jnp.int32)
+    (mine,) = split_sum(zero, [pieces[0]] + [along(pieces[s], s) for s in range(1, lines)], 1, scale)
+    in_line = in_place(others, [mine] + [along(mine, s) for s in range(1, lines)])
+    own_back, in_line = lax.optimization_barrier((own_back, in_line))
+    grad_half = in_place(groups, [in_line] + [across(in_line, s) for s in range(1, ways)])
+    grad_self, grad_neigh = call(
+        final_kernel,
+        in_specs=[SMEM] + [VMEM] * 2,
+        out_specs=(VMEM,) * 2,
+        out_shape=(shape(width, width, F32),) * 2,
+        cost_estimate=cost(0, 12 * width * width),
+        name="final",
+    )(core, grad_half, swap(grad_half))
     grad_packed = call(
         join_kernel,
         out_shape=shape(slots, width),
@@ -386,7 +470,7 @@
 
     hidden_own = unpack_own(hidden_in)
     grad_own = unpack_own(grad_in)
-    return (hidden_own, grad_own, whole[:width], whole[width:])
+    return (hidden_own, grad_own, grad_self, grad_neigh)
 
 
 def solution(mesh):

time: 309 us -> 281 us (0.909)
  Pallas kernels: 52.4 us -> 32.2 us
  between operations: 33.8 us -> 14.4 us
  local copies, waits for them, and re-layouts: 13.3 us -> 28.6 us
  starting transfers between devices: 57.8 us -> 47.6 us
  waiting for transfers between devices: 129 us -> 138 us
    unnamed x57 -> x63, local copies, waits for them, and re-layouts: 5.23 us -> 24.9 us
    all_to_all x2, waiting for transfers between devices: 45.7 us -> 30.7 us  [relay(): lax.all_to_all(there, everyone, split_axis=0, concat_axis=0, tiled=True)]
    ppermute x12 -> x14, waiting for transfers between devices: 48.5 us -> 59.1 us  [across(): return lax.ppermute(value, 'row', [(i, i ^ s) for i in range(ways)])]
    ppermute x14 -> x8, starting transfers between devices: 17.4 us -> 9.04 us  [the longest x6 8.9 us: along(): lax.ppermute(value, 'col', [(i, i ^ 2 * s) for i in range(col_devices)])]
    reduce_scatter x1, waiting for transfers between devices: 0.01 us -> 7.44 us  [on_device(): neigh_back = lax.psum_scatter(back, 'col', scatter_dimension=0, tiled=True)]
    pallas_call x5 -> x10, Pallas kernels: 25.3 us -> 18.5 us  [the longest x1 6.75 us: on_device(): call(functools.partial(spmm_back_kernel, ways, pieces), grid_spec=pltpu.P...]
    all_to_all x2, waiting for transfers between devices: 0.01 us -> 5.76 us  [col_phase(): lax.all_to_all(there, 'col', split_axis=0, concat_axis=0, tiled=True)]
    pallas_call x1, Pallas kernels: 8.43 us -> 3.89 us  [on_device(): call(functools.partial(spmm_kernel, ways), grid_spec=pltpu.PrefetchScalar...]
  transfers between devices with their start and end apart: 33 -> 29, of which waited for: 18 -> 25; matrix products, arithmetic and copies ran while one was open for 3% -> 1% of each run, Pallas kernels for 12% -> 8%
where the time goes in v4:
time: 281 us; the launch traced here: 280 us
  waiting for transfers between devices  138 us (49%)
  starting transfers between devices  47.6 us (17%)
  Pallas kernels  32.2 us (11%)
  local copies, waits for them, and re-layouts  28.6 us (10%)
  blocking collectives  19.5 us (7%)
  between operations  14.4 us (5%)
    ppermute x14, waiting for transfers between devices, across(): return lax.ppermute(value, 'row', [(i, i ^ s) for i in range(ways)])  59.1 us
    all_to_all x2, waiting for transfers between devices, relay(): lax.all_to_all(there, everyone, split_axis=0, concat_axis=0, tiled=True)  30.7 us
    unnamed x63, local copies, waits for them, and re-layouts  24.9 us
    all_gather x1, waiting for transfers between devices, on_device(): x_cols = lax.all_gather(x_node, 'col', axis=0, tiled=True)  24.2 us
    all_to_all x1, blocking collectives, row_phase(): lax.all_to_all(there, 'row', split_axis=0, concat_axis=0, tiled=True)  19.5 us
    ppermute x14, starting transfers between devices, across(): return lax.ppermute(value, 'row', [(i, i ^ s) for i in range(ways)])  16.1 us
    all_to_all x2, starting transfers between devices, relay(): lax.all_to_all(there, everyone, split_axis=0, concat_axis=0, tiled=True)  10.7 us
    ppermute x6, starting transfers between devices, along(): lax.ppermute(value, 'col', [(i, i ^ 2 * s) for i in range(col_devices)])  8.9 us
  transfers between devices with their start and end apart: 29, of which 25 were waited for; matrix products, arithmetic and copies ran while one was open for 1% of the time, Pallas kernels for 8%

profile of v4, /device:TPU:0, one launch (start us, length us, event | category | flops | bytes accessed | tf_op | source)
XLA Modules:
  0.0 280.2 jit_solution(2208308321813687770)
XLA Ops:
  7.2 1.0 copy-done.5
  8.9 2.1 pack_features.1
  11.0 7.3 %all-to-all-start = ((bf16[32,32,512]{2,1,0:T(8,128)(2,1)}), bf16[32,32,512]{2,1,0:T(8,128)(2,1)S(1)}, u32[]{:S(2)}, u32[]{:S(2)}) async-start(bf16[32,32,512]{2,1,0:T(8,128)(2,1)} %bitcast.3), calls=%async_computation | async-start | bytes 2097152 | tf_op jit(solution)/shard_map/all_to_all | solution.py:265
  18.6 1.4 index_cotangent.1
  21.4 24.5 %all-to-all-done = bf16[32,32,512]{2,1,0:T(8,128)(2,1)S(1)} async-done(((bf16[32,32,512]{2,1,0:T(8,128)(2,1)}), bf16[32,32,512]{2,1,0:T(8,128)(2,1)S(1)}, u32[]{:S(2)}, u32[]{:S(2)}) %all-to-all-start) | async-done | bytes 1048608 | tf_op jit(solution)/shard_map/all_to_all | solution.py:265
  45.9 0.9 copy-done.23
  46.8 1.5 unpack_features.1.refs_3_.x_ref
  48.4 19.5 %all_to_all.30 = bf16[4,256,640]{2,1,0:T(8,128)(2,1)S(1)} all-to-all(bf16[4,256,640]{2,1,0:T(8,128)(2,1)S(1)} %bitcast.38), channel_id=1, replica_groups=mesh['row'=4,'col'=8] {'row'}, dimensions={0} | all-to-all | bytes 2621440 | tf_op jit(solution)/shard_map/all_to_all | solution.py:269
  67.9 1.3 copy.18
  69.2 24.2 %all-gather.2.cloned.1.call-done.x_hbm = bf16[4096,512]{1,0:T(8,128)(2,1)} async-done(((bf16[512,512]{1,0:T(8,128)(2,1)}), bf16[4096,512]{1,0:T(8,128)(2,1)}) %all-gather.2.cloned.1.call-update) | async-done | bytes 4194320 | tf_op jit(solution)/shard_map/all_gather | solution.py:347
  93.3 3.6 %all-to-all-start.2 = ((bf16[8,128,640]{2,1,0:T(8,128)(2,1)}), bf16[8,128,640]{2,1,0:T(8,128)(2,1)S(1)}, u32[]{:S(2)}, u32[]{:S(2)}) async-start(bf16[8,128,640]{2,1,0:T(8,128)(2,1)} %bitcast.11), calls=%async_computation.2 | async-start | bytes 2621440 | tf_op jit(solution)/shard_map/all_to_all | solution.py:273
  96.9 2.2 copy-done
  99.1 2.2 copy-done.3
  101.3 3.9 %spmm.1 = (bf16[512,512]{1,0:T(8,128)(2,1)S(1)}, bf16[512,512]{1,0:T(8,128)(2,1)S(1)}, bf16[512,512]{1,0:T(8,128)(2,1)S(1)}, bf16[512,512]{1,0:T(8,128)(2,1)S(1)}) custom-call(s32[128]{0:T(128)S(1)} %reshape_squeeze.3.cols_ref, s32[4]{0:T(128)S(1)} %get-tuple-element.61.group_ref.index_ref, bf16[4096,512]{1,0:T(8,128)(2,1)S(1)} %copy-done.3, ...), custom_call_target="tpu_custom_call" | custom-call | flops 2147483648 | bytes 10485760 | tf_op jit(solution)/shard_map/spmm/pallas_call | solution.py:361
  105.3 1.5 collective-permute-start.1
  106.8 1.5 collective-permute-start
  108.3 5.6 %collective-permute-done.1.bottom_ref = bf16[256,512]{1,0:T(8,128)(2,1)S(1)} collective-permute-done((bf16[256,512]{1,0:T(8,128)(2,1)S(1)}, bf16[256,512]{1,0:T(8,128)(2,1)S(1)}, u32[]{:S(2)}, u32[]{:S(2)}) %collective-permute-start.1) | collective-permute-done | bytes 262176 | tf_op jit(solution)/shard_map/ppermute | solution.py:279
  114.0 1.2 collective-permute-done.top_ref
  115.3 1.5 collective-permute-start.2
  117.4 11.1 %collective-permute-done.2.refs_1_ = bf16[512,512]{1,0:T(8,128)(2,1)S(1)} collective-permute-done((bf16[512,512]{1,0:T(8,128)(2,1)S(1)}, bf16[512,512]{1,0:T(8,128)(2,1)S(1)}, u32[]{:S(2)}, u32[]{:S(2)}) %collective-permute-start.2) | collective-permute-done | bytes 524320 | tf_op jit(solution)/shard_map/ppermute | solution.py:279
  130.5 1.0 copy-done.11
  131.5 1.0 copy-done.15
  132.5 1.0 copy-done.17
  134.5 5.5 %layer.1 = (bf16[1024,512]{1,0:T(8,128)(2,1)}, bf16[512,512]{1,0:T(8,128)(2,1)S(1)}, bf16[512,512]{1,0:T(8,128)(2,1)S(1)}, bf16[512,512]{1,0:T(8,128)(2,1)S(1)}) custom-call(bf16[512,512]{1,0:T(8,128)(2,1)S(1)} %copy-done.11, bf16[512,512]{1,0:T(8,128)(2,1)S(1)} %copy-done.15, bf16[512,512]{1,0:T(8,128)(2,1)S(1)} %copy-done.17, ...), custom_call_target="tpu_custom_call" | custom-call | flops 1342177280 | bytes 6815744 | tf_op jit(solution)/shard_map/layer/pallas_call | solution.py:390
  142.2 1.1 collective-permute-start.4
  143.3 10.4 %collective-permute-done.5.refs_2_ = bf16[512,512]{1,0:T(8,128)(2,1)S(1)} collective-permute-done((bf16[512,512]{1,0:T(8,128)(2,1)S(1)}, bf16[512,512]{1,0:T(8,128)(2,1)S(1)}, u32[]{:S(2)}, u32[]{:S(2)}) %collective-permute-start.5) | collective-permute-done | bytes 524320 | tf_op jit(solution)/shard_map/ppermute | solution.py:279
  153.7 1.2 collective-permute-done.4.refs_1_
  154.9 4.2 %all-to-all-start.3 = ((bf16[8,128,512]{2,1,0:T(8,128)(2,1)}), bf16[8,128,512]{2,1,0:T(8,128)(2,1)}, u32[]{:S(2)}, u32[]{:S(2)}) async-start(bf16[8,128,512]{2,1,0:T(8,128)(2,1)} %bitcast.13), calls=%async_computation.3 | async-start | bytes 2097152 | tf_op jit(solution)/shard_map/all_to_all | solution.py:273
  159.2 1.5 collective-permute-start.6
  161.3 1.0 copy-done.9
  162.3 1.0 copy-done.25
  163.4 1.0 copy-done.27
  164.4 2.1 terms.1
  167.8 1.2 collective-permute-done.7.refs_4_
  169.0 2.2 copy-done.1
  171.2 6.7 %spmm_back.1 = bf16[4096,512]{1,0:T(8,128)(2,1)S(1)} custom-call(s32[128]{0:T(128)S(1)} %reshape_squeeze.3.cols_ref, s32[4]{0:T(128)S(1)} %get-tuple-element.61.group_ref.index_ref, bf16[512,512]{1,0:T(8,128)(2,1)S(1)} %get-tuple-element.84.refs_0_, bf16[512,512]{1,0:T(8,128)(2,1)S(1)} %collective-permute-done.4.refs_1_, ...), custom_call_target="tpu_custom_call" | custom-call | flops 2147483648 | bytes 10485760 | tf_op jit(solution)/shard_map/spmm_back/pallas_call | solution.py:417
  178.0 2.0 copy-done.2
  179.9 5.8 %all-to-all-done.3 = bf16[8,128,512]{2,1,0:T(8,128)(2,1)} async-done(((bf16[8,128,512]{2,1,0:T(8,128)(2,1)}), bf16[8,128,512]{2,1,0:T(8,128)(2,1)}, u32[]{:S(2)}, u32[]{:S(2)}) %all-to-all-start.3) | async-done | bytes 1048608 | tf_op jit(solution)/shard_map/all_to_all | solution.py:273
  185.7 2.3 copy.19
  188.0 3.8 %all-to-all-start.4 = ((bf16[4,256,512]{2,1,0:T(8,128)(2,1)}), bf16[4,256,512]{2,1,0:T(8,128)(2,1)S(1)}, u32[]{:S(2)}, u32[]{:S(2)}) async-start(bf16[4,256,512]{2,1,0:T(8,128)(2,1)} %bitcast.51), calls=%async_computation.4 | async-start | bytes 2097152 | tf_op jit(solution)/shard_map/all_to_all | solution.py:269
  192.0 1.9 collective-permute-done.8.refs_1_
  194.6 1.8 collective-permute-start.9
  196.4 1.5 collective-permute-start.10
  198.2 11.3 %collective-permute-done.9.refs_1_ = bf16[128,512]{1,0:T(8,128)(2,1)S(1)} collective-permute-done((bf16[128,512]{1,0:T(8,128)(2,1)S(1)}, bf16[128,512]{1,0:T(8,128)(2,1)S(1)}, u32[]{:S(2)}, u32[]{:S(2)}) %collective-permute-start.9) | collective-permute-done | bytes 131104 | tf_op jit(solution)/shard_map/ppermute | solution.py:279
  209.5 2.4 collective-permute-done.11.refs_3_
  212.6 2.2 collective-permute-start.13
  214.8 2.2 collective-permute-start.14
  217.4 2.5 collective-permute-done.13.refs_2_
  219.8 1.6 collective-permute-done.14.refs_3_
  221.4 2.3 collective-permute-start.17
  223.7 2.2 collective-permute-start.15
  225.9 2.3 collective-permute-done.17.refs_3_
  228.2 1.8 collective-permute-done.16.refs_2_
  230.6 7.4 %reduce-scatter.2.cloned.1.call-done.neigh_ref = bf16[512,512]{1,0:T(8,128)(2,1)} async-done(((bf16[4096,512]{1,0:T(8,128)(2,1)}), bf16[512,512]{1,0:T(8,128)(2,1)}) %reduce-scatter.2.cloned.1.call-update) | async-done | bytes 524304 | tf_op jit(solution)/shard_map/reduce_scatter | solution.py:433
  238.0 1.0 copy-done.4
  239.1 1.7 join_pack.1
  240.8 3.4 %all-to-all-start.5 = ((bf16[32,32,512]{2,1,0:T(8,128)(2,1)}), bf16[32,32,512]{2,1,0:T(8,128)(2,1)S(1)}, u32[]{:S(2)}, u32[]{:S(2)}) async-start(bf16[32,32,512]{2,1,0:T(8,128)(2,1)} %bitcast.20), calls=%async_computation.6 | async-start | bytes 2097152 | tf_op jit(solution)/shard_map/all_to_all | solution.py:265
  244.2 2.7 collective-permute-start.20
  247.8 11.5 %collective-permute-done.20.refs_3_ = bf16[128,512]{1,0:T(8,128)(2,1)S(1)} collective-permute-done((bf16[128,512]{1,0:T(8,128)(2,1)S(1)}, bf16[128,512]{1,0:T(8,128)(2,1)S(1)}, u32[]{:S(2)}, u32[]{:S(2)}) %collective-permute-start.20) | collective-permute-done | bytes 131104 | tf_op jit(solution)/shard_map/ppermute | solution.py:279
  259.3 1.6 collective-permute-done.19.refs_2_
  262.3 1.6 unpack_owner.2
  264.2 1.5 final.1
  265.6 6.2 %all-to-all-done.5 = bf16[32,32,512]{2,1,0:T(8,128)(2,1)S(1)} async-done(((bf16[32,32,512]{2,1,0:T(8,128)(2,1)}), bf16[32,32,512]{2,1,0:T(8,128)(2,1)S(1)}, u32[]{:S(2)}, u32[]{:S(2)}) %all-to-all-start.5) | async-done | bytes 1048608 | tf_op jit(solution)/shard_map/all_to_all | solution.py:265
  271.8 1.6 unpack_owner.3
  (84 shorter events, 15.4 us)
Async XLA Ops:
  7.2 1.0 copy-start.5
  8.2 0.7 copy-start.18
  11.0 7.4 %copy-start.30 = (s32[1,1,16,8]{2,3,1,0:T(8,128)S(1)}, s32[1,1,16,8]{2,3,1,0:T(8,128)}, u32[]{:S(2)}) copy-start(s32[1,1,16,8]{2,3,1,0:T(8,128)} %param.10) | copy-start | bytes 1540
  11.0 7.6 %copy-start.6 = (bf16[512,512]{1,0:T(8,128)(2,1)S(1)}, bf16[512,512]{1,0:T(8,128)(2,1)}, u32[]{:S(2)}) copy-start(bf16[512,512]{1,0:T(8,128)(2,1)} %cot_ref.1) | copy-start | bytes 1572868
  11.0 7.6 %copy-start.19 = (s32[512]{0:T(512)S(1)}, s32[512]{0:T(512)}, u32[]{:S(2)}) copy-start(s32[512]{0:T(512)} %param.13) | copy-start | bytes 6148
  11.0 7.6 %copy-start.20 = (s32[512]{0:T(512)S(1)}, s32[512]{0:T(512)}, u32[]{:S(2)}) copy-start(s32[512]{0:T(512)} %param.14) | copy-start | bytes 6148
  11.0 7.6 %copy-start.21 = (s32[512]{0:T(512)S(1)}, s32[512]{0:T(512)}, u32[]{:S(2)}) copy-start(s32[512]{0:T(512)} %param.12) | copy-start | bytes 6148
  11.0 34.9 %all-to-all-start = ((bf16[32,32,512]{2,1,0:T(8,128)(2,1)}), bf16[32,32,512]{2,1,0:T(8,128)(2,1)S(1)}, u32[]{:S(2)}, u32[]{:S(2)}) async-start(bf16[32,32,512]{2,1,0:T(8,128)(2,1)} %bitcast.3), calls=%async_computation | async-start | bytes 2097152 | tf_op jit(solution)/shard_map/all_to_all | solution.py:265
  18.3 75.0 %all-gather.2.cloned.1.call-start = ((), (), s32[]{:S(2)}) async-start(), calls=%async_computation.7 | async-start | bytes 4718592 | tf_op jit(solution)/shard_map/all_gather | solution.py:347
  20.0 0.7 copy-start.22
  20.7 0.7 copy-start.28
  45.9 1.0 copy-start.23
  93.3 37.1 %all-to-all-start.2 = ((bf16[8,128,640]{2,1,0:T(8,128)(2,1)}), bf16[8,128,640]{2,1,0:T(8,128)(2,1)S(1)}, u32[]{:S(2)}, u32[]{:S(2)}) async-start(bf16[8,128,640]{2,1,0:T(8,128)(2,1)} %bitcast.11), calls=%async_computation.2 | async-start | bytes 2621440 | tf_op jit(solution)/shard_map/all_to_all | solution.py:273
  96.9 2.2 copy-start
  99.1 2.2 copy-start.3
  105.2 10.1 %copy-start.10 = (bf16[512,512]{1,0:T(8,128)(2,1)}, bf16[512,512]{1,0:T(8,128)(2,1)S(1)}, u32[]{:S(2)}) copy-start(bf16[512,512]{1,0:T(8,128)(2,1)S(1)} %get-tuple-element.65.refs_0_) | copy-start | bytes 1572868
  105.2 25.2 %copy-start.7 = (bf16[512,512]{1,0:T(8,128)(2,1)S(1)}, bf16[512,512]{1,0:T(8,128)(2,1)}, u32[]{:S(2)}) copy-start(bf16[512,512]{1,0:T(8,128)(2,1)} %refs_8_.1) | copy-start | bytes 1572868
  105.2 25.2 %copy-start.8 = (bf16[512,512]{1,0:T(8,128)(2,1)S(1)}, bf16[512,512]{1,0:T(8,128)(2,1)}, u32[]{:S(2)}) copy-start(bf16[512,512]{1,0:T(8,128)(2,1)} %self_ref.1) | copy-start | bytes 1572868
  105.3 8.7 %collective-permute-start.1 = (bf16[256,512]{1,0:T(8,128)(2,1)S(1)}, bf16[256,512]{1,0:T(8,128)(2,1)S(1)}, u32[]{:S(2)}, u32[]{:S(2)}) collective-permute-start(bf16[256,512]{1,0:T(8,128)(2,1)S(1)} %get-tuple-element.110), channel_id=1, source_target_pairs={{0,16},{8,24},{16,0},{24,8},{1,17},{9,25},{17,1},{25,9},{2,18},{10... | collective-permute-start | bytes 786440 | tf_op jit(solution)/shard_map/ppermute | solution.py:279
  106.8 8.4 %collective-permute-start = (bf16[256,512]{1,0:T(8,128)(2,1)S(1)}, bf16[256,512]{1,0:T(8,128)(2,1)S(1)}, u32[]{:S(2)}, u32[]{:S(2)}) collective-permute-start(bf16[256,512]{1,0:T(8,128)(2,1)S(1)} %get-tuple-element.111), channel_id=1, source_target_pairs={{0,8},{8,0},{16,24},{24,16},{1,9},{9,1},{17,25},{25,17},{2,10},{10... | collective-permute-start | bytes 786440 | tf_op jit(solution)/shard_map/ppermute | solution.py:279
  115.3 13.2 %collective-permute-start.2 = (bf16[512,512]{1,0:T(8,128)(2,1)S(1)}, bf16[512,512]{1,0:T(8,128)(2,1)S(1)}, u32[]{:S(2)}, u32[]{:S(2)}) collective-permute-start(bf16[512,512]{1,0:T(8,128)(2,1)S(1)} %get-tuple-element.69), channel_id=1, source_target_pairs={{0,8},{8,0},{16,24},{24,16},{1,9},{9,1},{17,25},{25,17},{2,10},{10... | collective-permute-start | bytes 1572872 | tf_op jit(solution)/shard_map/ppermute | solution.py:279
  116.8 12.8 %collective-permute-start.3 = (bf16[512,512]{1,0:T(8,128)(2,1)S(1)}, bf16[512,512]{1,0:T(8,128)(2,1)S(1)}, u32[]{:S(2)}, u32[]{:S(2)}) collective-permute-start(bf16[512,512]{1,0:T(8,128)(2,1)S(1)} %get-tuple-element.70), channel_id=1, source_target_pairs={{0,16},{8,24},{16,0},{24,8},{1,17},{9,25},{17,1},{25,9},{2,18},{10... | collective-permute-start | bytes 1572872 | tf_op jit(solution)/shard_map/ppermute | solution.py:279
  128.5 0.8 copy-start.14
  129.6 0.8 copy-start.16
  130.4 1.0 copy-start.11
  131.5 1.0 copy-start.15
  132.5 1.0 copy-start.17
  133.6 0.9 copy-start.29
  140.0 0.8 copy-start.24
  140.8 0.8 copy-start.26
  141.6 12.1 %collective-permute-start.5 = (bf16[512,512]{1,0:T(8,128)(2,1)S(1)}, bf16[512,512]{1,0:T(8,128)(2,1)S(1)}, u32[]{:S(2)}, u32[]{:S(2)}) collective-permute-start(bf16[512,512]{1,0:T(8,128)(2,1)S(1)} %get-tuple-element.84.refs_0_), channel_id=1, source_target_pairs={{0,16},{8,24},{16,0},{24,8},{1,17},{9,25},{17,1},{25,9},{2,18},{10... | collective-permute-start | bytes 1572872 | tf_op jit(solution)/shard_map/ppermute | solution.py:279
  142.2 12.6 %collective-permute-start.4 = (bf16[512,512]{1,0:T(8,128)(2,1)S(1)}, bf16[512,512]{1,0:T(8,128)(2,1)S(1)}, u32[]{:S(2)}, u32[]{:S(2)}) collective-permute-start(bf16[512,512]{1,0:T(8,128)(2,1)S(1)} %get-tuple-element.84.refs_0_), channel_id=1, source_target_pairs={{0,8},{8,0},{16,24},{24,16},{1,9},{9,1},{17,25},{25,17},{2,10},{10... | collective-permute-start | bytes 1572872 | tf_op jit(solution)/shard_map/ppermute | solution.py:279
  154.9 30.8 %all-to-all-start.3 = ((bf16[8,128,512]{2,1,0:T(8,128)(2,1)}), bf16[8,128,512]{2,1,0:T(8,128)(2,1)}, u32[]{:S(2)}, u32[]{:S(2)}) async-start(bf16[8,128,512]{2,1,0:T(8,128)(2,1)} %bitcast.13), calls=%async_computation.3 | async-start | bytes 2097152 | tf_op jit(solution)/shard_map/all_to_all | solution.py:273
  159.1 78.9 %reduce-scatter.2.cloned.1.call-start = ((), (), s32[]{:S(2)}) async-start(), calls=%async_computation.8 | async-start | bytes 4718592 | tf_op jit(solution)/shard_map/reduce_scatter | solution.py:433
  159.2 8.6 %collective-permute-start.6 = (bf16[256,512]{1,0:T(8,128)(2,1)S(1)}, bf16[256,512]{1,0:T(8,128)(2,1)S(1)}, u32[]{:S(2)}, u32[]{:S(2)}) collective-permute-start(bf16[256,512]{1,0:T(8,128)(2,1)S(1)} %slice.14), channel_id=1, source_target_pairs={{0,8},{8,0},{16,24},{24,16},{1,9},{9,1},{17,25},{25,17},{2,10},{10... | collective-permute-start | bytes 786440 | tf_op jit(solution)/shard_map/ppermute | solution.py:279
  160.8 8.3 %collective-permute-start.7 = (bf16[256,512]{1,0:T(8,128)(2,1)S(1)}, bf16[256,512]{1,0:T(8,128)(2,1)S(1)}, u32[]{:S(2)}, u32[]{:S(2)}) collective-permute-start(bf16[256,512]{1,0:T(8,128)(2,1)S(1)} %slice.15), channel_id=1, source_target_pairs={{0,16},{8,24},{16,0},{24,8},{1,17},{9,25},{17,1},{25,9},{2,18},{10... | collective-permute-start | bytes 786440 | tf_op jit(solution)/shard_map/ppermute | solution.py:279
  161.3 1.0 copy-start.9
  162.3 1.0 copy-start.25
  163.4 1.0 copy-start.27
  166.5 0.8 copy-start.12
  169.0 2.2 copy-start.1
  178.0 2.0 copy-start.2
  188.0 3.8 %copy-start.13 = (bf16[512,512]{1,0:T(8,128)(2,1)S(1)}, bf16[512,512]{1,0:T(8,128)(2,1)}, u32[]{:S(2)}) copy-start(bf16[512,512]{1,0:T(8,128)(2,1)} %copy-done.12) | copy-start | bytes 1572868
  188.0 52.8 %all-to-all-start.4 = ((bf16[4,256,512]{2,1,0:T(8,128)(2,1)}), bf16[4,256,512]{2,1,0:T(8,128)(2,1)S(1)}, u32[]{:S(2)}, u32[]{:S(2)}) async-start(bf16[4,256,512]{2,1,0:T(8,128)(2,1)} %bitcast.51), calls=%async_computation.4 | async-start | bytes 2097152 | tf_op jit(solution)/shard_map/all_to_all | solution.py:269
  191.9 2.0 collective-permute-start.8
  194.6 14.9 %collective-permute-start.9 = (bf16[128,512]{1,0:T(8,128)(2,1)S(1)}, bf16[128,512]{1,0:T(8,128)(2,1)S(1)}, u32[]{:S(2)}, u32[]{:S(2)}) collective-permute-start(bf16[128,512]{1,0:T(8,128)(2,1)S(1)} %get-tuple-element.97), channel_id=1, source_target_pairs={{0,8},{8,0},{16,24},{24,16},{1,9},{9,1},{17,25},{25,17},{2,10},{10... | collective-permute-start | bytes 393224 | tf_op jit(solution)/shard_map/ppermute | solution.py:279
  196.4 13.1 %collective-permute-start.10 = (bf16[128,512]{1,0:T(8,128)(2,1)S(1)}, bf16[128,512]{1,0:T(8,128)(2,1)S(1)}, u32[]{:S(2)}, u32[]{:S(2)}) collective-permute-start(bf16[128,512]{1,0:T(8,128)(2,1)S(1)} %get-tuple-element.98), channel_id=1, source_target_pairs={{0,16},{8,24},{16,0},{24,8},{1,17},{9,25},{17,1},{25,9},{2,18},{10... | collective-permute-start | bytes 393224 | tf_op jit(solution)/shard_map/ppermute | solution.py:279
  197.9 14.0 %collective-permute-start.11 = (bf16[128,512]{1,0:T(8,128)(2,1)S(1)}, bf16[128,512]{1,0:T(8,128)(2,1)S(1)}, u32[]{:S(2)}, u32[]{:S(2)}) collective-permute-start(bf16[128,512]{1,0:T(8,128)(2,1)S(1)} %get-tuple-element.99), channel_id=1, source_target_pairs={{0,24},{8,16},{16,8},{24,0},{1,25},{9,17},{17,9},{25,1},{2,26},{10... | collective-permute-start | bytes 393224 | tf_op jit(solution)/shard_map/ppermute | solution.py:279
  212.6 4.8 %collective-permute-start.12 = (bf16[32,512]{1,0:T(8,128)(2,1)S(1)}, bf16[32,512]{1,0:T(8,128)(2,1)S(1)}, u32[]{:S(2)}, u32[]{:S(2)}) collective-permute-start(bf16[32,512]{1,0:T(8,128)(2,1)S(1)} %get-tuple-element.101), channel_id=1, source_target_pairs={{0,2},{1,3},{2,0},{3,1},{4,6},{5,7},{6,4},{7,5},{8,10},{9,11},{10,... | collective-permute-start | bytes 98312 | tf_op jit(solution)/shard_map/ppermute | solution.py:282
  212.6 7.2 %collective-permute-start.13 = (bf16[32,512]{1,0:T(8,128)(2,1)S(1)}, bf16[32,512]{1,0:T(8,128)(2,1)S(1)}, u32[]{:S(2)}, u32[]{:S(2)}) collective-permute-start(bf16[32,512]{1,0:T(8,128)(2,1)S(1)} %get-tuple-element.102), channel_id=1, source_target_pairs={{0,4},{1,5},{2,6},{3,7},{4,0},{5,1},{6,2},{7,3},{8,12},{9,13},{10,... | collective-permute-start | bytes 98312 | tf_op jit(solution)/shard_map/ppermute | solution.py:282
  214.8 6.6 %collective-permute-start.14 = (bf16[32,512]{1,0:T(8,128)(2,1)S(1)}, bf16[32,512]{1,0:T(8,128)(2,1)S(1)}, u32[]{:S(2)}, u32[]{:S(2)}) collective-permute-start(bf16[32,512]{1,0:T(8,128)(2,1)S(1)} %get-tuple-element.103), channel_id=1, source_target_pairs={{0,6},{1,7},{2,4},{3,5},{4,2},{5,3},{6,0},{7,1},{8,14},{9,15},{10,... | collective-permute-start | bytes 98312 | tf_op jit(solution)/shard_map/ppermute | solution.py:282
  221.4 6.8 %collective-permute-start.17 = (bf16[32,512]{1,0:T(8,128)(2,1)S(1)}, bf16[32,512]{1,0:T(8,128)(2,1)S(1)}, u32[]{:S(2)}, u32[]{:S(2)}) collective-permute-start(bf16[32,512]{1,0:T(8,128)(2,1)S(1)} %split_sum.5.refs_0_), channel_id=1, source_target_pairs={{0,6},{1,7},{2,4},{3,5},{4,2},{5,3},{6,0},{7,1},{8,14},{9,15},{10,... | collective-permute-start | bytes 98312 | tf_op jit(solution)/shard_map/ppermute | solution.py:282
  223.7 6.3 %collective-permute-start.16 = (bf16[32,512]{1,0:T(8,128)(2,1)S(1)}, bf16[32,512]{1,0:T(8,128)(2,1)S(1)}, u32[]{:S(2)}, u32[]{:S(2)}) collective-permute-start(bf16[32,512]{1,0:T(8,128)(2,1)S(1)} %split_sum.5.refs_0_), channel_id=1, source_target_pairs={{0,4},{1,5},{2,6},{3,7},{4,0},{5,1},{6,2},{7,3},{8,12},{9,13},{10,... | collective-permute-start | bytes 98312 | tf_op jit(solution)/shard_map/ppermute | solution.py:282
  223.7 6.3 %collective-permute-start.15 = (bf16[32,512]{1,0:T(8,128)(2,1)S(1)}, bf16[32,512]{1,0:T(8,128)(2,1)S(1)}, u32[]{:S(2)}, u32[]{:S(2)}) collective-permute-start(bf16[32,512]{1,0:T(8,128)(2,1)S(1)} %split_sum.5.refs_0_), channel_id=1, source_target_pairs={{0,2},{1,3},{2,0},{3,1},{4,6},{5,7},{6,4},{7,5},{8,10},{9,11},{10,... | collective-permute-start | bytes 98312 | tf_op jit(solution)/shard_map/ppermute | solution.py:282
  238.0 1.0 copy-start.4
  240.8 31.0 %all-to-all-start.5 = ((bf16[32,32,512]{2,1,0:T(8,128)(2,1)}), bf16[32,32,512]{2,1,0:T(8,128)(2,1)S(1)}, u32[]{:S(2)}, u32[]{:S(2)}) async-start(bf16[32,32,512]{2,1,0:T(8,128)(2,1)} %bitcast.20), calls=%async_computation.6 | async-start | bytes 2097152 | tf_op jit(solution)/shard_map/all_to_all | solution.py:265
  244.2 15.0 %collective-permute-start.20 = (bf16[128,512]{1,0:T(8,128)(2,1)S(1)}, bf16[128,512]{1,0:T(8,128)(2,1)S(1)}, u32[]{:S(2)}, u32[]{:S(2)}) collective-permute-start(bf16[128,512]{1,0:T(8,128)(2,1)S(1)} %bitcast.42), channel_id=1, source_target_pairs={{0,24},{8,16},{16,8},{24,0},{1,25},{9,17},{17,9},{25,1},{2,26},{10... | collective-permute-start | bytes 393224 | tf_op jit(solution)/shard_map/ppermute | solution.py:279
  247.0 13.9 %collective-permute-start.19 = (bf16[128,512]{1,0:T(8,128)(2,1)S(1)}, bf16[128,512]{1,0:T(8,128)(2,1)S(1)}, u32[]{:S(2)}, u32[]{:S(2)}) collective-permute-start(bf16[128,512]{1,0:T(8,128)(2,1)S(1)} %bitcast.43), channel_id=1, source_target_pairs={{0,16},{8,24},{16,0},{24,8},{1,17},{9,25},{17,1},{25,9},{2,18},{10... | collective-permute-start | bytes 393224 | tf_op jit(solution)/shard_map/ppermute | solution.py:279
  247.5 14.1 %collective-permute-start.18 = (bf16[128,512]{1,0:T(8,128)(2,1)S(1)}, bf16[128,512]{1,0:T(8,128)(2,1)S(1)}, u32[]{:S(2)}, u32[]{:S(2)}) collective-permute-start(bf16[128,512]{1,0:T(8,128)(2,1)S(1)} %bitcast.44), channel_id=1, source_target_pairs={{0,8},{8,0},{16,24},{24,16},{1,9},{9,1},{17,25},{25,17},{2,10},{10... | collective-permute-start | bytes 393224 | tf_op jit(solution)/shard_map/ppermute | solution.py:279
  262.2 2.0 collective-permute-start.21
Sparse Core Ops, SparseCore 0:
  48.5 44.7 all-gather.1
  185.8 52.1 reduce-scatter.1

commit v5 on v4

--- a/solution.py
+++ b/solution.py
@@ -12,6 +12,7 @@
 F32 = jnp.float32
 VMEM = pl.BlockSpec(memory_space=pltpu.VMEM)
 MIB = 1024 * 1024
+LARGE = 56
 
 
 def params(mib=16):
@@ -94,50 +95,124 @@
     out_ref[...] = dot(entries_onehot(col_ref[...], value_ref.shape[0]), value_ref[...]).astype(BF)
 
 
-def spmm_kernel(ways, cols_ref, group_ref, x_hbm, *refs):
-    masks, outs = refs[:ways], refs[ways : 2 * ways]
-    x_ref, sems = refs[2 * ways :]
-    q = pl.program_id(0)
-    depth = pl.num_programs(0)
-    _, breadth, tile, _ = masks[0].shape
-
-    @pl.when(q == 0)
+def load_masks(group_ref, masks_hbm, masks_ref, sems, ways, depth, q):
+    return [
+        pltpu.make_async_copy(masks_hbm.at[group_ref[s] * depth + q], masks_ref.at[q * ways + s], sems.at[q * ways + s])
+        for s in range(ways)
+    ]
+
+
+def spmm_kernel(ways, halves, cols_ref, group_ref, core_ref, own_hbm, other_hbm, masks_hbm, *refs):
+    outs = refs[:ways]
+    x_ref, masks_ref, x_sems, mask_sems = refs[ways:]
+    h, q = pl.program_id(0), pl.program_id(1)
+    depth = pl.num_programs(1)
+    steps = masks_ref.shape[0] // ways
+    _, breadth, tile, _ = masks_ref.shape
+    width = x_ref.shape[2]
+    block = tile * steps
+    lines = own_hbm.shape[0] // block
+
+    def load_x(half):
+        copies = []
+        for j, source in enumerate((own_hbm, other_hbm)):
+            for z in range(lines):
+                to = pl.multiple_of((2 * z + jnp.bitwise_xor(core_ref[0], j)) * block, block)
+                copies.append(
+                    pltpu.make_async_copy(
+                        source.at[pl.ds(z * block, block), pl.ds(half * width, width)],
+                        x_ref.at[half, pl.ds(to, block), :],
+                        x_sems.at[half, j * lines + z],
+                    )
+                )
+        return copies
+
+    @pl.when((h == 0) & (q == 0))
     def _():
-        count = sems.shape[0]
-        share = x_ref.shape[0] // count
-        copies = [
-            pltpu.make_async_copy(x_hbm.at[pl.ds(i * share, share)], x_ref.at[pl.ds(i * share, share)], sems.at[i])
-            for i in range(count)
-        ]
-        for copy in copies:
+        for copy in load_x(0):
             copy.start()
-        for copy in copies:
-            copy.wait()
+        for step in range(steps):
+            for copy in load_masks(group_ref, masks_hbm, masks_ref, mask_sems, ways, steps, step):
+                copy.start()
+        for half in range(1, halves):
+            for copy in load_x(half):
+                copy.start()
+
+    for half in range(halves):
+
+        @pl.when((h == half) & (q == 0))
+        def _():
+            for copy in load_x(half):
+                copy.wait()
+
+    for step in range(steps):
+
+        @pl.when((h == 0) & (q == step))
+        def _():
+            for copy in load_masks(group_ref, masks_hbm, masks_ref, mask_sems, ways, steps, step):
+                copy.wait()
 
     for s in range(ways):
         base = (group_ref[s] * depth + q) * breadth
+        at = q * ways + s
         total = None
         for p in range(0, breadth, 2):
-            width = min(2, breadth - p)
-            left = jnp.concatenate([masks[s][0, p + w] for w in range(width)], axis=1)
+            span = min(2, breadth - p)
+            left = jnp.concatenate([masks_ref[at, p + w] for w in range(span)], axis=1)
             right = jnp.concatenate(
-                [x_ref[pl.ds(pl.multiple_of(cols_ref[base + p + w] * tile, tile), tile), :] for w in range(width)], axis=0
+                [
+                    x_ref[h, pl.ds(pl.multiple_of(cols_ref[base + p + w] * tile, tile), tile), :]
+                    for w in range(span)
+                ],
+                axis=0,
             )
             term = dot(left, right)
             total = term if total is None else total + term
         outs[s][...] = total.astype(BF)
 
 
-def spmm_back_kernel(ways, pieces, cols_ref, group_ref, *refs):
+def spmm_back_kernel(ways, halves, pieces, cols_ref, group_ref, core_ref, *refs):
     given = sum(pieces)
-    spreads, masks, out_ref, total = refs[:given], refs[given : given + ways], refs[-2], refs[-1]
-    q = pl.program_id(0)
-    depth = pl.num_programs(0)
-    _, breadth, tile, _ = masks[0].shape
+    spreads = refs[:given]
+    masks_hbm, own_hbm, other_hbm, total, ready, masks_ref, out_sems, mask_sems = refs[given:]
+    h, q = pl.program_id(0), pl.program_id(1)
+    depth = pl.num_programs(1)
+    steps = masks_ref.shape[0] // ways
+    _, breadth, tile, _ = masks_ref.shape
+    width = total.shape[1]
+    block = tile * steps
+    lines = own_hbm.shape[0] // block
+
+    def store(half):
+        copies = []
+        for j, target in enumerate((own_hbm, other_hbm)):
+            for z in range(lines):
+                at = pl.multiple_of((2 * z + jnp.bitwise_xor(core_ref[0], j)) * block, block)
+                copies.append(
+                    pltpu.make_async_copy(
+                        ready.at[half, pl.ds(at, block), :],
+                        target.at[pl.ds(z * block, block), pl.ds(half * width, width)],
+                        out_sems.at[half, j * lines + z],
+                    )
+                )
+        return copies
+
+    @pl.when((h == 0) & (q == 0))
+    def _():
+        for step in range(steps):
+            for copy in load_masks(group_ref, masks_hbm, masks_ref, mask_sems, ways, steps, step):
+                copy.start()
 
     @pl.when(q == 0)
     def _():
         total[...] = jnp.zeros_like(total)
+
+    for step in range(steps):
+
+        @pl.when((h == 0) & (q == step))
+        def _():
+            for copy in load_masks(group_ref, masks_hbm, masks_ref, mask_sems, ways, steps, step):
+                copy.wait()
 
     at_piece = 0
     for s in range(ways):
@@ -148,11 +223,19 @@
         at_piece += pieces[s]
         for k in range(breadth):
             at = pl.ds(pl.multiple_of(cols_ref[base + k] * tile, tile), tile)
-            total[at, :] += dot(masks[s][0, k], rows, 0, 0)
-
-    @pl.when(q == depth - 1)
-    def _():
-        out_ref[...] = total[...].astype(BF)
+            total[at, :] += dot(masks_ref[q * ways + s, k], rows, 0, 0)
+
+    for half in range(halves):
+
+        @pl.when((h == half) & (q == depth - 1))
+        def _():
+            ready[half] = total[...].astype(BF)
+            for copy in store(half):
+                copy.start()
+            if half == halves - 1:
+                for earlier in range(halves):
+                    for copy in store(earlier):
+                        copy.wait()
 
 
 def pass_on_kernel(left_ref, right_ref, top_ref, bottom_ref, left_out, right_out):
@@ -315,6 +398,7 @@
         in_specs=[VMEM] * 2,
         out_specs=VMEM,
         cost_estimate=cost(2 * slots * slab, 6 * slab),
+        mib=LARGE,
         name="pack_features",
     )(nodes, features)
     inbound = relay(packed)
@@ -331,6 +415,7 @@
         in_specs=[VMEM] * 4,
         out_specs=(VMEM,) * 6,
         cost_estimate=cost(2 * slots * slab, 6 * slab),
+        mib=LARGE,
         name="index_cotangent",
     )(nodes, owner_position.reshape(1, rows), degree.reshape(1, rows), cotangent)
     x_node = call(
@@ -344,34 +429,40 @@
     cot_packed, x_node, cols, groups, core, others = lax.optimization_barrier(
         (cot_packed, x_node, cols, groups, core, others)
     )
-    x_cols = lax.all_gather(x_node, "col", axis=0, tiled=True)
+    same_core = [list(range(k, col_devices, 2)) for k in range(2)]
+    x_own = lax.all_gather(x_node, "col", axis_index_groups=same_core, axis=0, tiled=True)
     cot_mid = turn(row_phase(cot_packed), row_devices, col_devices)
-    x_cols, cot_mid = lax.optimization_barrier((x_cols, cot_mid))
+    x_own, cot_mid = lax.optimization_barrier((x_own, cot_mid))
+    x_other = swap(x_own)
     cot_in = col_phase(cot_mid)
-
-    def mask_spec(s):
-        return pl.BlockSpec((1, breadth, tile, tile), lambda q, c, g, s=s: (g[s] * depth + q, 0, 0, 0))
 
     def piece_spec(p, count):
         share = depth // count
-        return pl.BlockSpec((tile, width), lambda q, c, g: (jnp.clip(q - p * share, 0, share - 1), 0))
+        return pl.BlockSpec((tile, part), lambda h, q, *_: (jnp.clip(q - p * share, 0, share - 1), h))
+
+    halves = 2
+    part = width // halves
+    cell_rows = col_devices * rows
+    ANY = pl.BlockSpec(memory_space=pl.ANY)
+    masks_scratch = pltpu.VMEM(masks.shape, BF)
+    mask_sems = pltpu.SemaphoreType.DMA((masks.shape[0],))
+    x_sems = pltpu.SemaphoreType.DMA((halves, col_devices))
 
     spmm_flops = 2 * masks.size * width
-    copies = 8
     partials = call(
-        functools.partial(spmm_kernel, ways),
+        functools.partial(spmm_kernel, ways, halves),
         grid_spec=pltpu.PrefetchScalarGridSpec(
-            num_scalar_prefetch=2,
-            grid=(depth,),
-            in_specs=[pl.BlockSpec(memory_space=pl.ANY)] + [mask_spec(s) for s in range(ways)],
-            out_specs=[pl.BlockSpec((tile, width), lambda q, c, g: (q, 0)) for s in range(ways)],
-            scratch_shapes=[pltpu.VMEM(x_cols.shape, BF), pltpu.SemaphoreType.DMA((copies,))],
+            num_scalar_prefetch=3,
+            grid=(halves, depth),
+            in_specs=[ANY] * 3,
+            out_specs=[pl.BlockSpec((tile, part), lambda h, q, *_: (q, h)) for s in range(ways)],
+            scratch_shapes=[pltpu.VMEM((halves, cell_rows, part), BF), masks_scratch, x_sems, mask_sems],
         ),
         out_shape=[shape(rows, width) for s in range(ways)],
-        cost_estimate=cost(spmm_flops, 2 * masks.size + 2 * x_cols.size + 2 * ways * slab),
-        mib=12 + 3 * x_cols.size / MIB,
+        cost_estimate=cost(spmm_flops, 2 * masks.size + 2 * cell_rows * width + 2 * ways * slab),
+        mib=LARGE,
         name="spmm",
-    )(cols, groups, x_cols, *([masks] * ways))
+    )(cols, groups, core, x_own, x_other, masks)
     if ways == 4:
         half = rows // 2
         top = across(partials[3][:half], 1)
@@ -382,6 +473,7 @@
             in_specs=[VMEM] * 4,
             out_specs=(VMEM,) * 2,
             cost_estimate=cost(2 * slab, 10 * slab),
+            mib=LARGE,
             name="pass_on",
         )(partials[1], partials[2], top, bottom)
         terms = [partials[0], across(left, 1), across(right, 2)]
@@ -393,12 +485,11 @@
         in_specs=[VMEM] * (len(terms) + 6),
         out_specs=(VMEM,) * 4,
         cost_estimate=cost(10 * slab * width, 2 * slab * (ways + 9)),
-        mib=24,
+        mib=LARGE,
         name="layer",
     )(*terms, x_node, cot_in, turned_col, turned_row, self_weight, neigh_weight)
     if ways == 4:
         left, right = across(spread, 1), across(spread, 2)
-        left, right, hidden_packed = lax.optimization_barrier((left, right, hidden_packed))
         spreads = [spread, left, right, across(right[:half], 1), across(left[half:], 2)]
         pieces = (1, 1, 1, 2)
     else:
@@ -411,26 +502,34 @@
         in_specs=[SMEM] + [VMEM] * 4,
         out_specs=(VMEM,) * 3,
         cost_estimate=cost(6 * slab * width, 2 * slab * 9),
+        mib=LARGE,
         name="terms",
     )(core, x_node, agg, slopes, self_weight)
     *spreads, own_back, grad_kept, grad_sent = lax.optimization_barrier((*spreads, own_back, grad_kept, grad_sent))
-    back = call(
-        functools.partial(spmm_back_kernel, ways, pieces),
+    back_own, back_other = call(
+        functools.partial(spmm_back_kernel, ways, halves, pieces),
         grid_spec=pltpu.PrefetchScalarGridSpec(
-            num_scalar_prefetch=2,
-            grid=(depth,),
-            in_specs=[piece_spec(p, count) for count in pieces for p in range(count)]
-            + [mask_spec(s) for s in range(ways)],
-            out_specs=VMEM,
-            scratch_shapes=[pltpu.VMEM(x_cols.shape, F32)],
+            num_scalar_prefetch=3,
+            grid=(halves, depth),
+            in_specs=[piece_spec(p, count) for count in pieces for p in range(count)] + [ANY],
+            out_specs=[ANY] * 2,
+            scratch_shapes=[
+                pltpu.VMEM((cell_rows, part), F32),
+                pltpu.VMEM((halves, cell_rows, part), BF),
+                masks_scratch,
+                x_sems,
+                mask_sems,
+            ],
         ),
-        out_shape=shape(*x_cols.shape),
-        cost_estimate=cost(spmm_flops, 2 * masks.size + 2 * x_cols.size + 2 * ways * slab),
-        mib=12 + 7 * x_cols.size / MIB,
+        out_shape=[shape(cell_rows // 2, width)] * 2,
+        cost_estimate=cost(spmm_flops, 2 * masks.size + 2 * cell_rows * width + 2 * ways * slab),
+        mib=LARGE,
         name="spmm_back",
-    )(cols, groups, *spreads, *([masks] * ways))
+    )(cols, groups, core, *spreads, masks)
+    back_other, hidden_mid = lax.optimization_barrier((back_other, hidden_mid))
+    back = (back_own.astype(F32) + swap(back_other).astype(F32)).astype(BF)
     back, hidden_mid, grad_sent = lax.optimization_barrier((back, hidden_mid, grad_sent))
-    neigh_back = lax.psum_scatter(back, "col", scatter_dimension=0, tiled=True)
+    neigh_back = lax.psum_scatter(back, "col", scatter_dimension=0, axis_index_groups=same_core, tiled=True)
     hidden_in = row_phase(turn(hidden_mid, col_devices, row_devices))
     pieces = split_sum(groups, [grad_kept, swap(grad_sent)], ways)
     pieces = split_sum(others, [pieces[0]] + [across(pieces[s], s) for s in range(1, ways)], lines)

time: 281 us -> 281 us (level)
  local copies, waits for them, and re-layouts: 28.6 us -> 9.71 us
  Pallas kernels: 32.2 us -> 50.4 us
  other arithmetic: 0.01 us -> 4.14 us
  waiting for transfers between devices: 138 us -> 134 us
    unnamed x63 -> x43, local copies, waits for them, and re-layouts: 24.9 us -> 5.63 us
    pallas_call x2, Pallas kernels: 10.6 us -> 20.1 us  [the longest x1 12.1 us: on_device(): call(functools.partial(spmm_back_kernel, ways, halves, pieces), grid_spec...]
    reduce_scatter x1, waiting for transfers between devices: 7.44 us -> 0.22 us  [on_device(): lax.psum_scatter(back, 'col', scatter_dimension=0, axis_index_groups=same...]
    ppermute x2 -> x4, waiting for transfers between devices: 2.24 us -> 7.25 us  [swap(): return lax.ppermute(value, 'col', [(i, i ^ 1) for i in range(col_devices)])]
    ppermute x6, waiting for transfers between devices: 8.51 us -> 12.2 us  [along(): lax.ppermute(value, 'col', [(i, i ^ 2 * s) for i in range(col_devices)])]
    convert_element_type x0 -> x1, other arithmetic: none -> 3.65 us  [on_device(): back = (back_own.astype(F32) + swap(back_other).astype(F32)).astype(BF)]
  transfers between devices with their start and end apart: 29 -> 31, of which waited for: 25 -> 26; matrix products, arithmetic and copies ran while one was open for 1% -> 2% of each run, Pallas kernels for 8% -> 13%
where the time goes in v5:
time: 281 us; the launch traced here: 280 us
  waiting for transfers between devices  134 us (48%)
  Pallas kernels  50.4 us (18%)
  starting transfers between devices  47.7 us (17%)
  blocking collectives  19.5 us (7%)
  between operations  14.3 us (5%)
  local copies, waits for them, and re-layouts  9.71 us (3%)
  other arithmetic  4.14 us (1%)
    ppermute x14, waiting for transfers between devices, across(): return lax.ppermute(value, 'row', [(i, i ^ s) for i in range(ways)])  56.3 us
    all_to_all x2, waiting for transfers between devices, relay(): lax.all_to_all(there, everyone, split_axis=0, concat_axis=0, tiled=True)  28.8 us
    all_gather x1, waiting for transfers between devices, on_device(): lax.all_gather(x_node, 'col', axis_index_groups=same_core, axis=0, tiled=...  23 us
    all_to_all x1, blocking collectives, row_phase(): lax.all_to_all(there, 'row', split_axis=0, concat_axis=0, tiled=True)  19.5 us
    ppermute x14, starting transfers between devices, across(): return lax.ppermute(value, 'row', [(i, i ^ s) for i in range(ways)])  15.2 us
    ppermute x6, waiting for transfers between devices, along(): lax.ppermute(value, 'col', [(i, i ^ 2 * s) for i in range(col_devices)])  12.2 us
    pallas_call x1, Pallas kernels, on_device(): call(functools.partial(spmm_back_kernel, ways, halves, pieces), grid_spec...  12.1 us
    all_to_all x2, starting transfers between devices, relay(): lax.all_to_all(there, everyone, split_axis=0, concat_axis=0, tiled=True)  11.4 us
  transfers between devices with their start and end apart: 31, of which 26 were waited for; matrix products, arithmetic and copies ran while one was open for 2% of the time, Pallas kernels for 13%

profile of v5, /device:TPU:0, one launch (start us, length us, event | category | flops | bytes accessed | tf_op | source)
XLA Modules:
  0.0 279.7 jit_solution(15777156877665014483)
XLA Ops:
  7.2 3.1 %pack_features.1 = bf16[1024,512]{1,0:T(8,128)(2,1)} custom-call(s32[1,512]{1,0:T(1,128)} %bitcast.45, bf16[512,512]{1,0:T(8,128)(2,1)} %value_ref.1), custom_call_target="tpu_custom_call" | custom-call | flops 536870912 | bytes 1572864 | tf_op jit(solution)/shard_map/pack_features/pallas_call | solution.py:395
  10.3 7.3 %all-to-all-start = ((bf16[32,32,512]{2,1,0:T(8,128)(2,1)}), bf16[32,32,512]{2,1,0:T(8,128)(2,1)S(1)}, u32[]{:S(2)}, u32[]{:S(2)}) async-start(bf16[32,32,512]{2,1,0:T(8,128)(2,1)} %bitcast.44), calls=%async_computation | async-start | bytes 2097152 | tf_op jit(solution)/shard_map/all_to_all | solution.py:348
  18.4 3.7 %index_cotangent.1 = (bf16[1024,640]{1,0:T(8,128)(2,1)}, s32[512,128]{1,0:T(8,128)}, s32[8,512]{1,0:T(8,128)}, s32[512,128]{1,0:T(8,128)}, s32[8,512]{1,0:T(8,128)}, /*index=5*/s32[512,128]{1,0:T(8,128)}) custom-call(s32[1,512]{1,0:T(1,128)} %bitcast.46, s32[1,512]{1,0:T(1,128)} %bitcast.47, s32[1,512]{1,0:T(1,128)} %bitcast.48, bf16[512,512]{1,0:T(8,128)(2,1)} %cot_ref.1), custom_call_target="tpu_custom_call" | custom-call | flops 536870912 | bytes 1572864 | tf_op jit(solution)/shard_map/index_cotangent/pallas_call | solution.py:405
  22.6 22.6 %all-to-all-done = bf16[32,32,512]{2,1,0:T(8,128)(2,1)S(1)} async-done(((bf16[32,32,512]{2,1,0:T(8,128)(2,1)}), bf16[32,32,512]{2,1,0:T(8,128)(2,1)S(1)}, u32[]{:S(2)}, u32[]{:S(2)}) %all-to-all-start) | async-done | bytes 1048608 | tf_op jit(solution)/shard_map/all_to_all | solution.py:348
  45.2 0.9 copy-done.6
  46.2 1.5 unpack_features.1.refs_3_.x_ref
  47.7 19.5 %all_to_all.30 = bf16[4,256,640]{2,1,0:T(8,128)(2,1)S(1)} all-to-all(bf16[4,256,640]{2,1,0:T(8,128)(2,1)S(1)} %bitcast.42), channel_id=1, replica_groups=mesh['row'=4,'col'=8] {'row'}, dimensions={0} | all-to-all | bytes 2621440 | tf_op jit(solution)/shard_map/all_to_all | solution.py:352
  67.2 1.2 copy.18
  68.5 23.0 %all-gather.2.cloned.1.call-done.own_hbm = bf16[2048,512]{1,0:T(8,128)(2,1)} async-done(((bf16[512,512]{1,0:T(8,128)(2,1)}), bf16[2048,512]{1,0:T(8,128)(2,1)}) %all-gather.2.cloned.1.call-update) | async-done | bytes 2097168 | tf_op jit(solution)/shard_map/all_gather | solution.py:433
  91.4 3.6 %all-to-all-start.2 = ((bf16[8,128,640]{2,1,0:T(8,128)(2,1)}), bf16[8,128,640]{2,1,0:T(8,128)(2,1)S(1)}, u32[]{:S(2)}, u32[]{:S(2)}) async-start(bf16[8,128,640]{2,1,0:T(8,128)(2,1)} %bitcast.11), calls=%async_computation.2 | async-start | bytes 2621440 | tf_op jit(solution)/shard_map/all_to_all | solution.py:356
  95.0 0.8 collective-permute-done.other_hbm
  95.8 1.3 copy-done.7
  97.2 8.0 %spmm.1 = (bf16[512,512]{1,0:T(8,128)(2,1)}, bf16[512,512]{1,0:T(8,128)(2,1)}, bf16[512,512]{1,0:T(8,128)(2,1)}, bf16[512,512]{1,0:T(8,128)(2,1)}) custom-call(s32[128]{0:T(128)} %reshape_squeeze.3.cols_ref, s32[4]{0:T(128)} %get-tuple-element.62.group_ref.index_ref, s32[1]{0:T(128)} %bitcast.5.core_ref, ...), custom_call_target="tpu_custom_call" | custom-call | flops 2147483648 | bytes 10485760 | tf_op jit(solution)/shard_map/spmm/pallas_call | solution.py:452
  105.2 1.1 fusion
  106.3 1.5 collective-permute-start.2
  107.8 1.4 collective-permute-start.1
  109.2 5.4 %collective-permute-done.2.bottom_ref = bf16[256,512]{1,0:T(8,128)(2,1)S(1)} collective-permute-done((bf16[256,512]{1,0:T(8,128)(2,1)S(1)}, bf16[256,512]{1,0:T(8,128)(2,1)S(1)}, u32[]{:S(2)}, u32[]{:S(2)}) %collective-permute-start.2) | collective-permute-done | bytes 262176 | tf_op jit(solution)/shard_map/ppermute | solution.py:362
  114.7 1.2 collective-permute-done.1.top_ref
  115.9 0.7 copy-done.11
  116.6 2.4 pass_on.1
  119.0 1.4 collective-permute-start.3
  121.0 6.2 %all-to-all-done.2 = bf16[8,128,640]{2,1,0:T(8,128)(2,1)S(1)} async-done(((bf16[8,128,640]{2,1,0:T(8,128)(2,1)}), bf16[8,128,640]{2,1,0:T(8,128)(2,1)S(1)}, u32[]{:S(2)}, u32[]{:S(2)}) %all-to-all-start.2) | async-done | bytes 1310752 | tf_op jit(solution)/shard_map/all_to_all | solution.py:356
  127.2 4.8 %collective-permute-done.3.refs_1_ = bf16[512,512]{1,0:T(8,128)(2,1)S(1)} collective-permute-done((bf16[512,512]{1,0:T(8,128)(2,1)}, bf16[512,512]{1,0:T(8,128)(2,1)S(1)}, u32[]{:S(2)}, u32[]{:S(2)}) %collective-permute-start.3) | collective-permute-done | bytes 524320 | tf_op jit(solution)/shard_map/ppermute | solution.py:362
  132.0 1.2 collective-permute-done.4.refs_2_
  133.2 0.8 copy-done.18
  134.0 6.8 %layer.1 = (bf16[1024,512]{1,0:T(8,128)(2,1)}, bf16[512,512]{1,0:T(8,128)(2,1)}, bf16[512,512]{1,0:T(8,128)(2,1)}, bf16[512,512]{1,0:T(8,128)(2,1)}) custom-call(bf16[512,512]{1,0:T(8,128)(2,1)} %get-tuple-element.67.refs_0_, bf16[512,512]{1,0:T(8,128)(2,1)} %copy-done.17, bf16[512,512]{1,0:T(8,128)(2,1)} %copy-done.18, ...), custom_call_target="tpu_custom_call" | custom-call | flops 1342177280 | bytes 6815744 | tf_op jit(solution)/shard_map/layer/pallas_call | solution.py:482
  140.7 4.4 %all-to-all-start.3 = ((bf16[8,128,512]{2,1,0:T(8,128)(2,1)}), bf16[8,128,512]{2,1,0:T(8,128)(2,1)S(1)}, u32[]{:S(2)}, u32[]{:S(2)}) async-start(bf16[8,128,512]{2,1,0:T(8,128)(2,1)} %bitcast.43), calls=%async_computation.3 | async-start | bytes 2097152 | tf_op jit(solution)/shard_map/all_to_all | solution.py:356
  145.2 0.8 collective-permute-start.6
  146.5 13.0 %collective-permute-done.6.refs_2_ = bf16[512,512]{1,0:T(8,128)(2,1)S(1)} collective-permute-done((bf16[512,512]{1,0:T(8,128)(2,1)S(1)}, bf16[512,512]{1,0:T(8,128)(2,1)S(1)}, u32[]{:S(2)}, u32[]{:S(2)}) %collective-permute-start.6) | collective-permute-done | bytes 524320 | tf_op jit(solution)/shard_map/ppermute | solution.py:362
  160.2 1.1 collective-permute-start.8
  161.4 3.8 %terms.1 = (bf16[512,512]{1,0:T(8,128)(2,1)}, bf16[512,512]{1,0:T(8,128)(2,1)}, f32[512,512]{1,0:T(8,128)}) custom-call(s32[1]{0:T(128)} %bitcast.5.core_ref, bf16[512,512]{1,0:T(8,128)(2,1)} %unpack_features.1.refs_3_.x_ref, bf16[512,512]{1,0:T(8,128)(2,1)} %get-tuple-element.77.agg_ref, bf16[512,512]{1,0:T(8,128)(2,1)} %get-tuple-element.78.slopes_ref, ...), custom_call_target="tpu_custom_call" | custom-call | flops 805306368 | bytes 4718592 | tf_op jit(solution)/shard_map/terms/pallas_call | solution.py:499
  165.2 2.3 collective-permute-done.7.refs_3_
  168.6 12.1 %spmm_back.1 = (bf16[2048,512]{1,0:T(8,128)(2,1)}, bf16[2048,512]{1,0:T(8,128)(2,1)}) custom-call(s32[128]{0:T(128)} %reshape_squeeze.3.cols_ref, s32[4]{0:T(128)} %get-tuple-element.62.group_ref.index_ref, s32[1]{0:T(128)} %bitcast.5.core_ref, bf16[512,512]{1,0:T(8,128)(2,1)} %get-tuple-element.82.refs_0_, bf16[512,512]{1,0:T(8,128)(2,1)} %copy-done.13, ...), custom_call_target="tpu_custom_call" | custom-call | flops 2147483648 | bytes 10485760 | tf_op jit(solution)/shard_map/spmm_back/pallas_call | solution.py:509
  180.8 4.4 %collective-permute-done.9 = bf16[2048,512]{1,0:T(8,128)(2,1)S(1)} collective-permute-done((bf16[2048,512]{1,0:T(8,128)(2,1)}, bf16[2048,512]{1,0:T(8,128)(2,1)S(1)}, u32[]{:S(2)}, u32[]{:S(2)}) %collective-permute-start.9) | collective-permute-done | bytes 2097184 | tf_op jit(solution)/shard_map/ppermute | solution.py:368
  185.2 3.7 %add_convert_fusion = bf16[2048,512]{1,0:T(8,128)(2,1)} fusion(bf16[2048,512]{1,0:T(8,128)(2,1)S(1)} %collective-permute-done.9, bf16[2048,512]{1,0:T(8,128)(2,1)} %get-tuple-element.87), kind=kLoop, calls=%fused_computation | loop fusion | flops 4194304 | bytes 6291456 | tf_op jit(solution)/shard_map/convert_element_type | solution.py:530
  188.9 1.0 copy.19
  189.9 3.8 %all-to-all-start.4 = ((bf16[4,256,512]{2,1,0:T(8,128)(2,1)}), bf16[4,256,512]{2,1,0:T(8,128)(2,1)S(1)}, u32[]{:S(2)}, u32[]{:S(2)}) async-start(bf16[4,256,512]{2,1,0:T(8,128)(2,1)} %bitcast.39), calls=%async_computation.4 | async-start | bytes 2097152 | tf_op jit(solution)/shard_map/all_to_all | solution.py:352
  194.0 1.8 collective-permute-done.10.refs_1_
  195.8 0.8 split_sum.3
  196.5 1.8 collective-permute-start.11
  198.3 1.5 collective-permute-start.12
  200.1 11.3 %collective-permute-done.11.refs_1_ = bf16[128,512]{1,0:T(8,128)(2,1)S(1)} collective-permute-done((bf16[128,512]{1,0:T(8,128)(2,1)S(1)}, bf16[128,512]{1,0:T(8,128)(2,1)S(1)}, u32[]{:S(2)}, u32[]{:S(2)}) %collective-permute-start.11) | collective-permute-done | bytes 131104 | tf_op jit(solution)/shard_map/ppermute | solution.py:362
  211.4 2.9 %collective-permute-done.13.refs_3_ = bf16[128,512]{1,0:T(8,128)(2,1)S(1)} collective-permute-done((bf16[128,512]{1,0:T(8,128)(2,1)S(1)}, bf16[128,512]{1,0:T(8,128)(2,1)S(1)}, u32[]{:S(2)}, u32[]{:S(2)}) %collective-permute-start.13) | collective-permute-done | bytes 131104 | tf_op jit(solution)/shard_map/ppermute | solution.py:362
  214.9 1.4 collective-permute-start.14
  216.3 2.4 collective-permute-start.15
  218.7 0.7 collective-permute-start.16
  219.4 1.8 collective-permute-done.14.refs_1_
  221.2 1.8 collective-permute-done.15.refs_2_
  223.0 2.3 collective-permute-done.16.refs_3_
  225.3 1.9 collective-permute-start.19
  227.2 2.1 collective-permute-start.18
  229.8 2.4 collective-permute-done.19.refs_3_
  232.2 3.9 %collective-permute-done.18.refs_2_ = bf16[32,512]{1,0:T(8,128)(2,1)S(1)} collective-permute-done((bf16[32,512]{1,0:T(8,128)(2,1)S(1)}, bf16[32,512]{1,0:T(8,128)(2,1)S(1)}, u32[]{:S(2)}, u32[]{:S(2)}) %collective-permute-start.18) | collective-permute-done | bytes 32800 | tf_op jit(solution)/shard_map/ppermute | solution.py:365
  236.8 1.0 copy-done.1
  237.9 1.8 join_pack.1
  239.7 4.1 %all-to-all-start.5 = ((bf16[32,32,512]{2,1,0:T(8,128)(2,1)}), bf16[32,32,512]{2,1,0:T(8,128)(2,1)S(1)}, u32[]{:S(2)}, u32[]{:S(2)}) async-start(bf16[32,32,512]{2,1,0:T(8,128)(2,1)} %bitcast.20), calls=%async_computation.6 | async-start | bytes 2097152 | tf_op jit(solution)/shard_map/all_to_all | solution.py:348
  243.8 2.7 collective-permute-start.22
  247.3 11.5 %collective-permute-done.22.refs_3_ = bf16[128,512]{1,0:T(8,128)(2,1)S(1)} collective-permute-done((bf16[128,512]{1,0:T(8,128)(2,1)S(1)}, bf16[128,512]{1,0:T(8,128)(2,1)S(1)}, u32[]{:S(2)}, u32[]{:S(2)}) %collective-permute-start.22) | collective-permute-done | bytes 131104 | tf_op jit(solution)/shard_map/ppermute | solution.py:362
  258.8 1.6 collective-permute-done.21.refs_2_
  260.4 0.7 collective-permute-done.20.refs_1_
  261.8 1.6 unpack_owner.2
  263.7 1.5 final.1
  265.1 6.2 %all-to-all-done.5 = bf16[32,32,512]{2,1,0:T(8,128)(2,1)S(1)} async-done(((bf16[32,32,512]{2,1,0:T(8,128)(2,1)}), bf16[32,32,512]{2,1,0:T(8,128)(2,1)S(1)}, u32[]{:S(2)}, u32[]{:S(2)}) %all-to-all-start.5) | async-done | bytes 1048608 | tf_op jit(solution)/shard_map/all_to_all | solution.py:348
  271.3 1.5 unpack_owner.3
  (69 shorter events, 8.7 us)
Async XLA Ops:
  7.2 10.5 %copy-start.14 = (s32[1,1,16,8]{2,3,1,0:T(8,128)S(1)}, s32[1,1,16,8]{2,3,1,0:T(8,128)}, u32[]{:S(2)}) copy-start(s32[1,1,16,8]{2,3,1,0:T(8,128)} %param.10) | copy-start | bytes 1540
  10.3 34.9 %all-to-all-start = ((bf16[32,32,512]{2,1,0:T(8,128)(2,1)}), bf16[32,32,512]{2,1,0:T(8,128)(2,1)S(1)}, u32[]{:S(2)}, u32[]{:S(2)}) async-start(bf16[32,32,512]{2,1,0:T(8,128)(2,1)} %bitcast.44), calls=%async_computation | async-start | bytes 2097152 | tf_op jit(solution)/shard_map/all_to_all | solution.py:348
  17.6 73.8 %all-gather.2.cloned.1.call-start = ((), (), s32[]{:S(2)}) async-start(), calls=%async_computation.7 | async-start | bytes 2621440 | tf_op jit(solution)/shard_map/all_gather | solution.py:433
  45.2 1.0 copy-start.6
  46.2 1.6 copy-start.9
  91.4 4.4 %collective-permute-start = (bf16[2048,512]{1,0:T(8,128)(2,1)}, bf16[2048,512]{1,0:T(8,128)(2,1)S(1)}, u32[]{:S(2)}, u32[]{:S(2)}) collective-permute-start(bf16[2048,512]{1,0:T(8,128)(2,1)} %all-gather.2.cloned.1.call-done.own_hbm), channel_id=1, source_target_pairs={{0,1},{1,0},{2,3},{3,2},{4,5},{5,4},{6,7},{7,6},{8,9},{9,8},{10,11... | collective-permute-start | bytes 6291464 | tf_op jit(solution)/shard_map/ppermute | solution.py:368
  91.4 35.7 %all-to-all-start.2 = ((bf16[8,128,640]{2,1,0:T(8,128)(2,1)}), bf16[8,128,640]{2,1,0:T(8,128)(2,1)S(1)}, u32[]{:S(2)}, u32[]{:S(2)}) async-start(bf16[8,128,640]{2,1,0:T(8,128)(2,1)} %bitcast.11), calls=%async_computation.2 | async-start | bytes 2621440 | tf_op jit(solution)/shard_map/all_to_all | solution.py:356
  95.8 1.3 copy-start.7
  106.3 8.4 %collective-permute-start.2 = (bf16[256,512]{1,0:T(8,128)(2,1)S(1)}, bf16[256,512]{1,0:T(8,128)(2,1)S(1)}, u32[]{:S(2)}, u32[]{:S(2)}) collective-permute-start(bf16[256,512]{1,0:T(8,128)(2,1)S(1)} %get-tuple-element.112), channel_id=1, source_target_pairs={{0,16},{8,24},{16,0},{24,8},{1,17},{9,25},{17,1},{25,9},{2,18},{10... | collective-permute-start | bytes 786440 | tf_op jit(solution)/shard_map/ppermute | solution.py:362
  107.8 8.1 %collective-permute-start.1 = (bf16[256,512]{1,0:T(8,128)(2,1)S(1)}, bf16[256,512]{1,0:T(8,128)(2,1)S(1)}, u32[]{:S(2)}, u32[]{:S(2)}) collective-permute-start(bf16[256,512]{1,0:T(8,128)(2,1)S(1)} %get-tuple-element.113), channel_id=1, source_target_pairs={{0,8},{8,0},{16,24},{24,16},{1,9},{9,1},{17,25},{25,17},{2,10},{10... | collective-permute-start | bytes 786440 | tf_op jit(solution)/shard_map/ppermute | solution.py:362
  114.7 1.2 copy-start.10
  115.9 0.7 copy-start.11
  119.0 13.0 %collective-permute-start.3 = (bf16[512,512]{1,0:T(8,128)(2,1)}, bf16[512,512]{1,0:T(8,128)(2,1)S(1)}, u32[]{:S(2)}, u32[]{:S(2)}) collective-permute-start(bf16[512,512]{1,0:T(8,128)(2,1)} %get-tuple-element.71), channel_id=1, source_target_pairs={{0,8},{8,0},{16,24},{24,16},{1,9},{9,1},{17,25},{25,17},{2,10},{10... | collective-permute-start | bytes 1572872 | tf_op jit(solution)/shard_map/ppermute | solution.py:362
  120.4 12.7 %collective-permute-start.4 = (bf16[512,512]{1,0:T(8,128)(2,1)}, bf16[512,512]{1,0:T(8,128)(2,1)S(1)}, u32[]{:S(2)}, u32[]{:S(2)}) collective-permute-start(bf16[512,512]{1,0:T(8,128)(2,1)} %get-tuple-element.72), channel_id=1, source_target_pairs={{0,16},{8,24},{16,0},{24,8},{1,17},{9,25},{17,1},{25,9},{2,18},{10... | collective-permute-start | bytes 1572872 | tf_op jit(solution)/shard_map/ppermute | solution.py:362
  127.2 6.0 %copy-start.8 = (bf16[8,128,640]{2,1,0:T(8,128)(2,1)}, bf16[8,128,640]{2,1,0:T(8,128)(2,1)S(1)}, u32[]{:S(2)}) copy-start(bf16[8,128,640]{2,1,0:T(8,128)(2,1)S(1)} %all-to-all-done.2) | copy-start | bytes 3932164
  132.0 1.2 copy-start.17
  133.2 0.8 copy-start.18
  140.7 4.4 %copy-start.15 = (bf16[512,512]{1,0:T(8,128)(2,1)S(1)}, bf16[512,512]{1,0:T(8,128)(2,1)}, u32[]{:S(2)}) copy-start(bf16[512,512]{1,0:T(8,128)(2,1)} %get-tuple-element.82.refs_0_) | copy-start | bytes 1572868
  140.7 40.0 %all-to-all-start.3 = ((bf16[8,128,512]{2,1,0:T(8,128)(2,1)}), bf16[8,128,512]{2,1,0:T(8,128)(2,1)S(1)}, u32[]{:S(2)}, u32[]{:S(2)}) async-start(bf16[8,128,512]{2,1,0:T(8,128)(2,1)} %bitcast.43), calls=%async_computation.3 | async-start | bytes 2097152 | tf_op jit(solution)/shard_map/all_to_all | solution.py:356
  145.1 91.7 %reduce-scatter.2.cloned.1.call-start = ((), (), s32[]{:S(2)}) async-start(), calls=%async_computation.8 | async-start | bytes 2621440 | tf_op jit(solution)/shard_map/reduce_scatter | solution.py:532
  145.2 14.4 %collective-permute-start.6 = (bf16[512,512]{1,0:T(8,128)(2,1)S(1)}, bf16[512,512]{1,0:T(8,128)(2,1)S(1)}, u32[]{:S(2)}, u32[]{:S(2)}) collective-permute-start(bf16[512,512]{1,0:T(8,128)(2,1)S(1)} %copy-done.15), channel_id=1, source_target_pairs={{0,16},{8,24},{16,0},{24,8},{1,17},{9,25},{17,1},{25,9},{2,18},{10... | collective-permute-start | bytes 1572872 | tf_op jit(solution)/shard_map/ppermute | solution.py:362
  145.9 14.3 %collective-permute-start.5 = (bf16[512,512]{1,0:T(8,128)(2,1)S(1)}, bf16[512,512]{1,0:T(8,128)(2,1)S(1)}, u32[]{:S(2)}, u32[]{:S(2)}) collective-permute-start(bf16[512,512]{1,0:T(8,128)(2,1)S(1)} %copy-done.15), channel_id=1, source_target_pairs={{0,8},{8,0},{16,24},{24,16},{1,9},{9,1},{17,25},{25,17},{2,10},{10... | collective-permute-start | bytes 1572872 | tf_op jit(solution)/shard_map/ppermute | solution.py:362
  159.5 8.4 %copy-start.12 = (bf16[512,512]{1,0:T(8,128)(2,1)}, bf16[512,512]{1,0:T(8,128)(2,1)S(1)}, u32[]{:S(2)}) copy-start(bf16[512,512]{1,0:T(8,128)(2,1)S(1)} %collective-permute-done.6.refs_2_) | copy-start | bytes 1572868
  159.6 7.9 %collective-permute-start.7 = (bf16[256,512]{1,0:T(8,128)(2,1)S(1)}, bf16[256,512]{1,0:T(8,128)(2,1)S(1)}, u32[]{:S(2)}, u32[]{:S(2)}) collective-permute-start(bf16[256,512]{1,0:T(8,128)(2,1)S(1)} %slice.16), channel_id=1, source_target_pairs={{0,8},{8,0},{16,24},{24,16},{1,9},{9,1},{17,25},{25,17},{2,10},{10... | collective-permute-start | bytes 786440 | tf_op jit(solution)/shard_map/ppermute | solution.py:362
  160.2 7.7 %copy-start.13 = (bf16[512,512]{1,0:T(8,128)(2,1)}, bf16[512,512]{1,0:T(8,128)(2,1)S(1)}, u32[]{:S(2)}) copy-start(bf16[512,512]{1,0:T(8,128)(2,1)S(1)} %collective-permute-done.5.refs_1_) | copy-start | bytes 1572868
  160.2 7.7 %collective-permute-start.8 = (bf16[256,512]{1,0:T(8,128)(2,1)S(1)}, bf16[256,512]{1,0:T(8,128)(2,1)S(1)}, u32[]{:S(2)}, u32[]{:S(2)}) collective-permute-start(bf16[256,512]{1,0:T(8,128)(2,1)S(1)} %slice.17), channel_id=1, source_target_pairs={{0,16},{8,24},{16,0},{24,8},{1,17},{9,25},{17,1},{25,9},{2,18},{10... | collective-permute-start | bytes 786440 | tf_op jit(solution)/shard_map/ppermute | solution.py:362
  167.5 0.7 copy-start.19
  167.9 0.7 copy-start.20
  180.7 4.4 %collective-permute-start.9 = (bf16[2048,512]{1,0:T(8,128)(2,1)}, bf16[2048,512]{1,0:T(8,128)(2,1)S(1)}, u32[]{:S(2)}, u32[]{:S(2)}) collective-permute-start(bf16[2048,512]{1,0:T(8,128)(2,1)} %get-tuple-element.90), channel_id=1, source_target_pairs={{0,1},{1,0},{2,3},{3,2},{4,5},{5,4},{6,7},{7,6},{8,9},{9,8},{10,11... | collective-permute-start | bytes 6291464 | tf_op jit(solution)/shard_map/ppermute | solution.py:368
  188.9 4.9 %copy-start.16 = (bf16[512,512]{1,0:T(8,128)(2,1)S(1)}, bf16[512,512]{1,0:T(8,128)(2,1)}, u32[]{:S(2)}) copy-start(bf16[512,512]{1,0:T(8,128)(2,1)} %get-tuple-element.97) | copy-start | bytes 1572868
  188.9 6.9 %copy-start.2 = (bf16[512,512]{1,0:T(8,128)(2,1)S(1)}, bf16[512,512]{1,0:T(8,128)(2,1)}, u32[]{:S(2)}) copy-start(bf16[512,512]{1,0:T(8,128)(2,1)} %get-tuple-element.96.refs_0_) | copy-start | bytes 1572868
  188.9 6.9 %copy-start.4 = (s32[4]{0:T(128)S(1)}, s32[4]{0:T(128)}, u32[]{:S(2)}) copy-start(s32[4]{0:T(128)} %get-tuple-element.62.group_ref.index_ref) | copy-start | bytes 52
  189.9 46.9 %copy-start = (f32[512,512]{1,0:T(8,128)S(1)}, f32[512,512]{1,0:T(8,128)}, u32[]{:S(2)}) copy-start(f32[512,512]{1,0:T(8,128)} %get-tuple-element.106.own_ref) | copy-start | bytes 3145732
  189.9 46.9 %copy-start.3 = (s32[8,512]{1,0:T(8,128)S(1)}, s32[8,512]{1,0:T(8,128)}, u32[]{:S(2)}) copy-start(s32[8,512]{1,0:T(8,128)} %get-tuple-element.108.row_ref) | copy-start | bytes 49156
  189.9 49.7 %all-to-all-start.4 = ((bf16[4,256,512]{2,1,0:T(8,128)(2,1)}), bf16[4,256,512]{2,1,0:T(8,128)(2,1)S(1)}, u32[]{:S(2)}, u32[]{:S(2)}) async-start(bf16[4,256,512]{2,1,0:T(8,128)(2,1)} %bitcast.39), calls=%async_computation.4 | async-start | bytes 2097152 | tf_op jit(solution)/shard_map/all_to_all | solution.py:352
  193.8 2.0 collective-permute-start.10
  196.5 14.9 %collective-permute-start.11 = (bf16[128,512]{1,0:T(8,128)(2,1)S(1)}, bf16[128,512]{1,0:T(8,128)(2,1)S(1)}, u32[]{:S(2)}, u32[]{:S(2)}) collective-permute-start(bf16[128,512]{1,0:T(8,128)(2,1)S(1)} %get-tuple-element.99), channel_id=1, source_target_pairs={{0,8},{8,0},{16,24},{24,16},{1,9},{9,1},{17,25},{25,17},{2,10},{10... | collective-permute-start | bytes 393224 | tf_op jit(solution)/shard_map/ppermute | solution.py:362
  198.3 13.1 %collective-permute-start.12 = (bf16[128,512]{1,0:T(8,128)(2,1)S(1)}, bf16[128,512]{1,0:T(8,128)(2,1)S(1)}, u32[]{:S(2)}, u32[]{:S(2)}) collective-permute-start(bf16[128,512]{1,0:T(8,128)(2,1)S(1)} %get-tuple-element.100), channel_id=1, source_target_pairs={{0,16},{8,24},{16,0},{24,8},{1,17},{9,25},{17,1},{25,9},{2,18},{10... | collective-permute-start | bytes 393224 | tf_op jit(solution)/shard_map/ppermute | solution.py:362
  199.8 14.5 %collective-permute-start.13 = (bf16[128,512]{1,0:T(8,128)(2,1)S(1)}, bf16[128,512]{1,0:T(8,128)(2,1)S(1)}, u32[]{:S(2)}, u32[]{:S(2)}) collective-permute-start(bf16[128,512]{1,0:T(8,128)(2,1)S(1)} %get-tuple-element.101), channel_id=1, source_target_pairs={{0,24},{8,16},{16,8},{24,0},{1,25},{9,17},{17,9},{25,1},{2,26},{10... | collective-permute-start | bytes 393224 | tf_op jit(solution)/shard_map/ppermute | solution.py:362
  214.9 6.3 %collective-permute-start.14 = (bf16[32,512]{1,0:T(8,128)(2,1)S(1)}, bf16[32,512]{1,0:T(8,128)(2,1)S(1)}, u32[]{:S(2)}, u32[]{:S(2)}) collective-permute-start(bf16[32,512]{1,0:T(8,128)(2,1)S(1)} %get-tuple-element.103), channel_id=1, source_target_pairs={{0,2},{1,3},{2,0},{3,1},{4,6},{5,7},{6,4},{7,5},{8,10},{9,11},{10,... | collective-permute-start | bytes 98312 | tf_op jit(solution)/shard_map/ppermute | solution.py:365
  216.3 6.7 %collective-permute-start.15 = (bf16[32,512]{1,0:T(8,128)(2,1)S(1)}, bf16[32,512]{1,0:T(8,128)(2,1)S(1)}, u32[]{:S(2)}, u32[]{:S(2)}) collective-permute-start(bf16[32,512]{1,0:T(8,128)(2,1)S(1)} %get-tuple-element.104), channel_id=1, source_target_pairs={{0,4},{1,5},{2,6},{3,7},{4,0},{5,1},{6,2},{7,3},{8,12},{9,13},{10,... | collective-permute-start | bytes 98312 | tf_op jit(solution)/shard_map/ppermute | solution.py:365
  218.7 6.6 %collective-permute-start.16 = (bf16[32,512]{1,0:T(8,128)(2,1)S(1)}, bf16[32,512]{1,0:T(8,128)(2,1)S(1)}, u32[]{:S(2)}, u32[]{:S(2)}) collective-permute-start(bf16[32,512]{1,0:T(8,128)(2,1)S(1)} %get-tuple-element.105), channel_id=1, source_target_pairs={{0,6},{1,7},{2,4},{3,5},{4,2},{5,3},{6,0},{7,1},{8,14},{9,15},{10,... | collective-permute-start | bytes 98312 | tf_op jit(solution)/shard_map/ppermute | solution.py:365
  225.3 6.9 %collective-permute-start.19 = (bf16[32,512]{1,0:T(8,128)(2,1)S(1)}, bf16[32,512]{1,0:T(8,128)(2,1)S(1)}, u32[]{:S(2)}, u32[]{:S(2)}) collective-permute-start(bf16[32,512]{1,0:T(8,128)(2,1)S(1)} %split_sum.5.refs_0_), channel_id=1, source_target_pairs={{0,6},{1,7},{2,4},{3,5},{4,2},{5,3},{6,0},{7,1},{8,14},{9,15},{10,... | collective-permute-start | bytes 98312 | tf_op jit(solution)/shard_map/ppermute | solution.py:365
  227.2 8.9 %collective-permute-start.18 = (bf16[32,512]{1,0:T(8,128)(2,1)S(1)}, bf16[32,512]{1,0:T(8,128)(2,1)S(1)}, u32[]{:S(2)}, u32[]{:S(2)}) collective-permute-start(bf16[32,512]{1,0:T(8,128)(2,1)S(1)} %split_sum.5.refs_0_), channel_id=1, source_target_pairs={{0,4},{1,5},{2,6},{3,7},{4,0},{5,1},{6,2},{7,3},{8,12},{9,13},{10,... | collective-permute-start | bytes 98312 | tf_op jit(solution)/shard_map/ppermute | solution.py:365
  229.3 6.8 %collective-permute-start.17 = (bf16[32,512]{1,0:T(8,128)(2,1)S(1)}, bf16[32,512]{1,0:T(8,128)(2,1)S(1)}, u32[]{:S(2)}, u32[]{:S(2)}) collective-permute-start(bf16[32,512]{1,0:T(8,128)(2,1)S(1)} %split_sum.5.refs_0_), channel_id=1, source_target_pairs={{0,2},{1,3},{2,0},{3,1},{4,6},{5,7},{6,4},{7,5},{8,10},{9,11},{10,... | collective-permute-start | bytes 98312 | tf_op jit(solution)/shard_map/ppermute | solution.py:365
  236.8 1.0 copy-start.1
  239.7 22.1 %copy-start.5 = (s32[512,128]{1,0:T(8,128)S(1)}, s32[512,128]{1,0:T(8,128)}, u32[]{:S(2)}) copy-start(s32[512,128]{1,0:T(8,128)} %get-tuple-element.58.col_ref) | copy-start | bytes 786436
  239.7 31.7 %all-to-all-start.5 = ((bf16[32,32,512]{2,1,0:T(8,128)(2,1)}), bf16[32,32,512]{2,1,0:T(8,128)(2,1)S(1)}, u32[]{:S(2)}, u32[]{:S(2)}) async-start(bf16[32,32,512]{2,1,0:T(8,128)(2,1)} %bitcast.20), calls=%async_computation.6 | async-start | bytes 2097152 | tf_op jit(solution)/shard_map/all_to_all | solution.py:348
  243.8 15.0 %collective-permute-start.22 = (bf16[128,512]{1,0:T(8,128)(2,1)S(1)}, bf16[128,512]{1,0:T(8,128)(2,1)S(1)}, u32[]{:S(2)}, u32[]{:S(2)}) collective-permute-start(bf16[128,512]{1,0:T(8,128)(2,1)S(1)} %bitcast.32), channel_id=1, source_target_pairs={{0,24},{8,16},{16,8},{24,0},{1,25},{9,17},{17,9},{25,1},{2,26},{10... | collective-permute-start | bytes 393224 | tf_op jit(solution)/shard_map/ppermute | solution.py:362
  246.5 13.9 %collective-permute-start.21 = (bf16[128,512]{1,0:T(8,128)(2,1)S(1)}, bf16[128,512]{1,0:T(8,128)(2,1)S(1)}, u32[]{:S(2)}, u32[]{:S(2)}) collective-permute-start(bf16[128,512]{1,0:T(8,128)(2,1)S(1)} %bitcast.33), channel_id=1, source_target_pairs={{0,16},{8,24},{16,0},{24,8},{1,17},{9,25},{17,1},{25,9},{2,18},{10... | collective-permute-start | bytes 393224 | tf_op jit(solution)/shard_map/ppermute | solution.py:362
  247.0 14.1 %collective-permute-start.20 = (bf16[128,512]{1,0:T(8,128)(2,1)S(1)}, bf16[128,512]{1,0:T(8,128)(2,1)S(1)}, u32[]{:S(2)}, u32[]{:S(2)}) collective-permute-start(bf16[128,512]{1,0:T(8,128)(2,1)S(1)} %bitcast.34), channel_id=1, source_target_pairs={{0,8},{8,0},{16,24},{24,16},{1,9},{9,1},{17,25},{25,17},{2,10},{10... | collective-permute-start | bytes 393224 | tf_op jit(solution)/shard_map/ppermute | solution.py:362
  261.7 2.0 collective-permute-start.23
Sparse Core Ops, SparseCore 0:
  47.8 43.5 all-gather.1
  189.0 47.8 reduce-scatter.1

commit v6 on v4

--- a/solution.py
+++ b/solution.py
@@ -12,6 +12,7 @@
 F32 = jnp.float32
 VMEM = pl.BlockSpec(memory_space=pltpu.VMEM)
 MIB = 1024 * 1024
+LARGE = 56
 
 
 def params(mib=16):
@@ -94,65 +95,86 @@
     out_ref[...] = dot(entries_onehot(col_ref[...], value_ref.shape[0]), value_ref[...]).astype(BF)
 
 
-def spmm_kernel(ways, cols_ref, group_ref, x_hbm, *refs):
-    masks, outs = refs[:ways], refs[ways : 2 * ways]
-    x_ref, sems = refs[2 * ways :]
+def spmm_kernel(ways, cols_ref, group_ref, x_ref, *refs):
+    masks, outs = refs[:ways], refs[ways:]
     q = pl.program_id(0)
     depth = pl.num_programs(0)
     _, breadth, tile, _ = masks[0].shape
-
-    @pl.when(q == 0)
-    def _():
-        count = sems.shape[0]
-        share = x_ref.shape[0] // count
-        copies = [
-            pltpu.make_async_copy(x_hbm.at[pl.ds(i * share, share)], x_ref.at[pl.ds(i * share, share)], sems.at[i])
-            for i in range(count)
-        ]
-        for copy in copies:
-            copy.start()
-        for copy in copies:
-            copy.wait()
-
     for s in range(ways):
         base = (group_ref[s] * depth + q) * breadth
         total = None
         for p in range(0, breadth, 2):
-            width = min(2, breadth - p)
-            left = jnp.concatenate([masks[s][0, p + w] for w in range(width)], axis=1)
+            span = range(p, min(p + 2, breadth))
+            left = jnp.concatenate([masks[s][0, k] for k in span], axis=1)
             right = jnp.concatenate(
-                [x_ref[pl.ds(pl.multiple_of(cols_ref[base + p + w] * tile, tile), tile), :] for w in range(width)], axis=0
+                [x_ref[pl.ds(pl.multiple_of(cols_ref[base + k] * tile, tile), tile), :] for k in span], axis=0
             )
             term = dot(left, right)
             total = term if total is None else total + term
         outs[s][...] = total.astype(BF)
 
 
+def load_masks(group_ref, masks_hbm, masks_ref, sems, ways, depth, q):
+    return [
+        pltpu.make_async_copy(masks_hbm.at[group_ref[s] * depth + q], masks_ref.at[q * ways + s], sems.at[q * ways + s])
+        for s in range(ways)
+    ]
+
+
 def spmm_back_kernel(ways, pieces, cols_ref, group_ref, *refs):
     given = sum(pieces)
-    spreads, masks, out_ref, total = refs[:given], refs[given : given + ways], refs[-2], refs[-1]
-    q = pl.program_id(0)
-    depth = pl.num_programs(0)
-    _, breadth, tile, _ = masks[0].shape
+    spreads = refs[:given]
+    masks_hbm, out_hbm, total, ready, masks_ref, sems, mask_sems = refs[given:]
+    h, q = pl.program_id(0), pl.program_id(1)
+    halves, depth = sems.shape[0], pl.num_programs(1)
+    steps = masks_ref.shape[0] // ways
+    _, breadth, tile, _ = masks_ref.shape
+    part = total.shape[0]
+    blocks, _, rows = out_hbm.shape
+
+    @pl.when((h == 0) & (q == 0))
+    def _():
+        for step in range(steps):
+            for copy in load_masks(group_ref, masks_hbm, masks_ref, mask_sems, ways, steps, step):
+                copy.start()
 
     @pl.when(q == 0)
     def _():
         total[...] = jnp.zeros_like(total)
 
+    for step in range(steps):
+
+        @pl.when((h == 0) & (q == step))
+        def _():
+            for copy in load_masks(group_ref, masks_hbm, masks_ref, mask_sems, ways, steps, step):
+                copy.wait()
+
     at_piece = 0
     for s in range(ways):
-        base = (group_ref[s] * depth + q) * breadth
-        rows = spreads[at_piece][...]
+        row = group_ref[s] * depth + q
+        left = spreads[at_piece][...]
         for p in range(1, pieces[s]):
-            rows = jnp.where(q * pieces[s] >= p * depth, spreads[at_piece + p][...], rows)
+            left = jnp.where(h >= p, spreads[at_piece + p][...], left)
         at_piece += pieces[s]
-        for k in range(breadth):
-            at = pl.ds(pl.multiple_of(cols_ref[base + k] * tile, tile), tile)
-            total[at, :] += dot(masks[s][0, k], rows, 0, 0)
-
-    @pl.when(q == depth - 1)
-    def _():
-        out_ref[...] = total[...].astype(BF)
+        for p in range(0, breadth, 2):
+            span = range(p, min(p + 2, breadth))
+            term = dot(left, jnp.concatenate([masks_ref[q * ways + s, k] for k in span], axis=1))
+            for k in span:
+                at = pl.ds(pl.multiple_of(cols_ref[row * breadth + k] * tile, tile), tile)
+                total[:, at] += term[:, (k - p) * tile : (k - p + 1) * tile]
+
+    for half in range(halves):
+        store = pltpu.make_async_copy(ready.at[half], out_hbm.at[:, pl.ds(half * part, part), :], sems.at[half])
+
+        @pl.when((h == half) & (q == depth - 1))
+        def _():
+            for block in range(blocks):
+                ready[half, block] = total[:, block * rows : (block + 1) * rows].astype(BF)
+            store.start()
+
+        @pl.when((h == halves - 1) & (q == depth - 1))
+        def _():
+            store.wait()
 
 
 def pass_on_kernel(left_ref, right_ref, top_ref, bottom_ref, left_out, right_out):
@@ -179,13 +201,14 @@
     hidden = (preact * gate).astype(BF)
     slopes = (cot[:, :width] * gate * (1.0 + preact * (1.0 - gate))).astype(BF)
     slopes_out[...] = slopes
-    spread_out[...] = (dot(slopes, neigh_ref[...], 1, 1) / degrees).astype(BF)
+    degree_row = jnp.broadcast_to(degrees, (degrees.shape[0], 128)).T[:1]
+    spread_out[...] = (dot(neigh_ref[...], slopes, 1, 1) / degree_row).astype(BF)
     packed_out[...] = dot(slots_onehot(row_ref[...][:1], packed_out.shape[0]), hidden).astype(BF)
 
 
 def terms_kernel(core_ref, x_ref, agg_ref, slopes_ref, self_ref, kept_out, sent_out, back_out):
     slopes = slopes_ref[...]
-    back_out[...] = dot(slopes, self_ref[...], 1, 1)
+    back_out[...] = dot(self_ref[...], slopes, 1, 1)
     grad_self = dot(x_ref[...], slopes, 0, 0).astype(BF)
     grad_neigh = dot(agg_ref[...], slopes, 0, 0).astype(BF)
     first = core_ref[0] == 0
@@ -219,7 +242,7 @@
 
 def join_kernel(own_ref, neigh_ref, row_ref, out_ref):
     joined = (own_ref[...] + neigh_ref[...].astype(F32)).astype(BF)
-    out_ref[...] = dot(slots_onehot(row_ref[...][:1], out_ref.shape[0]), joined).astype(BF)
+    out_ref[...] = dot(slots_onehot(row_ref[...][:1], out_ref.shape[0]), joined, 1, 1).astype(BF)
 
 
 def on_device(
@@ -243,7 +266,11 @@
     tile = masks.shape[-1]
     breadth = masks.shape[1]
     depth = rows // tile
+    ring = [list(range(0, col_devices, 2)) + list(range(1, col_devices, 2))[::-1]]
     cols = tile_cols[0, 0].reshape(-1)
+    block = lax.div(cols, depth)
+    pair = lax.div(block, 2)
+    cols = jnp.where(block == 2 * pair, pair, col_devices - 1 - pair) * depth + lax.rem(cols, depth)
     me = lax.axis_index("row")
     ways = row_devices
     groups = jnp.bitwise_xor(me, jnp.arange(ways, dtype=jnp.int32)).astype(jnp.int32)
@@ -315,6 +342,7 @@
         in_specs=[VMEM] * 2,
         out_specs=VMEM,
         cost_estimate=cost(2 * slots * slab, 6 * slab),
+        mib=LARGE,
         name="pack_features",
     )(nodes, features)
     inbound = relay(packed)
@@ -331,8 +359,10 @@
         in_specs=[VMEM] * 4,
         out_specs=(VMEM,) * 6,
         cost_estimate=cost(2 * slots * slab, 6 * slab),
+        mib=LARGE,
         name="index_cotangent",
     )(nodes, owner_position.reshape(1, rows), degree.reshape(1, rows), cotangent)
+    ANY = pl.BlockSpec(memory_space=pl.ANY)
     x_node = call(
         unpack_kernel,
         out_shape=shape(rows, width),
@@ -344,32 +374,28 @@
     cot_packed, x_node, cols, groups, core, others = lax.optimization_barrier(
         (cot_packed, x_node, cols, groups, core, others)
     )
-    x_cols = lax.all_gather(x_node, "col", axis=0, tiled=True)
+    x_cols = lax.all_gather(x_node, "col", axis_index_groups=ring, axis=0, tiled=True)
     cot_mid = turn(row_phase(cot_packed), row_devices, col_devices)
     x_cols, cot_mid = lax.optimization_barrier((x_cols, cot_mid))
     cot_in = col_phase(cot_mid)
 
+    spmm_flops = 2 * masks.size * width
+    halves = 2
+    part = width // halves
     def mask_spec(s):
-        return pl.BlockSpec((1, breadth, tile, tile), lambda q, c, g, s=s: (g[s] * depth + q, 0, 0, 0))
-
-    def piece_spec(p, count):
-        share = depth // count
-        return pl.BlockSpec((tile, width), lambda q, c, g: (jnp.clip(q - p * share, 0, share - 1), 0))
-
-    spmm_flops = 2 * masks.size * width
-    copies = 8
+        return pl.BlockSpec((1, breadth, tile, tile), lambda q, c, g: (g[s] * depth + q, 0, 0, 0))
+
     partials = call(
         functools.partial(spmm_kernel, ways),
         grid_spec=pltpu.PrefetchScalarGridSpec(
             num_scalar_prefetch=2,
             grid=(depth,),
-            in_specs=[pl.BlockSpec(memory_space=pl.ANY)] + [mask_spec(s) for s in range(ways)],
+            in_specs=[VMEM] + [mask_spec(s) for s in range(ways)],
             out_specs=[pl.BlockSpec((tile, width), lambda q, c, g: (q, 0)) for s in range(ways)],
-            scratch_shapes=[pltpu.VMEM(x_cols.shape, BF), pltpu.SemaphoreType.DMA((copies,))],
         ),
         out_shape=[shape(rows, width) for s in range(ways)],
         cost_estimate=cost(spmm_flops, 2 * masks.size + 2 * x_cols.size + 2 * ways * slab),
-        mib=12 + 3 * x_cols.size / MIB,
+        mib=LARGE,
         name="spmm",
     )(cols, groups, x_cols, *([masks] * ways))
     if ways == 4:
@@ -389,17 +415,16 @@
         terms = [partials[0]] + [across(partials[s], s) for s in range(1, ways)]
     hidden_packed, slopes, agg, spread = call(
         functools.partial(layer_kernel, len(terms)),
-        out_shape=(shape(slots, width),) + (shape(rows, width),) * 3,
+        out_shape=(shape(slots, width),) + (shape(rows, width),) * 2 + (shape(width, rows),),
         in_specs=[VMEM] * (len(terms) + 6),
         out_specs=(VMEM,) * 4,
         cost_estimate=cost(10 * slab * width, 2 * slab * (ways + 9)),
-        mib=24,
+        mib=LARGE,
         name="layer",
     )(*terms, x_node, cot_in, turned_col, turned_row, self_weight, neigh_weight)
     if ways == 4:
         left, right = across(spread, 1), across(spread, 2)
-        left, right, hidden_packed = lax.optimization_barrier((left, right, hidden_packed))
-        spreads = [spread, left, right, across(right[:half], 1), across(left[half:], 2)]
+        spreads = [spread, left, right, across(right[:part], 1), across(left[part:], 2)]
         pieces = (1, 1, 1, 2)
     else:
         spreads = [spread] + [across(spread, s) for s in range(1, ways)]
@@ -407,10 +432,11 @@
     hidden_mid = col_phase(hidden_packed)
     grad_kept, grad_sent, own_back = call(
         terms_kernel,
-        out_shape=(shape(width, width), shape(width, width), shape(rows, width, F32)),
+        out_shape=(shape(width, width), shape(width, width), shape(width, rows, F32)),
         in_specs=[SMEM] + [VMEM] * 4,
         out_specs=(VMEM,) * 3,
         cost_estimate=cost(6 * slab * width, 2 * slab * 9),
+        mib=LARGE,
         name="terms",
     )(core, x_node, agg, slopes, self_weight)
     *spreads, own_back, grad_kept, grad_sent = lax.optimization_barrier((*spreads, own_back, grad_kept, grad_sent))
@@ -418,19 +444,31 @@
         functools.partial(spmm_back_kernel, ways, pieces),
         grid_spec=pltpu.PrefetchScalarGridSpec(
             num_scalar_prefetch=2,
-            grid=(depth,),
-            in_specs=[piece_spec(p, count) for count in pieces for p in range(count)]
-            + [mask_spec(s) for s in range(ways)],
-            out_specs=VMEM,
-            scratch_shapes=[pltpu.VMEM(x_cols.shape, F32)],
+            grid=(halves, depth),
+            in_specs=[
+                pl.BlockSpec((part, tile), (lambda h, q, *_: (h, q)) if count == 1 else (lambda h, q, *_: (0, q)))
+                for count in pieces
+                for _ in range(count)
+            ]
+            + [ANY],
+            out_specs=ANY,
+            scratch_shapes=[
+                pltpu.VMEM((part, x_cols.shape[0]), F32),
+                pltpu.VMEM((halves, col_devices, part, rows), BF),
+                pltpu.VMEM(masks.shape, BF),
+                pltpu.SemaphoreType.DMA((halves,)),
+                pltpu.SemaphoreType.DMA((masks.shape[0],)),
+            ],
         ),
-        out_shape=shape(*x_cols.shape),
+        out_shape=jax.ShapeDtypeStruct((col_devices, width, rows), BF),
         cost_estimate=cost(spmm_flops, 2 * masks.size + 2 * x_cols.size + 2 * ways * slab),
-        mib=12 + 7 * x_cols.size / MIB,
+        mib=LARGE,
         name="spmm_back",
-    )(cols, groups, *spreads, *([masks] * ways))
+    )(cols, groups, *spreads, masks)
     back, hidden_mid, grad_sent = lax.optimization_barrier((back, hidden_mid, grad_sent))
-    neigh_back = lax.psum_scatter(back, "col", scatter_dimension=0, tiled=True)
+    neigh_back = lax.psum_scatter(
+        back.reshape(-1, rows), "col", scatter_dimension=0, axis_index_groups=ring, tiled=True
+    )
     hidden_in = row_phase(turn(hidden_mid, col_devices, row_devices))
     pieces = split_sum(groups, [grad_kept, swap(grad_sent)], ways)
     pieces = split_sum(others, [pieces[0]] + [across(pieces[s], s) for s in range(1, ways)], lines)

time: 281 us -> 280 us (level)
  local copies, waits for them, and re-layouts: 28.6 us -> 7.65 us
  Pallas kernels: 32.2 us -> 52.3 us
    unnamed x63 -> x41, local copies, waits for them, and re-layouts: 24.9 us -> 4.07 us
    pallas_call x1, Pallas kernels: 6.75 us -> 16.6 us  [on_device(): call(functools.partial(spmm_back_kernel, ways, pieces), grid_spec=pltpu.P...]
    all_to_all x2, waiting for transfers between devices: 5.76 us -> 0.01 us  [col_phase(): lax.all_to_all(there, 'col', split_axis=0, concat_axis=0, tiled=True)]
    pallas_call x1, Pallas kernels: 3.89 us -> 7.65 us  [on_device(): call(functools.partial(spmm_kernel, ways), grid_spec=pltpu.PrefetchScalar...]
  transfers between devices with their start and end apart: 29 -> 29, of which waited for: 25 -> 24; matrix products, arithmetic and copies ran while one was open for 1% -> 2% of each run, Pallas kernels for 8% -> 14%
where the time goes in v6:
time: 280 us
  waiting for transfers between devices  136 us (49%)
  Pallas kernels  52.3 us (19%)
  starting transfers between devices  48.7 us (17%)
  blocking collectives  19.5 us (7%)
  between operations  14.3 us (5%)
  local copies, waits for them, and re-layouts  7.65 us (3%)
    ppermute x14, waiting for transfers between devices, across(): return lax.ppermute(value, 'row', [(i, i ^ s) for i in range(ways)])  61.3 us
    all_to_all x2, waiting for transfers between devices, relay(): lax.all_to_all(there, everyone, split_axis=0, concat_axis=0, tiled=True)  28.7 us
    all_gather x1, waiting for transfers between devices, on_device(): lax.all_gather(x_node, 'col', axis_index_groups=ring, axis=0, tiled=True)  24.9 us
    all_to_all x1, blocking collectives, row_phase(): lax.all_to_all(there, 'row', split_axis=0, concat_axis=0, tiled=True)  19.5 us
    pallas_call x1, Pallas kernels, on_device(): call(functools.partial(spmm_back_kernel, ways, pieces), grid_spec=pltpu.P...  16.6 us
    ppermute x14, starting transfers between devices, across(): return lax.ppermute(value, 'row', [(i, i ^ s) for i in range(ways)])  15.2 us
    all_to_all x2, starting transfers between devices, relay(): lax.all_to_all(there, everyone, split_axis=0, concat_axis=0, tiled=True)  12.4 us
    reduce_scatter x1, waiting for transfers between devices, on_device(): lax.psum_scatter(back.reshape(-1, rows), 'col', scatter_dimension=0, axis...  10.2 us
  transfers between devices with their start and end apart: 29, of which 24 were waited for; matrix products, arithmetic and copies ran while one was open for 2% of the time, Pallas kernels for 14%

profile of v6, /device:TPU:0, one launch (start us, length us, event | category | flops | bytes accessed | tf_op | source)
XLA Modules:
  0.0 279.5 jit_solution(2438969268869548417)
XLA Ops:
  7.2 3.1 %pack_features.1 = bf16[1024,512]{1,0:T(8,128)(2,1)} custom-call(s32[1,512]{1,0:T(1,128)} %bitcast.49, bf16[512,512]{1,0:T(8,128)(2,1)} %value_ref.1), custom_call_target="tpu_custom_call" | custom-call | flops 536870912 | bytes 1572864 | tf_op jit(solution)/shard_map/pack_features/pallas_call | solution.py:339
  10.3 7.3 %all-to-all-start = ((bf16[32,32,512]{2,1,0:T(8,128)(2,1)}), bf16[32,32,512]{2,1,0:T(8,128)(2,1)S(1)}, u32[]{:S(2)}, u32[]{:S(2)}) async-start(bf16[32,32,512]{2,1,0:T(8,128)(2,1)} %bitcast.48), calls=%async_computation | async-start | bytes 2097152 | tf_op jit(solution)/shard_map/all_to_all | solution.py:292
  17.8 3.7 %index_cotangent.1 = (bf16[1024,640]{1,0:T(8,128)(2,1)}, s32[512,128]{1,0:T(8,128)}, s32[8,512]{1,0:T(8,128)}, s32[512,128]{1,0:T(8,128)}, s32[8,512]{1,0:T(8,128)}, /*index=5*/s32[512,128]{1,0:T(8,128)}) custom-call(s32[1,512]{1,0:T(1,128)} %bitcast.50, s32[1,512]{1,0:T(1,128)} %bitcast.51, s32[1,512]{1,0:T(1,128)} %bitcast.52, bf16[512,512]{1,0:T(8,128)(2,1)} %cot_ref.1), custom_call_target="tpu_custom_call" | custom-call | flops 536870912 | bytes 1572864 | tf_op jit(solution)/shard_map/index_cotangent/pallas_call | solution.py:349
  21.6 0.6 iota_xor_fusion
  22.7 22.5 %all-to-all-done = bf16[32,32,512]{2,1,0:T(8,128)(2,1)S(1)} async-done(((bf16[32,32,512]{2,1,0:T(8,128)(2,1)}), bf16[32,32,512]{2,1,0:T(8,128)(2,1)S(1)}, u32[]{:S(2)}, u32[]{:S(2)}) %all-to-all-start) | async-done | bytes 1048608 | tf_op jit(solution)/shard_map/all_to_all | solution.py:292
  45.2 0.9 copy-done.8
  46.1 1.5 unpack_features.1.refs_3_.x_ref
  47.7 19.5 %all_to_all.30 = bf16[4,256,640]{2,1,0:T(8,128)(2,1)S(1)} all-to-all(bf16[4,256,640]{2,1,0:T(8,128)(2,1)S(1)} %bitcast.46), channel_id=1, replica_groups=mesh['row'=4,'col'=8] {'row'}, dimensions={0} | all-to-all | bytes 2621440 | tf_op jit(solution)/shard_map/all_to_all | solution.py:296
  67.2 1.3 copy.18
  68.5 24.9 %all-gather.2.cloned.1.call-done.x_ref = bf16[4096,512]{1,0:T(8,128)(2,1)} async-done(((bf16[512,512]{1,0:T(8,128)(2,1)}), bf16[4096,512]{1,0:T(8,128)(2,1)}) %all-gather.2.cloned.1.call-update) | async-done | bytes 4194320 | tf_op jit(solution)/shard_map/all_gather | solution.py:377
  93.4 3.7 %all-to-all-start.2 = ((bf16[8,128,640]{2,1,0:T(8,128)(2,1)}), bf16[8,128,640]{2,1,0:T(8,128)(2,1)S(1)}, u32[]{:S(2)}, u32[]{:S(2)}) async-start(bf16[8,128,640]{2,1,0:T(8,128)(2,1)} %bitcast.11), calls=%async_computation.2 | async-start | bytes 2621440 | tf_op jit(solution)/shard_map/all_to_all | solution.py:300
  97.1 7.7 %spmm.1 = (bf16[512,512]{1,0:T(8,128)(2,1)}, bf16[512,512]{1,0:T(8,128)(2,1)}, bf16[512,512]{1,0:T(8,128)(2,1)}, bf16[512,512]{1,0:T(8,128)(2,1)}) custom-call(s32[128]{0:T(128)} %fusion.cols_ref, s32[4]{0:T(128)} %get-tuple-element.58.group_ref.index_ref, bf16[4096,512]{1,0:T(8,128)(2,1)} %all-gather.2.cloned.1.call-done.x_ref, ...), custom_call_target="tpu_custom_call" | custom-call | flops 2147483648 | bytes 10485760 | tf_op jit(solution)/shard_map/spmm/pallas_call | solution.py:388
  104.8 1.2 fusion.2
  105.9 1.5 collective-permute-start.1
  107.4 1.5 collective-permute-start
  108.9 5.8 %collective-permute-done.1.bottom_ref = bf16[256,512]{1,0:T(8,128)(2,1)S(1)} collective-permute-done((bf16[256,512]{1,0:T(8,128)(2,1)S(1)}, bf16[256,512]{1,0:T(8,128)(2,1)S(1)}, u32[]{:S(2)}, u32[]{:S(2)}) %collective-permute-start.1) | collective-permute-done | bytes 262176 | tf_op jit(solution)/shard_map/ppermute | solution.py:306
  114.7 1.2 collective-permute-done.top_ref
  116.0 1.5 collective-permute-start.2
  118.1 11.2 %collective-permute-done.2.refs_1_ = bf16[512,512]{1,0:T(8,128)(2,1)S(1)} collective-permute-done((bf16[512,512]{1,0:T(8,128)(2,1)S(1)}, bf16[512,512]{1,0:T(8,128)(2,1)S(1)}, u32[]{:S(2)}, u32[]{:S(2)}) %collective-permute-start.2) | collective-permute-done | bytes 524320 | tf_op jit(solution)/shard_map/ppermute | solution.py:306
  129.3 1.2 collective-permute-done.3.refs_2_
  130.5 0.8 copy-done.19
  131.8 6.8 %layer.1 = (bf16[1024,512]{1,0:T(8,128)(2,1)}, bf16[512,512]{1,0:T(8,128)(2,1)}, bf16[512,512]{1,0:T(8,128)(2,1)}, bf16[512,512]{1,0:T(8,128)(2,1)}) custom-call(bf16[512,512]{1,0:T(8,128)(2,1)} %get-tuple-element.62.refs_0_, bf16[512,512]{1,0:T(8,128)(2,1)} %copy-done.18, bf16[512,512]{1,0:T(8,128)(2,1)} %copy-done.19, ...), custom_call_target="tpu_custom_call" | custom-call | flops 1342177280 | bytes 6815744 | tf_op jit(solution)/shard_map/layer/pallas_call | solution.py:416
  138.6 4.4 %all-to-all-start.3 = ((bf16[8,128,512]{2,1,0:T(8,128)(2,1)}), bf16[8,128,512]{2,1,0:T(8,128)(2,1)S(1)}, u32[]{:S(2)}, u32[]{:S(2)}) async-start(bf16[8,128,512]{2,1,0:T(8,128)(2,1)} %bitcast.47), calls=%async_computation.3 | async-start | bytes 2097152 | tf_op jit(solution)/shard_map/all_to_all | solution.py:300
  143.1 0.7 collective-permute-start.5
  143.8 0.6 collective-permute-start.4
  144.3 13.1 %collective-permute-done.5.refs_2_ = bf16[512,512]{1,0:T(8,128)(2,1)S(1)} collective-permute-done((bf16[512,512]{1,0:T(8,128)(2,1)S(1)}, bf16[512,512]{1,0:T(8,128)(2,1)S(1)}, u32[]{:S(2)}, u32[]{:S(2)}) %collective-permute-start.5) | collective-permute-done | bytes 524320 | tf_op jit(solution)/shard_map/ppermute | solution.py:306
  157.5 0.6 collective-permute-start.6
  158.1 1.2 collective-permute-start.7
  159.3 3.8 %terms.1 = (bf16[512,512]{1,0:T(8,128)(2,1)}, bf16[512,512]{1,0:T(8,128)(2,1)}, f32[512,512]{1,0:T(8,128)}) custom-call(s32[1]{0:T(128)} %bitcast.5.core_ref, bf16[512,512]{1,0:T(8,128)(2,1)} %unpack_features.1.refs_3_.x_ref, bf16[512,512]{1,0:T(8,128)(2,1)} %get-tuple-element.73.agg_ref, bf16[512,512]{1,0:T(8,128)(2,1)} %get-tuple-element.74.slopes_ref, ...), custom_call_target="tpu_custom_call" | custom-call | flops 805306368 | bytes 4718592 | tf_op jit(solution)/shard_map/terms/pallas_call | solution.py:433
  163.1 2.3 collective-permute-done.6.refs_3_
  166.5 16.6 %spmm_back.1 = bf16[8,512,512]{2,1,0:T(8,128)(2,1)} custom-call(s32[128]{0:T(128)} %fusion.cols_ref, s32[4]{0:T(128)} %get-tuple-element.58.group_ref.index_ref, bf16[512,512]{1,0:T(8,128)(2,1)} %get-tuple-element.78.refs_0_, bf16[512,512]{1,0:T(8,128)(2,1)} %copy-done.12, bf16[512,512]{1,0:T(8,128)(2,1)} %copy-done.11, bf16[256,512]{1,0:T(8,128)(2,1)} %copy-done.14, ...), custom_call_target="tpu_custom_call" | custom-call | flops 2147483648 | bytes 10485760 | tf_op jit(solution)/shard_map/spmm_back/pallas_call | solution.py:443
  183.1 1.0 copy.19
  184.1 3.8 %all-to-all-start.4 = ((bf16[4,256,512]{2,1,0:T(8,128)(2,1)}), bf16[4,256,512]{2,1,0:T(8,128)(2,1)S(1)}, u32[]{:S(2)}, u32[]{:S(2)}) async-start(bf16[4,256,512]{2,1,0:T(8,128)(2,1)} %bitcast.17), calls=%async_computation.4 | async-start | bytes 2097152 | tf_op jit(solution)/shard_map/all_to_all | solution.py:296
  188.1 2.1 collective-permute-done.8.refs_1_
  190.2 0.8 split_sum.3
  191.0 1.8 collective-permute-start.9
  192.8 1.5 collective-permute-start.10
  194.5 10.1 %collective-permute-done.9.refs_1_ = bf16[128,512]{1,0:T(8,128)(2,1)S(1)} collective-permute-done((bf16[128,512]{1,0:T(8,128)(2,1)S(1)}, bf16[128,512]{1,0:T(8,128)(2,1)S(1)}, u32[]{:S(2)}, u32[]{:S(2)}) %collective-permute-start.9) | collective-permute-done | bytes 131104 | tf_op jit(solution)/shard_map/ppermute | solution.py:306
  204.6 2.3 collective-permute-done.11.refs_3_
  206.9 0.6 split_sum.4
  207.5 1.0 collective-permute-start.12
  208.5 2.4 collective-permute-start.13
  210.9 1.1 collective-permute-start.14
  212.0 0.6 collective-permute-done.12.refs_1_
  212.6 1.9 collective-permute-done.13.refs_2_
  214.5 3.1 %collective-permute-done.14.refs_3_ = bf16[32,512]{1,0:T(8,128)(2,1)S(1)} collective-permute-done((bf16[32,512]{1,0:T(8,128)(2,1)S(1)}, bf16[32,512]{1,0:T(8,128)(2,1)S(1)}, u32[]{:S(2)}, u32[]{:S(2)}) %collective-permute-start.14) | collective-permute-done | bytes 32800 | tf_op jit(solution)/shard_map/ppermute | solution.py:309
  217.6 1.0 collective-permute-start.17
  218.6 3.4 %collective-permute-start.15 = (bf16[32,512]{1,0:T(8,128)(2,1)S(1)}, bf16[32,512]{1,0:T(8,128)(2,1)S(1)}, u32[]{:S(2)}, u32[]{:S(2)}) collective-permute-start(bf16[32,512]{1,0:T(8,128)(2,1)S(1)} %split_sum.5.refs_0_), channel_id=1, source_target_pairs={{0,2},{1,3},{2,0},{3,1},{4,6},{5,7},{6,4},{7,5},{8,10},{9,11},{10,... | collective-permute-start | bytes 98312 | tf_op jit(solution)/shard_map/ppermute | solution.py:309
  222.1 2.2 collective-permute-done.17.refs_3_
  224.2 0.6 collective-permute-done.16.refs_2_
  225.5 10.2 %reduce-scatter.2.cloned.1.call-done.neigh_ref = bf16[512,512]{1,0:T(8,128)(2,1)} async-done(((bf16[4096,512]{1,0:T(8,128)(2,1)}), bf16[512,512]{1,0:T(8,128)(2,1)}) %reduce-scatter.2.cloned.1.call-update) | async-done | bytes 524304 | tf_op jit(solution)/shard_map/reduce_scatter | solution.py:469
  235.7 1.0 copy-done.1
  236.7 1.8 join_pack.1
  238.5 5.1 %all-to-all-start.5 = ((bf16[32,32,512]{2,1,0:T(8,128)(2,1)}), bf16[32,32,512]{2,1,0:T(8,128)(2,1)S(1)}, u32[]{:S(2)}, u32[]{:S(2)}) async-start(bf16[32,32,512]{2,1,0:T(8,128)(2,1)} %bitcast.21), calls=%async_computation.6 | async-start | bytes 2097152 | tf_op jit(solution)/shard_map/all_to_all | solution.py:292
  243.6 2.7 collective-permute-start.20
  246.3 0.6 collective-permute-start.19
  247.1 11.5 %collective-permute-done.20.refs_3_ = bf16[128,512]{1,0:T(8,128)(2,1)S(1)} collective-permute-done((bf16[128,512]{1,0:T(8,128)(2,1)S(1)}, bf16[128,512]{1,0:T(8,128)(2,1)S(1)}, u32[]{:S(2)}, u32[]{:S(2)}) %collective-permute-start.20) | collective-permute-done | bytes 131104 | tf_op jit(solution)/shard_map/ppermute | solution.py:306
  258.6 1.6 collective-permute-done.19.refs_2_
  260.2 0.7 collective-permute-done.18.refs_1_
  260.9 0.6 in_place.3
  261.6 1.6 unpack_owner.2
  263.5 1.5 final.1
  265.0 6.2 %all-to-all-done.5 = bf16[32,32,512]{2,1,0:T(8,128)(2,1)S(1)} async-done(((bf16[32,32,512]{2,1,0:T(8,128)(2,1)}), bf16[32,32,512]{2,1,0:T(8,128)(2,1)S(1)}, u32[]{:S(2)}, u32[]{:S(2)}) %all-to-all-start.5) | async-done | bytes 1048608 | tf_op jit(solution)/shard_map/all_to_all | solution.py:292
  271.2 1.5 unpack_owner.3
  (63 shorter events, 4.9 us)
Async XLA Ops:
  10.3 7.4 %copy-start.16 = (s32[1,1,16,8]{2,3,1,0:T(8,128)S(1)}, s32[1,1,16,8]{2,3,1,0:T(8,128)}, u32[]{:S(2)}) copy-start(s32[1,1,16,8]{2,3,1,0:T(8,128)} %param.10) | copy-start | bytes 1540
  10.3 34.9 %all-to-all-start = ((bf16[32,32,512]{2,1,0:T(8,128)(2,1)}), bf16[32,32,512]{2,1,0:T(8,128)(2,1)S(1)}, u32[]{:S(2)}, u32[]{:S(2)}) async-start(bf16[32,32,512]{2,1,0:T(8,128)(2,1)} %bitcast.48), calls=%async_computation | async-start | bytes 2097152 | tf_op jit(solution)/shard_map/all_to_all | solution.py:292
  17.6 75.8 %all-gather.2.cloned.1.call-start = ((), (), s32[]{:S(2)}) async-start(), calls=%async_computation.7 | async-start | bytes 4718592 | tf_op jit(solution)/shard_map/all_gather | solution.py:377
  45.2 1.0 copy-start.8
  46.1 1.6 copy-start.10
  93.4 37.2 %all-to-all-start.2 = ((bf16[8,128,640]{2,1,0:T(8,128)(2,1)}), bf16[8,128,640]{2,1,0:T(8,128)(2,1)S(1)}, u32[]{:S(2)}, u32[]{:S(2)}) async-start(bf16[8,128,640]{2,1,0:T(8,128)(2,1)} %bitcast.11), calls=%async_computation.2 | async-start | bytes 2621440 | tf_op jit(solution)/shard_map/all_to_all | solution.py:300
  104.7 11.1 %copy-start.2 = (bf16[512,512]{1,0:T(8,128)(2,1)S(1)}, bf16[512,512]{1,0:T(8,128)(2,1)}, u32[]{:S(2)}) copy-start(bf16[512,512]{1,0:T(8,128)(2,1)} %get-tuple-element.63.left_ref) | copy-start | bytes 1572868
  104.7 11.1 %copy-start.3 = (bf16[512,512]{1,0:T(8,128)(2,1)S(1)}, bf16[512,512]{1,0:T(8,128)(2,1)}, u32[]{:S(2)}) copy-start(bf16[512,512]{1,0:T(8,128)(2,1)} %get-tuple-element.64.right_ref) | copy-start | bytes 1572868
  105.9 8.8 %collective-permute-start.1 = (bf16[256,512]{1,0:T(8,128)(2,1)S(1)}, bf16[256,512]{1,0:T(8,128)(2,1)S(1)}, u32[]{:S(2)}, u32[]{:S(2)}) collective-permute-start(bf16[256,512]{1,0:T(8,128)(2,1)S(1)} %get-tuple-element.104), channel_id=1, source_target_pairs={{0,16},{8,24},{16,0},{24,8},{1,17},{9,25},{17,1},{25,9},{2,18},{10... | collective-permute-start | bytes 786440 | tf_op jit(solution)/shard_map/ppermute | solution.py:306
  107.4 8.4 %collective-permute-start = (bf16[256,512]{1,0:T(8,128)(2,1)S(1)}, bf16[256,512]{1,0:T(8,128)(2,1)S(1)}, u32[]{:S(2)}, u32[]{:S(2)}) collective-permute-start(bf16[256,512]{1,0:T(8,128)(2,1)S(1)} %get-tuple-element.105), channel_id=1, source_target_pairs={{0,8},{8,0},{16,24},{24,16},{1,9},{9,1},{17,25},{25,17},{2,10},{10... | collective-permute-start | bytes 786440 | tf_op jit(solution)/shard_map/ppermute | solution.py:306
  116.0 13.3 %collective-permute-start.2 = (bf16[512,512]{1,0:T(8,128)(2,1)S(1)}, bf16[512,512]{1,0:T(8,128)(2,1)S(1)}, u32[]{:S(2)}, u32[]{:S(2)}) collective-permute-start(bf16[512,512]{1,0:T(8,128)(2,1)S(1)} %get-tuple-element.66), channel_id=1, source_target_pairs={{0,8},{8,0},{16,24},{24,16},{1,9},{9,1},{17,25},{25,17},{2,10},{10... | collective-permute-start | bytes 1572872 | tf_op jit(solution)/shard_map/ppermute | solution.py:306
  117.6 13.0 %collective-permute-start.3 = (bf16[512,512]{1,0:T(8,128)(2,1)S(1)}, bf16[512,512]{1,0:T(8,128)(2,1)S(1)}, u32[]{:S(2)}, u32[]{:S(2)}) collective-permute-start(bf16[512,512]{1,0:T(8,128)(2,1)S(1)} %get-tuple-element.67), channel_id=1, source_target_pairs={{0,16},{8,24},{16,0},{24,8},{1,17},{9,25},{17,1},{25,9},{2,18},{10... | collective-permute-start | bytes 1572872 | tf_op jit(solution)/shard_map/ppermute | solution.py:306
  129.3 1.2 copy-start.18
  130.5 0.8 copy-start.19
  130.5 1.3 copy-start.9
  138.6 4.5 %copy-start.13 = (bf16[512,512]{1,0:T(8,128)(2,1)S(1)}, bf16[512,512]{1,0:T(8,128)(2,1)}, u32[]{:S(2)}) copy-start(bf16[512,512]{1,0:T(8,128)(2,1)} %get-tuple-element.78.refs_0_) | copy-start | bytes 1572868
  138.6 44.5 %all-to-all-start.3 = ((bf16[8,128,512]{2,1,0:T(8,128)(2,1)}), bf16[8,128,512]{2,1,0:T(8,128)(2,1)S(1)}, u32[]{:S(2)}, u32[]{:S(2)}) async-start(bf16[8,128,512]{2,1,0:T(8,128)(2,1)} %bitcast.47), calls=%async_computation.3 | async-start | bytes 2097152 | tf_op jit(solution)/shard_map/all_to_all | solution.py:300
  143.0 92.6 %reduce-scatter.2.cloned.1.call-start = ((), (), s32[]{:S(2)}) async-start(), calls=%async_computation.8 | async-start | bytes 4718592 | tf_op jit(solution)/shard_map/reduce_scatter | solution.py:469
  143.1 14.4 %collective-permute-start.5 = (bf16[512,512]{1,0:T(8,128)(2,1)S(1)}, bf16[512,512]{1,0:T(8,128)(2,1)S(1)}, u32[]{:S(2)}, u32[]{:S(2)}) collective-permute-start(bf16[512,512]{1,0:T(8,128)(2,1)S(1)} %copy-done.13), channel_id=1, source_target_pairs={{0,16},{8,24},{16,0},{24,8},{1,17},{9,25},{17,1},{25,9},{2,18},{10... | collective-permute-start | bytes 1572872 | tf_op jit(solution)/shard_map/ppermute | solution.py:306
  143.8 14.3 %collective-permute-start.4 = (bf16[512,512]{1,0:T(8,128)(2,1)S(1)}, bf16[512,512]{1,0:T(8,128)(2,1)S(1)}, u32[]{:S(2)}, u32[]{:S(2)}) collective-permute-start(bf16[512,512]{1,0:T(8,128)(2,1)S(1)} %copy-done.13), channel_id=1, source_target_pairs={{0,8},{8,0},{16,24},{24,16},{1,9},{9,1},{17,25},{25,17},{2,10},{10... | collective-permute-start | bytes 1572872 | tf_op jit(solution)/shard_map/ppermute | solution.py:306
  157.4 5.7 %copy-start.11 = (bf16[512,512]{1,0:T(8,128)(2,1)}, bf16[512,512]{1,0:T(8,128)(2,1)S(1)}, u32[]{:S(2)}) copy-start(bf16[512,512]{1,0:T(8,128)(2,1)S(1)} %collective-permute-done.5.refs_2_) | copy-start | bytes 1572868
  157.5 7.9 %collective-permute-start.6 = (bf16[256,512]{1,0:T(8,128)(2,1)S(1)}, bf16[256,512]{1,0:T(8,128)(2,1)S(1)}, u32[]{:S(2)}, u32[]{:S(2)}) collective-permute-start(bf16[256,512]{1,0:T(8,128)(2,1)S(1)} %slice.16), channel_id=1, source_target_pairs={{0,8},{8,0},{16,24},{24,16},{1,9},{9,1},{17,25},{25,17},{2,10},{10... | collective-permute-start | bytes 786440 | tf_op jit(solution)/shard_map/ppermute | solution.py:306
  158.1 5.0 %copy-start.12 = (bf16[512,512]{1,0:T(8,128)(2,1)}, bf16[512,512]{1,0:T(8,128)(2,1)S(1)}, u32[]{:S(2)}) copy-start(bf16[512,512]{1,0:T(8,128)(2,1)S(1)} %collective-permute-done.4.refs_1_) | copy-start | bytes 1572868
  158.1 7.7 %collective-permute-start.7 = (bf16[256,512]{1,0:T(8,128)(2,1)S(1)}, bf16[256,512]{1,0:T(8,128)(2,1)S(1)}, u32[]{:S(2)}, u32[]{:S(2)}) collective-permute-start(bf16[256,512]{1,0:T(8,128)(2,1)S(1)} %slice.17), channel_id=1, source_target_pairs={{0,16},{8,24},{16,0},{24,8},{1,17},{9,25},{17,1},{25,9},{2,18},{10... | collective-permute-start | bytes 786440 | tf_op jit(solution)/shard_map/ppermute | solution.py:306
  165.4 0.7 copy-start.14
  165.8 0.7 copy-start.15
  184.1 3.8 %copy-start.17 = (bf16[512,512]{1,0:T(8,128)(2,1)S(1)}, bf16[512,512]{1,0:T(8,128)(2,1)}, u32[]{:S(2)}) copy-start(bf16[512,512]{1,0:T(8,128)(2,1)} %get-tuple-element.89) | copy-start | bytes 1572868
  184.1 6.1 %copy-start.4 = (bf16[512,512]{1,0:T(8,128)(2,1)S(1)}, bf16[512,512]{1,0:T(8,128)(2,1)}, u32[]{:S(2)}) copy-start(bf16[512,512]{1,0:T(8,128)(2,1)} %get-tuple-element.88.refs_0_) | copy-start | bytes 1572868
  184.1 6.1 %copy-start.6 = (s32[4]{0:T(128)S(1)}, s32[4]{0:T(128)}, u32[]{:S(2)}) copy-start(s32[4]{0:T(128)} %get-tuple-element.58.group_ref.index_ref) | copy-start | bytes 52
  184.1 54.4 %all-to-all-start.4 = ((bf16[4,256,512]{2,1,0:T(8,128)(2,1)}), bf16[4,256,512]{2,1,0:T(8,128)(2,1)S(1)}, u32[]{:S(2)}, u32[]{:S(2)}) async-start(bf16[4,256,512]{2,1,0:T(8,128)(2,1)} %bitcast.17), calls=%async_computation.4 | async-start | bytes 2097152 | tf_op jit(solution)/shard_map/all_to_all | solution.py:296
  188.0 47.7 %copy-start = (f32[512,512]{1,0:T(8,128)S(1)}, f32[512,512]{1,0:T(8,128)}, u32[]{:S(2)}) copy-start(f32[512,512]{1,0:T(8,128)} %get-tuple-element.98.own_ref) | copy-start | bytes 3145732
  188.0 47.7 %copy-start.5 = (s32[8,512]{1,0:T(8,128)S(1)}, s32[8,512]{1,0:T(8,128)}, u32[]{:S(2)}) copy-start(s32[8,512]{1,0:T(8,128)} %get-tuple-element.100.row_ref) | copy-start | bytes 49156
  188.0 2.2 collective-permute-start.8
  191.0 13.6 %collective-permute-start.9 = (bf16[128,512]{1,0:T(8,128)(2,1)S(1)}, bf16[128,512]{1,0:T(8,128)(2,1)S(1)}, u32[]{:S(2)}, u32[]{:S(2)}) collective-permute-start(bf16[128,512]{1,0:T(8,128)(2,1)S(1)} %get-tuple-element.91), channel_id=1, source_target_pairs={{0,8},{8,0},{16,24},{24,16},{1,9},{9,1},{17,25},{25,17},{2,10},{10... | collective-permute-start | bytes 393224 | tf_op jit(solution)/shard_map/ppermute | solution.py:306
  192.8 11.8 %collective-permute-start.10 = (bf16[128,512]{1,0:T(8,128)(2,1)S(1)}, bf16[128,512]{1,0:T(8,128)(2,1)S(1)}, u32[]{:S(2)}, u32[]{:S(2)}) collective-permute-start(bf16[128,512]{1,0:T(8,128)(2,1)S(1)} %get-tuple-element.92), channel_id=1, source_target_pairs={{0,16},{8,24},{16,0},{24,8},{1,17},{9,25},{17,1},{25,9},{2,18},{10... | collective-permute-start | bytes 393224 | tf_op jit(solution)/shard_map/ppermute | solution.py:306
  194.3 12.6 %collective-permute-start.11 = (bf16[128,512]{1,0:T(8,128)(2,1)S(1)}, bf16[128,512]{1,0:T(8,128)(2,1)S(1)}, u32[]{:S(2)}, u32[]{:S(2)}) collective-permute-start(bf16[128,512]{1,0:T(8,128)(2,1)S(1)} %get-tuple-element.93), channel_id=1, source_target_pairs={{0,24},{8,16},{16,8},{24,0},{1,25},{9,17},{17,9},{25,1},{2,26},{10... | collective-permute-start | bytes 393224 | tf_op jit(solution)/shard_map/ppermute | solution.py:306
  207.5 5.1 %collective-permute-start.12 = (bf16[32,512]{1,0:T(8,128)(2,1)S(1)}, bf16[32,512]{1,0:T(8,128)(2,1)S(1)}, u32[]{:S(2)}, u32[]{:S(2)}) collective-permute-start(bf16[32,512]{1,0:T(8,128)(2,1)S(1)} %get-tuple-element.95), channel_id=1, source_target_pairs={{0,2},{1,3},{2,0},{3,1},{4,6},{5,7},{6,4},{7,5},{8,10},{9,11},{10,... | collective-permute-start | bytes 98312 | tf_op jit(solution)/shard_map/ppermute | solution.py:309
  208.5 6.0 %collective-permute-start.13 = (bf16[32,512]{1,0:T(8,128)(2,1)S(1)}, bf16[32,512]{1,0:T(8,128)(2,1)S(1)}, u32[]{:S(2)}, u32[]{:S(2)}) collective-permute-start(bf16[32,512]{1,0:T(8,128)(2,1)S(1)} %get-tuple-element.96), channel_id=1, source_target_pairs={{0,4},{1,5},{2,6},{3,7},{4,0},{5,1},{6,2},{7,3},{8,12},{9,13},{10,... | collective-permute-start | bytes 98312 | tf_op jit(solution)/shard_map/ppermute | solution.py:309
  210.9 6.7 %collective-permute-start.14 = (bf16[32,512]{1,0:T(8,128)(2,1)S(1)}, bf16[32,512]{1,0:T(8,128)(2,1)S(1)}, u32[]{:S(2)}, u32[]{:S(2)}) collective-permute-start(bf16[32,512]{1,0:T(8,128)(2,1)S(1)} %get-tuple-element.97), channel_id=1, source_target_pairs={{0,6},{1,7},{2,4},{3,5},{4,2},{5,3},{6,0},{7,1},{8,14},{9,15},{10,... | collective-permute-start | bytes 98312 | tf_op jit(solution)/shard_map/ppermute | solution.py:309
  217.6 6.6 %collective-permute-start.17 = (bf16[32,512]{1,0:T(8,128)(2,1)S(1)}, bf16[32,512]{1,0:T(8,128)(2,1)S(1)}, u32[]{:S(2)}, u32[]{:S(2)}) collective-permute-start(bf16[32,512]{1,0:T(8,128)(2,1)S(1)} %split_sum.5.refs_0_), channel_id=1, source_target_pairs={{0,6},{1,7},{2,4},{3,5},{4,2},{5,3},{6,0},{7,1},{8,14},{9,15},{10,... | collective-permute-start | bytes 98312 | tf_op jit(solution)/shard_map/ppermute | solution.py:309
  218.6 6.2 %collective-permute-start.16 = (bf16[32,512]{1,0:T(8,128)(2,1)S(1)}, bf16[32,512]{1,0:T(8,128)(2,1)S(1)}, u32[]{:S(2)}, u32[]{:S(2)}) collective-permute-start(bf16[32,512]{1,0:T(8,128)(2,1)S(1)} %split_sum.5.refs_0_), channel_id=1, source_target_pairs={{0,4},{1,5},{2,6},{3,7},{4,0},{5,1},{6,2},{7,3},{8,12},{9,13},{10,... | collective-permute-start | bytes 98312 | tf_op jit(solution)/shard_map/ppermute | solution.py:309
  218.6 6.3 %collective-permute-start.15 = (bf16[32,512]{1,0:T(8,128)(2,1)S(1)}, bf16[32,512]{1,0:T(8,128)(2,1)S(1)}, u32[]{:S(2)}, u32[]{:S(2)}) collective-permute-start(bf16[32,512]{1,0:T(8,128)(2,1)S(1)} %split_sum.5.refs_0_), channel_id=1, source_target_pairs={{0,2},{1,3},{2,0},{3,1},{4,6},{5,7},{6,4},{7,5},{8,10},{9,11},{10,... | collective-permute-start | bytes 98312 | tf_op jit(solution)/shard_map/ppermute | solution.py:309
  235.7 1.0 copy-start.1
  238.5 23.1 %copy-start.7 = (s32[512,128]{1,0:T(8,128)S(1)}, s32[512,128]{1,0:T(8,128)}, u32[]{:S(2)}) copy-start(s32[512,128]{1,0:T(8,128)} %get-tuple-element.54.col_ref) | copy-start | bytes 786436
  238.5 32.7 %all-to-all-start.5 = ((bf16[32,32,512]{2,1,0:T(8,128)(2,1)}), bf16[32,32,512]{2,1,0:T(8,128)(2,1)S(1)}, u32[]{:S(2)}, u32[]{:S(2)}) async-start(bf16[32,32,512]{2,1,0:T(8,128)(2,1)} %bitcast.21), calls=%async_computation.6 | async-start | bytes 2097152 | tf_op jit(solution)/shard_map/all_to_all | solution.py:292
  243.6 15.0 %collective-permute-start.20 = (bf16[128,512]{1,0:T(8,128)(2,1)S(1)}, bf16[128,512]{1,0:T(8,128)(2,1)S(1)}, u32[]{:S(2)}, u32[]{:S(2)}) collective-permute-start(bf16[128,512]{1,0:T(8,128)(2,1)S(1)} %bitcast.33), channel_id=1, source_target_pairs={{0,24},{8,16},{16,8},{24,0},{1,25},{9,17},{17,9},{25,1},{2,26},{10... | collective-permute-start | bytes 393224 | tf_op jit(solution)/shard_map/ppermute | solution.py:306
  246.3 13.9 %collective-permute-start.19 = (bf16[128,512]{1,0:T(8,128)(2,1)S(1)}, bf16[128,512]{1,0:T(8,128)(2,1)S(1)}, u32[]{:S(2)}, u32[]{:S(2)}) collective-permute-start(bf16[128,512]{1,0:T(8,128)(2,1)S(1)} %bitcast.34), channel_id=1, source_target_pairs={{0,16},{8,24},{16,0},{24,8},{1,17},{9,25},{17,1},{25,9},{2,18},{10... | collective-permute-start | bytes 393224 | tf_op jit(solution)/shard_map/ppermute | solution.py:306
  246.9 14.1 %collective-permute-start.18 = (bf16[128,512]{1,0:T(8,128)(2,1)S(1)}, bf16[128,512]{1,0:T(8,128)(2,1)S(1)}, u32[]{:S(2)}, u32[]{:S(2)}) collective-permute-start(bf16[128,512]{1,0:T(8,128)(2,1)S(1)} %bitcast.35), channel_id=1, source_target_pairs={{0,8},{8,0},{16,24},{24,16},{1,9},{9,1},{17,25},{25,17},{2,10},{10... | collective-permute-start | bytes 393224 | tf_op jit(solution)/shard_map/ppermute | solution.py:306
  261.5 2.0 collective-permute-start.21
Sparse Core Ops, SparseCore 0:
  47.8 45.4 all-gather.1
  183.2 52.4 reduce-scatter.1

commit v7 on v4

--- a/solution.py
+++ b/solution.py
@@ -12,6 +12,7 @@
 F32 = jnp.float32
 VMEM = pl.BlockSpec(memory_space=pltpu.VMEM)
 MIB = 1024 * 1024
+LARGE = 56
 
 
 def params(mib=16):
@@ -94,43 +95,38 @@
     out_ref[...] = dot(entries_onehot(col_ref[...], value_ref.shape[0]), value_ref[...]).astype(BF)
 
 
-def spmm_kernel(ways, cols_ref, group_ref, x_hbm, *refs):
-    masks, outs = refs[:ways], refs[ways : 2 * ways]
-    x_ref, sems = refs[2 * ways :]
+def spmm_kernel(pieces, cols_ref, group_ref, x_ref, *refs):
+    ways = len(pieces)
+    masks, outs = refs[:ways], refs[ways:]
     q = pl.program_id(0)
     depth = pl.num_programs(0)
     _, breadth, tile, _ = masks[0].shape
-
-    @pl.when(q == 0)
-    def _():
-        count = sems.shape[0]
-        share = x_ref.shape[0] // count
-        copies = [
-            pltpu.make_async_copy(x_hbm.at[pl.ds(i * share, share)], x_ref.at[pl.ds(i * share, share)], sems.at[i])
-            for i in range(count)
-        ]
-        for copy in copies:
-            copy.start()
-        for copy in copies:
-            copy.wait()
-
+    at_piece = 0
     for s in range(ways):
         base = (group_ref[s] * depth + q) * breadth
         total = None
         for p in range(0, breadth, 2):
-            width = min(2, breadth - p)
-            left = jnp.concatenate([masks[s][0, p + w] for w in range(width)], axis=1)
+            span = range(p, min(p + 2, breadth))
+            left = jnp.concatenate([masks[s][0, k] for k in span], axis=1)
             right = jnp.concatenate(
-                [x_ref[pl.ds(pl.multiple_of(cols_ref[base + p + w] * tile, tile), tile), :] for w in range(width)], axis=0
+                [x_ref[pl.ds(pl.multiple_of(cols_ref[base + k] * tile, tile), tile), :] for k in span], axis=0
             )
             term = dot(left, right)
             total = term if total is None else total + term
-        outs[s][...] = total.astype(BF)
+        for p in range(pieces[s]):
+            out_ref = outs[at_piece + p]
+
+            @pl.when((q * pieces[s] >= p * depth) & (q * pieces[s] < (p + 1) * depth))
+            def _():
+                out_ref[...] = total.astype(BF)
+
+        at_piece += pieces[s]
 
 
 def spmm_back_kernel(ways, pieces, cols_ref, group_ref, *refs):
     given = sum(pieces)
-    spreads, masks, out_ref, total = refs[:given], refs[given : given + ways], refs[-2], refs[-1]
+    spreads, masks = refs[:given], refs[given : given + ways]
+    out_hbm, total, ready, sems = refs[given + ways :]
     q = pl.program_id(0)
     depth = pl.num_programs(0)
     _, breadth, tile, _ = masks[0].shape
@@ -152,7 +148,16 @@
 
     @pl.when(q == depth - 1)
     def _():
-        out_ref[...] = total[...].astype(BF)
+        count = sems.shape[0]
+        share = total.shape[0] // count
+        copies = []
+        for i in range(count):
+            at = pl.ds(i * share, share)
+            ready[at, :] = total[at, :].astype(BF)
+            copies.append(pltpu.make_async_copy(ready.at[at], out_hbm.at[at], sems.at[i]))
+            copies[-1].start()
+        for copy in copies:
+            copy.wait()
 
 
 def pass_on_kernel(left_ref, right_ref, top_ref, bottom_ref, left_out, right_out):
@@ -315,6 +320,7 @@
         in_specs=[VMEM] * 2,
         out_specs=VMEM,
         cost_estimate=cost(2 * slots * slab, 6 * slab),
+        mib=LARGE,
         name="pack_features",
     )(nodes, features)
     inbound = relay(packed)
@@ -331,8 +337,10 @@
         in_specs=[VMEM] * 4,
         out_specs=(VMEM,) * 6,
         cost_estimate=cost(2 * slots * slab, 6 * slab),
+        mib=LARGE,
         name="index_cotangent",
     )(nodes, owner_position.reshape(1, rows), degree.reshape(1, rows), cotangent)
+    ANY = pl.BlockSpec(memory_space=pl.ANY)
     x_node = call(
         unpack_kernel,
         out_shape=shape(rows, width),
@@ -349,33 +357,31 @@
     x_cols, cot_mid = lax.optimization_barrier((x_cols, cot_mid))
     cot_in = col_phase(cot_mid)
 
-    def mask_spec(s):
-        return pl.BlockSpec((1, breadth, tile, tile), lambda q, c, g, s=s: (g[s] * depth + q, 0, 0, 0))
-
+    spmm_flops = 2 * masks.size * width
     def piece_spec(p, count):
         share = depth // count
         return pl.BlockSpec((tile, width), lambda q, c, g: (jnp.clip(q - p * share, 0, share - 1), 0))
 
-    spmm_flops = 2 * masks.size * width
-    copies = 8
+    def mask_spec(s):
+        return pl.BlockSpec((1, breadth, tile, tile), lambda q, c, g: (g[s] * depth + q, 0, 0, 0))
+
+    pieces = (1, 1, 1, 2) if ways == 4 else (1,) * ways
+    half = rows // 2
     partials = call(
-        functools.partial(spmm_kernel, ways),
+        functools.partial(spmm_kernel, pieces),
         grid_spec=pltpu.PrefetchScalarGridSpec(
             num_scalar_prefetch=2,
             grid=(depth,),
-            in_specs=[pl.BlockSpec(memory_space=pl.ANY)] + [mask_spec(s) for s in range(ways)],
-            out_specs=[pl.BlockSpec((tile, width), lambda q, c, g: (q, 0)) for s in range(ways)],
-            scratch_shapes=[pltpu.VMEM(x_cols.shape, BF), pltpu.SemaphoreType.DMA((copies,))],
+            in_specs=[VMEM] + [mask_spec(s) for s in range(ways)],
+            out_specs=[piece_spec(p, count) for count in pieces for p in range(count)],
         ),
-        out_shape=[shape(rows, width) for s in range(ways)],
+        out_shape=[shape(rows // count, width) for count in pieces for _ in range(count)],
         cost_estimate=cost(spmm_flops, 2 * masks.size + 2 * x_cols.size + 2 * ways * slab),
-        mib=12 + 3 * x_cols.size / MIB,
+        mib=LARGE,
         name="spmm",
     )(cols, groups, x_cols, *([masks] * ways))
     if ways == 4:
-        half = rows // 2
-        top = across(partials[3][:half], 1)
-        bottom = across(partials[3][half:], 2)
+        top, bottom = across(partials[3], 1), across(partials[4], 2)
         left, right = call(
             pass_on_kernel,
             out_shape=(shape(rows, width),) * 2,
@@ -393,17 +399,14 @@
         in_specs=[VMEM] * (len(terms) + 6),
         out_specs=(VMEM,) * 4,
         cost_estimate=cost(10 * slab * width, 2 * slab * (ways + 9)),
-        mib=24,
+        mib=LARGE,
         name="layer",
     )(*terms, x_node, cot_in, turned_col, turned_row, self_weight, neigh_weight)
     if ways == 4:
         left, right = across(spread, 1), across(spread, 2)
-        left, right, hidden_packed = lax.optimization_barrier((left, right, hidden_packed))
         spreads = [spread, left, right, across(right[:half], 1), across(left[half:], 2)]
-        pieces = (1, 1, 1, 2)
     else:
         spreads = [spread] + [across(spread, s) for s in range(1, ways)]
-        pieces = (1,) * ways
     hidden_mid = col_phase(hidden_packed)
     grad_kept, grad_sent, own_back = call(
         terms_kernel,
@@ -411,6 +414,7 @@
         in_specs=[SMEM] + [VMEM] * 4,
         out_specs=(VMEM,) * 3,
         cost_estimate=cost(6 * slab * width, 2 * slab * 9),
+        mib=LARGE,
         name="terms",
     )(core, x_node, agg, slopes, self_weight)
     *spreads, own_back, grad_kept, grad_sent = lax.optimization_barrier((*spreads, own_back, grad_kept, grad_sent))
@@ -421,12 +425,16 @@
             grid=(depth,),
             in_specs=[piece_spec(p, count) for count in pieces for p in range(count)]
             + [mask_spec(s) for s in range(ways)],
-            out_specs=VMEM,
-            scratch_shapes=[pltpu.VMEM(x_cols.shape, F32)],
+            out_specs=ANY,
+            scratch_shapes=[
+                pltpu.VMEM(x_cols.shape, F32),
+                pltpu.VMEM(x_cols.shape, BF),
+                pltpu.SemaphoreType.DMA((col_devices,)),
+            ],
         ),
         out_shape=shape(*x_cols.shape),
         cost_estimate=cost(spmm_flops, 2 * masks.size + 2 * x_cols.size + 2 * ways * slab),
-        mib=12 + 7 * x_cols.size / MIB,
+        mib=LARGE,
         name="spmm_back",
     )(cols, groups, *spreads, *([masks] * ways))
     back, hidden_mid, grad_sent = lax.optimization_barrier((back, hidden_mid, grad_sent))

time: 281 us -> 277 us (0.986)
  local copies, waits for them, and re-layouts: 28.6 us -> 9.14 us
  Pallas kernels: 32.2 us -> 48.3 us
  waiting for transfers between devices: 138 us -> 134 us
    unnamed x63 -> x41, local copies, waits for them, and re-layouts: 24.9 us -> 6.13 us
    pallas_call x1, Pallas kernels: 3.89 us -> 9.8 us  [on_device(): call(functools.partial(spmm_kernel, pieces), grid_spec=pltpu.PrefetchScal...]
    all_to_all x2, waiting for transfers between devices: 5.76 us -> 0.01 us  [col_phase(): lax.all_to_all(there, 'col', split_axis=0, concat_axis=0, tiled=True)]
    reduce_scatter x1, waiting for transfers between devices: 7.44 us -> 11.3 us  [on_device(): neigh_back = lax.psum_scatter(back, 'col', scatter_dimension=0, tiled=True)]
    pallas_call x1, Pallas kernels: 6.75 us -> 10.5 us  [on_device(): call(functools.partial(spmm_back_kernel, ways, pieces), grid_spec=pltpu.P...]
  transfers between devices with their start and end apart: 29 -> 29, of which waited for: 25 -> 24; matrix products, arithmetic and copies ran while one was open for 1% -> 1% of each run, Pallas kernels for 8% -> 13%
where the time goes in v7:
time: 277 us; the launch traced here: 276 us
  waiting for transfers between devices  134 us (48%)
  starting transfers between devices  50 us (18%)
  Pallas kernels  48.3 us (17%)
  blocking collectives  19.5 us (7%)
  between operations  14.2 us (5%)
  local copies, waits for them, and re-layouts  9.14 us (3%)
    ppermute x14, waiting for transfers between devices, across(): return lax.ppermute(value, 'row', [(i, i ^ s) for i in range(ways)])  58.2 us
    all_to_all x2, waiting for transfers between devices, relay(): lax.all_to_all(there, everyone, split_axis=0, concat_axis=0, tiled=True)  28.7 us
    all_gather x1, waiting for transfers between devices, on_device(): x_cols = lax.all_gather(x_node, 'col', axis=0, tiled=True)  24.2 us
    all_to_all x1, blocking collectives, row_phase(): lax.all_to_all(there, 'row', split_axis=0, concat_axis=0, tiled=True)  19.5 us
    ppermute x14, starting transfers between devices, across(): return lax.ppermute(value, 'row', [(i, i ^ s) for i in range(ways)])  18.2 us
    reduce_scatter x1, waiting for transfers between devices, on_device(): neigh_back = lax.psum_scatter(back, 'col', scatter_dimension=0, tiled=True)  11.3 us
    all_to_all x2, starting transfers between devices, relay(): lax.all_to_all(there, everyone, split_axis=0, concat_axis=0, tiled=True)  10.7 us
    pallas_call x1, Pallas kernels, on_device(): call(functools.partial(spmm_back_kernel, ways, pieces), grid_spec=pltpu.P...  10.5 us
  transfers between devices with their start and end apart: 29, of which 24 were waited for; matrix products, arithmetic and copies ran while one was open for 1% of the time, Pallas kernels for 13%

profile of v7, /device:TPU:0, one launch (start us, length us, event | category | flops | bytes accessed | tf_op | source)
XLA Modules:
  0.0 275.7 jit_solution(4586532122173208950)
XLA Ops:
  7.2 3.1 %pack_features.1 = bf16[1024,512]{1,0:T(8,128)(2,1)} custom-call(s32[1,512]{1,0:T(1,128)} %bitcast.50, bf16[512,512]{1,0:T(8,128)(2,1)} %value_ref.1), custom_call_target="tpu_custom_call" | custom-call | flops 536870912 | bytes 1572864 | tf_op jit(solution)/shard_map/pack_features/pallas_call | solution.py:317
  10.3 7.3 %all-to-all-start = ((bf16[32,32,512]{2,1,0:T(8,128)(2,1)}), bf16[32,32,512]{2,1,0:T(8,128)(2,1)S(1)}, u32[]{:S(2)}, u32[]{:S(2)}) async-start(bf16[32,32,512]{2,1,0:T(8,128)(2,1)} %bitcast.49), calls=%async_computation | async-start | bytes 2097152 | tf_op jit(solution)/shard_map/all_to_all | solution.py:270
  17.7 0.7 reshape_squeeze.3.cols_ref
  18.4 3.7 %index_cotangent.1 = (bf16[1024,640]{1,0:T(8,128)(2,1)}, s32[512,128]{1,0:T(8,128)}, s32[8,512]{1,0:T(8,128)}, s32[512,128]{1,0:T(8,128)}, s32[8,512]{1,0:T(8,128)}, /*index=5*/s32[512,128]{1,0:T(8,128)}) custom-call(s32[1,512]{1,0:T(1,128)} %bitcast.51, s32[1,512]{1,0:T(1,128)} %bitcast.52, s32[1,512]{1,0:T(1,128)} %bitcast.53, bf16[512,512]{1,0:T(8,128)(2,1)} %cot_ref.1), custom_call_target="tpu_custom_call" | custom-call | flops 536870912 | bytes 1572864 | tf_op jit(solution)/shard_map/index_cotangent/pallas_call | solution.py:327
  22.7 22.5 %all-to-all-done = bf16[32,32,512]{2,1,0:T(8,128)(2,1)S(1)} async-done(((bf16[32,32,512]{2,1,0:T(8,128)(2,1)}), bf16[32,32,512]{2,1,0:T(8,128)(2,1)S(1)}, u32[]{:S(2)}, u32[]{:S(2)}) %all-to-all-start) | async-done | bytes 1048608 | tf_op jit(solution)/shard_map/all_to_all | solution.py:270
  45.2 0.9 copy-done.8
  46.1 1.5 unpack_features.1.refs_3_.x_ref
  47.7 19.5 %all_to_all.30 = bf16[4,256,640]{2,1,0:T(8,128)(2,1)S(1)} all-to-all(bf16[4,256,640]{2,1,0:T(8,128)(2,1)S(1)} %bitcast.47), channel_id=1, replica_groups=mesh['row'=4,'col'=8] {'row'}, dimensions={0} | all-to-all | bytes 2621440 | tf_op jit(solution)/shard_map/all_to_all | solution.py:274
  67.2 1.3 copy.18
  68.5 24.2 %all-gather.2.cloned.1.call-done.x_ref = bf16[4096,512]{1,0:T(8,128)(2,1)} async-done(((bf16[512,512]{1,0:T(8,128)(2,1)}), bf16[4096,512]{1,0:T(8,128)(2,1)}) %all-gather.2.cloned.1.call-update) | async-done | bytes 4194320 | tf_op jit(solution)/shard_map/all_gather | solution.py:355
  92.7 3.6 %all-to-all-start.2 = ((bf16[8,128,640]{2,1,0:T(8,128)(2,1)}), bf16[8,128,640]{2,1,0:T(8,128)(2,1)S(1)}, u32[]{:S(2)}, u32[]{:S(2)}) async-start(bf16[8,128,640]{2,1,0:T(8,128)(2,1)} %bitcast.11), calls=%async_computation.2 | async-start | bytes 2621440 | tf_op jit(solution)/shard_map/all_to_all | solution.py:278
  96.2 9.8 %spmm.1 = (bf16[512,512]{1,0:T(8,128)(2,1)}, bf16[512,512]{1,0:T(8,128)(2,1)}, bf16[512,512]{1,0:T(8,128)(2,1)}, bf16[256,512]{1,0:T(8,128)(2,1)}, bf16[256,512]{1,0:T(8,128)(2,1)}) custom-call(s32[128]{0:T(128)} %reshape_squeeze.3.cols_ref, s32[4]{0:T(128)} %get-tuple-element.59.group_ref.index_ref, bf16[4096,512]{1,0:T(8,128)(2,1)} %all-gather.2.cloned.1.call-done.x_ref, ...), custom_call_target="tpu_custom_call" | custom-call | flops 2147483648 | bytes 10485760 | tf_op jit(solution)/shard_map/spmm/pallas_call | solution.py:370
  106.0 1.5 collective-permute-start
  107.6 1.5 collective-permute-start.1
  109.0 5.9 %collective-permute-done.top_ref = bf16[256,512]{1,0:T(8,128)(2,1)S(1)} collective-permute-done((bf16[256,512]{1,0:T(8,128)(2,1)}, bf16[256,512]{1,0:T(8,128)(2,1)S(1)}, u32[]{:S(2)}, u32[]{:S(2)}) %collective-permute-start) | collective-permute-done | bytes 262176 | tf_op jit(solution)/shard_map/ppermute | solution.py:284
  114.9 1.1 collective-permute-done.1.bottom_ref
  116.1 1.0 copy-done.2
  117.1 1.0 copy-done.3
  118.3 0.7 collective-permute-start.2
  119.0 1.4 collective-permute-start.3
  120.4 11.0 %collective-permute-done.2.refs_1_ = bf16[512,512]{1,0:T(8,128)(2,1)S(1)} collective-permute-done((bf16[512,512]{1,0:T(8,128)(2,1)S(1)}, bf16[512,512]{1,0:T(8,128)(2,1)S(1)}, u32[]{:S(2)}, u32[]{:S(2)}) %collective-permute-start.2) | collective-permute-done | bytes 524320 | tf_op jit(solution)/shard_map/ppermute | solution.py:284
  133.1 6.8 %layer.1 = (bf16[1024,512]{1,0:T(8,128)(2,1)}, bf16[512,512]{1,0:T(8,128)(2,1)}, bf16[512,512]{1,0:T(8,128)(2,1)}, bf16[512,512]{1,0:T(8,128)(2,1)}) custom-call(bf16[512,512]{1,0:T(8,128)(2,1)} %get-tuple-element.63.refs_0_, bf16[512,512]{1,0:T(8,128)(2,1)} %copy-done.18, bf16[512,512]{1,0:T(8,128)(2,1)} %copy-done.19, ...), custom_call_target="tpu_custom_call" | custom-call | flops 1342177280 | bytes 6815744 | tf_op jit(solution)/shard_map/layer/pallas_call | solution.py:396
  139.9 4.6 %all-to-all-start.3 = ((bf16[8,128,512]{2,1,0:T(8,128)(2,1)}), bf16[8,128,512]{2,1,0:T(8,128)(2,1)S(1)}, u32[]{:S(2)}, u32[]{:S(2)}) async-start(bf16[8,128,512]{2,1,0:T(8,128)(2,1)} %bitcast.48), calls=%async_computation.3 | async-start | bytes 2097152 | tf_op jit(solution)/shard_map/all_to_all | solution.py:278
  144.5 1.5 collective-permute-start.5
  146.0 1.4 collective-permute-start.4
  147.5 11.4 %collective-permute-done.5.refs_2_ = bf16[512,512]{1,0:T(8,128)(2,1)S(1)} collective-permute-done((bf16[512,512]{1,0:T(8,128)(2,1)S(1)}, bf16[512,512]{1,0:T(8,128)(2,1)S(1)}, u32[]{:S(2)}, u32[]{:S(2)}) %collective-permute-start.5) | collective-permute-done | bytes 524320 | tf_op jit(solution)/shard_map/ppermute | solution.py:284
  158.9 1.5 collective-permute-start.6
  160.4 1.5 collective-permute-start.7
  161.9 3.8 %terms.1 = (bf16[512,512]{1,0:T(8,128)(2,1)}, bf16[512,512]{1,0:T(8,128)(2,1)}, f32[512,512]{1,0:T(8,128)}) custom-call(s32[1]{0:T(128)} %bitcast.5.core_ref, bf16[512,512]{1,0:T(8,128)(2,1)} %unpack_features.1.refs_3_.x_ref, bf16[512,512]{1,0:T(8,128)(2,1)} %get-tuple-element.75.agg_ref, bf16[512,512]{1,0:T(8,128)(2,1)} %get-tuple-element.76.slopes_ref, ...), custom_call_target="tpu_custom_call" | custom-call | flops 805306368 | bytes 4718592 | tf_op jit(solution)/shard_map/terms/pallas_call | solution.py:411
  165.8 1.1 collective-permute-done.6.refs_3_
  166.8 1.2 collective-permute-done.7.refs_4_
  168.1 0.7 copy-done.15
  168.8 10.5 %spmm_back.1 = bf16[4096,512]{1,0:T(8,128)(2,1)} custom-call(s32[128]{0:T(128)} %reshape_squeeze.3.cols_ref, s32[4]{0:T(128)} %get-tuple-element.59.group_ref.index_ref, bf16[512,512]{1,0:T(8,128)(2,1)} %get-tuple-element.80.refs_0_, bf16[512,512]{1,0:T(8,128)(2,1)} %copy-done.12, bf16[512,512]{1,0:T(8,128)(2,1)} %copy-done.11, bf16[256,512]{1,0:T(8,128)(2,1)} %copy-done.14, ...), custom_call_target="tpu_custom_call" | custom-call | flops 2147483648 | bytes 10485760 | tf_op jit(solution)/shard_map/spmm_back/pallas_call | solution.py:421
  179.3 1.0 copy.19
  180.3 3.8 %all-to-all-start.4 = ((bf16[4,256,512]{2,1,0:T(8,128)(2,1)}), bf16[4,256,512]{2,1,0:T(8,128)(2,1)S(1)}, u32[]{:S(2)}, u32[]{:S(2)}) async-start(bf16[4,256,512]{2,1,0:T(8,128)(2,1)} %bitcast.17), calls=%async_computation.4 | async-start | bytes 2097152 | tf_op jit(solution)/shard_map/all_to_all | solution.py:274
  184.3 2.2 collective-permute-done.8.refs_1_
  186.4 0.8 split_sum.3
  187.2 1.8 collective-permute-start.9
  189.0 1.5 collective-permute-start.10
  190.8 9.9 %collective-permute-done.9.refs_1_ = bf16[128,512]{1,0:T(8,128)(2,1)S(1)} collective-permute-done((bf16[128,512]{1,0:T(8,128)(2,1)S(1)}, bf16[128,512]{1,0:T(8,128)(2,1)S(1)}, u32[]{:S(2)}, u32[]{:S(2)}) %collective-permute-start.9) | collective-permute-done | bytes 131104 | tf_op jit(solution)/shard_map/ppermute | solution.py:284
  200.7 2.3 collective-permute-done.11.refs_3_
  203.0 0.6 split_sum.4
  203.7 1.0 collective-permute-start.12
  204.7 2.4 collective-permute-start.13
  207.1 1.1 collective-permute-start.14
  208.1 0.9 collective-permute-done.12.refs_1_
  209.1 1.8 collective-permute-done.13.refs_2_
  210.9 2.8 %collective-permute-done.14.refs_3_ = bf16[32,512]{1,0:T(8,128)(2,1)S(1)} collective-permute-done((bf16[32,512]{1,0:T(8,128)(2,1)S(1)}, bf16[32,512]{1,0:T(8,128)(2,1)S(1)}, u32[]{:S(2)}, u32[]{:S(2)}) %collective-permute-start.14) | collective-permute-done | bytes 32800 | tf_op jit(solution)/shard_map/ppermute | solution.py:287
  213.7 1.1 collective-permute-start.17
  215.1 3.1 %collective-permute-start.15 = (bf16[32,512]{1,0:T(8,128)(2,1)S(1)}, bf16[32,512]{1,0:T(8,128)(2,1)S(1)}, u32[]{:S(2)}, u32[]{:S(2)}) collective-permute-start(bf16[32,512]{1,0:T(8,128)(2,1)S(1)} %split_sum.5.refs_0_), channel_id=1, source_target_pairs={{0,2},{1,3},{2,0},{3,1},{4,6},{5,7},{6,4},{7,5},{8,10},{9,11},{10,... | collective-permute-start | bytes 98312 | tf_op jit(solution)/shard_map/ppermute | solution.py:287
  218.1 2.2 collective-permute-done.17.refs_3_
  220.3 1.2 collective-permute-done.16.refs_2_
  222.2 11.3 %reduce-scatter.2.cloned.1.call-done.neigh_ref = bf16[512,512]{1,0:T(8,128)(2,1)} async-done(((bf16[4096,512]{1,0:T(8,128)(2,1)}), bf16[512,512]{1,0:T(8,128)(2,1)}) %reduce-scatter.2.cloned.1.call-update) | async-done | bytes 524304 | tf_op jit(solution)/shard_map/reduce_scatter | solution.py:441
  233.5 1.0 copy-done.1
  234.5 1.8 join_pack.1
  236.3 3.4 %all-to-all-start.5 = ((bf16[32,32,512]{2,1,0:T(8,128)(2,1)}), bf16[32,32,512]{2,1,0:T(8,128)(2,1)S(1)}, u32[]{:S(2)}, u32[]{:S(2)}) async-start(bf16[32,32,512]{2,1,0:T(8,128)(2,1)} %bitcast.20), calls=%async_computation.6 | async-start | bytes 2097152 | tf_op jit(solution)/shard_map/all_to_all | solution.py:270
  239.8 2.7 collective-permute-start.20
  243.3 11.5 %collective-permute-done.20.refs_3_ = bf16[128,512]{1,0:T(8,128)(2,1)S(1)} collective-permute-done((bf16[128,512]{1,0:T(8,128)(2,1)S(1)}, bf16[128,512]{1,0:T(8,128)(2,1)S(1)}, u32[]{:S(2)}, u32[]{:S(2)}) %collective-permute-start.20) | collective-permute-done | bytes 131104 | tf_op jit(solution)/shard_map/ppermute | solution.py:284
  254.8 1.6 collective-permute-done.19.refs_2_
  256.4 0.7 collective-permute-done.18.refs_1_
  257.8 1.6 unpack_owner.2
  259.7 1.5 final.1
  261.1 6.2 %all-to-all-done.5 = bf16[32,32,512]{2,1,0:T(8,128)(2,1)S(1)} async-done(((bf16[32,32,512]{2,1,0:T(8,128)(2,1)}), bf16[32,32,512]{2,1,0:T(8,128)(2,1)S(1)}, u32[]{:S(2)}, u32[]{:S(2)}) %all-to-all-start.5) | async-done | bytes 1048608 | tf_op jit(solution)/shard_map/all_to_all | solution.py:270
  267.3 1.5 unpack_owner.3
  (61 shorter events, 5.8 us)
Async XLA Ops:
  10.3 7.4 %copy-start.16 = (s32[1,1,16,8]{2,3,1,0:T(8,128)S(1)}, s32[1,1,16,8]{2,3,1,0:T(8,128)}, u32[]{:S(2)}) copy-start(s32[1,1,16,8]{2,3,1,0:T(8,128)} %param.10) | copy-start | bytes 1540
  10.3 34.9 %all-to-all-start = ((bf16[32,32,512]{2,1,0:T(8,128)(2,1)}), bf16[32,32,512]{2,1,0:T(8,128)(2,1)S(1)}, u32[]{:S(2)}, u32[]{:S(2)}) async-start(bf16[32,32,512]{2,1,0:T(8,128)(2,1)} %bitcast.49), calls=%async_computation | async-start | bytes 2097152 | tf_op jit(solution)/shard_map/all_to_all | solution.py:270
  17.6 75.0 %all-gather.2.cloned.1.call-start = ((), (), s32[]{:S(2)}) async-start(), calls=%async_computation.7 | async-start | bytes 4718592 | tf_op jit(solution)/shard_map/all_gather | solution.py:355
  45.2 1.0 copy-start.8
  46.1 1.6 copy-start.10
  92.7 39.2 %all-to-all-start.2 = ((bf16[8,128,640]{2,1,0:T(8,128)(2,1)}), bf16[8,128,640]{2,1,0:T(8,128)(2,1)S(1)}, u32[]{:S(2)}, u32[]{:S(2)}) async-start(bf16[8,128,640]{2,1,0:T(8,128)(2,1)} %bitcast.11), calls=%async_computation.2 | async-start | bytes 2621440 | tf_op jit(solution)/shard_map/all_to_all | solution.py:278
  106.0 8.9 %collective-permute-start = (bf16[256,512]{1,0:T(8,128)(2,1)}, bf16[256,512]{1,0:T(8,128)(2,1)S(1)}, u32[]{:S(2)}, u32[]{:S(2)}) collective-permute-start(bf16[256,512]{1,0:T(8,128)(2,1)} %get-tuple-element.66), channel_id=1, source_target_pairs={{0,8},{8,0},{16,24},{24,16},{1,9},{9,1},{17,25},{25,17},{2,10},{10... | collective-permute-start | bytes 786440 | tf_op jit(solution)/shard_map/ppermute | solution.py:284
  107.6 8.5 %collective-permute-start.1 = (bf16[256,512]{1,0:T(8,128)(2,1)}, bf16[256,512]{1,0:T(8,128)(2,1)S(1)}, u32[]{:S(2)}, u32[]{:S(2)}) collective-permute-start(bf16[256,512]{1,0:T(8,128)(2,1)} %get-tuple-element.67), channel_id=1, source_target_pairs={{0,16},{8,24},{16,0},{24,8},{1,17},{9,25},{17,1},{25,9},{2,18},{10... | collective-permute-start | bytes 786440 | tf_op jit(solution)/shard_map/ppermute | solution.py:284
  116.1 1.0 copy-start.2
  117.1 1.0 copy-start.3
  118.3 13.1 %collective-permute-start.2 = (bf16[512,512]{1,0:T(8,128)(2,1)S(1)}, bf16[512,512]{1,0:T(8,128)(2,1)S(1)}, u32[]{:S(2)}, u32[]{:S(2)}) collective-permute-start(bf16[512,512]{1,0:T(8,128)(2,1)S(1)} %get-tuple-element.68), channel_id=1, source_target_pairs={{0,8},{8,0},{16,24},{24,16},{1,9},{9,1},{17,25},{25,17},{2,10},{10... | collective-permute-start | bytes 1572872 | tf_op jit(solution)/shard_map/ppermute | solution.py:284
  119.0 12.9 %collective-permute-start.3 = (bf16[512,512]{1,0:T(8,128)(2,1)S(1)}, bf16[512,512]{1,0:T(8,128)(2,1)S(1)}, u32[]{:S(2)}, u32[]{:S(2)}) collective-permute-start(bf16[512,512]{1,0:T(8,128)(2,1)S(1)} %get-tuple-element.69), channel_id=1, source_target_pairs={{0,16},{8,24},{16,0},{24,8},{1,17},{9,25},{17,1},{25,9},{2,18},{10... | collective-permute-start | bytes 1572872 | tf_op jit(solution)/shard_map/ppermute | solution.py:284
  131.4 0.8 copy-start.18
  131.8 0.8 copy-start.19
  131.8 1.3 copy-start.9
  139.9 4.6 %copy-start.13 = (bf16[512,512]{1,0:T(8,128)(2,1)S(1)}, bf16[512,512]{1,0:T(8,128)(2,1)}, u32[]{:S(2)}) copy-start(bf16[512,512]{1,0:T(8,128)(2,1)} %get-tuple-element.80.refs_0_) | copy-start | bytes 1572868
  139.9 39.4 %all-to-all-start.3 = ((bf16[8,128,512]{2,1,0:T(8,128)(2,1)}), bf16[8,128,512]{2,1,0:T(8,128)(2,1)S(1)}, u32[]{:S(2)}, u32[]{:S(2)}) async-start(bf16[8,128,512]{2,1,0:T(8,128)(2,1)} %bitcast.48), calls=%async_computation.3 | async-start | bytes 2097152 | tf_op jit(solution)/shard_map/all_to_all | solution.py:278
  144.5 89.0 %reduce-scatter.2.cloned.1.call-start = ((), (), s32[]{:S(2)}) async-start(), calls=%async_computation.8 | async-start | bytes 4718592 | tf_op jit(solution)/shard_map/reduce_scatter | solution.py:441
  144.5 14.4 %collective-permute-start.5 = (bf16[512,512]{1,0:T(8,128)(2,1)S(1)}, bf16[512,512]{1,0:T(8,128)(2,1)S(1)}, u32[]{:S(2)}, u32[]{:S(2)}) collective-permute-start(bf16[512,512]{1,0:T(8,128)(2,1)S(1)} %copy-done.13), channel_id=1, source_target_pairs={{0,16},{8,24},{16,0},{24,8},{1,17},{9,25},{17,1},{25,9},{2,18},{10... | collective-permute-start | bytes 1572872 | tf_op jit(solution)/shard_map/ppermute | solution.py:284
  146.0 14.3 %collective-permute-start.4 = (bf16[512,512]{1,0:T(8,128)(2,1)S(1)}, bf16[512,512]{1,0:T(8,128)(2,1)S(1)}, u32[]{:S(2)}, u32[]{:S(2)}) collective-permute-start(bf16[512,512]{1,0:T(8,128)(2,1)S(1)} %copy-done.13), channel_id=1, source_target_pairs={{0,8},{8,0},{16,24},{24,16},{1,9},{9,1},{17,25},{25,17},{2,10},{10... | collective-permute-start | bytes 1572872 | tf_op jit(solution)/shard_map/ppermute | solution.py:284
  158.9 6.9 %copy-start.11 = (bf16[512,512]{1,0:T(8,128)(2,1)}, bf16[512,512]{1,0:T(8,128)(2,1)S(1)}, u32[]{:S(2)}) copy-start(bf16[512,512]{1,0:T(8,128)(2,1)S(1)} %collective-permute-done.5.refs_2_) | copy-start | bytes 1572868
  158.9 7.9 %collective-permute-start.6 = (bf16[256,512]{1,0:T(8,128)(2,1)S(1)}, bf16[256,512]{1,0:T(8,128)(2,1)S(1)}, u32[]{:S(2)}, u32[]{:S(2)}) collective-permute-start(bf16[256,512]{1,0:T(8,128)(2,1)S(1)} %slice.8), channel_id=1, source_target_pairs={{0,8},{8,0},{16,24},{24,16},{1,9},{9,1},{17,25},{25,17},{2,10},{10... | collective-permute-start | bytes 786440 | tf_op jit(solution)/shard_map/ppermute | solution.py:284
  160.4 5.4 %copy-start.12 = (bf16[512,512]{1,0:T(8,128)(2,1)}, bf16[512,512]{1,0:T(8,128)(2,1)S(1)}, u32[]{:S(2)}) copy-start(bf16[512,512]{1,0:T(8,128)(2,1)S(1)} %collective-permute-done.4.refs_1_) | copy-start | bytes 1572868
  160.4 7.7 %collective-permute-start.7 = (bf16[256,512]{1,0:T(8,128)(2,1)S(1)}, bf16[256,512]{1,0:T(8,128)(2,1)S(1)}, u32[]{:S(2)}, u32[]{:S(2)}) collective-permute-start(bf16[256,512]{1,0:T(8,128)(2,1)S(1)} %slice.9), channel_id=1, source_target_pairs={{0,16},{8,24},{16,0},{24,8},{1,17},{9,25},{17,1},{25,9},{2,18},{10... | collective-permute-start | bytes 786440 | tf_op jit(solution)/shard_map/ppermute | solution.py:284
  166.8 1.2 copy-start.14
  168.1 0.7 copy-start.15
  180.3 3.8 %copy-start.17 = (bf16[512,512]{1,0:T(8,128)(2,1)S(1)}, bf16[512,512]{1,0:T(8,128)(2,1)}, u32[]{:S(2)}) copy-start(bf16[512,512]{1,0:T(8,128)(2,1)} %get-tuple-element.91) | copy-start | bytes 1572868
  180.3 6.1 %copy-start.4 = (bf16[512,512]{1,0:T(8,128)(2,1)S(1)}, bf16[512,512]{1,0:T(8,128)(2,1)}, u32[]{:S(2)}) copy-start(bf16[512,512]{1,0:T(8,128)(2,1)} %get-tuple-element.90.refs_0_) | copy-start | bytes 1572868
  180.3 6.1 %copy-start.6 = (s32[4]{0:T(128)S(1)}, s32[4]{0:T(128)}, u32[]{:S(2)}) copy-start(s32[4]{0:T(128)} %get-tuple-element.59.group_ref.index_ref) | copy-start | bytes 52
  180.3 56.0 %all-to-all-start.4 = ((bf16[4,256,512]{2,1,0:T(8,128)(2,1)}), bf16[4,256,512]{2,1,0:T(8,128)(2,1)S(1)}, u32[]{:S(2)}, u32[]{:S(2)}) async-start(bf16[4,256,512]{2,1,0:T(8,128)(2,1)} %bitcast.17), calls=%async_computation.4 | async-start | bytes 2097152 | tf_op jit(solution)/shard_map/all_to_all | solution.py:274
  184.2 49.3 %copy-start = (f32[512,512]{1,0:T(8,128)S(1)}, f32[512,512]{1,0:T(8,128)}, u32[]{:S(2)}) copy-start(f32[512,512]{1,0:T(8,128)} %get-tuple-element.100.own_ref) | copy-start | bytes 3145732
  184.2 49.3 %copy-start.5 = (s32[8,512]{1,0:T(8,128)S(1)}, s32[8,512]{1,0:T(8,128)}, u32[]{:S(2)}) copy-start(s32[8,512]{1,0:T(8,128)} %get-tuple-element.102.row_ref) | copy-start | bytes 49156
  184.2 2.2 collective-permute-start.8
  187.2 13.5 %collective-permute-start.9 = (bf16[128,512]{1,0:T(8,128)(2,1)S(1)}, bf16[128,512]{1,0:T(8,128)(2,1)S(1)}, u32[]{:S(2)}, u32[]{:S(2)}) collective-permute-start(bf16[128,512]{1,0:T(8,128)(2,1)S(1)} %get-tuple-element.93), channel_id=1, source_target_pairs={{0,8},{8,0},{16,24},{24,16},{1,9},{9,1},{17,25},{25,17},{2,10},{10... | collective-permute-start | bytes 393224 | tf_op jit(solution)/shard_map/ppermute | solution.py:284
  189.0 11.7 %collective-permute-start.10 = (bf16[128,512]{1,0:T(8,128)(2,1)S(1)}, bf16[128,512]{1,0:T(8,128)(2,1)S(1)}, u32[]{:S(2)}, u32[]{:S(2)}) collective-permute-start(bf16[128,512]{1,0:T(8,128)(2,1)S(1)} %get-tuple-element.94), channel_id=1, source_target_pairs={{0,16},{8,24},{16,0},{24,8},{1,17},{9,25},{17,1},{25,9},{2,18},{10... | collective-permute-start | bytes 393224 | tf_op jit(solution)/shard_map/ppermute | solution.py:284
  190.5 12.6 %collective-permute-start.11 = (bf16[128,512]{1,0:T(8,128)(2,1)S(1)}, bf16[128,512]{1,0:T(8,128)(2,1)S(1)}, u32[]{:S(2)}, u32[]{:S(2)}) collective-permute-start(bf16[128,512]{1,0:T(8,128)(2,1)S(1)} %get-tuple-element.95), channel_id=1, source_target_pairs={{0,24},{8,16},{16,8},{24,0},{1,25},{9,17},{17,9},{25,1},{2,26},{10... | collective-permute-start | bytes 393224 | tf_op jit(solution)/shard_map/ppermute | solution.py:284
  203.7 5.4 %collective-permute-start.12 = (bf16[32,512]{1,0:T(8,128)(2,1)S(1)}, bf16[32,512]{1,0:T(8,128)(2,1)S(1)}, u32[]{:S(2)}, u32[]{:S(2)}) collective-permute-start(bf16[32,512]{1,0:T(8,128)(2,1)S(1)} %get-tuple-element.97), channel_id=1, source_target_pairs={{0,2},{1,3},{2,0},{3,1},{4,6},{5,7},{6,4},{7,5},{8,10},{9,11},{10,... | collective-permute-start | bytes 98312 | tf_op jit(solution)/shard_map/ppermute | solution.py:287
  204.7 6.2 %collective-permute-start.13 = (bf16[32,512]{1,0:T(8,128)(2,1)S(1)}, bf16[32,512]{1,0:T(8,128)(2,1)S(1)}, u32[]{:S(2)}, u32[]{:S(2)}) collective-permute-start(bf16[32,512]{1,0:T(8,128)(2,1)S(1)} %get-tuple-element.98), channel_id=1, source_target_pairs={{0,4},{1,5},{2,6},{3,7},{4,0},{5,1},{6,2},{7,3},{8,12},{9,13},{10,... | collective-permute-start | bytes 98312 | tf_op jit(solution)/shard_map/ppermute | solution.py:287
  207.1 6.6 %collective-permute-start.14 = (bf16[32,512]{1,0:T(8,128)(2,1)S(1)}, bf16[32,512]{1,0:T(8,128)(2,1)S(1)}, u32[]{:S(2)}, u32[]{:S(2)}) collective-permute-start(bf16[32,512]{1,0:T(8,128)(2,1)S(1)} %get-tuple-element.99), channel_id=1, source_target_pairs={{0,6},{1,7},{2,4},{3,5},{4,2},{5,3},{6,0},{7,1},{8,14},{9,15},{10,... | collective-permute-start | bytes 98312 | tf_op jit(solution)/shard_map/ppermute | solution.py:287
  213.7 6.7 %collective-permute-start.17 = (bf16[32,512]{1,0:T(8,128)(2,1)S(1)}, bf16[32,512]{1,0:T(8,128)(2,1)S(1)}, u32[]{:S(2)}, u32[]{:S(2)}) collective-permute-start(bf16[32,512]{1,0:T(8,128)(2,1)S(1)} %split_sum.5.refs_0_), channel_id=1, source_target_pairs={{0,6},{1,7},{2,4},{3,5},{4,2},{5,3},{6,0},{7,1},{8,14},{9,15},{10,... | collective-permute-start | bytes 98312 | tf_op jit(solution)/shard_map/ppermute | solution.py:287
  214.8 6.7 %collective-permute-start.16 = (bf16[32,512]{1,0:T(8,128)(2,1)S(1)}, bf16[32,512]{1,0:T(8,128)(2,1)S(1)}, u32[]{:S(2)}, u32[]{:S(2)}) collective-permute-start(bf16[32,512]{1,0:T(8,128)(2,1)S(1)} %split_sum.5.refs_0_), channel_id=1, source_target_pairs={{0,4},{1,5},{2,6},{3,7},{4,0},{5,1},{6,2},{7,3},{8,12},{9,13},{10,... | collective-permute-start | bytes 98312 | tf_op jit(solution)/shard_map/ppermute | solution.py:287
  215.1 6.6 %collective-permute-start.15 = (bf16[32,512]{1,0:T(8,128)(2,1)S(1)}, bf16[32,512]{1,0:T(8,128)(2,1)S(1)}, u32[]{:S(2)}, u32[]{:S(2)}) collective-permute-start(bf16[32,512]{1,0:T(8,128)(2,1)S(1)} %split_sum.5.refs_0_), channel_id=1, source_target_pairs={{0,2},{1,3},{2,0},{3,1},{4,6},{5,7},{6,4},{7,5},{8,10},{9,11},{10,... | collective-permute-start | bytes 98312 | tf_op jit(solution)/shard_map/ppermute | solution.py:287
  233.5 1.0 copy-start.1
  236.3 21.5 %copy-start.7 = (s32[512,128]{1,0:T(8,128)S(1)}, s32[512,128]{1,0:T(8,128)}, u32[]{:S(2)}) copy-start(s32[512,128]{1,0:T(8,128)} %get-tuple-element.55.col_ref) | copy-start | bytes 786436
  236.3 31.0 %all-to-all-start.5 = ((bf16[32,32,512]{2,1,0:T(8,128)(2,1)}), bf16[32,32,512]{2,1,0:T(8,128)(2,1)S(1)}, u32[]{:S(2)}, u32[]{:S(2)}) async-start(bf16[32,32,512]{2,1,0:T(8,128)(2,1)} %bitcast.20), calls=%async_computation.6 | async-start | bytes 2097152 | tf_op jit(solution)/shard_map/all_to_all | solution.py:270
  239.8 15.0 %collective-permute-start.20 = (bf16[128,512]{1,0:T(8,128)(2,1)S(1)}, bf16[128,512]{1,0:T(8,128)(2,1)S(1)}, u32[]{:S(2)}, u32[]{:S(2)}) collective-permute-start(bf16[128,512]{1,0:T(8,128)(2,1)S(1)} %bitcast.32), channel_id=1, source_target_pairs={{0,24},{8,16},{16,8},{24,0},{1,25},{9,17},{17,9},{25,1},{2,26},{10... | collective-permute-start | bytes 393224 | tf_op jit(solution)/shard_map/ppermute | solution.py:284
  242.5 13.9 %collective-permute-start.19 = (bf16[128,512]{1,0:T(8,128)(2,1)S(1)}, bf16[128,512]{1,0:T(8,128)(2,1)S(1)}, u32[]{:S(2)}, u32[]{:S(2)}) collective-permute-start(bf16[128,512]{1,0:T(8,128)(2,1)S(1)} %bitcast.33), channel_id=1, source_target_pairs={{0,16},{8,24},{16,0},{24,8},{1,17},{9,25},{17,1},{25,9},{2,18},{10... | collective-permute-start | bytes 393224 | tf_op jit(solution)/shard_map/ppermute | solution.py:284
  243.0 14.1 %collective-permute-start.18 = (bf16[128,512]{1,0:T(8,128)(2,1)S(1)}, bf16[128,512]{1,0:T(8,128)(2,1)S(1)}, u32[]{:S(2)}, u32[]{:S(2)}) collective-permute-start(bf16[128,512]{1,0:T(8,128)(2,1)S(1)} %bitcast.34), channel_id=1, source_target_pairs={{0,8},{8,0},{16,24},{24,16},{1,9},{9,1},{17,25},{25,17},{2,10},{10... | collective-permute-start | bytes 393224 | tf_op jit(solution)/shard_map/ppermute | solution.py:284
  257.7 2.0 collective-permute-start.21
Sparse Core Ops, SparseCore 0:
  47.8 44.7 all-gather.1
  179.4 54.0 reduce-scatter.1

commit v8 on v7

--- a/solution.py
+++ b/solution.py
@@ -13,6 +13,7 @@
 VMEM = pl.BlockSpec(memory_space=pltpu.VMEM)
 MIB = 1024 * 1024
 LARGE = 56
+WEIGHT = 6
 
 
 def params(mib=16):
@@ -95,13 +96,11 @@
     out_ref[...] = dot(entries_onehot(col_ref[...], value_ref.shape[0]), value_ref[...]).astype(BF)
 
 
-def spmm_kernel(pieces, cols_ref, group_ref, x_ref, *refs):
-    ways = len(pieces)
+def spmm_kernel(ways, cols_ref, group_ref, x_ref, *refs):
     masks, outs = refs[:ways], refs[ways:]
     q = pl.program_id(0)
     depth = pl.num_programs(0)
     _, breadth, tile, _ = masks[0].shape
-    at_piece = 0
     for s in range(ways):
         base = (group_ref[s] * depth + q) * breadth
         total = None
@@ -113,14 +112,7 @@
             )
             term = dot(left, right)
             total = term if total is None else total + term
-        for p in range(pieces[s]):
-            out_ref = outs[at_piece + p]
-
-            @pl.when((q * pieces[s] >= p * depth) & (q * pieces[s] < (p + 1) * depth))
-            def _():
-                out_ref[...] = total.astype(BF)
-
-        at_piece += pieces[s]
+        outs[s][...] = total.astype(BF)
 
 
 def spmm_back_kernel(ways, pieces, cols_ref, group_ref, *refs):
@@ -168,24 +160,31 @@
     right_out[half:, :] = right_ref[half:, :]
 
 
+def prepare_kernel(x_ref, cot_ref, col_ref, self_ref, base_out, cot_out):
+    base_out[...] = dot(x_ref[...], self_ref[...])
+    cot_out[...] = dot(entries_onehot(col_ref[...], cot_ref.shape[0]), cot_ref[...]).astype(BF)
+
+
 def layer_kernel(ways, *refs):
     terms = refs[:ways]
-    (x_ref, cot_ref, col_ref, row_ref, self_ref, neigh_ref, packed_out, slopes_out, agg_out, spread_out) = refs[ways:]
-    width = x_ref.shape[1]
+    (base_ref, cot_ref, neigh_ref, hidden_out, slopes_out, agg_out, spread_out) = refs[ways:]
+    width = base_ref.shape[1]
     summed = terms[0][...].astype(F32)
     for s in range(1, ways):
         summed = summed + terms[s][...].astype(F32)
-    cot = dot(entries_onehot(col_ref[...], cot_ref.shape[0]), cot_ref[...])
-    degrees = cot[:, width : width + 1]
+    degrees = cot_ref[:, width : width + 128].astype(F32)[:, :1]
     agg = (summed / degrees).astype(BF)
     agg_out[...] = agg
-    preact = dot(x_ref[...], self_ref[...]) + dot(agg, neigh_ref[...])
+    preact = base_ref[...] + dot(agg, neigh_ref[...])
     gate = jax.nn.sigmoid(preact)
-    hidden = (preact * gate).astype(BF)
-    slopes = (cot[:, :width] * gate * (1.0 + preact * (1.0 - gate))).astype(BF)
+    hidden_out[...] = (preact * gate).astype(BF)
+    slopes = (cot_ref[:, :width].astype(F32) * gate * (1.0 + preact * (1.0 - gate))).astype(BF)
     slopes_out[...] = slopes
     spread_out[...] = (dot(slopes, neigh_ref[...], 1, 1) / degrees).astype(BF)
-    packed_out[...] = dot(slots_onehot(row_ref[...][:1], packed_out.shape[0]), hidden).astype(BF)
+
+
+def pack_node_kernel(row_ref, value_ref, out_ref):
+    out_ref[...] = dot(slots_onehot(row_ref[...][:1], out_ref.shape[0]), value_ref[...]).astype(BF)
 
 
 def terms_kernel(core_ref, x_ref, agg_ref, slopes_ref, self_ref, kept_out, sent_out, back_out):
@@ -357,7 +356,7 @@
     x_cols, cot_mid = lax.optimization_barrier((x_cols, cot_mid))
     cot_in = col_phase(cot_mid)
 
-    spmm_flops = 2 * masks.size * width
+    spmm_flops = 2 * masks.size * width * WEIGHT
     def piece_spec(p, count):
         share = depth // count
         return pl.BlockSpec((tile, width), lambda q, c, g: (jnp.clip(q - p * share, 0, share - 1), 0))
@@ -368,20 +367,20 @@
     pieces = (1, 1, 1, 2) if ways == 4 else (1,) * ways
     half = rows // 2
     partials = call(
-        functools.partial(spmm_kernel, pieces),
+        functools.partial(spmm_kernel, ways),
         grid_spec=pltpu.PrefetchScalarGridSpec(
             num_scalar_prefetch=2,
             grid=(depth,),
             in_specs=[VMEM] + [mask_spec(s) for s in range(ways)],
-            out_specs=[piece_spec(p, count) for count in pieces for p in range(count)],
+            out_specs=[pl.BlockSpec((tile, width), lambda q, c, g: (q, 0)) for s in range(ways)],
         ),
-        out_shape=[shape(rows // count, width) for count in pieces for _ in range(count)],
+        out_shape=[shape(rows, width) for s in range(ways)],
         cost_estimate=cost(spmm_flops, 2 * masks.size + 2 * x_cols.size + 2 * ways * slab),
         mib=LARGE,
         name="spmm",
     )(cols, groups, x_cols, *([masks] * ways))
     if ways == 4:
-        top, bottom = across(partials[3], 1), across(partials[4], 2)
+        top, bottom = across(partials[3][:half], 1), across(partials[3][half:], 2)
         left, right = call(
             pass_on_kernel,
             out_shape=(shape(rows, width),) * 2,
@@ -393,17 +392,40 @@
         terms = [partials[0], across(left, 1), across(right, 2)]
     else:
         terms = [partials[0]] + [across(partials[s], s) for s in range(1, ways)]
-    hidden_packed, slopes, agg, spread = call(
+    base, cot_node = call(
+        prepare_kernel,
+        out_shape=(shape(rows, width, F32), shape(rows, width + 128)),
+        in_specs=[VMEM] * 4,
+        out_specs=(VMEM,) * 2,
+        cost_estimate=cost(6 * slab * width, 2 * slab * 8),
+        mib=LARGE,
+        name="prepare",
+    )(x_node, cot_in, turned_col, self_weight)
+
+    def by_rows(columns):
+        return pl.BlockSpec((half, columns), lambda i: (i, 0))
+
+    hidden, slopes, agg, spread = call(
         functools.partial(layer_kernel, len(terms)),
-        out_shape=(shape(slots, width),) + (shape(rows, width),) * 3,
-        in_specs=[VMEM] * (len(terms) + 6),
-        out_specs=(VMEM,) * 4,
-        cost_estimate=cost(10 * slab * width, 2 * slab * (ways + 9)),
+        grid=(2,),
+        out_shape=(shape(rows, width),) * 4,
+        in_specs=[by_rows(width)] * (len(terms) + 1) + [by_rows(width + 128), VMEM],
+        out_specs=(by_rows(width),) * 4,
+        cost_estimate=cost(8 * slab * width, 2 * slab * (len(terms) + 9)),
         mib=LARGE,
         name="layer",
-    )(*terms, x_node, cot_in, turned_col, turned_row, self_weight, neigh_weight)
+    )(*terms, base, cot_node, neigh_weight)
+    hidden_packed = call(
+        pack_node_kernel,
+        out_shape=shape(slots, width),
+        in_specs=[VMEM] * 2,
+        out_specs=VMEM,
+        cost_estimate=cost(2 * slots * slab, 6 * slab),
+        name="pack_hidden",
+    )(turned_row, hidden)
     if ways == 4:
         left, right = across(spread, 1), across(spread, 2)
+        left, right, _ = lax.optimization_barrier((left, right, hidden_packed))
         spreads = [spread, left, right, across(right[:half], 1), across(left[half:], 2)]
     else:
         spreads = [spread] + [across(spread, s) for s in range(1, ways)]

time: 277 us -> 268 us (0.968)
  waiting for transfers between devices: 134 us -> 127 us
    ppermute x14, waiting for transfers between devices: 58.2 us -> 41.9 us  [across(): return lax.ppermute(value, 'row', [(i, i ^ s) for i in range(ways)])]
    all_to_all x2, waiting for transfers between devices: 0.01 us -> 13.2 us  [col_phase(): lax.all_to_all(there, 'col', split_axis=0, concat_axis=0, tiled=True)]
    reduce_scatter x1, waiting for transfers between devices: 11.3 us -> 7.77 us  [on_device(): neigh_back = lax.psum_scatter(back, 'col', scatter_dimension=0, tiled=True)]
    pallas_call x2 -> x4, Pallas kernels: 16.6 us -> 17.2 us  [the longest x1 7.54 us: on_device(): call(functools.partial(spmm_kernel, ways), grid_spec=pltpu.PrefetchScalar...]
  transfers between devices with their start and end apart: 29 -> 29, of which waited for: 24 -> 24; matrix products, arithmetic and copies ran while one was open for 1% -> 2% of each run, Pallas kernels for 13% -> 14%
where the time goes in v8:
time: 268 us
  waiting for transfers between devices  127 us (47%)
  Pallas kernels  48.8 us (18%)
  starting transfers between devices  48.1 us (18%)
  blocking collectives  19.5 us (7%)
  between operations  14.3 us (5%)
  local copies, waits for them, and re-layouts  9.92 us (4%)
    ppermute x14, waiting for transfers between devices, across(): return lax.ppermute(value, 'row', [(i, i ^ s) for i in range(ways)])  41.9 us
    all_to_all x2, waiting for transfers between devices, relay(): lax.all_to_all(there, everyone, split_axis=0, concat_axis=0, tiled=True)  28.7 us
    all_gather x1, waiting for transfers between devices, on_device(): x_cols = lax.all_gather(x_node, 'col', axis=0, tiled=True)  24.2 us
    all_to_all x1, blocking collectives, row_phase(): lax.all_to_all(there, 'row', split_axis=0, concat_axis=0, tiled=True)  19.5 us
    ppermute x14, starting transfers between devices, across(): return lax.ppermute(value, 'row', [(i, i ^ s) for i in range(ways)])  17.3 us
    all_to_all x2, waiting for transfers between devices, col_phase(): lax.all_to_all(there, 'col', split_axis=0, concat_axis=0, tiled=True)  13.2 us
    all_to_all x2, starting transfers between devices, relay(): lax.all_to_all(there, everyone, split_axis=0, concat_axis=0, tiled=True)  10.8 us
    pallas_call x1, Pallas kernels, on_device(): call(functools.partial(spmm_back_kernel, ways, pieces), grid_spec=pltpu.P...  10.3 us
  transfers between devices with their start and end apart: 29, of which 24 were waited for; matrix products, arithmetic and copies ran while one was open for 2% of the time, Pallas kernels for 14%

profile of v8, /device:TPU:0, one launch (start us, length us, event | category | flops | bytes accessed | tf_op | source)
XLA Modules:
  0.0 267.6 jit_solution(3344947293954808124)
XLA Ops:
  7.2 3.1 %pack_features.1 = bf16[1024,512]{1,0:T(8,128)(2,1)} custom-call(s32[1,512]{1,0:T(1,128)} %bitcast.49, bf16[512,512]{1,0:T(8,128)(2,1)} %value_ref.1), custom_call_target="tpu_custom_call" | custom-call | flops 536870912 | bytes 1572864 | tf_op jit(solution)/shard_map/pack_features/pallas_call | solution.py:316
  10.3 7.3 %all-to-all-start = ((bf16[32,32,512]{2,1,0:T(8,128)(2,1)}), bf16[32,32,512]{2,1,0:T(8,128)(2,1)S(1)}, u32[]{:S(2)}, u32[]{:S(2)}) async-start(bf16[32,32,512]{2,1,0:T(8,128)(2,1)} %bitcast.40), calls=%async_computation | async-start | bytes 2097152 | tf_op jit(solution)/shard_map/all_to_all | solution.py:269
  18.4 3.7 %index_cotangent.1 = (bf16[1024,640]{1,0:T(8,128)(2,1)}, s32[512,128]{1,0:T(8,128)}, s32[8,512]{1,0:T(8,128)}, s32[512,128]{1,0:T(8,128)}, s32[8,512]{1,0:T(8,128)}, /*index=5*/s32[512,128]{1,0:T(8,128)}) custom-call(s32[1,512]{1,0:T(1,128)} %bitcast.50, s32[1,512]{1,0:T(1,128)} %bitcast.51, s32[1,512]{1,0:T(1,128)} %bitcast.52, bf16[512,512]{1,0:T(8,128)(2,1)} %cot_ref.1), custom_call_target="tpu_custom_call" | custom-call | flops 536870912 | bytes 1572864 | tf_op jit(solution)/shard_map/index_cotangent/pallas_call | solution.py:326
  22.7 22.5 %all-to-all-done = bf16[32,32,512]{2,1,0:T(8,128)(2,1)S(1)} async-done(((bf16[32,32,512]{2,1,0:T(8,128)(2,1)}), bf16[32,32,512]{2,1,0:T(8,128)(2,1)S(1)}, u32[]{:S(2)}, u32[]{:S(2)}) %all-to-all-start) | async-done | bytes 1048608 | tf_op jit(solution)/shard_map/all_to_all | solution.py:269
  45.2 0.9 copy-done.9
  46.1 1.6 unpack_features.1.x_ref
  47.7 19.5 %all_to_all.30 = bf16[4,256,640]{2,1,0:T(8,128)(2,1)S(1)} all-to-all(bf16[4,256,640]{2,1,0:T(8,128)(2,1)S(1)} %bitcast.39), channel_id=1, replica_groups=mesh['row'=4,'col'=8] {'row'}, dimensions={0} | all-to-all | bytes 2621440 | tf_op jit(solution)/shard_map/all_to_all | solution.py:273
  67.2 1.3 copy.18
  68.5 24.2 %all-gather.2.cloned.1.call-done.x_ref = bf16[4096,512]{1,0:T(8,128)(2,1)} async-done(((bf16[512,512]{1,0:T(8,128)(2,1)}), bf16[4096,512]{1,0:T(8,128)(2,1)}) %all-gather.2.cloned.1.call-update) | async-done | bytes 4194320 | tf_op jit(solution)/shard_map/all_gather | solution.py:354
  92.7 3.6 %all-to-all-start.2 = ((bf16[8,128,640]{2,1,0:T(8,128)(2,1)}), bf16[8,128,640]{2,1,0:T(8,128)(2,1)S(1)}, u32[]{:S(2)}, u32[]{:S(2)}) async-start(bf16[8,128,640]{2,1,0:T(8,128)(2,1)} %bitcast.11), calls=%async_computation.2 | async-start | bytes 2621440 | tf_op jit(solution)/shard_map/all_to_all | solution.py:277
  96.2 7.5 %spmm.1 = (bf16[512,512]{1,0:T(8,128)(2,1)}, bf16[512,512]{1,0:T(8,128)(2,1)}, bf16[512,512]{1,0:T(8,128)(2,1)}, bf16[512,512]{1,0:T(8,128)(2,1)}) custom-call(s32[128]{0:T(128)} %reshape_squeeze.3.cols_ref, s32[4]{0:T(128)} %get-tuple-element.62.group_ref.index_ref, bf16[4096,512]{1,0:T(8,128)(2,1)} %all-gather.2.cloned.1.call-done.x_ref, ...), custom_call_target="tpu_custom_call" | custom-call | flops 12884901888 | bytes 10485760 | tf_op jit(solution)/shard_map/spmm/pallas_call | solution.py:369
  103.8 1.2 fusion
  104.9 1.6 collective-permute-start.1
  106.5 1.5 collective-permute-start
  108.0 5.6 %collective-permute-done.1.bottom_ref = bf16[256,512]{1,0:T(8,128)(2,1)S(1)} collective-permute-done((bf16[256,512]{1,0:T(8,128)(2,1)S(1)}, bf16[256,512]{1,0:T(8,128)(2,1)S(1)}, u32[]{:S(2)}, u32[]{:S(2)}) %collective-permute-start.1) | collective-permute-done | bytes 262176 | tf_op jit(solution)/shard_map/ppermute | solution.py:283
  113.6 1.2 collective-permute-done.top_ref
  115.0 1.5 collective-permute-start.2
  117.1 11.3 %all-to-all-done.2 = bf16[8,128,640]{2,1,0:T(8,128)(2,1)S(1)} async-done(((bf16[8,128,640]{2,1,0:T(8,128)(2,1)}), bf16[8,128,640]{2,1,0:T(8,128)(2,1)S(1)}, u32[]{:S(2)}, u32[]{:S(2)}) %all-to-all-start.2) | async-done | bytes 1310752 | tf_op jit(solution)/shard_map/all_to_all | solution.py:277
  128.4 1.1 copy-done.11
  129.5 3.8 %prepare.1 = (f32[512,512]{1,0:T(8,128)}, bf16[512,640]{1,0:T(8,128)(2,1)}) custom-call(bf16[512,512]{1,0:T(8,128)(2,1)} %unpack_features.1.x_ref, bf16[1024,640]{1,0:T(8,128)(2,1)} %bitcast.38, s32[512,128]{1,0:T(8,128)} %get-tuple-element.73.col_ref, bf16[512,512]{1,0:T(8,128)(2,1)} %self_ref.3), custom_call_target="tpu_custom_call" | custom-call | flops 805306368 | bytes 4194304 | tf_op jit(solution)/shard_map/prepare/pallas_call | solution.py:395
  133.3 0.8 copy-done.17
  134.1 4.1 %layer.1 = (bf16[512,512]{1,0:T(8,128)(2,1)}, bf16[512,512]{1,0:T(8,128)(2,1)}, bf16[512,512]{1,0:T(8,128)(2,1)}, bf16[512,512]{1,0:T(8,128)(2,1)}) custom-call(bf16[512,512]{1,0:T(8,128)(2,1)} %get-tuple-element.66.refs_0_, bf16[512,512]{1,0:T(8,128)(2,1)} %copy-done.17, bf16[512,512]{1,0:T(8,128)(2,1)} %collective-permute-done.3.refs_2_, ...), custom_call_target="tpu_custom_call" | custom-call | flops 1073741824 | bytes 6291456 | tf_op jit(solution)/shard_map/layer/pallas_call | solution.py:408
  138.2 1.5 collective-permute-start.5
  139.7 1.5 collective-permute-start.4
  141.2 1.0 copy-done.7
  142.2 1.7 pack_hidden.1
  143.9 3.6 %all-to-all-start.3 = ((bf16[8,128,512]{2,1,0:T(8,128)(2,1)}), bf16[8,128,512]{2,1,0:T(8,128)(2,1)S(1)}, u32[]{:S(2)}, u32[]{:S(2)}) async-start(bf16[8,128,512]{2,1,0:T(8,128)(2,1)} %bitcast.13), calls=%async_computation.3 | async-start | bytes 2097152 | tf_op jit(solution)/shard_map/all_to_all | solution.py:277
  147.5 4.4 %collective-permute-done.5.refs_2_ = bf16[512,512]{1,0:T(8,128)(2,1)S(1)} collective-permute-done((bf16[512,512]{1,0:T(8,128)(2,1)}, bf16[512,512]{1,0:T(8,128)(2,1)S(1)}, u32[]{:S(2)}, u32[]{:S(2)}) %collective-permute-start.5) | collective-permute-done | bytes 524320 | tf_op jit(solution)/shard_map/ppermute | solution.py:283
  151.9 1.2 collective-permute-done.4.refs_1_
  153.1 1.5 collective-permute-start.6
  155.2 3.8 %terms.1 = (bf16[512,512]{1,0:T(8,128)(2,1)}, bf16[512,512]{1,0:T(8,128)(2,1)}, f32[512,512]{1,0:T(8,128)}) custom-call(s32[1]{0:T(128)} %bitcast.5.core_ref, bf16[512,512]{1,0:T(8,128)(2,1)} %unpack_features.1.x_ref, bf16[512,512]{1,0:T(8,128)(2,1)} %get-tuple-element.82.agg_ref, bf16[512,512]{1,0:T(8,128)(2,1)} %get-tuple-element.83.slopes_ref, ...), custom_call_target="tpu_custom_call" | custom-call | flops 805306368 | bytes 4718592 | tf_op jit(solution)/shard_map/terms/pallas_call | solution.py:433
  159.1 0.8 collective-permute-done.6.refs_3_
  159.9 1.2 collective-permute-done.7.refs_4_
  161.1 0.7 copy-done.19
  161.8 10.3 %spmm_back.1 = bf16[4096,512]{1,0:T(8,128)(2,1)} custom-call(s32[128]{0:T(128)} %reshape_squeeze.3.cols_ref, s32[4]{0:T(128)} %get-tuple-element.62.group_ref.index_ref, bf16[512,512]{1,0:T(8,128)(2,1)} %get-tuple-element.87.refs_0_, bf16[512,512]{1,0:T(8,128)(2,1)} %copy-done.14, bf16[512,512]{1,0:T(8,128)(2,1)} %copy-done.13, bf16[256,512]{1,0:T(8,128)(2,1)} %copy-done.18, ...), custom_call_target="tpu_custom_call" | custom-call | flops 12884901888 | bytes 10485760 | tf_op jit(solution)/shard_map/spmm_back/pallas_call | solution.py:443
  172.1 1.9 all-to-all-done.3
  174.0 1.0 copy.19
  175.0 3.8 %all-to-all-start.4 = ((bf16[4,256,512]{2,1,0:T(8,128)(2,1)}), bf16[4,256,512]{2,1,0:T(8,128)(2,1)S(1)}, u32[]{:S(2)}, u32[]{:S(2)}) async-start(bf16[4,256,512]{2,1,0:T(8,128)(2,1)} %bitcast.17), calls=%async_computation.4 | async-start | bytes 2097152 | tf_op jit(solution)/shard_map/all_to_all | solution.py:273
  179.0 1.9 collective-permute-done.8.refs_1_
  180.9 0.8 split_sum.3
  181.7 1.8 collective-permute-start.9
  183.5 1.5 collective-permute-start.10
  185.2 11.3 %collective-permute-done.9.refs_1_ = bf16[128,512]{1,0:T(8,128)(2,1)S(1)} collective-permute-done((bf16[128,512]{1,0:T(8,128)(2,1)S(1)}, bf16[128,512]{1,0:T(8,128)(2,1)S(1)}, u32[]{:S(2)}, u32[]{:S(2)}) %collective-permute-start.9) | collective-permute-done | bytes 131104 | tf_op jit(solution)/shard_map/ppermute | solution.py:283
  196.5 2.4 collective-permute-done.11.refs_3_
  199.7 2.2 collective-permute-start.13
  201.8 2.2 collective-permute-start.14
  204.4 2.5 collective-permute-done.13.refs_2_
  206.9 1.6 collective-permute-done.14.refs_3_
  208.5 2.3 collective-permute-start.17
  210.8 2.1 collective-permute-start.15
  212.9 2.3 collective-permute-done.17.refs_3_
  215.2 1.8 collective-permute-done.16.refs_2_
  217.6 7.8 %reduce-scatter.2.cloned.1.call-done.neigh_ref = bf16[512,512]{1,0:T(8,128)(2,1)} async-done(((bf16[4096,512]{1,0:T(8,128)(2,1)}), bf16[512,512]{1,0:T(8,128)(2,1)}) %reduce-scatter.2.cloned.1.call-update) | async-done | bytes 524304 | tf_op jit(solution)/shard_map/reduce_scatter | solution.py:463
  225.4 1.0 copy-done.1
  226.4 1.7 join_pack.1
  228.2 3.5 %all-to-all-start.5 = ((bf16[32,32,512]{2,1,0:T(8,128)(2,1)}), bf16[32,32,512]{2,1,0:T(8,128)(2,1)S(1)}, u32[]{:S(2)}, u32[]{:S(2)}) async-start(bf16[32,32,512]{2,1,0:T(8,128)(2,1)} %bitcast.20), calls=%async_computation.6 | async-start | bytes 2097152 | tf_op jit(solution)/shard_map/all_to_all | solution.py:269
  231.6 2.7 %collective-permute-start.20 = (bf16[128,512]{1,0:T(8,128)(2,1)S(1)}, bf16[128,512]{1,0:T(8,128)(2,1)S(1)}, u32[]{:S(2)}, u32[]{:S(2)}) collective-permute-start(bf16[128,512]{1,0:T(8,128)(2,1)S(1)} %bitcast.32), channel_id=1, source_target_pairs={{0,24},{8,16},{16,8},{24,0},{1,25},{9,17},{17,9},{25,1},{2,26},{10... | collective-permute-start | bytes 393224 | tf_op jit(solution)/shard_map/ppermute | solution.py:283
  235.2 11.5 %collective-permute-done.20.refs_3_ = bf16[128,512]{1,0:T(8,128)(2,1)S(1)} collective-permute-done((bf16[128,512]{1,0:T(8,128)(2,1)S(1)}, bf16[128,512]{1,0:T(8,128)(2,1)S(1)}, u32[]{:S(2)}, u32[]{:S(2)}) %collective-permute-start.20) | collective-permute-done | bytes 131104 | tf_op jit(solution)/shard_map/ppermute | solution.py:283
  246.6 1.6 collective-permute-done.19.refs_2_
  248.3 0.7 collective-permute-done.18.refs_1_
  249.7 1.6 unpack_owner.2
  251.5 1.5 final.1
  253.0 6.2 %all-to-all-done.5 = bf16[32,32,512]{2,1,0:T(8,128)(2,1)S(1)} async-done(((bf16[32,32,512]{2,1,0:T(8,128)(2,1)}), bf16[32,32,512]{2,1,0:T(8,128)(2,1)S(1)}, u32[]{:S(2)}, u32[]{:S(2)}) %all-to-all-start.5) | async-done | bytes 1048608 | tf_op jit(solution)/shard_map/all_to_all | solution.py:269
  259.2 1.5 unpack_owner.3
  (64 shorter events, 6.6 us)
Async XLA Ops:
  10.3 7.4 %copy-start.15 = (s32[1,1,16,8]{2,3,1,0:T(8,128)S(1)}, s32[1,1,16,8]{2,3,1,0:T(8,128)}, u32[]{:S(2)}) copy-start(s32[1,1,16,8]{2,3,1,0:T(8,128)} %param.10) | copy-start | bytes 1540
  10.3 34.9 %all-to-all-start = ((bf16[32,32,512]{2,1,0:T(8,128)(2,1)}), bf16[32,32,512]{2,1,0:T(8,128)(2,1)S(1)}, u32[]{:S(2)}, u32[]{:S(2)}) async-start(bf16[32,32,512]{2,1,0:T(8,128)(2,1)} %bitcast.40), calls=%async_computation | async-start | bytes 2097152 | tf_op jit(solution)/shard_map/all_to_all | solution.py:269
  17.6 75.1 %all-gather.2.cloned.1.call-start = ((), (), s32[]{:S(2)}) async-start(), calls=%async_computation.7 | async-start | bytes 4718592 | tf_op jit(solution)/shard_map/all_gather | solution.py:354
  45.2 1.0 copy-start.9
  46.1 1.6 copy-start.12
  92.7 35.7 %all-to-all-start.2 = ((bf16[8,128,640]{2,1,0:T(8,128)(2,1)}), bf16[8,128,640]{2,1,0:T(8,128)(2,1)S(1)}, u32[]{:S(2)}, u32[]{:S(2)}) async-start(bf16[8,128,640]{2,1,0:T(8,128)(2,1)} %bitcast.11), calls=%async_computation.2 | async-start | bytes 2621440 | tf_op jit(solution)/shard_map/all_to_all | solution.py:277
  103.8 11.0 %copy-start.2 = (bf16[512,512]{1,0:T(8,128)(2,1)S(1)}, bf16[512,512]{1,0:T(8,128)(2,1)}, u32[]{:S(2)}) copy-start(bf16[512,512]{1,0:T(8,128)(2,1)} %get-tuple-element.67.left_ref) | copy-start | bytes 1572868
  103.8 11.0 %copy-start.3 = (bf16[512,512]{1,0:T(8,128)(2,1)S(1)}, bf16[512,512]{1,0:T(8,128)(2,1)}, u32[]{:S(2)}) copy-start(bf16[512,512]{1,0:T(8,128)(2,1)} %get-tuple-element.68.right_ref) | copy-start | bytes 1572868
  104.9 8.7 %collective-permute-start.1 = (bf16[256,512]{1,0:T(8,128)(2,1)S(1)}, bf16[256,512]{1,0:T(8,128)(2,1)S(1)}, u32[]{:S(2)}, u32[]{:S(2)}) collective-permute-start(bf16[256,512]{1,0:T(8,128)(2,1)S(1)} %get-tuple-element.112), channel_id=1, source_target_pairs={{0,16},{8,24},{16,0},{24,8},{1,17},{9,25},{17,1},{25,9},{2,18},{10... | collective-permute-start | bytes 786440 | tf_op jit(solution)/shard_map/ppermute | solution.py:283
  106.5 8.3 %collective-permute-start = (bf16[256,512]{1,0:T(8,128)(2,1)S(1)}, bf16[256,512]{1,0:T(8,128)(2,1)S(1)}, u32[]{:S(2)}, u32[]{:S(2)}) collective-permute-start(bf16[256,512]{1,0:T(8,128)(2,1)S(1)} %get-tuple-element.113), channel_id=1, source_target_pairs={{0,8},{8,0},{16,24},{24,16},{1,9},{9,1},{17,25},{25,17},{2,10},{10... | collective-permute-start | bytes 786440 | tf_op jit(solution)/shard_map/ppermute | solution.py:283
  115.0 18.3 %collective-permute-start.2 = (bf16[512,512]{1,0:T(8,128)(2,1)S(1)}, bf16[512,512]{1,0:T(8,128)(2,1)S(1)}, u32[]{:S(2)}, u32[]{:S(2)}) collective-permute-start(bf16[512,512]{1,0:T(8,128)(2,1)S(1)} %get-tuple-element.70), channel_id=1, source_target_pairs={{0,8},{8,0},{16,24},{24,16},{1,9},{9,1},{17,25},{25,17},{2,10},{10... | collective-permute-start | bytes 1572872 | tf_op jit(solution)/shard_map/ppermute | solution.py:283
  116.5 16.8 %collective-permute-start.3 = (bf16[512,512]{1,0:T(8,128)(2,1)S(1)}, bf16[512,512]{1,0:T(8,128)(2,1)}, u32[]{:S(2)}, u32[]{:S(2)}) collective-permute-start(bf16[512,512]{1,0:T(8,128)(2,1)S(1)} %get-tuple-element.71), channel_id=1, source_target_pairs={{0,16},{8,24},{16,0},{24,8},{1,17},{9,25},{17,1},{25,9},{2,18},{10... | collective-permute-start | bytes 1572872 | tf_op jit(solution)/shard_map/ppermute | solution.py:283
  128.4 1.1 copy-start.11
  133.3 0.8 copy-start.17
  134.1 7.1 %copy-start.10 = (s32[8,512]{1,0:T(8,128)S(1)}, s32[8,512]{1,0:T(8,128)}, u32[]{:S(2)}) copy-start(s32[8,512]{1,0:T(8,128)} %get-tuple-element.77.row_ref) | copy-start | bytes 49156
  138.2 13.7 %collective-permute-start.5 = (bf16[512,512]{1,0:T(8,128)(2,1)}, bf16[512,512]{1,0:T(8,128)(2,1)S(1)}, u32[]{:S(2)}, u32[]{:S(2)}) collective-permute-start(bf16[512,512]{1,0:T(8,128)(2,1)} %get-tuple-element.87.refs_0_), channel_id=1, source_target_pairs={{0,16},{8,24},{16,0},{24,8},{1,17},{9,25},{17,1},{25,9},{2,18},{10... | collective-permute-start | bytes 1572872 | tf_op jit(solution)/shard_map/ppermute | solution.py:283
  139.7 13.4 %collective-permute-start.4 = (bf16[512,512]{1,0:T(8,128)(2,1)}, bf16[512,512]{1,0:T(8,128)(2,1)S(1)}, u32[]{:S(2)}, u32[]{:S(2)}) collective-permute-start(bf16[512,512]{1,0:T(8,128)(2,1)} %get-tuple-element.87.refs_0_), channel_id=1, source_target_pairs={{0,8},{8,0},{16,24},{24,16},{1,9},{9,1},{17,25},{25,17},{2,10},{10... | collective-permute-start | bytes 1572872 | tf_op jit(solution)/shard_map/ppermute | solution.py:283
  141.2 1.0 copy-start.7
  143.9 30.1 %all-to-all-start.3 = ((bf16[8,128,512]{2,1,0:T(8,128)(2,1)}), bf16[8,128,512]{2,1,0:T(8,128)(2,1)S(1)}, u32[]{:S(2)}, u32[]{:S(2)}) async-start(bf16[8,128,512]{2,1,0:T(8,128)(2,1)} %bitcast.13), calls=%async_computation.3 | async-start | bytes 2097152 | tf_op jit(solution)/shard_map/all_to_all | solution.py:277
  147.5 77.9 %reduce-scatter.2.cloned.1.call-start = ((), (), s32[]{:S(2)}) async-start(), calls=%async_computation.8 | async-start | bytes 4718592 | tf_op jit(solution)/shard_map/reduce_scatter | solution.py:463
  151.9 7.2 %copy-start.13 = (bf16[512,512]{1,0:T(8,128)(2,1)}, bf16[512,512]{1,0:T(8,128)(2,1)S(1)}, u32[]{:S(2)}) copy-start(bf16[512,512]{1,0:T(8,128)(2,1)S(1)} %collective-permute-done.5.refs_2_) | copy-start | bytes 1572868
  153.1 6.0 %copy-start.14 = (bf16[512,512]{1,0:T(8,128)(2,1)}, bf16[512,512]{1,0:T(8,128)(2,1)S(1)}, u32[]{:S(2)}) copy-start(bf16[512,512]{1,0:T(8,128)(2,1)S(1)} %collective-permute-done.4.refs_1_) | copy-start | bytes 1572868
  153.1 6.7 %collective-permute-start.6 = (bf16[256,512]{1,0:T(8,128)(2,1)S(1)}, bf16[256,512]{1,0:T(8,128)(2,1)S(1)}, u32[]{:S(2)}, u32[]{:S(2)}) collective-permute-start(bf16[256,512]{1,0:T(8,128)(2,1)S(1)} %slice.14), channel_id=1, source_target_pairs={{0,8},{8,0},{16,24},{24,16},{1,9},{9,1},{17,25},{25,17},{2,10},{10... | collective-permute-start | bytes 786440 | tf_op jit(solution)/shard_map/ppermute | solution.py:283
  154.7 6.4 %collective-permute-start.7 = (bf16[256,512]{1,0:T(8,128)(2,1)S(1)}, bf16[256,512]{1,0:T(8,128)(2,1)S(1)}, u32[]{:S(2)}, u32[]{:S(2)}) collective-permute-start(bf16[256,512]{1,0:T(8,128)(2,1)S(1)} %slice.15), channel_id=1, source_target_pairs={{0,16},{8,24},{16,0},{24,8},{1,17},{9,25},{17,1},{25,9},{2,18},{10... | collective-permute-start | bytes 786440 | tf_op jit(solution)/shard_map/ppermute | solution.py:283
  159.9 1.2 copy-start.18
  161.1 0.7 copy-start.19
  175.0 3.9 %copy-start.16 = (bf16[512,512]{1,0:T(8,128)(2,1)S(1)}, bf16[512,512]{1,0:T(8,128)(2,1)}, u32[]{:S(2)}) copy-start(bf16[512,512]{1,0:T(8,128)(2,1)} %get-tuple-element.97) | copy-start | bytes 1572868
  175.0 5.9 %copy-start.4 = (bf16[512,512]{1,0:T(8,128)(2,1)S(1)}, bf16[512,512]{1,0:T(8,128)(2,1)}, u32[]{:S(2)}) copy-start(bf16[512,512]{1,0:T(8,128)(2,1)} %get-tuple-element.96.refs_0_) | copy-start | bytes 1572868
  175.0 5.9 %copy-start.6 = (s32[4]{0:T(128)S(1)}, s32[4]{0:T(128)}, u32[]{:S(2)}) copy-start(s32[4]{0:T(128)} %get-tuple-element.62.group_ref.index_ref) | copy-start | bytes 52
  175.0 53.1 %all-to-all-start.4 = ((bf16[4,256,512]{2,1,0:T(8,128)(2,1)}), bf16[4,256,512]{2,1,0:T(8,128)(2,1)S(1)}, u32[]{:S(2)}, u32[]{:S(2)}) async-start(bf16[4,256,512]{2,1,0:T(8,128)(2,1)} %bitcast.17), calls=%async_computation.4 | async-start | bytes 2097152 | tf_op jit(solution)/shard_map/all_to_all | solution.py:273
  178.9 46.5 %copy-start = (f32[512,512]{1,0:T(8,128)S(1)}, f32[512,512]{1,0:T(8,128)}, u32[]{:S(2)}) copy-start(f32[512,512]{1,0:T(8,128)} %get-tuple-element.106.own_ref) | copy-start | bytes 3145732
  178.9 46.5 %copy-start.5 = (s32[8,512]{1,0:T(8,128)S(1)}, s32[8,512]{1,0:T(8,128)}, u32[]{:S(2)}) copy-start(s32[8,512]{1,0:T(8,128)} %get-tuple-element.108.row_ref) | copy-start | bytes 49156
  178.9 2.0 collective-permute-start.8
  181.7 14.9 %collective-permute-start.9 = (bf16[128,512]{1,0:T(8,128)(2,1)S(1)}, bf16[128,512]{1,0:T(8,128)(2,1)S(1)}, u32[]{:S(2)}, u32[]{:S(2)}) collective-permute-start(bf16[128,512]{1,0:T(8,128)(2,1)S(1)} %get-tuple-element.99), channel_id=1, source_target_pairs={{0,8},{8,0},{16,24},{24,16},{1,9},{9,1},{17,25},{25,17},{2,10},{10... | collective-permute-start | bytes 393224 | tf_op jit(solution)/shard_map/ppermute | solution.py:283
  183.5 13.0 %collective-permute-start.10 = (bf16[128,512]{1,0:T(8,128)(2,1)S(1)}, bf16[128,512]{1,0:T(8,128)(2,1)S(1)}, u32[]{:S(2)}, u32[]{:S(2)}) collective-permute-start(bf16[128,512]{1,0:T(8,128)(2,1)S(1)} %get-tuple-element.100), channel_id=1, source_target_pairs={{0,16},{8,24},{16,0},{24,8},{1,17},{9,25},{17,1},{25,9},{2,18},{10... | collective-permute-start | bytes 393224 | tf_op jit(solution)/shard_map/ppermute | solution.py:283
  185.0 14.0 %collective-permute-start.11 = (bf16[128,512]{1,0:T(8,128)(2,1)S(1)}, bf16[128,512]{1,0:T(8,128)(2,1)S(1)}, u32[]{:S(2)}, u32[]{:S(2)}) collective-permute-start(bf16[128,512]{1,0:T(8,128)(2,1)S(1)} %get-tuple-element.101), channel_id=1, source_target_pairs={{0,24},{8,16},{16,8},{24,0},{1,25},{9,17},{17,9},{25,1},{2,26},{10... | collective-permute-start | bytes 393224 | tf_op jit(solution)/shard_map/ppermute | solution.py:283
  199.6 4.8 %collective-permute-start.12 = (bf16[32,512]{1,0:T(8,128)(2,1)S(1)}, bf16[32,512]{1,0:T(8,128)(2,1)S(1)}, u32[]{:S(2)}, u32[]{:S(2)}) collective-permute-start(bf16[32,512]{1,0:T(8,128)(2,1)S(1)} %get-tuple-element.103), channel_id=1, source_target_pairs={{0,2},{1,3},{2,0},{3,1},{4,6},{5,7},{6,4},{7,5},{8,10},{9,11},{10,... | collective-permute-start | bytes 98312 | tf_op jit(solution)/shard_map/ppermute | solution.py:286
  199.7 7.2 %collective-permute-start.13 = (bf16[32,512]{1,0:T(8,128)(2,1)S(1)}, bf16[32,512]{1,0:T(8,128)(2,1)S(1)}, u32[]{:S(2)}, u32[]{:S(2)}) collective-permute-start(bf16[32,512]{1,0:T(8,128)(2,1)S(1)} %get-tuple-element.104), channel_id=1, source_target_pairs={{0,4},{1,5},{2,6},{3,7},{4,0},{5,1},{6,2},{7,3},{8,12},{9,13},{10,... | collective-permute-start | bytes 98312 | tf_op jit(solution)/shard_map/ppermute | solution.py:286
  201.8 6.6 %collective-permute-start.14 = (bf16[32,512]{1,0:T(8,128)(2,1)S(1)}, bf16[32,512]{1,0:T(8,128)(2,1)S(1)}, u32[]{:S(2)}, u32[]{:S(2)}) collective-permute-start(bf16[32,512]{1,0:T(8,128)(2,1)S(1)} %get-tuple-element.105), channel_id=1, source_target_pairs={{0,6},{1,7},{2,4},{3,5},{4,2},{5,3},{6,0},{7,1},{8,14},{9,15},{10,... | collective-permute-start | bytes 98312 | tf_op jit(solution)/shard_map/ppermute | solution.py:286
  208.5 6.8 %collective-permute-start.17 = (bf16[32,512]{1,0:T(8,128)(2,1)S(1)}, bf16[32,512]{1,0:T(8,128)(2,1)S(1)}, u32[]{:S(2)}, u32[]{:S(2)}) collective-permute-start(bf16[32,512]{1,0:T(8,128)(2,1)S(1)} %split_sum.5.refs_0_), channel_id=1, source_target_pairs={{0,6},{1,7},{2,4},{3,5},{4,2},{5,3},{6,0},{7,1},{8,14},{9,15},{10,... | collective-permute-start | bytes 98312 | tf_op jit(solution)/shard_map/ppermute | solution.py:286
  210.7 6.3 %collective-permute-start.16 = (bf16[32,512]{1,0:T(8,128)(2,1)S(1)}, bf16[32,512]{1,0:T(8,128)(2,1)S(1)}, u32[]{:S(2)}, u32[]{:S(2)}) collective-permute-start(bf16[32,512]{1,0:T(8,128)(2,1)S(1)} %split_sum.5.refs_0_), channel_id=1, source_target_pairs={{0,4},{1,5},{2,6},{3,7},{4,0},{5,1},{6,2},{7,3},{8,12},{9,13},{10,... | collective-permute-start | bytes 98312 | tf_op jit(solution)/shard_map/ppermute | solution.py:286
  210.8 6.3 %collective-permute-start.15 = (bf16[32,512]{1,0:T(8,128)(2,1)S(1)}, bf16[32,512]{1,0:T(8,128)(2,1)S(1)}, u32[]{:S(2)}, u32[]{:S(2)}) collective-permute-start(bf16[32,512]{1,0:T(8,128)(2,1)S(1)} %split_sum.5.refs_0_), channel_id=1, source_target_pairs={{0,2},{1,3},{2,0},{3,1},{4,6},{5,7},{6,4},{7,5},{8,10},{9,11},{10,... | collective-permute-start | bytes 98312 | tf_op jit(solution)/shard_map/ppermute | solution.py:286
  225.4 1.0 copy-start.1
  228.2 21.5 %copy-start.8 = (s32[512,128]{1,0:T(8,128)S(1)}, s32[512,128]{1,0:T(8,128)}, u32[]{:S(2)}) copy-start(s32[512,128]{1,0:T(8,128)} %get-tuple-element.58.col_ref) | copy-start | bytes 786436
  228.2 31.0 %all-to-all-start.5 = ((bf16[32,32,512]{2,1,0:T(8,128)(2,1)}), bf16[32,32,512]{2,1,0:T(8,128)(2,1)S(1)}, u32[]{:S(2)}, u32[]{:S(2)}) async-start(bf16[32,32,512]{2,1,0:T(8,128)(2,1)} %bitcast.20), calls=%async_computation.6 | async-start | bytes 2097152 | tf_op jit(solution)/shard_map/all_to_all | solution.py:269
  231.6 15.0 %collective-permute-start.20 = (bf16[128,512]{1,0:T(8,128)(2,1)S(1)}, bf16[128,512]{1,0:T(8,128)(2,1)S(1)}, u32[]{:S(2)}, u32[]{:S(2)}) collective-permute-start(bf16[128,512]{1,0:T(8,128)(2,1)S(1)} %bitcast.32), channel_id=1, source_target_pairs={{0,24},{8,16},{16,8},{24,0},{1,25},{9,17},{17,9},{25,1},{2,26},{10... | collective-permute-start | bytes 393224 | tf_op jit(solution)/shard_map/ppermute | solution.py:283
  234.4 13.9 %collective-permute-start.19 = (bf16[128,512]{1,0:T(8,128)(2,1)S(1)}, bf16[128,512]{1,0:T(8,128)(2,1)S(1)}, u32[]{:S(2)}, u32[]{:S(2)}) collective-permute-start(bf16[128,512]{1,0:T(8,128)(2,1)S(1)} %bitcast.33), channel_id=1, source_target_pairs={{0,16},{8,24},{16,0},{24,8},{1,17},{9,25},{17,1},{25,9},{2,18},{10... | collective-permute-start | bytes 393224 | tf_op jit(solution)/shard_map/ppermute | solution.py:283
  234.9 14.1 %collective-permute-start.18 = (bf16[128,512]{1,0:T(8,128)(2,1)S(1)}, bf16[128,512]{1,0:T(8,128)(2,1)S(1)}, u32[]{:S(2)}, u32[]{:S(2)}) collective-permute-start(bf16[128,512]{1,0:T(8,128)(2,1)S(1)} %bitcast.34), channel_id=1, source_target_pairs={{0,8},{8,0},{16,24},{24,16},{1,9},{9,1},{17,25},{25,17},{2,10},{10... | collective-permute-start | bytes 393224 | tf_op jit(solution)/shard_map/ppermute | solution.py:283
  249.6 2.0 collective-permute-start.21
Sparse Core Ops, SparseCore 0:
  47.8 44.7 all-gather.1
  174.1 51.2 reduce-scatter.1

commit v9 on v8

--- a/solution.py
+++ b/solution.py
@@ -68,32 +68,27 @@
     out_ref[...] = dot(slots_onehot(dest * cap + rank, out_ref.shape[0]), value_ref[...]).astype(BF)
 
 
-def index_kernel(
-    cap, ways, nodes_ref, position_ref, degree_ref, cot_ref, cot_out, own_col, node_row, node_col, turned_row, turned_col
-):
+def index_kernel(cap, ways, nodes_ref, position_ref, degree_ref, cot_ref, cot_out, degree_out, own_row, node_row, turned_row):
     n = nodes_ref.shape[1]
-    width = cot_ref.shape[1]
+    devices = degree_out.shape[0]
     dest, rank = own_slots(nodes_ref[...], cap)
     flat = dest * cap + rank
-    own_col[...] = as_column(flat)
-    packing = slots_onehot(flat, cot_out.shape[0])
-    cot_out[:, :width] = dot(packing, cot_ref[...]).astype(BF)
-    cot_out[:, width:] = dot(packing, as_column(degree_ref[...].astype(F32)).astype(BF)).astype(BF)
+    own_row[...] = jnp.broadcast_to(flat, own_row.shape)
+    cot_out[...] = dot(slots_onehot(flat, cot_out.shape[0]), cot_ref[...]).astype(BF)
+    by_dest = jnp.where(lax.broadcasted_iota(jnp.int32, (devices, n), 0) == dest, degree_ref[...].astype(F32), 0.0)
+    degree_out[...] = dot(by_dest.astype(BF), entries_onehot(as_column(rank), cap))
     position = position_ref[...]
     source = block_of(position, n)
     rank = rank_row(source, position)
-    place = source * cap + rank
-    node_row[...] = jnp.broadcast_to(place, node_row.shape)
-    node_col[...] = as_column(place)
+    node_row[...] = jnp.broadcast_to(source * cap + rank, node_row.shape)
     across = cot_out.shape[0] // (cap * ways)
     down = block_of(source, across)
     turned = ((source - down * across) * ways + down) * cap + rank
     turned_row[...] = jnp.broadcast_to(turned, turned_row.shape)
-    turned_col[...] = as_column(turned)
-
-
-def unpack_kernel(col_ref, value_ref, out_ref):
-    out_ref[...] = dot(entries_onehot(col_ref[...], value_ref.shape[0]), value_ref[...]).astype(BF)
+
+
+def unpack_kernel(row_ref, value_ref, out_ref):
+    out_ref[...] = dot(entries_onehot(as_column(row_ref[...][:1]), value_ref.shape[0]), value_ref[...]).astype(BF)
 
 
 def spmm_kernel(ways, cols_ref, group_ref, x_ref, *refs):
@@ -160,25 +155,31 @@
     right_out[half:, :] = right_ref[half:, :]
 
 
-def prepare_kernel(x_ref, cot_ref, col_ref, self_ref, base_out, cot_out):
+def prepare_kernel(x_ref, degree_ref, row_ref, self_ref, base_out, degree_out):
+    devices, cap = degree_ref.shape
     base_out[...] = dot(x_ref[...], self_ref[...])
-    cot_out[...] = dot(entries_onehot(col_ref[...], cot_ref.shape[0]), cot_ref[...]).astype(BF)
+    place = as_column(row_ref[...][:1])[:, :1]
+    source = block_of(place, cap)
+    rank = place - source * cap
+    degrees = dot(entries_onehot(source, devices), degree_ref[...].astype(BF))
+    picked = lax.broadcasted_iota(jnp.int32, degrees.shape, 1) == rank
+    degrees = jnp.sum(jnp.where(picked, degrees, 0.0), axis=1, keepdims=True)
+    degree_out[...] = jnp.broadcast_to(degrees, degree_out.shape)
 
 
 def layer_kernel(ways, *refs):
     terms = refs[:ways]
-    (base_ref, cot_ref, neigh_ref, hidden_out, slopes_out, agg_out, spread_out) = refs[ways:]
-    width = base_ref.shape[1]
+    (base_ref, degree_ref, cot_ref, neigh_ref, hidden_out, slopes_out, agg_out, spread_out) = refs[ways:]
     summed = terms[0][...].astype(F32)
     for s in range(1, ways):
         summed = summed + terms[s][...].astype(F32)
-    degrees = cot_ref[:, width : width + 128].astype(F32)[:, :1]
+    degrees = degree_ref[...][:, :1]
     agg = (summed / degrees).astype(BF)
     agg_out[...] = agg
     preact = base_ref[...] + dot(agg, neigh_ref[...])
     gate = jax.nn.sigmoid(preact)
     hidden_out[...] = (preact * gate).astype(BF)
-    slopes = (cot_ref[:, :width].astype(F32) * gate * (1.0 + preact * (1.0 - gate))).astype(BF)
+    slopes = (cot_ref[...].astype(F32) * gate * (1.0 + preact * (1.0 - gate))).astype(BF)
     slopes_out[...] = slopes
     spread_out[...] = (dot(slopes, neigh_ref[...], 1, 1) / degrees).astype(BF)
 
@@ -323,18 +324,11 @@
         name="pack_features",
     )(nodes, features)
     inbound = relay(packed)
-    cot_packed, own_col, node_row, node_col, turned_row, turned_col = call(
+    cot_packed, degree_packed, own_row, node_row, turned_row = call(
         functools.partial(index_kernel, cap, ways),
-        out_shape=(
-            shape(slots, width + 128),
-            shape(rows, 128, jnp.int32),
-            shape(8, rows, jnp.int32),
-            shape(rows, 128, jnp.int32),
-            shape(8, rows, jnp.int32),
-            shape(rows, 128, jnp.int32),
-        ),
+        out_shape=(shape(slots, width), shape(devices, cap, F32)) + (shape(8, rows, jnp.int32),) * 3,
         in_specs=[VMEM] * 4,
-        out_specs=(VMEM,) * 6,
+        out_specs=(VMEM,) * 5,
         cost_estimate=cost(2 * slots * slab, 6 * slab),
         mib=LARGE,
         name="index_cotangent",
@@ -347,13 +341,23 @@
         out_specs=VMEM,
         cost_estimate=cost(2 * slots * slab, 6 * slab),
         name="unpack_features",
-    )(node_col, inbound)
-    cot_packed, x_node, cols, groups, core, others = lax.optimization_barrier(
-        (cot_packed, x_node, cols, groups, core, others)
+    )(node_row, inbound)
+    cot_packed, degree_packed, x_node, cols, groups, core, others = lax.optimization_barrier(
+        (cot_packed, degree_packed, x_node, cols, groups, core, others)
     )
     x_cols = lax.all_gather(x_node, "col", axis=0, tiled=True)
     cot_mid = turn(row_phase(cot_packed), row_devices, col_devices)
-    x_cols, cot_mid = lax.optimization_barrier((x_cols, cot_mid))
+    degree_in = lax.all_to_all(degree_packed, everyone, split_axis=0, concat_axis=0, tiled=True)
+    base, degrees = call(
+        prepare_kernel,
+        out_shape=(shape(rows, width, F32), shape(rows, 128, F32)),
+        in_specs=[VMEM] * 4,
+        out_specs=(VMEM,) * 2,
+        cost_estimate=cost(2 * slab * width, 2 * slab * 4),
+        mib=LARGE,
+        name="prepare",
+    )(x_node, degree_in, node_row, self_weight)
+    x_cols, cot_mid, base, degrees = lax.optimization_barrier((x_cols, cot_mid, base, degrees))
     cot_in = col_phase(cot_mid)
 
     spmm_flops = 2 * masks.size * width * WEIGHT
@@ -392,15 +396,14 @@
         terms = [partials[0], across(left, 1), across(right, 2)]
     else:
         terms = [partials[0]] + [across(partials[s], s) for s in range(1, ways)]
-    base, cot_node = call(
-        prepare_kernel,
-        out_shape=(shape(rows, width, F32), shape(rows, width + 128)),
-        in_specs=[VMEM] * 4,
-        out_specs=(VMEM,) * 2,
-        cost_estimate=cost(6 * slab * width, 2 * slab * 8),
-        mib=LARGE,
-        name="prepare",
-    )(x_node, cot_in, turned_col, self_weight)
+    cot_node = call(
+        unpack_kernel,
+        out_shape=shape(rows, width),
+        in_specs=[VMEM] * 2,
+        out_specs=VMEM,
+        cost_estimate=cost(2 * slots * slab, 6 * slab),
+        name="unpack_cotangent",
+    )(turned_row, cot_in)
 
     def by_rows(columns):
         return pl.BlockSpec((half, columns), lambda i: (i, 0))
@@ -409,12 +412,12 @@
         functools.partial(layer_kernel, len(terms)),
         grid=(2,),
         out_shape=(shape(rows, width),) * 4,
-        in_specs=[by_rows(width)] * (len(terms) + 1) + [by_rows(width + 128), VMEM],
+        in_specs=[by_rows(width)] * (len(terms) + 1) + [by_rows(128), by_rows(width), VMEM],
         out_specs=(by_rows(width),) * 4,
         cost_estimate=cost(8 * slab * width, 2 * slab * (len(terms) + 9)),
         mib=LARGE,
         name="layer",
-    )(*terms, base, cot_node, neigh_weight)
+    )(*terms, base, degrees, cot_node, neigh_weight)
     hidden_packed = call(
         pack_node_kernel,
         out_shape=shape(slots, width),
@@ -496,7 +499,7 @@
             out_specs=VMEM,
             cost_estimate=cost(2 * slots * slab, 6 * slab),
             name="unpack_owner",
-        )(own_col, value)
+        )(own_row, value)
 
     hidden_own = unpack_own(hidden_in)
     grad_own = unpack_own(grad_in)

time: 268 us -> 268 us (level)
  blocking collectives: 19.5 us -> 10.2 us
  waiting for transfers between devices: 127 us -> 131 us
    all_to_all x1 -> x2, waiting for transfers between devices: 0.01 us -> 11.3 us  [row_phase(): lax.all_to_all(there, 'row', split_axis=0, concat_axis=0, tiled=True)]
    all_to_all x1, blocking collectives: 19.5 us -> 10.2 us  [on_device(): lax.all_to_all(degree_packed, everyone, split_axis=0, concat_axis=0, tile...]
    all_gather x1, waiting for transfers between devices: 24.2 us -> 16.1 us  [on_device(): x_cols = lax.all_gather(x_node, 'col', axis=0, tiled=True)]
    all_to_all x2, waiting for transfers between devices: 13.2 us -> 7.38 us  [col_phase(): lax.all_to_all(there, 'col', split_axis=0, concat_axis=0, tiled=True)]
    ppermute x14, waiting for transfers between devices: 41.9 us -> 47.1 us  [across(): return lax.ppermute(value, 'row', [(i, i ^ s) for i in range(ways)])]
    all_to_all x1 -> x2, starting transfers between devices: 3.84 us -> 7.22 us  [row_phase(): lax.all_to_all(there, 'row', split_axis=0, concat_axis=0, tiled=True)]
    unnamed x41 -> x39, local copies, waits for them, and re-layouts: 5.74 us -> 7.97 us
  transfers between devices with their start and end apart: 29 -> 30, of which waited for: 24 -> 27; matrix products, arithmetic and copies ran while one was open for 2% -> 2% of each run, Pallas kernels for 14% -> 14%
where the time goes in v9:
time: 268 us; the launch traced here: 267 us
  waiting for transfers between devices  131 us (49%)
  starting transfers between devices  50.3 us (19%)
  Pallas kernels  49.4 us (18%)
  between operations  14.3 us (5%)
  local copies, waits for them, and re-layouts  11.8 us (4%)
  blocking collectives  10.2 us (4%)
    ppermute x14, waiting for transfers between devices, across(): return lax.ppermute(value, 'row', [(i, i ^ s) for i in range(ways)])  47.1 us
    all_to_all x2, waiting for transfers between devices, relay(): lax.all_to_all(there, everyone, split_axis=0, concat_axis=0, tiled=True)  28.4 us
    all_gather x1, waiting for transfers between devices, on_device(): x_cols = lax.all_gather(x_node, 'col', axis=0, tiled=True)  16.1 us
    ppermute x14, starting transfers between devices, across(): return lax.ppermute(value, 'row', [(i, i ^ s) for i in range(ways)])  15.4 us
    all_to_all x2, waiting for transfers between devices, row_phase(): lax.all_to_all(there, 'row', split_axis=0, concat_axis=0, tiled=True)  11.3 us
    all_to_all x2, starting transfers between devices, relay(): lax.all_to_all(there, everyone, split_axis=0, concat_axis=0, tiled=True)  10.7 us
    pallas_call x1, Pallas kernels, on_device(): call(functools.partial(spmm_back_kernel, ways, pieces), grid_spec=pltpu.P...  10.5 us
    all_to_all x1, blocking collectives, on_device(): lax.all_to_all(degree_packed, everyone, split_axis=0, concat_axis=0, tile...  10.2 us
  transfers between devices with their start and end apart: 30, of which 27 were waited for; matrix products, arithmetic and copies ran while one was open for 2% of the time, Pallas kernels for 14%

profile of v9, /device:TPU:0, one launch (start us, length us, event | category | flops | bytes accessed | tf_op | source)
XLA Modules:
  0.0 267.2 jit_solution(6036865734416806928)
XLA Ops:
  7.2 3.1 %pack_features.1 = bf16[1024,512]{1,0:T(8,128)(2,1)} custom-call(s32[1,512]{1,0:T(1,128)} %bitcast.56, bf16[512,512]{1,0:T(8,128)(2,1)} %value_ref.1), custom_call_target="tpu_custom_call" | custom-call | flops 536870912 | bytes 1572864 | tf_op jit(solution)/shard_map/pack_features/pallas_call | solution.py:317
  10.3 7.3 %all-to-all-start = ((bf16[32,32,512]{2,1,0:T(8,128)(2,1)}), bf16[32,32,512]{2,1,0:T(8,128)(2,1)S(1)}, u32[]{:S(2)}, u32[]{:S(2)}) async-start(bf16[32,32,512]{2,1,0:T(8,128)(2,1)} %bitcast.44), calls=%async_computation | async-start | bytes 2097152 | tf_op jit(solution)/shard_map/all_to_all | solution.py:270
  17.7 0.8 copy.20
  19.1 3.3 %index_cotangent.1 = (bf16[1024,512]{1,0:T(8,128)(2,1)}, f32[32,32]{1,0:T(8,128)}, s32[8,512]{1,0:T(8,128)}, s32[8,512]{1,0:T(8,128)}, s32[8,512]{1,0:T(8,128)}) custom-call(s32[1,512]{1,0:T(1,128)} %bitcast.57, s32[1,512]{1,0:T(1,128)} %bitcast.58, s32[1,512]{1,0:T(1,128)} %bitcast.59, bf16[512,512]{1,0:T(8,128)(2,1)} %cot_ref.1), custom_call_target="tpu_custom_call" | custom-call | flops 536870912 | bytes 1572864 | tf_op jit(solution)/shard_map/index_cotangent/pallas_call | solution.py:327
  23.0 22.2 %all-to-all-done = bf16[32,32,512]{2,1,0:T(8,128)(2,1)S(1)} async-done(((bf16[32,32,512]{2,1,0:T(8,128)(2,1)}), bf16[32,32,512]{2,1,0:T(8,128)(2,1)S(1)}, u32[]{:S(2)}, u32[]{:S(2)}) %all-to-all-start) | async-done | bytes 1048608 | tf_op jit(solution)/shard_map/all_to_all | solution.py:270
  45.9 1.8 unpack_features.1.x_ref
  47.7 10.2 %all_to_all.41 = f32[32,1,32]{2,1,0:T(1,128)} all-to-all(f32[32,1,32]{2,1,0:T(1,128)} %bitcast.47), channel_id=1, replica_groups=mesh['row'=4,'col'=8] {'row','col'}, dimensions={0} | all-to-all | bytes 8192 | tf_op jit(solution)/shard_map/all_to_all | solution.py:350
  57.9 3.5 %all-to-all-start.1 = ((bf16[4,256,512]{2,1,0:T(8,128)(2,1)}), bf16[4,256,512]{2,1,0:T(8,128)(2,1)S(1)}, u32[]{:S(2)}, u32[]{:S(2)}) async-start(bf16[4,256,512]{2,1,0:T(8,128)(2,1)} %bitcast.45), calls=%async_computation.1 | async-start | bytes 2097152 | tf_op jit(solution)/shard_map/all_to_all | solution.py:274
  61.4 2.8 %prepare.1 = (f32[512,512]{1,0:T(8,128)}, f32[512,128]{1,0:T(8,128)}) custom-call(bf16[512,512]{1,0:T(8,128)(2,1)} %unpack_features.1.x_ref, f32[32,32]{1,0:T(8,128)} %bitcast.46, s32[8,512]{1,0:T(8,128)} %get-tuple-element.63.row_ref, bf16[512,512]{1,0:T(8,128)(2,1)} %self_ref.3), custom_call_target="tpu_custom_call" | custom-call | flops 268435456 | bytes 2097152 | tf_op jit(solution)/shard_map/prepare/pallas_call | solution.py:351
  64.3 11.3 %all-to-all-done.1 = bf16[4,256,512]{2,1,0:T(8,128)(2,1)S(1)} async-done(((bf16[4,256,512]{2,1,0:T(8,128)(2,1)}), bf16[4,256,512]{2,1,0:T(8,128)(2,1)S(1)}, u32[]{:S(2)}, u32[]{:S(2)}) %all-to-all-start.1) | async-done | bytes 1048608 | tf_op jit(solution)/shard_map/all_to_all | solution.py:274
  75.5 1.0 copy.21
  76.6 16.1 %all-gather.2.cloned.1.call-done.x_ref = bf16[4096,512]{1,0:T(8,128)(2,1)} async-done(((bf16[512,512]{1,0:T(8,128)(2,1)}), bf16[4096,512]{1,0:T(8,128)(2,1)}) %all-gather.2.cloned.1.call-update) | async-done | bytes 4194320 | tf_op jit(solution)/shard_map/all_gather | solution.py:348
  92.7 3.6 %all-to-all-start.3 = ((bf16[8,128,512]{2,1,0:T(8,128)(2,1)}), bf16[8,128,512]{2,1,0:T(8,128)(2,1)S(1)}, u32[]{:S(2)}, u32[]{:S(2)}) async-start(bf16[8,128,512]{2,1,0:T(8,128)(2,1)} %bitcast.14), calls=%async_computation.3 | async-start | bytes 2097152 | tf_op jit(solution)/shard_map/all_to_all | solution.py:278
  96.2 7.6 %spmm.1 = (bf16[512,512]{1,0:T(8,128)(2,1)}, bf16[512,512]{1,0:T(8,128)(2,1)}, bf16[512,512]{1,0:T(8,128)(2,1)}, bf16[512,512]{1,0:T(8,128)(2,1)}) custom-call(s32[128]{0:T(128)} %reshape_squeeze.3.cols_ref, s32[4]{0:T(128)} %get-tuple-element.65.group_ref.index_ref, bf16[4096,512]{1,0:T(8,128)(2,1)} %all-gather.2.cloned.1.call-done.x_ref, ...), custom_call_target="tpu_custom_call" | custom-call | flops 12884901888 | bytes 10485760 | tf_op jit(solution)/shard_map/spmm/pallas_call | solution.py:373
  103.9 1.1 fusion
  105.0 1.5 collective-permute-start.1
  106.4 1.5 collective-permute-start
  107.9 5.8 %collective-permute-done.1.bottom_ref = bf16[256,512]{1,0:T(8,128)(2,1)S(1)} collective-permute-done((bf16[256,512]{1,0:T(8,128)(2,1)S(1)}, bf16[256,512]{1,0:T(8,128)(2,1)S(1)}, u32[]{:S(2)}, u32[]{:S(2)}) %collective-permute-start.1) | collective-permute-done | bytes 262176 | tf_op jit(solution)/shard_map/ppermute | solution.py:284
  113.7 1.2 collective-permute-done.top_ref
  114.9 1.0 copy-done.2
  115.9 1.0 copy-done.3
  117.1 1.5 collective-permute-start.2
  119.2 3.5 %all-to-all-done.3 = bf16[8,128,512]{2,1,0:T(8,128)(2,1)S(1)} async-done(((bf16[8,128,512]{2,1,0:T(8,128)(2,1)}), bf16[8,128,512]{2,1,0:T(8,128)(2,1)S(1)}, u32[]{:S(2)}, u32[]{:S(2)}) %all-to-all-start.3) | async-done | bytes 1048608 | tf_op jit(solution)/shard_map/all_to_all | solution.py:278
  122.8 1.0 unpack_cotangent.1.refs_5_
  123.8 0.8 copy-done.8
  124.6 5.8 %collective-permute-done.2.refs_1_ = bf16[512,512]{1,0:T(8,128)(2,1)S(1)} collective-permute-done((bf16[512,512]{1,0:T(8,128)(2,1)S(1)}, bf16[512,512]{1,0:T(8,128)(2,1)S(1)}, u32[]{:S(2)}, u32[]{:S(2)}) %collective-permute-start.2) | collective-permute-done | bytes 524320 | tf_op jit(solution)/shard_map/ppermute | solution.py:284
  130.4 1.2 collective-permute-done.3.refs_2_
  131.6 0.8 copy-done.16
  132.4 4.2 %layer.1 = (bf16[512,512]{1,0:T(8,128)(2,1)}, bf16[512,512]{1,0:T(8,128)(2,1)}, bf16[512,512]{1,0:T(8,128)(2,1)}, bf16[512,512]{1,0:T(8,128)(2,1)}) custom-call(bf16[512,512]{1,0:T(8,128)(2,1)} %get-tuple-element.72.refs_0_, bf16[512,512]{1,0:T(8,128)(2,1)} %copy-done.15, bf16[512,512]{1,0:T(8,128)(2,1)} %copy-done.16, ...), custom_call_target="tpu_custom_call" | custom-call | flops 1073741824 | bytes 6291456 | tf_op jit(solution)/shard_map/layer/pallas_call | solution.py:411
  137.8 1.0 copy-done.9
  138.8 1.7 pack_hidden.1
  140.5 4.4 %all-to-all-start.4 = ((bf16[8,128,512]{2,1,0:T(8,128)(2,1)}), bf16[8,128,512]{2,1,0:T(8,128)(2,1)S(1)}, u32[]{:S(2)}, u32[]{:S(2)}) async-start(bf16[8,128,512]{2,1,0:T(8,128)(2,1)} %bitcast.16), calls=%async_computation.4 | async-start | bytes 2097152 | tf_op jit(solution)/shard_map/all_to_all | solution.py:278
  144.9 4.0 %collective-permute-done.5.refs_2_ = bf16[512,512]{1,0:T(8,128)(2,1)S(1)} collective-permute-done((bf16[512,512]{1,0:T(8,128)(2,1)}, bf16[512,512]{1,0:T(8,128)(2,1)S(1)}, u32[]{:S(2)}, u32[]{:S(2)}) %collective-permute-start.5) | collective-permute-done | bytes 524320 | tf_op jit(solution)/shard_map/ppermute | solution.py:284
  150.1 1.4 collective-permute-start.7
  151.5 3.8 %terms.1 = (bf16[512,512]{1,0:T(8,128)(2,1)}, bf16[512,512]{1,0:T(8,128)(2,1)}, f32[512,512]{1,0:T(8,128)}) custom-call(s32[1]{0:T(128)} %bitcast.5.core_ref, bf16[512,512]{1,0:T(8,128)(2,1)} %unpack_features.1.x_ref, bf16[512,512]{1,0:T(8,128)(2,1)} %get-tuple-element.87.agg_ref, bf16[512,512]{1,0:T(8,128)(2,1)} %get-tuple-element.88.slopes_ref, ...), custom_call_target="tpu_custom_call" | custom-call | flops 805306368 | bytes 4718592 | tf_op jit(solution)/shard_map/terms/pallas_call | solution.py:436
  157.2 10.5 %spmm_back.1 = bf16[4096,512]{1,0:T(8,128)(2,1)} custom-call(s32[128]{0:T(128)} %reshape_squeeze.3.cols_ref, s32[4]{0:T(128)} %get-tuple-element.65.group_ref.index_ref, bf16[512,512]{1,0:T(8,128)(2,1)} %get-tuple-element.92.refs_0_, bf16[512,512]{1,0:T(8,128)(2,1)} %copy-done.13, bf16[512,512]{1,0:T(8,128)(2,1)} %copy-done.12, bf16[256,512]{1,0:T(8,128)(2,1)} %copy-done.17, ...), custom_call_target="tpu_custom_call" | custom-call | flops 12884901888 | bytes 10485760 | tf_op jit(solution)/shard_map/spmm_back/pallas_call | solution.py:446
  167.7 3.8 %all-to-all-done.4 = bf16[8,128,512]{2,1,0:T(8,128)(2,1)S(1)} async-done(((bf16[8,128,512]{2,1,0:T(8,128)(2,1)}), bf16[8,128,512]{2,1,0:T(8,128)(2,1)S(1)}, u32[]{:S(2)}, u32[]{:S(2)}) %all-to-all-start.4) | async-done | bytes 1048608 | tf_op jit(solution)/shard_map/all_to_all | solution.py:278
  171.5 1.0 copy.23
  172.6 3.7 %all-to-all-start.5 = ((bf16[4,256,512]{2,1,0:T(8,128)(2,1)}), bf16[4,256,512]{2,1,0:T(8,128)(2,1)S(1)}, u32[]{:S(2)}, u32[]{:S(2)}) async-start(bf16[4,256,512]{2,1,0:T(8,128)(2,1)} %bitcast.41), calls=%async_computation.5 | async-start | bytes 2097152 | tf_op jit(solution)/shard_map/all_to_all | solution.py:274
  176.4 1.9 collective-permute-done.8.refs_1_
  178.3 0.8 split_sum.3
  179.1 1.9 collective-permute-start.9
  181.0 1.5 collective-permute-start.10
  182.6 11.4 %collective-permute-done.9.refs_1_ = bf16[128,512]{1,0:T(8,128)(2,1)S(1)} collective-permute-done((bf16[128,512]{1,0:T(8,128)(2,1)S(1)}, bf16[128,512]{1,0:T(8,128)(2,1)S(1)}, u32[]{:S(2)}, u32[]{:S(2)}) %collective-permute-start.9) | collective-permute-done | bytes 131104 | tf_op jit(solution)/shard_map/ppermute | solution.py:284
  194.0 2.3 collective-permute-done.11.refs_3_
  197.0 2.2 collective-permute-start.13
  199.3 2.1 collective-permute-start.14
  201.7 2.4 collective-permute-done.13.refs_2_
  204.0 1.8 collective-permute-done.14.refs_3_
  205.9 2.2 collective-permute-start.17
  208.1 2.3 collective-permute-start.15
  210.3 2.3 collective-permute-done.17.refs_3_
  212.6 1.8 collective-permute-done.16.refs_2_
  215.0 9.7 %reduce-scatter.2.cloned.1.call-done.neigh_ref = bf16[512,512]{1,0:T(8,128)(2,1)} async-done(((bf16[4096,512]{1,0:T(8,128)(2,1)}), bf16[512,512]{1,0:T(8,128)(2,1)}) %reduce-scatter.2.cloned.1.call-update) | async-done | bytes 524304 | tf_op jit(solution)/shard_map/reduce_scatter | solution.py:466
  224.7 1.0 copy-done.1
  225.8 1.8 join_pack.1
  227.5 3.4 %all-to-all-start.6 = ((bf16[32,32,512]{2,1,0:T(8,128)(2,1)}), bf16[32,32,512]{2,1,0:T(8,128)(2,1)S(1)}, u32[]{:S(2)}, u32[]{:S(2)}) async-start(bf16[32,32,512]{2,1,0:T(8,128)(2,1)} %bitcast.23), calls=%async_computation.7 | async-start | bytes 2097152 | tf_op jit(solution)/shard_map/all_to_all | solution.py:270
  230.9 2.7 %collective-permute-start.20 = (bf16[128,512]{1,0:T(8,128)(2,1)S(1)}, bf16[128,512]{1,0:T(8,128)(2,1)S(1)}, u32[]{:S(2)}, u32[]{:S(2)}) collective-permute-start(bf16[128,512]{1,0:T(8,128)(2,1)S(1)} %bitcast.37), channel_id=1, source_target_pairs={{0,24},{8,16},{16,8},{24,0},{1,25},{9,17},{17,9},{25,1},{2,26},{10... | collective-permute-start | bytes 393224 | tf_op jit(solution)/shard_map/ppermute | solution.py:284
  234.5 11.5 %collective-permute-done.20.refs_3_ = bf16[128,512]{1,0:T(8,128)(2,1)S(1)} collective-permute-done((bf16[128,512]{1,0:T(8,128)(2,1)S(1)}, bf16[128,512]{1,0:T(8,128)(2,1)S(1)}, u32[]{:S(2)}, u32[]{:S(2)}) %collective-permute-start.20) | collective-permute-done | bytes 131104 | tf_op jit(solution)/shard_map/ppermute | solution.py:284
  246.0 1.6 collective-permute-done.19.refs_2_
  249.0 1.8 unpack_owner.2
  250.9 1.5 final.1
  252.3 6.2 %all-to-all-done.6 = bf16[32,32,512]{2,1,0:T(8,128)(2,1)S(1)} async-done(((bf16[32,32,512]{2,1,0:T(8,128)(2,1)}), bf16[32,32,512]{2,1,0:T(8,128)(2,1)S(1)}, u32[]{:S(2)}, u32[]{:S(2)}) %all-to-all-start.6) | async-done | bytes 1048608 | tf_op jit(solution)/shard_map/all_to_all | solution.py:270
  258.5 1.8 unpack_owner.3
  (65 shorter events, 11.1 us)
Async XLA Ops:
  10.3 34.9 %all-to-all-start = ((bf16[32,32,512]{2,1,0:T(8,128)(2,1)}), bf16[32,32,512]{2,1,0:T(8,128)(2,1)S(1)}, u32[]{:S(2)}, u32[]{:S(2)}) async-start(bf16[32,32,512]{2,1,0:T(8,128)(2,1)} %bitcast.44), calls=%async_computation | async-start | bytes 2097152 | tf_op jit(solution)/shard_map/all_to_all | solution.py:270
  17.6 75.1 %all-gather.2.cloned.1.call-start = ((), (), s32[]{:S(2)}) async-start(), calls=%async_computation.8 | async-start | bytes 4718592 | tf_op jit(solution)/shard_map/all_gather | solution.py:348
  45.2 0.7 copy-start.5
  57.9 17.6 %all-to-all-start.1 = ((bf16[4,256,512]{2,1,0:T(8,128)(2,1)}), bf16[4,256,512]{2,1,0:T(8,128)(2,1)S(1)}, u32[]{:S(2)}, u32[]{:S(2)}) async-start(bf16[4,256,512]{2,1,0:T(8,128)(2,1)} %bitcast.45), calls=%async_computation.1 | async-start | bytes 2097152 | tf_op jit(solution)/shard_map/all_to_all | solution.py:274
  92.7 30.1 %all-to-all-start.3 = ((bf16[8,128,512]{2,1,0:T(8,128)(2,1)}), bf16[8,128,512]{2,1,0:T(8,128)(2,1)S(1)}, u32[]{:S(2)}, u32[]{:S(2)}) async-start(bf16[8,128,512]{2,1,0:T(8,128)(2,1)} %bitcast.14), calls=%async_computation.3 | async-start | bytes 2097152 | tf_op jit(solution)/shard_map/all_to_all | solution.py:278
  96.2 26.5 %copy-start.11 = (s32[8,512]{1,0:T(8,128)S(1)}, s32[8,512]{1,0:T(8,128)}, u32[]{:S(2)}) copy-start(s32[8,512]{1,0:T(8,128)} %get-tuple-element.80.row_ref) | copy-start | bytes 49156
  105.0 8.8 %collective-permute-start.1 = (bf16[256,512]{1,0:T(8,128)(2,1)S(1)}, bf16[256,512]{1,0:T(8,128)(2,1)S(1)}, u32[]{:S(2)}, u32[]{:S(2)}) collective-permute-start(bf16[256,512]{1,0:T(8,128)(2,1)S(1)} %get-tuple-element.116), channel_id=1, source_target_pairs={{0,16},{8,24},{16,0},{24,8},{1,17},{9,25},{17,1},{25,9},{2,18},{10... | collective-permute-start | bytes 786440 | tf_op jit(solution)/shard_map/ppermute | solution.py:284
  106.4 8.4 %collective-permute-start = (bf16[256,512]{1,0:T(8,128)(2,1)S(1)}, bf16[256,512]{1,0:T(8,128)(2,1)S(1)}, u32[]{:S(2)}, u32[]{:S(2)}) collective-permute-start(bf16[256,512]{1,0:T(8,128)(2,1)S(1)} %get-tuple-element.117), channel_id=1, source_target_pairs={{0,8},{8,0},{16,24},{24,16},{1,9},{9,1},{17,25},{25,17},{2,10},{10... | collective-permute-start | bytes 786440 | tf_op jit(solution)/shard_map/ppermute | solution.py:284
  114.9 1.0 copy-start.2
  115.9 1.0 copy-start.3
  117.1 13.3 %collective-permute-start.2 = (bf16[512,512]{1,0:T(8,128)(2,1)S(1)}, bf16[512,512]{1,0:T(8,128)(2,1)S(1)}, u32[]{:S(2)}, u32[]{:S(2)}) collective-permute-start(bf16[512,512]{1,0:T(8,128)(2,1)S(1)} %get-tuple-element.76), channel_id=1, source_target_pairs={{0,8},{8,0},{16,24},{24,16},{1,9},{9,1},{17,25},{25,17},{2,10},{10... | collective-permute-start | bytes 1572872 | tf_op jit(solution)/shard_map/ppermute | solution.py:284
  118.6 13.0 %collective-permute-start.3 = (bf16[512,512]{1,0:T(8,128)(2,1)S(1)}, bf16[512,512]{1,0:T(8,128)(2,1)S(1)}, u32[]{:S(2)}, u32[]{:S(2)}) collective-permute-start(bf16[512,512]{1,0:T(8,128)(2,1)S(1)} %get-tuple-element.77), channel_id=1, source_target_pairs={{0,16},{8,24},{16,0},{24,8},{1,17},{9,25},{17,1},{25,9},{2,18},{10... | collective-permute-start | bytes 1572872 | tf_op jit(solution)/shard_map/ppermute | solution.py:284
  123.8 0.8 copy-start.8
  130.4 1.2 copy-start.15
  131.6 0.8 copy-start.16
  136.6 12.3 %collective-permute-start.5 = (bf16[512,512]{1,0:T(8,128)(2,1)}, bf16[512,512]{1,0:T(8,128)(2,1)S(1)}, u32[]{:S(2)}, u32[]{:S(2)}) collective-permute-start(bf16[512,512]{1,0:T(8,128)(2,1)} %get-tuple-element.92.refs_0_), channel_id=1, source_target_pairs={{0,16},{8,24},{16,0},{24,8},{1,17},{9,25},{17,1},{25,9},{2,18},{10... | collective-permute-start | bytes 1572872 | tf_op jit(solution)/shard_map/ppermute | solution.py:284
  137.3 12.2 %collective-permute-start.4 = (bf16[512,512]{1,0:T(8,128)(2,1)}, bf16[512,512]{1,0:T(8,128)(2,1)S(1)}, u32[]{:S(2)}, u32[]{:S(2)}) collective-permute-start(bf16[512,512]{1,0:T(8,128)(2,1)} %get-tuple-element.92.refs_0_), channel_id=1, source_target_pairs={{0,8},{8,0},{16,24},{24,16},{1,9},{9,1},{17,25},{25,17},{2,10},{10... | collective-permute-start | bytes 1572872 | tf_op jit(solution)/shard_map/ppermute | solution.py:284
  137.8 1.0 copy-start.9
  140.5 31.0 %all-to-all-start.4 = ((bf16[8,128,512]{2,1,0:T(8,128)(2,1)}), bf16[8,128,512]{2,1,0:T(8,128)(2,1)S(1)}, u32[]{:S(2)}, u32[]{:S(2)}) async-start(bf16[8,128,512]{2,1,0:T(8,128)(2,1)} %bitcast.16), calls=%async_computation.4 | async-start | bytes 2097152 | tf_op jit(solution)/shard_map/all_to_all | solution.py:278
  144.9 79.8 %reduce-scatter.2.cloned.1.call-start = ((), (), s32[]{:S(2)}) async-start(), calls=%async_computation.9 | async-start | bytes 4718592 | tf_op jit(solution)/shard_map/reduce_scatter | solution.py:466
  148.9 7.6 %copy-start.12 = (bf16[512,512]{1,0:T(8,128)(2,1)}, bf16[512,512]{1,0:T(8,128)(2,1)S(1)}, u32[]{:S(2)}) copy-start(bf16[512,512]{1,0:T(8,128)(2,1)S(1)} %collective-permute-done.5.refs_2_) | copy-start | bytes 1572868
  149.5 7.0 %copy-start.13 = (bf16[512,512]{1,0:T(8,128)(2,1)}, bf16[512,512]{1,0:T(8,128)(2,1)S(1)}, u32[]{:S(2)}) copy-start(bf16[512,512]{1,0:T(8,128)(2,1)S(1)} %collective-permute-done.4.refs_1_) | copy-start | bytes 1572868
  149.5 6.4 %collective-permute-start.6 = (bf16[256,512]{1,0:T(8,128)(2,1)S(1)}, bf16[256,512]{1,0:T(8,128)(2,1)S(1)}, u32[]{:S(2)}, u32[]{:S(2)}) collective-permute-start(bf16[256,512]{1,0:T(8,128)(2,1)S(1)} %slice.14), channel_id=1, source_target_pairs={{0,8},{8,0},{16,24},{24,16},{1,9},{9,1},{17,25},{25,17},{2,10},{10... | collective-permute-start | bytes 786440 | tf_op jit(solution)/shard_map/ppermute | solution.py:284
  150.1 6.4 %collective-permute-start.7 = (bf16[256,512]{1,0:T(8,128)(2,1)S(1)}, bf16[256,512]{1,0:T(8,128)(2,1)S(1)}, u32[]{:S(2)}, u32[]{:S(2)}) collective-permute-start(bf16[256,512]{1,0:T(8,128)(2,1)S(1)} %slice.15), channel_id=1, source_target_pairs={{0,16},{8,24},{16,0},{24,8},{1,17},{9,25},{17,1},{25,9},{2,18},{10... | collective-permute-start | bytes 786440 | tf_op jit(solution)/shard_map/ppermute | solution.py:284
  155.9 0.7 copy-start.17
  156.5 0.7 copy-start.18
  171.5 4.8 %copy-start.14 = (bf16[512,512]{1,0:T(8,128)(2,1)S(1)}, bf16[512,512]{1,0:T(8,128)(2,1)}, u32[]{:S(2)}) copy-start(bf16[512,512]{1,0:T(8,128)(2,1)} %get-tuple-element.102) | copy-start | bytes 1572868
  171.5 6.8 %copy-start.4 = (bf16[512,512]{1,0:T(8,128)(2,1)S(1)}, bf16[512,512]{1,0:T(8,128)(2,1)}, u32[]{:S(2)}) copy-start(bf16[512,512]{1,0:T(8,128)(2,1)} %get-tuple-element.101.refs_0_) | copy-start | bytes 1572868
  171.5 6.8 %copy-start.7 = (s32[4]{0:T(128)S(1)}, s32[4]{0:T(128)}, u32[]{:S(2)}) copy-start(s32[4]{0:T(128)} %get-tuple-element.65.group_ref.index_ref) | copy-start | bytes 52
  171.5 53.2 %copy-start = (f32[512,512]{1,0:T(8,128)S(1)}, f32[512,512]{1,0:T(8,128)}, u32[]{:S(2)}) copy-start(f32[512,512]{1,0:T(8,128)} %get-tuple-element.111.own_ref) | copy-start | bytes 3145732
  171.5 53.2 %copy-start.6 = (s32[8,512]{1,0:T(8,128)S(1)}, s32[8,512]{1,0:T(8,128)}, u32[]{:S(2)}) copy-start(s32[8,512]{1,0:T(8,128)} %get-tuple-element.63.row_ref) | copy-start | bytes 49156
  172.6 54.9 %all-to-all-start.5 = ((bf16[4,256,512]{2,1,0:T(8,128)(2,1)}), bf16[4,256,512]{2,1,0:T(8,128)(2,1)S(1)}, u32[]{:S(2)}, u32[]{:S(2)}) async-start(bf16[4,256,512]{2,1,0:T(8,128)(2,1)} %bitcast.41), calls=%async_computation.5 | async-start | bytes 2097152 | tf_op jit(solution)/shard_map/all_to_all | solution.py:274
  176.3 72.7 %copy-start.10 = (s32[8,512]{1,0:T(8,128)S(1)}, s32[8,512]{1,0:T(8,128)}, u32[]{:S(2)}) copy-start(s32[8,512]{1,0:T(8,128)} %get-tuple-element.60.row_ref) | copy-start | bytes 49156
  176.3 2.0 collective-permute-start.8
  179.1 14.9 %collective-permute-start.9 = (bf16[128,512]{1,0:T(8,128)(2,1)S(1)}, bf16[128,512]{1,0:T(8,128)(2,1)S(1)}, u32[]{:S(2)}, u32[]{:S(2)}) collective-permute-start(bf16[128,512]{1,0:T(8,128)(2,1)S(1)} %get-tuple-element.104), channel_id=1, source_target_pairs={{0,8},{8,0},{16,24},{24,16},{1,9},{9,1},{17,25},{25,17},{2,10},{10... | collective-permute-start | bytes 393224 | tf_op jit(solution)/shard_map/ppermute | solution.py:284
  181.0 13.1 %collective-permute-start.10 = (bf16[128,512]{1,0:T(8,128)(2,1)S(1)}, bf16[128,512]{1,0:T(8,128)(2,1)S(1)}, u32[]{:S(2)}, u32[]{:S(2)}) collective-permute-start(bf16[128,512]{1,0:T(8,128)(2,1)S(1)} %get-tuple-element.105), channel_id=1, source_target_pairs={{0,16},{8,24},{16,0},{24,8},{1,17},{9,25},{17,1},{25,9},{2,18},{10... | collective-permute-start | bytes 393224 | tf_op jit(solution)/shard_map/ppermute | solution.py:284
  182.4 13.9 %collective-permute-start.11 = (bf16[128,512]{1,0:T(8,128)(2,1)S(1)}, bf16[128,512]{1,0:T(8,128)(2,1)S(1)}, u32[]{:S(2)}, u32[]{:S(2)}) collective-permute-start(bf16[128,512]{1,0:T(8,128)(2,1)S(1)} %get-tuple-element.106), channel_id=1, source_target_pairs={{0,24},{8,16},{16,8},{24,0},{1,25},{9,17},{17,9},{25,1},{2,26},{10... | collective-permute-start | bytes 393224 | tf_op jit(solution)/shard_map/ppermute | solution.py:284
  197.0 4.7 %collective-permute-start.12 = (bf16[32,512]{1,0:T(8,128)(2,1)S(1)}, bf16[32,512]{1,0:T(8,128)(2,1)S(1)}, u32[]{:S(2)}, u32[]{:S(2)}) collective-permute-start(bf16[32,512]{1,0:T(8,128)(2,1)S(1)} %get-tuple-element.108), channel_id=1, source_target_pairs={{0,2},{1,3},{2,0},{3,1},{4,6},{5,7},{6,4},{7,5},{8,10},{9,11},{10,... | collective-permute-start | bytes 98312 | tf_op jit(solution)/shard_map/ppermute | solution.py:287
  197.0 7.0 %collective-permute-start.13 = (bf16[32,512]{1,0:T(8,128)(2,1)S(1)}, bf16[32,512]{1,0:T(8,128)(2,1)S(1)}, u32[]{:S(2)}, u32[]{:S(2)}) collective-permute-start(bf16[32,512]{1,0:T(8,128)(2,1)S(1)} %get-tuple-element.109), channel_id=1, source_target_pairs={{0,4},{1,5},{2,6},{3,7},{4,0},{5,1},{6,2},{7,3},{8,12},{9,13},{10,... | collective-permute-start | bytes 98312 | tf_op jit(solution)/shard_map/ppermute | solution.py:287
  199.3 6.6 %collective-permute-start.14 = (bf16[32,512]{1,0:T(8,128)(2,1)S(1)}, bf16[32,512]{1,0:T(8,128)(2,1)S(1)}, u32[]{:S(2)}, u32[]{:S(2)}) collective-permute-start(bf16[32,512]{1,0:T(8,128)(2,1)S(1)} %get-tuple-element.110), channel_id=1, source_target_pairs={{0,6},{1,7},{2,4},{3,5},{4,2},{5,3},{6,0},{7,1},{8,14},{9,15},{10,... | collective-permute-start | bytes 98312 | tf_op jit(solution)/shard_map/ppermute | solution.py:287
  205.9 6.7 %collective-permute-start.17 = (bf16[32,512]{1,0:T(8,128)(2,1)S(1)}, bf16[32,512]{1,0:T(8,128)(2,1)S(1)}, u32[]{:S(2)}, u32[]{:S(2)}) collective-permute-start(bf16[32,512]{1,0:T(8,128)(2,1)S(1)} %split_sum.5.refs_0_), channel_id=1, source_target_pairs={{0,6},{1,7},{2,4},{3,5},{4,2},{5,3},{6,0},{7,1},{8,14},{9,15},{10,... | collective-permute-start | bytes 98312 | tf_op jit(solution)/shard_map/ppermute | solution.py:287
  208.1 6.3 %collective-permute-start.16 = (bf16[32,512]{1,0:T(8,128)(2,1)S(1)}, bf16[32,512]{1,0:T(8,128)(2,1)S(1)}, u32[]{:S(2)}, u32[]{:S(2)}) collective-permute-start(bf16[32,512]{1,0:T(8,128)(2,1)S(1)} %split_sum.5.refs_0_), channel_id=1, source_target_pairs={{0,4},{1,5},{2,6},{3,7},{4,0},{5,1},{6,2},{7,3},{8,12},{9,13},{10,... | collective-permute-start | bytes 98312 | tf_op jit(solution)/shard_map/ppermute | solution.py:287
  208.1 6.3 %collective-permute-start.15 = (bf16[32,512]{1,0:T(8,128)(2,1)S(1)}, bf16[32,512]{1,0:T(8,128)(2,1)S(1)}, u32[]{:S(2)}, u32[]{:S(2)}) collective-permute-start(bf16[32,512]{1,0:T(8,128)(2,1)S(1)} %split_sum.5.refs_0_), channel_id=1, source_target_pairs={{0,2},{1,3},{2,0},{3,1},{4,6},{5,7},{6,4},{7,5},{8,10},{9,11},{10,... | collective-permute-start | bytes 98312 | tf_op jit(solution)/shard_map/ppermute | solution.py:287
  224.7 1.0 copy-start.1
  227.5 31.0 %all-to-all-start.6 = ((bf16[32,32,512]{2,1,0:T(8,128)(2,1)}), bf16[32,32,512]{2,1,0:T(8,128)(2,1)S(1)}, u32[]{:S(2)}, u32[]{:S(2)}) async-start(bf16[32,32,512]{2,1,0:T(8,128)(2,1)} %bitcast.23), calls=%async_computation.7 | async-start | bytes 2097152 | tf_op jit(solution)/shard_map/all_to_all | solution.py:270
  230.9 15.0 %collective-permute-start.20 = (bf16[128,512]{1,0:T(8,128)(2,1)S(1)}, bf16[128,512]{1,0:T(8,128)(2,1)S(1)}, u32[]{:S(2)}, u32[]{:S(2)}) collective-permute-start(bf16[128,512]{1,0:T(8,128)(2,1)S(1)} %bitcast.37), channel_id=1, source_target_pairs={{0,24},{8,16},{16,8},{24,0},{1,25},{9,17},{17,9},{25,1},{2,26},{10... | collective-permute-start | bytes 393224 | tf_op jit(solution)/shard_map/ppermute | solution.py:284
  233.7 13.9 %collective-permute-start.19 = (bf16[128,512]{1,0:T(8,128)(2,1)S(1)}, bf16[128,512]{1,0:T(8,128)(2,1)S(1)}, u32[]{:S(2)}, u32[]{:S(2)}) collective-permute-start(bf16[128,512]{1,0:T(8,128)(2,1)S(1)} %bitcast.38), channel_id=1, source_target_pairs={{0,16},{8,24},{16,0},{24,8},{1,17},{9,25},{17,1},{25,9},{2,18},{10... | collective-permute-start | bytes 393224 | tf_op jit(solution)/shard_map/ppermute | solution.py:284
  234.2 14.1 %collective-permute-start.18 = (bf16[128,512]{1,0:T(8,128)(2,1)S(1)}, bf16[128,512]{1,0:T(8,128)(2,1)S(1)}, u32[]{:S(2)}, u32[]{:S(2)}) collective-permute-start(bf16[128,512]{1,0:T(8,128)(2,1)S(1)} %bitcast.39), channel_id=1, source_target_pairs={{0,8},{8,0},{16,24},{24,16},{1,9},{9,1},{17,25},{25,17},{2,10},{10... | collective-permute-start | bytes 393224 | tf_op jit(solution)/shard_map/ppermute | solution.py:284
  248.9 2.0 collective-permute-start.21
Sparse Core Ops, SparseCore 0:
  47.9 44.7 all-gather.1
  171.7 52.9 reduce-scatter.1

commit v10 on v9

--- a/solution.py
+++ b/solution.py
@@ -92,22 +92,23 @@
 
 
 def spmm_kernel(ways, cols_ref, group_ref, x_ref, *refs):
-    masks, outs = refs[:ways], refs[ways:]
-    q = pl.program_id(0)
-    depth = pl.num_programs(0)
+    masks, outs = refs[: 2 * ways], refs[2 * ways :]
+    i = pl.program_id(0)
+    share = pl.num_programs(0)
     _, breadth, tile, _ = masks[0].shape
-    for s in range(ways):
-        base = (group_ref[s] * depth + q) * breadth
+    for at, (mask_ref, out_ref) in enumerate(zip(masks, outs)):
+        s, part = divmod(at, 2)
+        base = ((group_ref[s] * 2 + part) * share + i) * breadth
         total = None
         for p in range(0, breadth, 2):
             span = range(p, min(p + 2, breadth))
-            left = jnp.concatenate([masks[s][0, k] for k in span], axis=1)
+            left = jnp.concatenate([mask_ref[0, k] for k in span], axis=1)
             right = jnp.concatenate(
                 [x_ref[pl.ds(pl.multiple_of(cols_ref[base + k] * tile, tile), tile), :] for k in span], axis=0
             )
             term = dot(left, right)
             total = term if total is None else total + term
-        outs[s][...] = total.astype(BF)
+        out_ref[...] = total.astype(BF)
 
 
 def spmm_back_kernel(ways, pieces, cols_ref, group_ref, *refs):
@@ -147,12 +148,9 @@
             copy.wait()
 
 
-def pass_on_kernel(left_ref, right_ref, top_ref, bottom_ref, left_out, right_out):
-    half = top_ref.shape[0]
-    left_out[:half, :] = left_ref[:half, :]
-    left_out[half:, :] = (left_ref[half:, :].astype(F32) + bottom_ref[...].astype(F32)).astype(BF)
-    right_out[:half, :] = (right_ref[:half, :].astype(F32) + top_ref[...].astype(F32)).astype(BF)
-    right_out[half:, :] = right_ref[half:, :]
+def pass_on_kernel(left_ref, right_ref, to_left_ref, to_right_ref, left_out, right_out):
+    left_out[...] = (left_ref[...].astype(F32) + to_left_ref[...].astype(F32)).astype(BF)
+    right_out[...] = (right_ref[...].astype(F32) + to_right_ref[...].astype(F32)).astype(BF)
 
 
 def prepare_kernel(x_ref, degree_ref, row_ref, self_ref, base_out, degree_out):
@@ -168,11 +166,12 @@
 
 
 def layer_kernel(ways, *refs):
-    terms = refs[:ways]
-    (base_ref, degree_ref, cot_ref, neigh_ref, hidden_out, slopes_out, agg_out, spread_out) = refs[ways:]
-    summed = terms[0][...].astype(F32)
-    for s in range(1, ways):
-        summed = summed + terms[s][...].astype(F32)
+    uppers, lowers = refs[:ways], refs[ways : 2 * ways]
+    (base_ref, degree_ref, cot_ref, neigh_ref, hidden_out, slopes_out, agg_out, spread_out) = refs[2 * ways :]
+    lower = pl.program_id(0) == 1
+    summed = 0.0
+    for up_ref, low_ref in zip(uppers, lowers):
+        summed = summed + jnp.where(lower, low_ref[...], up_ref[...]).astype(F32)
     degrees = degree_ref[...][:, :1]
     agg = (summed / degrees).astype(BF)
     agg_out[...] = agg
@@ -370,32 +369,41 @@
 
     pieces = (1, 1, 1, 2) if ways == 4 else (1,) * ways
     half = rows // 2
+    share = depth // 2
+
+    def half_spec(s, part):
+        return pl.BlockSpec((1, breadth, tile, tile), lambda i, c, g: ((g[s] * 2 + part) * share + i, 0, 0, 0))
+
     partials = call(
         functools.partial(spmm_kernel, ways),
         grid_spec=pltpu.PrefetchScalarGridSpec(
             num_scalar_prefetch=2,
-            grid=(depth,),
-            in_specs=[VMEM] + [mask_spec(s) for s in range(ways)],
-            out_specs=[pl.BlockSpec((tile, width), lambda q, c, g: (q, 0)) for s in range(ways)],
+            grid=(share,),
+            in_specs=[VMEM] + [half_spec(s, part) for s in range(ways) for part in range(2)],
+            out_specs=[pl.BlockSpec((tile, width), lambda i, c, g: (i, 0))] * (2 * ways),
         ),
-        out_shape=[shape(rows, width) for s in range(ways)],
+        out_shape=[shape(half, width)] * (2 * ways),
         cost_estimate=cost(spmm_flops, 2 * masks.size + 2 * x_cols.size + 2 * ways * slab),
         mib=LARGE,
         name="spmm",
-    )(cols, groups, x_cols, *([masks] * ways))
+    )(cols, groups, x_cols, *([masks] * (2 * ways)))
+    uppers, lowers = partials[::2], partials[1::2]
     if ways == 4:
-        top, bottom = across(partials[3][:half], 1), across(partials[3][half:], 2)
-        left, right = call(
+        to_right, to_left = across(uppers[3], 1), across(lowers[3], 2)
+        left_upper, right_lower = across(uppers[1], 1), across(lowers[2], 2)
+        left_lower, right_upper = call(
             pass_on_kernel,
-            out_shape=(shape(rows, width),) * 2,
+            out_shape=(shape(half, width),) * 2,
             in_specs=[VMEM] * 4,
             out_specs=(VMEM,) * 2,
-            cost_estimate=cost(2 * slab, 10 * slab),
+            cost_estimate=cost(2 * slab, 6 * slab),
             name="pass_on",
-        )(partials[1], partials[2], top, bottom)
-        terms = [partials[0], across(left, 1), across(right, 2)]
+        )(lowers[1], uppers[2], to_left, to_right)
+        uppers = [uppers[0], left_upper, across(right_upper, 2)]
+        lowers = [lowers[0], across(left_lower, 1), right_lower]
     else:
-        terms = [partials[0]] + [across(partials[s], s) for s in range(1, ways)]
+        uppers = [uppers[0]] + [across(uppers[s], s) for s in range(1, ways)]
+        lowers = [lowers[0]] + [across(lowers[s], s) for s in range(1, ways)]
     cot_node = call(
         unpack_kernel,
         out_shape=shape(rows, width),
@@ -409,15 +417,15 @@
         return pl.BlockSpec((half, columns), lambda i: (i, 0))
 
     hidden, slopes, agg, spread = call(
-        functools.partial(layer_kernel, len(terms)),
+        functools.partial(layer_kernel, len(uppers)),
         grid=(2,),
         out_shape=(shape(rows, width),) * 4,
-        in_specs=[by_rows(width)] * (len(terms) + 1) + [by_rows(128), by_rows(width), VMEM],
+        in_specs=[VMEM] * (2 * len(uppers)) + [by_rows(width)] + [by_rows(128), by_rows(width), VMEM],
         out_specs=(by_rows(width),) * 4,
-        cost_estimate=cost(8 * slab * width, 2 * slab * (len(terms) + 9)),
+        cost_estimate=cost(8 * slab * width, 2 * slab * (len(uppers) + 9)),
         mib=LARGE,
         name="layer",
-    )(*terms, base, degrees, cot_node, neigh_weight)
+    )(*uppers, *lowers, base, degrees, cot_node, neigh_weight)
     hidden_packed = call(
         pack_node_kernel,
         out_shape=shape(slots, width),

time: 268 us -> 262 us (0.978)
  waiting for transfers between devices: 131 us -> 123 us
  starting transfers between devices: 50.3 us -> 53 us
    ppermute x14 -> x16, waiting for transfers between devices: 47.1 us -> 41.7 us  [across(): return lax.ppermute(value, 'row', [(i, i ^ s) for i in range(ways)])]
    ppermute x14 -> x16, starting transfers between devices: 15.4 us -> 18.1 us  [across(): return lax.ppermute(value, 'row', [(i, i ^ s) for i in range(ways)])]
    unnamed x39 -> x43, local copies, waits for them, and re-layouts: 7.97 us -> 7.67 us
  transfers between devices with their start and end apart: 30 -> 32, of which waited for: 27 -> 26; matrix products, arithmetic and copies ran while one was open for 2% -> 2% of each run, Pallas kernels for 14% -> 15%
where the time goes in v10:
time: 262 us; the launch traced here: 261 us
  waiting for transfers between devices  123 us (47%)
  starting transfers between devices  53 us (20%)
  Pallas kernels  49.3 us (19%)
  between operations  14.3 us (5%)
  local copies, waits for them, and re-layouts  10.5 us (4%)
  blocking collectives  10.2 us (4%)
    ppermute x16, waiting for transfers between devices, across(): return lax.ppermute(value, 'row', [(i, i ^ s) for i in range(ways)])  41.7 us
    all_to_all x2, waiting for transfers between devices, relay(): lax.all_to_all(there, everyone, split_axis=0, concat_axis=0, tiled=True)  28.5 us
    ppermute x16, starting transfers between devices, across(): return lax.ppermute(value, 'row', [(i, i ^ s) for i in range(ways)])  18.1 us
    all_gather x1, waiting for transfers between devices, on_device(): x_cols = lax.all_gather(x_node, 'col', axis=0, tiled=True)  16.1 us
    all_to_all x2, waiting for transfers between devices, row_phase(): lax.all_to_all(there, 'row', split_axis=0, concat_axis=0, tiled=True)  11.3 us
    all_to_all x2, starting transfers between devices, relay(): lax.all_to_all(there, everyone, split_axis=0, concat_axis=0, tiled=True)  10.7 us
    pallas_call x1, Pallas kernels, on_device(): call(functools.partial(spmm_back_kernel, ways, pieces), grid_spec=pltpu.P...  10.5 us
    all_to_all x1, blocking collectives, on_device(): lax.all_to_all(degree_packed, everyone, split_axis=0, concat_axis=0, tile...  10.2 us
  transfers between devices with their start and end apart: 32, of which 26 were waited for; matrix products, arithmetic and copies ran while one was open for 2% of the time, Pallas kernels for 15%

profile of v10, /device:TPU:0, one launch (start us, length us, event | category | flops | bytes accessed | tf_op | source)
XLA Modules:
  0.0 261.0 jit_solution(7837645764378643369)
XLA Ops:
  7.2 3.1 %pack_features.1 = bf16[1024,512]{1,0:T(8,128)(2,1)} custom-call(s32[1,512]{1,0:T(1,128)} %bitcast.60, bf16[512,512]{1,0:T(8,128)(2,1)} %value_ref.1), custom_call_target="tpu_custom_call" | custom-call | flops 536870912 | bytes 1572864 | tf_op jit(solution)/shard_map/pack_features/pallas_call | solution.py:316
  10.3 7.3 %all-to-all-start = ((bf16[32,32,512]{2,1,0:T(8,128)(2,1)}), bf16[32,32,512]{2,1,0:T(8,128)(2,1)S(1)}, u32[]{:S(2)}, u32[]{:S(2)}) async-start(bf16[32,32,512]{2,1,0:T(8,128)(2,1)} %bitcast.44), calls=%async_computation | async-start | bytes 2097152 | tf_op jit(solution)/shard_map/all_to_all | solution.py:269
  17.7 0.8 copy.20
  19.1 3.3 %index_cotangent.1 = (bf16[1024,512]{1,0:T(8,128)(2,1)}, f32[32,32]{1,0:T(8,128)}, s32[8,512]{1,0:T(8,128)}, s32[8,512]{1,0:T(8,128)}, s32[8,512]{1,0:T(8,128)}) custom-call(s32[1,512]{1,0:T(1,128)} %bitcast.61, s32[1,512]{1,0:T(1,128)} %bitcast.62, s32[1,512]{1,0:T(1,128)} %bitcast.63, bf16[512,512]{1,0:T(8,128)(2,1)} %cot_ref.1), custom_call_target="tpu_custom_call" | custom-call | flops 536870912 | bytes 1572864 | tf_op jit(solution)/shard_map/index_cotangent/pallas_call | solution.py:326
  22.9 22.3 %all-to-all-done = bf16[32,32,512]{2,1,0:T(8,128)(2,1)S(1)} async-done(((bf16[32,32,512]{2,1,0:T(8,128)(2,1)}), bf16[32,32,512]{2,1,0:T(8,128)(2,1)S(1)}, u32[]{:S(2)}, u32[]{:S(2)}) %all-to-all-start) | async-done | bytes 1048608 | tf_op jit(solution)/shard_map/all_to_all | solution.py:269
  45.9 1.8 unpack_features.1.x_ref
  47.7 10.2 %all_to_all.41 = f32[32,1,32]{2,1,0:T(1,128)} all-to-all(f32[32,1,32]{2,1,0:T(1,128)} %bitcast.47), channel_id=1, replica_groups=mesh['row'=4,'col'=8] {'row','col'}, dimensions={0} | all-to-all | bytes 8192 | tf_op jit(solution)/shard_map/all_to_all | solution.py:349
  57.9 3.5 %all-to-all-start.1 = ((bf16[4,256,512]{2,1,0:T(8,128)(2,1)}), bf16[4,256,512]{2,1,0:T(8,128)(2,1)S(1)}, u32[]{:S(2)}, u32[]{:S(2)}) async-start(bf16[4,256,512]{2,1,0:T(8,128)(2,1)} %bitcast.45), calls=%async_computation.1 | async-start | bytes 2097152 | tf_op jit(solution)/shard_map/all_to_all | solution.py:273
  61.4 2.8 %prepare.1 = (f32[512,512]{1,0:T(8,128)}, f32[512,128]{1,0:T(8,128)}) custom-call(bf16[512,512]{1,0:T(8,128)(2,1)} %unpack_features.1.x_ref, f32[32,32]{1,0:T(8,128)} %bitcast.46, s32[8,512]{1,0:T(8,128)} %get-tuple-element.67.row_ref, bf16[512,512]{1,0:T(8,128)(2,1)} %self_ref.3), custom_call_target="tpu_custom_call" | custom-call | flops 268435456 | bytes 2097152 | tf_op jit(solution)/shard_map/prepare/pallas_call | solution.py:350
  64.2 11.3 %all-to-all-done.1 = bf16[4,256,512]{2,1,0:T(8,128)(2,1)S(1)} async-done(((bf16[4,256,512]{2,1,0:T(8,128)(2,1)}), bf16[4,256,512]{2,1,0:T(8,128)(2,1)S(1)}, u32[]{:S(2)}, u32[]{:S(2)}) %all-to-all-start.1) | async-done | bytes 1048608 | tf_op jit(solution)/shard_map/all_to_all | solution.py:273
  75.5 1.0 copy.21
  76.6 16.1 %all-gather.2.cloned.1.call-done.x_ref = bf16[4096,512]{1,0:T(8,128)(2,1)} async-done(((bf16[512,512]{1,0:T(8,128)(2,1)}), bf16[4096,512]{1,0:T(8,128)(2,1)}) %all-gather.2.cloned.1.call-update) | async-done | bytes 4194320 | tf_op jit(solution)/shard_map/all_gather | solution.py:347
  92.7 3.6 %all-to-all-start.3 = ((bf16[8,128,512]{2,1,0:T(8,128)(2,1)}), bf16[8,128,512]{2,1,0:T(8,128)(2,1)S(1)}, u32[]{:S(2)}, u32[]{:S(2)}) async-start(bf16[8,128,512]{2,1,0:T(8,128)(2,1)} %bitcast.14), calls=%async_computation.3 | async-start | bytes 2097152 | tf_op jit(solution)/shard_map/all_to_all | solution.py:277
  96.2 7.5 %spmm.1 = (bf16[256,512]{1,0:T(8,128)(2,1)}, bf16[256,512]{1,0:T(8,128)(2,1)}, bf16[256,512]{1,0:T(8,128)(2,1)}, bf16[256,512]{1,0:T(8,128)(2,1)}, bf16[256,512]...) custom-call(s32[128]{0:T(128)} %reshape_squeeze.3.cols_ref, ...), custom_call_target="tpu_custom_call" | custom-call | flops 12884901888 | bytes 10485760 | tf_op jit(solution)/shard_map/spmm/pallas_call | solution.py:377
  103.8 1.5 collective-permute-start.1
  105.3 1.5 collective-permute-start.2
  107.9 5.3 %collective-permute-done.1.to_left_ref = bf16[256,512]{1,0:T(8,128)(2,1)S(1)} collective-permute-done((bf16[256,512]{1,0:T(8,128)(2,1)}, bf16[256,512]{1,0:T(8,128)(2,1)S(1)}, u32[]{:S(2)}, u32[]{:S(2)}) %collective-permute-start.1) | collective-permute-done | bytes 262176 | tf_op jit(solution)/shard_map/ppermute | solution.py:283
  113.1 1.5 collective-permute-done.2.to_right_ref
  114.6 0.9 copy-done.3
  115.6 0.9 copy-done.4
  117.3 1.5 collective-permute-start.4
  118.8 4.0 %all-to-all-done.3 = bf16[8,128,512]{2,1,0:T(8,128)(2,1)S(1)} async-done(((bf16[8,128,512]{2,1,0:T(8,128)(2,1)}), bf16[8,128,512]{2,1,0:T(8,128)(2,1)S(1)}, u32[]{:S(2)}, u32[]{:S(2)}) %all-to-all-start.3) | async-done | bytes 1048608 | tf_op jit(solution)/shard_map/all_to_all | solution.py:277
  122.8 1.0 unpack_cotangent.1.refs_8_
  123.8 0.8 copy-done.8
  125.8 4.1 %layer.1 = (bf16[512,512]{1,0:T(8,128)(2,1)}, bf16[512,512]{1,0:T(8,128)(2,1)}, bf16[512,512]{1,0:T(8,128)(2,1)}, bf16[512,512]{1,0:T(8,128)(2,1)}) custom-call(bf16[256,512]{1,0:T(8,128)(2,1)} %get-tuple-element.76.refs_0_, bf16[256,512]{1,0:T(8,128)(2,1)} %copy-done.15, bf16[256,512]{1,0:T(8,128)(2,1)} %copy-done.17, ...), custom_call_target="tpu_custom_call" | custom-call | flops 1073741824 | bytes 6291456 | tf_op jit(solution)/shard_map/layer/pallas_call | solution.py:419
  130.0 1.2 collective-permute-start.7
  131.2 1.5 collective-permute-start.6
  132.6 1.0 copy-done.9
  133.7 1.7 pack_hidden.1
  135.3 4.2 %all-to-all-start.4 = ((bf16[8,128,512]{2,1,0:T(8,128)(2,1)}), bf16[8,128,512]{2,1,0:T(8,128)(2,1)S(1)}, u32[]{:S(2)}, u32[]{:S(2)}) async-start(bf16[8,128,512]{2,1,0:T(8,128)(2,1)} %bitcast.16), calls=%async_computation.4 | async-start | bytes 2097152 | tf_op jit(solution)/shard_map/all_to_all | solution.py:277
  139.6 3.8 %collective-permute-done.7.refs_2_ = bf16[512,512]{1,0:T(8,128)(2,1)S(1)} collective-permute-done((bf16[512,512]{1,0:T(8,128)(2,1)}, bf16[512,512]{1,0:T(8,128)(2,1)S(1)}, u32[]{:S(2)}, u32[]{:S(2)}) %collective-permute-start.7) | collective-permute-done | bytes 524320 | tf_op jit(solution)/shard_map/ppermute | solution.py:283
  143.4 1.1 collective-permute-done.6.refs_1_
  144.6 1.5 collective-permute-start.8
  146.7 3.8 %terms.1 = (bf16[512,512]{1,0:T(8,128)(2,1)}, bf16[512,512]{1,0:T(8,128)(2,1)}, f32[512,512]{1,0:T(8,128)}) custom-call(s32[1]{0:T(128)} %bitcast.5.core_ref, bf16[512,512]{1,0:T(8,128)(2,1)} %unpack_features.1.x_ref, bf16[512,512]{1,0:T(8,128)(2,1)} %get-tuple-element.95.agg_ref, bf16[512,512]{1,0:T(8,128)(2,1)} %get-tuple-element.96.slopes_ref, ...), custom_call_target="tpu_custom_call" | custom-call | flops 805306368 | bytes 4718592 | tf_op jit(solution)/shard_map/terms/pallas_call | solution.py:444
  151.3 1.2 collective-permute-done.9.refs_4_
  153.2 10.5 %spmm_back.1 = bf16[4096,512]{1,0:T(8,128)(2,1)} custom-call(s32[128]{0:T(128)} %reshape_squeeze.3.cols_ref, s32[4]{0:T(128)} %get-tuple-element.69.group_ref.index_ref, bf16[512,512]{1,0:T(8,128)(2,1)} %get-tuple-element.100.refs_0_, bf16[512,512]{1,0:T(8,128)(2,1)} %copy-done.13, bf16[512,512]{1,0:T(8,128)(2,1)} %copy-done.12, ...), custom_call_target="tpu_custom_call" | custom-call | flops 12884901888 | bytes 10485760 | tf_op jit(solution)/shard_map/spmm_back/pallas_call | solution.py:454
  163.7 2.5 all-to-all-done.4
  166.2 1.0 copy.23
  167.2 3.8 %all-to-all-start.5 = ((bf16[4,256,512]{2,1,0:T(8,128)(2,1)}), bf16[4,256,512]{2,1,0:T(8,128)(2,1)S(1)}, u32[]{:S(2)}, u32[]{:S(2)}) async-start(bf16[4,256,512]{2,1,0:T(8,128)(2,1)} %bitcast.41), calls=%async_computation.5 | async-start | bytes 2097152 | tf_op jit(solution)/shard_map/all_to_all | solution.py:273
  171.1 1.9 collective-permute-done.10.refs_1_
  173.0 0.8 split_sum.3
  173.8 2.0 collective-permute-start.11
  175.8 1.5 collective-permute-start.12
  177.3 11.5 %collective-permute-done.11.refs_1_ = bf16[128,512]{1,0:T(8,128)(2,1)S(1)} collective-permute-done((bf16[128,512]{1,0:T(8,128)(2,1)S(1)}, bf16[128,512]{1,0:T(8,128)(2,1)S(1)}, u32[]{:S(2)}, u32[]{:S(2)}) %collective-permute-start.11) | collective-permute-done | bytes 131104 | tf_op jit(solution)/shard_map/ppermute | solution.py:283
  188.8 2.3 collective-permute-done.13.refs_3_
  191.9 2.2 collective-permute-start.15
  194.1 2.1 collective-permute-start.16
  196.5 2.4 collective-permute-done.15.refs_2_
  198.9 1.8 collective-permute-done.16.refs_3_
  200.7 2.2 collective-permute-start.19
  202.9 2.3 collective-permute-start.17
  205.2 2.3 collective-permute-done.19.refs_3_
  207.5 1.8 collective-permute-done.18.refs_2_
  209.8 8.6 %reduce-scatter.2.cloned.1.call-done.neigh_ref = bf16[512,512]{1,0:T(8,128)(2,1)} async-done(((bf16[4096,512]{1,0:T(8,128)(2,1)}), bf16[512,512]{1,0:T(8,128)(2,1)}) %reduce-scatter.2.cloned.1.call-update) | async-done | bytes 524304 | tf_op jit(solution)/shard_map/reduce_scatter | solution.py:474
  218.5 1.0 copy-done.1
  219.5 1.8 join_pack.1
  221.3 3.4 %all-to-all-start.6 = ((bf16[32,32,512]{2,1,0:T(8,128)(2,1)}), bf16[32,32,512]{2,1,0:T(8,128)(2,1)S(1)}, u32[]{:S(2)}, u32[]{:S(2)}) async-start(bf16[32,32,512]{2,1,0:T(8,128)(2,1)} %bitcast.23), calls=%async_computation.7 | async-start | bytes 2097152 | tf_op jit(solution)/shard_map/all_to_all | solution.py:269
  224.7 2.7 %collective-permute-start.22 = (bf16[128,512]{1,0:T(8,128)(2,1)S(1)}, bf16[128,512]{1,0:T(8,128)(2,1)S(1)}, u32[]{:S(2)}, u32[]{:S(2)}) collective-permute-start(bf16[128,512]{1,0:T(8,128)(2,1)S(1)} %bitcast.37), channel_id=1, source_target_pairs={{0,24},{8,16},{16,8},{24,0},{1,25},{9,17},{17,9},{25,1},{2,26},{10... | collective-permute-start | bytes 393224 | tf_op jit(solution)/shard_map/ppermute | solution.py:283
  228.3 11.5 %collective-permute-done.22.refs_3_ = bf16[128,512]{1,0:T(8,128)(2,1)S(1)} collective-permute-done((bf16[128,512]{1,0:T(8,128)(2,1)S(1)}, bf16[128,512]{1,0:T(8,128)(2,1)S(1)}, u32[]{:S(2)}, u32[]{:S(2)}) %collective-permute-start.22) | collective-permute-done | bytes 131104 | tf_op jit(solution)/shard_map/ppermute | solution.py:283
  239.7 1.6 collective-permute-done.21.refs_2_
  242.7 1.8 unpack_owner.2
  244.6 1.5 final.1
  246.1 6.2 %all-to-all-done.6 = bf16[32,32,512]{2,1,0:T(8,128)(2,1)S(1)} async-done(((bf16[32,32,512]{2,1,0:T(8,128)(2,1)}), bf16[32,32,512]{2,1,0:T(8,128)(2,1)S(1)}, u32[]{:S(2)}, u32[]{:S(2)}) %all-to-all-start.6) | async-done | bytes 1048608 | tf_op jit(solution)/shard_map/all_to_all | solution.py:269
  252.3 1.8 unpack_owner.3
  (72 shorter events, 11.3 us)
Async XLA Ops:
  10.3 34.9 %all-to-all-start = ((bf16[32,32,512]{2,1,0:T(8,128)(2,1)}), bf16[32,32,512]{2,1,0:T(8,128)(2,1)S(1)}, u32[]{:S(2)}, u32[]{:S(2)}) async-start(bf16[32,32,512]{2,1,0:T(8,128)(2,1)} %bitcast.44), calls=%async_computation | async-start | bytes 2097152 | tf_op jit(solution)/shard_map/all_to_all | solution.py:269
  17.6 75.1 %all-gather.2.cloned.1.call-start = ((), (), s32[]{:S(2)}) async-start(), calls=%async_computation.8 | async-start | bytes 4718592 | tf_op jit(solution)/shard_map/all_gather | solution.py:347
  45.2 0.7 copy-start.5
  57.9 17.6 %all-to-all-start.1 = ((bf16[4,256,512]{2,1,0:T(8,128)(2,1)}), bf16[4,256,512]{2,1,0:T(8,128)(2,1)S(1)}, u32[]{:S(2)}, u32[]{:S(2)}) async-start(bf16[4,256,512]{2,1,0:T(8,128)(2,1)} %bitcast.45), calls=%async_computation.1 | async-start | bytes 2097152 | tf_op jit(solution)/shard_map/all_to_all | solution.py:273
  92.7 30.1 %all-to-all-start.3 = ((bf16[8,128,512]{2,1,0:T(8,128)(2,1)}), bf16[8,128,512]{2,1,0:T(8,128)(2,1)S(1)}, u32[]{:S(2)}, u32[]{:S(2)}) async-start(bf16[8,128,512]{2,1,0:T(8,128)(2,1)} %bitcast.14), calls=%async_computation.3 | async-start | bytes 2097152 | tf_op jit(solution)/shard_map/all_to_all | solution.py:277
  96.2 26.5 %copy-start.11 = (s32[8,512]{1,0:T(8,128)S(1)}, s32[8,512]{1,0:T(8,128)}, u32[]{:S(2)}) copy-start(s32[8,512]{1,0:T(8,128)} %get-tuple-element.88.row_ref) | copy-start | bytes 49156
  103.8 9.4 %collective-permute-start.1 = (bf16[256,512]{1,0:T(8,128)(2,1)}, bf16[256,512]{1,0:T(8,128)(2,1)S(1)}, u32[]{:S(2)}, u32[]{:S(2)}) collective-permute-start(bf16[256,512]{1,0:T(8,128)(2,1)} %get-tuple-element.80), channel_id=1, source_target_pairs={{0,16},{8,24},{16,0},{24,8},{1,17},{9,25},{17,1},{25,9},{2,18},{10... | collective-permute-start | bytes 786440 | tf_op jit(solution)/shard_map/ppermute | solution.py:283
  105.3 9.4 %collective-permute-start.2 = (bf16[256,512]{1,0:T(8,128)(2,1)}, bf16[256,512]{1,0:T(8,128)(2,1)S(1)}, u32[]{:S(2)}, u32[]{:S(2)}) collective-permute-start(bf16[256,512]{1,0:T(8,128)(2,1)} %get-tuple-element.81), channel_id=1, source_target_pairs={{0,8},{8,0},{16,24},{24,16},{1,9},{9,1},{17,25},{25,17},{2,10},{10... | collective-permute-start | bytes 786440 | tf_op jit(solution)/shard_map/ppermute | solution.py:283
  106.7 17.9 %collective-permute-start = (bf16[256,512]{1,0:T(8,128)(2,1)}, bf16[256,512]{1,0:T(8,128)(2,1)S(1)}, u32[]{:S(2)}, u32[]{:S(2)}) collective-permute-start(bf16[256,512]{1,0:T(8,128)(2,1)} %get-tuple-element.77), channel_id=1, source_target_pairs={{0,8},{8,0},{16,24},{24,16},{1,9},{9,1},{17,25},{25,17},{2,10},{10... | collective-permute-start | bytes 786440 | tf_op jit(solution)/shard_map/ppermute | solution.py:283
  107.3 17.3 %collective-permute-start.5 = (bf16[256,512]{1,0:T(8,128)(2,1)}, bf16[256,512]{1,0:T(8,128)(2,1)S(1)}, u32[]{:S(2)}, u32[]{:S(2)}) collective-permute-start(bf16[256,512]{1,0:T(8,128)(2,1)} %get-tuple-element.85), channel_id=1, source_target_pairs={{0,16},{8,24},{16,0},{24,8},{1,17},{9,25},{17,1},{25,9},{2,18},{10... | collective-permute-start | bytes 786440 | tf_op jit(solution)/shard_map/ppermute | solution.py:283
  114.6 1.0 copy-start.3
  115.6 0.9 copy-start.4
  116.6 7.9 %collective-permute-start.3 = (bf16[256,512]{1,0:T(8,128)(2,1)S(1)}, bf16[256,512]{1,0:T(8,128)(2,1)S(1)}, u32[]{:S(2)}, u32[]{:S(2)}) collective-permute-start(bf16[256,512]{1,0:T(8,128)(2,1)S(1)} %get-tuple-element.82), channel_id=1, source_target_pairs={{0,16},{8,24},{16,0},{24,8},{1,17},{9,25},{17,1},{25,9},{2,18},{10... | collective-permute-start | bytes 786440 | tf_op jit(solution)/shard_map/ppermute | solution.py:283
  117.3 7.8 %collective-permute-start.4 = (bf16[256,512]{1,0:T(8,128)(2,1)S(1)}, bf16[256,512]{1,0:T(8,128)(2,1)S(1)}, u32[]{:S(2)}, u32[]{:S(2)}) collective-permute-start(bf16[256,512]{1,0:T(8,128)(2,1)S(1)} %get-tuple-element.84), channel_id=1, source_target_pairs={{0,8},{8,0},{16,24},{24,16},{1,9},{9,1},{17,25},{25,17},{2,10},{10... | collective-permute-start | bytes 786440 | tf_op jit(solution)/shard_map/ppermute | solution.py:283
  123.8 0.8 copy-start.8
  124.6 0.7 copy-start.15
  124.6 0.8 copy-start.16
  124.6 0.9 copy-start.17
  125.1 0.7 copy-start.18
  130.0 13.4 %collective-permute-start.7 = (bf16[512,512]{1,0:T(8,128)(2,1)}, bf16[512,512]{1,0:T(8,128)(2,1)S(1)}, u32[]{:S(2)}, u32[]{:S(2)}) collective-permute-start(bf16[512,512]{1,0:T(8,128)(2,1)} %get-tuple-element.100.refs_0_), channel_id=1, source_target_pairs={{0,16},{8,24},{16,0},{24,8},{1,17},{9,25},{17,1},{25,9},{2,18},{10... | collective-permute-start | bytes 1572872 | tf_op jit(solution)/shard_map/ppermute | solution.py:283
  131.2 13.4 %collective-permute-start.6 = (bf16[512,512]{1,0:T(8,128)(2,1)}, bf16[512,512]{1,0:T(8,128)(2,1)S(1)}, u32[]{:S(2)}, u32[]{:S(2)}) collective-permute-start(bf16[512,512]{1,0:T(8,128)(2,1)} %get-tuple-element.100.refs_0_), channel_id=1, source_target_pairs={{0,8},{8,0},{16,24},{24,16},{1,9},{9,1},{17,25},{25,17},{2,10},{10... | collective-permute-start | bytes 1572872 | tf_op jit(solution)/shard_map/ppermute | solution.py:283
  132.6 1.0 copy-start.9
  135.3 30.8 %all-to-all-start.4 = ((bf16[8,128,512]{2,1,0:T(8,128)(2,1)}), bf16[8,128,512]{2,1,0:T(8,128)(2,1)S(1)}, u32[]{:S(2)}, u32[]{:S(2)}) async-start(bf16[8,128,512]{2,1,0:T(8,128)(2,1)} %bitcast.16), calls=%async_computation.4 | async-start | bytes 2097152 | tf_op jit(solution)/shard_map/all_to_all | solution.py:277
  139.6 78.9 %reduce-scatter.2.cloned.1.call-start = ((), (), s32[]{:S(2)}) async-start(), calls=%async_computation.9 | async-start | bytes 4718592 | tf_op jit(solution)/shard_map/reduce_scatter | solution.py:474
  143.4 9.1 %copy-start.12 = (bf16[512,512]{1,0:T(8,128)(2,1)}, bf16[512,512]{1,0:T(8,128)(2,1)S(1)}, u32[]{:S(2)}) copy-start(bf16[512,512]{1,0:T(8,128)(2,1)S(1)} %collective-permute-done.7.refs_2_) | copy-start | bytes 1572868
  144.5 8.0 %copy-start.13 = (bf16[512,512]{1,0:T(8,128)(2,1)}, bf16[512,512]{1,0:T(8,128)(2,1)S(1)}, u32[]{:S(2)}) copy-start(bf16[512,512]{1,0:T(8,128)(2,1)S(1)} %collective-permute-done.6.refs_1_) | copy-start | bytes 1572868
  144.6 6.7 %collective-permute-start.8 = (bf16[256,512]{1,0:T(8,128)(2,1)S(1)}, bf16[256,512]{1,0:T(8,128)(2,1)S(1)}, u32[]{:S(2)}, u32[]{:S(2)}) collective-permute-start(bf16[256,512]{1,0:T(8,128)(2,1)S(1)} %slice.6), channel_id=1, source_target_pairs={{0,8},{8,0},{16,24},{24,16},{1,9},{9,1},{17,25},{25,17},{2,10},{10... | collective-permute-start | bytes 786440 | tf_op jit(solution)/shard_map/ppermute | solution.py:283
  146.1 6.4 %collective-permute-start.9 = (bf16[256,512]{1,0:T(8,128)(2,1)S(1)}, bf16[256,512]{1,0:T(8,128)(2,1)S(1)}, u32[]{:S(2)}, u32[]{:S(2)}) collective-permute-start(bf16[256,512]{1,0:T(8,128)(2,1)S(1)} %slice.7), channel_id=1, source_target_pairs={{0,16},{8,24},{16,0},{24,8},{1,17},{9,25},{17,1},{25,9},{2,18},{10... | collective-permute-start | bytes 786440 | tf_op jit(solution)/shard_map/ppermute | solution.py:283
  151.3 1.2 copy-start.19
  152.5 0.7 copy-start.20
  166.2 4.9 %copy-start.14 = (bf16[512,512]{1,0:T(8,128)(2,1)S(1)}, bf16[512,512]{1,0:T(8,128)(2,1)}, u32[]{:S(2)}) copy-start(bf16[512,512]{1,0:T(8,128)(2,1)} %get-tuple-element.110) | copy-start | bytes 1572868
  166.2 6.9 %copy-start.2 = (bf16[512,512]{1,0:T(8,128)(2,1)S(1)}, bf16[512,512]{1,0:T(8,128)(2,1)}, u32[]{:S(2)}) copy-start(bf16[512,512]{1,0:T(8,128)(2,1)} %get-tuple-element.109.refs_0_) | copy-start | bytes 1572868
  166.2 6.9 %copy-start.7 = (s32[4]{0:T(128)S(1)}, s32[4]{0:T(128)}, u32[]{:S(2)}) copy-start(s32[4]{0:T(128)} %get-tuple-element.69.group_ref.index_ref) | copy-start | bytes 52
  166.2 52.3 %copy-start = (f32[512,512]{1,0:T(8,128)S(1)}, f32[512,512]{1,0:T(8,128)}, u32[]{:S(2)}) copy-start(f32[512,512]{1,0:T(8,128)} %get-tuple-element.119.own_ref) | copy-start | bytes 3145732
  166.2 52.3 %copy-start.6 = (s32[8,512]{1,0:T(8,128)S(1)}, s32[8,512]{1,0:T(8,128)}, u32[]{:S(2)}) copy-start(s32[8,512]{1,0:T(8,128)} %get-tuple-element.67.row_ref) | copy-start | bytes 49156
  167.2 54.1 %all-to-all-start.5 = ((bf16[4,256,512]{2,1,0:T(8,128)(2,1)}), bf16[4,256,512]{2,1,0:T(8,128)(2,1)S(1)}, u32[]{:S(2)}, u32[]{:S(2)}) async-start(bf16[4,256,512]{2,1,0:T(8,128)(2,1)} %bitcast.41), calls=%async_computation.5 | async-start | bytes 2097152 | tf_op jit(solution)/shard_map/all_to_all | solution.py:273
  171.0 71.7 %copy-start.10 = (s32[8,512]{1,0:T(8,128)S(1)}, s32[8,512]{1,0:T(8,128)}, u32[]{:S(2)}) copy-start(s32[8,512]{1,0:T(8,128)} %get-tuple-element.64.row_ref) | copy-start | bytes 49156
  171.0 2.0 collective-permute-start.10
  173.8 15.1 %collective-permute-start.11 = (bf16[128,512]{1,0:T(8,128)(2,1)S(1)}, bf16[128,512]{1,0:T(8,128)(2,1)S(1)}, u32[]{:S(2)}, u32[]{:S(2)}) collective-permute-start(bf16[128,512]{1,0:T(8,128)(2,1)S(1)} %get-tuple-element.112), channel_id=1, source_target_pairs={{0,8},{8,0},{16,24},{24,16},{1,9},{9,1},{17,25},{25,17},{2,10},{10... | collective-permute-start | bytes 393224 | tf_op jit(solution)/shard_map/ppermute | solution.py:283
  175.8 13.1 %collective-permute-start.12 = (bf16[128,512]{1,0:T(8,128)(2,1)S(1)}, bf16[128,512]{1,0:T(8,128)(2,1)S(1)}, u32[]{:S(2)}, u32[]{:S(2)}) collective-permute-start(bf16[128,512]{1,0:T(8,128)(2,1)S(1)} %get-tuple-element.113), channel_id=1, source_target_pairs={{0,16},{8,24},{16,0},{24,8},{1,17},{9,25},{17,1},{25,9},{2,18},{10... | collective-permute-start | bytes 393224 | tf_op jit(solution)/shard_map/ppermute | solution.py:283
  177.2 13.9 %collective-permute-start.13 = (bf16[128,512]{1,0:T(8,128)(2,1)S(1)}, bf16[128,512]{1,0:T(8,128)(2,1)S(1)}, u32[]{:S(2)}, u32[]{:S(2)}) collective-permute-start(bf16[128,512]{1,0:T(8,128)(2,1)S(1)} %get-tuple-element.114), channel_id=1, source_target_pairs={{0,24},{8,16},{16,8},{24,0},{1,25},{9,17},{17,9},{25,1},{2,26},{10... | collective-permute-start | bytes 393224 | tf_op jit(solution)/shard_map/ppermute | solution.py:283
  191.8 4.7 %collective-permute-start.14 = (bf16[32,512]{1,0:T(8,128)(2,1)S(1)}, bf16[32,512]{1,0:T(8,128)(2,1)S(1)}, u32[]{:S(2)}, u32[]{:S(2)}) collective-permute-start(bf16[32,512]{1,0:T(8,128)(2,1)S(1)} %get-tuple-element.116), channel_id=1, source_target_pairs={{0,2},{1,3},{2,0},{3,1},{4,6},{5,7},{6,4},{7,5},{8,10},{9,11},{10,... | collective-permute-start | bytes 98312 | tf_op jit(solution)/shard_map/ppermute | solution.py:286
  191.9 7.0 %collective-permute-start.15 = (bf16[32,512]{1,0:T(8,128)(2,1)S(1)}, bf16[32,512]{1,0:T(8,128)(2,1)S(1)}, u32[]{:S(2)}, u32[]{:S(2)}) collective-permute-start(bf16[32,512]{1,0:T(8,128)(2,1)S(1)} %get-tuple-element.117), channel_id=1, source_target_pairs={{0,4},{1,5},{2,6},{3,7},{4,0},{5,1},{6,2},{7,3},{8,12},{9,13},{10,... | collective-permute-start | bytes 98312 | tf_op jit(solution)/shard_map/ppermute | solution.py:286
  194.1 6.6 %collective-permute-start.16 = (bf16[32,512]{1,0:T(8,128)(2,1)S(1)}, bf16[32,512]{1,0:T(8,128)(2,1)S(1)}, u32[]{:S(2)}, u32[]{:S(2)}) collective-permute-start(bf16[32,512]{1,0:T(8,128)(2,1)S(1)} %get-tuple-element.118), channel_id=1, source_target_pairs={{0,6},{1,7},{2,4},{3,5},{4,2},{5,3},{6,0},{7,1},{8,14},{9,15},{10,... | collective-permute-start | bytes 98312 | tf_op jit(solution)/shard_map/ppermute | solution.py:286
  200.7 6.8 %collective-permute-start.19 = (bf16[32,512]{1,0:T(8,128)(2,1)S(1)}, bf16[32,512]{1,0:T(8,128)(2,1)S(1)}, u32[]{:S(2)}, u32[]{:S(2)}) collective-permute-start(bf16[32,512]{1,0:T(8,128)(2,1)S(1)} %split_sum.5.refs_0_), channel_id=1, source_target_pairs={{0,6},{1,7},{2,4},{3,5},{4,2},{5,3},{6,0},{7,1},{8,14},{9,15},{10,... | collective-permute-start | bytes 98312 | tf_op jit(solution)/shard_map/ppermute | solution.py:286
  202.9 6.3 %collective-permute-start.18 = (bf16[32,512]{1,0:T(8,128)(2,1)S(1)}, bf16[32,512]{1,0:T(8,128)(2,1)S(1)}, u32[]{:S(2)}, u32[]{:S(2)}) collective-permute-start(bf16[32,512]{1,0:T(8,128)(2,1)S(1)} %split_sum.5.refs_0_), channel_id=1, source_target_pairs={{0,4},{1,5},{2,6},{3,7},{4,0},{5,1},{6,2},{7,3},{8,12},{9,13},{10,... | collective-permute-start | bytes 98312 | tf_op jit(solution)/shard_map/ppermute | solution.py:286
  202.9 6.3 %collective-permute-start.17 = (bf16[32,512]{1,0:T(8,128)(2,1)S(1)}, bf16[32,512]{1,0:T(8,128)(2,1)S(1)}, u32[]{:S(2)}, u32[]{:S(2)}) collective-permute-start(bf16[32,512]{1,0:T(8,128)(2,1)S(1)} %split_sum.5.refs_0_), channel_id=1, source_target_pairs={{0,2},{1,3},{2,0},{3,1},{4,6},{5,7},{6,4},{7,5},{8,10},{9,11},{10,... | collective-permute-start | bytes 98312 | tf_op jit(solution)/shard_map/ppermute | solution.py:286
  218.5 1.0 copy-start.1
  221.3 31.0 %all-to-all-start.6 = ((bf16[32,32,512]{2,1,0:T(8,128)(2,1)}), bf16[32,32,512]{2,1,0:T(8,128)(2,1)S(1)}, u32[]{:S(2)}, u32[]{:S(2)}) async-start(bf16[32,32,512]{2,1,0:T(8,128)(2,1)} %bitcast.23), calls=%async_computation.7 | async-start | bytes 2097152 | tf_op jit(solution)/shard_map/all_to_all | solution.py:269
  224.7 15.0 %collective-permute-start.22 = (bf16[128,512]{1,0:T(8,128)(2,1)S(1)}, bf16[128,512]{1,0:T(8,128)(2,1)S(1)}, u32[]{:S(2)}, u32[]{:S(2)}) collective-permute-start(bf16[128,512]{1,0:T(8,128)(2,1)S(1)} %bitcast.37), channel_id=1, source_target_pairs={{0,24},{8,16},{16,8},{24,0},{1,25},{9,17},{17,9},{25,1},{2,26},{10... | collective-permute-start | bytes 393224 | tf_op jit(solution)/shard_map/ppermute | solution.py:283
  227.5 13.9 %collective-permute-start.21 = (bf16[128,512]{1,0:T(8,128)(2,1)S(1)}, bf16[128,512]{1,0:T(8,128)(2,1)S(1)}, u32[]{:S(2)}, u32[]{:S(2)}) collective-permute-start(bf16[128,512]{1,0:T(8,128)(2,1)S(1)} %bitcast.38), channel_id=1, source_target_pairs={{0,16},{8,24},{16,0},{24,8},{1,17},{9,25},{17,1},{25,9},{2,18},{10... | collective-permute-start | bytes 393224 | tf_op jit(solution)/shard_map/ppermute | solution.py:283
  228.0 14.1 %collective-permute-start.20 = (bf16[128,512]{1,0:T(8,128)(2,1)S(1)}, bf16[128,512]{1,0:T(8,128)(2,1)S(1)}, u32[]{:S(2)}, u32[]{:S(2)}) collective-permute-start(bf16[128,512]{1,0:T(8,128)(2,1)S(1)} %bitcast.39), channel_id=1, source_target_pairs={{0,8},{8,0},{16,24},{24,16},{1,9},{9,1},{17,25},{25,17},{2,10},{10... | collective-permute-start | bytes 393224 | tf_op jit(solution)/shard_map/ppermute | solution.py:283
  242.7 2.0 collective-permute-start.23
Sparse Core Ops, SparseCore 0:
  47.9 44.7 all-gather.1
  166.3 52.0 reduce-scatter.1

commit v11 on v10

--- a/solution.py
+++ b/solution.py
@@ -397,6 +397,7 @@
             in_specs=[VMEM] * 4,
             out_specs=(VMEM,) * 2,
             cost_estimate=cost(2 * slab, 6 * slab),
+            mib=LARGE,
             name="pass_on",
         )(lowers[1], uppers[2], to_left, to_right)
         uppers = [uppers[0], left_upper, across(right_upper, 2)]
@@ -432,6 +433,7 @@
         in_specs=[VMEM] * 2,
         out_specs=VMEM,
         cost_estimate=cost(2 * slots * slab, 6 * slab),
+        mib=LARGE,
         name="pack_hidden",
     )(turned_row, hidden)
     if ways == 4:

time: 262 us -> 262 us (level)
  Pallas kernels: 49.3 us -> 52.3 us
    unnamed x43 -> x41, local copies, waits for them, and re-layouts: 7.67 us -> 5.43 us
  transfers between devices with their start and end apart: 32 -> 32, of which waited for: 26 -> 26; matrix products, arithmetic and copies ran while one was open for 2% -> 2% of each run, Pallas kernels for 15% -> 16%
where the time goes in v11:
time: 262 us; the launch traced here: 261 us
  waiting for transfers between devices  122 us (47%)
  starting transfers between devices  53.5 us (20%)
  Pallas kernels  52.3 us (20%)
  between operations  14.3 us (5%)
  blocking collectives  10.1 us (4%)
  local copies, waits for them, and re-layouts  8.18 us (3%)
    ppermute x16, waiting for transfers between devices, across(): return lax.ppermute(value, 'row', [(i, i ^ s) for i in range(ways)])  41.3 us
    all_to_all x2, waiting for transfers between devices, relay(): lax.all_to_all(there, everyone, split_axis=0, concat_axis=0, tiled=True)  28.5 us
    ppermute x16, starting transfers between devices, across(): return lax.ppermute(value, 'row', [(i, i ^ s) for i in range(ways)])  17.9 us
    all_gather x1, waiting for transfers between devices, on_device(): x_cols = lax.all_gather(x_node, 'col', axis=0, tiled=True)  16.1 us
    all_to_all x2, waiting for transfers between devices, row_phase(): lax.all_to_all(there, 'row', split_axis=0, concat_axis=0, tiled=True)  11.2 us
    all_to_all x2, starting transfers between devices, relay(): lax.all_to_all(there, everyone, split_axis=0, concat_axis=0, tiled=True)  10.7 us
    pallas_call x1, Pallas kernels, on_device(): call(functools.partial(spmm_back_kernel, ways, pieces), grid_spec=pltpu.P...  10.5 us
    all_to_all x1, blocking collectives, on_device(): lax.all_to_all(degree_packed, everyone, split_axis=0, concat_axis=0, tile...  10.1 us
  transfers between devices with their start and end apart: 32, of which 26 were waited for; matrix products, arithmetic and copies ran while one was open for 2% of the time, Pallas kernels for 16%

profile of v11, /device:TPU:0, one launch (start us, length us, event | category | flops | bytes accessed | tf_op | source)
XLA Modules:
  0.0 261.0 jit_solution(6623941961498501591)
XLA Ops:
  7.2 3.1 %pack_features.1 = bf16[1024,512]{1,0:T(8,128)(2,1)} custom-call(s32[1,512]{1,0:T(1,128)} %bitcast.61, bf16[512,512]{1,0:T(8,128)(2,1)} %value_ref.1), custom_call_target="tpu_custom_call" | custom-call | flops 536870912 | bytes 1572864 | tf_op jit(solution)/shard_map/pack_features/pallas_call | solution.py:316
  10.3 7.3 %all-to-all-start = ((bf16[32,32,512]{2,1,0:T(8,128)(2,1)}), bf16[32,32,512]{2,1,0:T(8,128)(2,1)S(1)}, u32[]{:S(2)}, u32[]{:S(2)}) async-start(bf16[32,32,512]{2,1,0:T(8,128)(2,1)} %bitcast.44), calls=%async_computation | async-start | bytes 2097152 | tf_op jit(solution)/shard_map/all_to_all | solution.py:269
  17.7 0.8 copy.20
  19.0 3.3 %index_cotangent.1 = (bf16[1024,512]{1,0:T(8,128)(2,1)}, f32[32,32]{1,0:T(8,128)}, s32[8,512]{1,0:T(8,128)}, s32[8,512]{1,0:T(8,128)}, s32[8,512]{1,0:T(8,128)}) custom-call(s32[1,512]{1,0:T(1,128)} %bitcast.62, s32[1,512]{1,0:T(1,128)} %bitcast.63, s32[1,512]{1,0:T(1,128)} %bitcast.64, bf16[512,512]{1,0:T(8,128)(2,1)} %cot_ref.1), custom_call_target="tpu_custom_call" | custom-call | flops 536870912 | bytes 1572864 | tf_op jit(solution)/shard_map/index_cotangent/pallas_call | solution.py:326
  22.9 22.3 %all-to-all-done = bf16[32,32,512]{2,1,0:T(8,128)(2,1)S(1)} async-done(((bf16[32,32,512]{2,1,0:T(8,128)(2,1)}), bf16[32,32,512]{2,1,0:T(8,128)(2,1)S(1)}, u32[]{:S(2)}, u32[]{:S(2)}) %all-to-all-start) | async-done | bytes 1048608 | tf_op jit(solution)/shard_map/all_to_all | solution.py:269
  45.2 0.7 copy-done.3
  45.9 1.8 unpack_features.1.x_ref
  47.7 10.1 %all_to_all.41 = f32[32,1,32]{2,1,0:T(1,128)} all-to-all(f32[32,1,32]{2,1,0:T(1,128)} %bitcast.48), channel_id=1, replica_groups=mesh['row'=4,'col'=8] {'row','col'}, dimensions={0} | all-to-all | bytes 8192 | tf_op jit(solution)/shard_map/all_to_all | solution.py:349
  57.9 3.5 %all-to-all-start.1 = ((bf16[4,256,512]{2,1,0:T(8,128)(2,1)}), bf16[4,256,512]{2,1,0:T(8,128)(2,1)S(1)}, u32[]{:S(2)}, u32[]{:S(2)}) async-start(bf16[4,256,512]{2,1,0:T(8,128)(2,1)} %bitcast.46), calls=%async_computation.1 | async-start | bytes 2097152 | tf_op jit(solution)/shard_map/all_to_all | solution.py:273
  61.4 2.9 %prepare.1 = (f32[512,512]{1,0:T(8,128)}, f32[512,128]{1,0:T(8,128)}) custom-call(bf16[512,512]{1,0:T(8,128)(2,1)} %unpack_features.1.x_ref, f32[32,32]{1,0:T(8,128)} %bitcast.47, s32[8,512]{1,0:T(8,128)} %get-tuple-element.67.row_ref, bf16[512,512]{1,0:T(8,128)(2,1)} %self_ref.3), custom_call_target="tpu_custom_call" | custom-call | flops 268435456 | bytes 2097152 | tf_op jit(solution)/shard_map/prepare/pallas_call | solution.py:350
  64.3 11.2 %all-to-all-done.1 = bf16[4,256,512]{2,1,0:T(8,128)(2,1)S(1)} async-done(((bf16[4,256,512]{2,1,0:T(8,128)(2,1)}), bf16[4,256,512]{2,1,0:T(8,128)(2,1)S(1)}, u32[]{:S(2)}, u32[]{:S(2)}) %all-to-all-start.1) | async-done | bytes 1048608 | tf_op jit(solution)/shard_map/all_to_all | solution.py:273
  75.5 1.0 copy.21
  76.6 16.1 %all-gather.2.cloned.1.call-done.x_ref = bf16[4096,512]{1,0:T(8,128)(2,1)} async-done(((bf16[512,512]{1,0:T(8,128)(2,1)}), bf16[4096,512]{1,0:T(8,128)(2,1)}) %all-gather.2.cloned.1.call-update) | async-done | bytes 4194320 | tf_op jit(solution)/shard_map/all_gather | solution.py:347
  92.7 3.6 %all-to-all-start.3 = ((bf16[8,128,512]{2,1,0:T(8,128)(2,1)}), bf16[8,128,512]{2,1,0:T(8,128)(2,1)S(1)}, u32[]{:S(2)}, u32[]{:S(2)}) async-start(bf16[8,128,512]{2,1,0:T(8,128)(2,1)} %bitcast.14), calls=%async_computation.3 | async-start | bytes 2097152 | tf_op jit(solution)/shard_map/all_to_all | solution.py:277
  96.2 7.5 %spmm.1 = (bf16[256,512]{1,0:T(8,128)(2,1)}, bf16[256,512]{1,0:T(8,128)(2,1)}, bf16[256,512]{1,0:T(8,128)(2,1)}, bf16[256,512]{1,0:T(8,128)(2,1)}, bf16[256,512]...) custom-call(s32[128]{0:T(128)} %reshape_squeeze.3.cols_ref, ...), custom_call_target="tpu_custom_call" | custom-call | flops 12884901888 | bytes 10485760 | tf_op jit(solution)/shard_map/spmm/pallas_call | solution.py:377
  103.7 1.5 collective-permute-start.1
  105.3 1.5 collective-permute-start.2
  107.9 5.3 %collective-permute-done.1.to_left_ref = bf16[256,512]{1,0:T(8,128)(2,1)S(1)} collective-permute-done((bf16[256,512]{1,0:T(8,128)(2,1)}, bf16[256,512]{1,0:T(8,128)(2,1)S(1)}, u32[]{:S(2)}, u32[]{:S(2)}) %collective-permute-start.1) | collective-permute-done | bytes 262176 | tf_op jit(solution)/shard_map/ppermute | solution.py:283
  113.1 1.5 collective-permute-done.2.to_right_ref
  115.3 2.1 pass_on.1
  117.9 1.5 collective-permute-start.4
  119.4 3.3 %all-to-all-done.3 = bf16[8,128,512]{2,1,0:T(8,128)(2,1)S(1)} async-done(((bf16[8,128,512]{2,1,0:T(8,128)(2,1)}), bf16[8,128,512]{2,1,0:T(8,128)(2,1)S(1)}, u32[]{:S(2)}, u32[]{:S(2)}) %all-to-all-start.3) | async-done | bytes 1048608 | tf_op jit(solution)/shard_map/all_to_all | solution.py:277
  122.8 1.0 unpack_cotangent.1.refs_8_
  123.8 0.8 copy-done.6
  125.9 4.2 %layer.1 = (bf16[512,512]{1,0:T(8,128)(2,1)}, bf16[512,512]{1,0:T(8,128)(2,1)}, bf16[512,512]{1,0:T(8,128)(2,1)}, bf16[512,512]{1,0:T(8,128)(2,1)}) custom-call(bf16[256,512]{1,0:T(8,128)(2,1)} %get-tuple-element.76.refs_0_, bf16[256,512]{1,0:T(8,128)(2,1)} %copy-done.14, bf16[256,512]{1,0:T(8,128)(2,1)} %copy-done.16, ...), custom_call_target="tpu_custom_call" | custom-call | flops 1073741824 | bytes 6291456 | tf_op jit(solution)/shard_map/layer/pallas_call | solution.py:420
  130.0 1.1 collective-permute-start.7
  131.2 1.5 collective-permute-start.6
  132.7 2.7 %pack_hidden.1 = bf16[1024,512]{1,0:T(8,128)(2,1)} custom-call(s32[8,512]{1,0:T(8,128)} %get-tuple-element.88.row_ref, bf16[512,512]{1,0:T(8,128)(2,1)} %get-tuple-element.91.value_ref), custom_call_target="tpu_custom_call" | custom-call | flops 536870912 | bytes 1572864 | tf_op jit(solution)/shard_map/pack_hidden/pallas_call | solution.py:430
  135.4 4.9 %all-to-all-start.4 = ((bf16[8,128,512]{2,1,0:T(8,128)(2,1)}), bf16[8,128,512]{2,1,0:T(8,128)(2,1)S(1)}, u32[]{:S(2)}, u32[]{:S(2)}) async-start(bf16[8,128,512]{2,1,0:T(8,128)(2,1)} %bitcast.45), calls=%async_computation.4 | async-start | bytes 2097152 | tf_op jit(solution)/shard_map/all_to_all | solution.py:277
  140.3 3.1 %collective-permute-done.7.refs_2_ = bf16[512,512]{1,0:T(8,128)(2,1)S(1)} collective-permute-done((bf16[512,512]{1,0:T(8,128)(2,1)}, bf16[512,512]{1,0:T(8,128)(2,1)S(1)}, u32[]{:S(2)}, u32[]{:S(2)}) %collective-permute-start.7) | collective-permute-done | bytes 524320 | tf_op jit(solution)/shard_map/ppermute | solution.py:283
  143.4 1.2 collective-permute-done.6.refs_1_
  144.6 1.5 collective-permute-start.8
  146.7 3.8 %terms.1 = (bf16[512,512]{1,0:T(8,128)(2,1)}, bf16[512,512]{1,0:T(8,128)(2,1)}, f32[512,512]{1,0:T(8,128)}) custom-call(s32[1]{0:T(128)} %bitcast.5.core_ref, bf16[512,512]{1,0:T(8,128)(2,1)} %unpack_features.1.x_ref, bf16[512,512]{1,0:T(8,128)(2,1)} %get-tuple-element.95.agg_ref, bf16[512,512]{1,0:T(8,128)(2,1)} %get-tuple-element.96.slopes_ref, ...), custom_call_target="tpu_custom_call" | custom-call | flops 805306368 | bytes 4718592 | tf_op jit(solution)/shard_map/terms/pallas_call | solution.py:446
  150.6 0.8 collective-permute-done.8.refs_3_
  151.4 1.2 collective-permute-done.9.refs_4_
  153.2 10.5 %spmm_back.1 = bf16[4096,512]{1,0:T(8,128)(2,1)} custom-call(s32[128]{0:T(128)} %reshape_squeeze.3.cols_ref, s32[4]{0:T(128)} %get-tuple-element.69.group_ref.index_ref, bf16[512,512]{1,0:T(8,128)(2,1)} %get-tuple-element.100.refs_0_, bf16[512,512]{1,0:T(8,128)(2,1)} %copy-done.12, bf16[512,512]{1,0:T(8,128)(2,1)} %copy-done.11, ...), custom_call_target="tpu_custom_call" | custom-call | flops 12884901888 | bytes 10485760 | tf_op jit(solution)/shard_map/spmm_back/pallas_call | solution.py:456
  163.7 3.2 %all-to-all-done.4 = bf16[8,128,512]{2,1,0:T(8,128)(2,1)S(1)} async-done(((bf16[8,128,512]{2,1,0:T(8,128)(2,1)}), bf16[8,128,512]{2,1,0:T(8,128)(2,1)S(1)}, u32[]{:S(2)}, u32[]{:S(2)}) %all-to-all-start.4) | async-done | bytes 1048608 | tf_op jit(solution)/shard_map/all_to_all | solution.py:277
  166.9 1.0 copy.23
  168.0 3.7 %all-to-all-start.5 = ((bf16[4,256,512]{2,1,0:T(8,128)(2,1)}), bf16[4,256,512]{2,1,0:T(8,128)(2,1)S(1)}, u32[]{:S(2)}, u32[]{:S(2)}) async-start(bf16[4,256,512]{2,1,0:T(8,128)(2,1)} %bitcast.41), calls=%async_computation.5 | async-start | bytes 2097152 | tf_op jit(solution)/shard_map/all_to_all | solution.py:273
  171.8 1.9 collective-permute-done.10.refs_1_
  173.7 0.8 split_sum.3
  174.5 2.0 collective-permute-start.11
  176.4 1.5 collective-permute-start.12
  178.0 11.5 %collective-permute-done.11.refs_1_ = bf16[128,512]{1,0:T(8,128)(2,1)S(1)} collective-permute-done((bf16[128,512]{1,0:T(8,128)(2,1)S(1)}, bf16[128,512]{1,0:T(8,128)(2,1)S(1)}, u32[]{:S(2)}, u32[]{:S(2)}) %collective-permute-start.11) | collective-permute-done | bytes 131104 | tf_op jit(solution)/shard_map/ppermute | solution.py:283
  189.5 2.4 collective-permute-done.13.refs_3_
  192.6 2.2 collective-permute-start.15
  194.8 2.2 collective-permute-start.16
  197.3 2.5 collective-permute-done.15.refs_2_
  199.8 1.7 collective-permute-done.16.refs_3_
  201.5 2.2 collective-permute-start.19
  203.7 2.2 collective-permute-start.17
  205.9 2.3 collective-permute-done.19.refs_3_
  208.2 1.8 collective-permute-done.18.refs_2_
  210.6 8.0 %reduce-scatter.2.cloned.1.call-done.neigh_ref = bf16[512,512]{1,0:T(8,128)(2,1)} async-done(((bf16[4096,512]{1,0:T(8,128)(2,1)}), bf16[512,512]{1,0:T(8,128)(2,1)}) %reduce-scatter.2.cloned.1.call-update) | async-done | bytes 524304 | tf_op jit(solution)/shard_map/reduce_scatter | solution.py:476
  218.6 1.0 copy-done.1
  219.6 1.8 join_pack.1
  221.4 3.4 %all-to-all-start.6 = ((bf16[32,32,512]{2,1,0:T(8,128)(2,1)}), bf16[32,32,512]{2,1,0:T(8,128)(2,1)S(1)}, u32[]{:S(2)}, u32[]{:S(2)}) async-start(bf16[32,32,512]{2,1,0:T(8,128)(2,1)} %bitcast.23), calls=%async_computation.7 | async-start | bytes 2097152 | tf_op jit(solution)/shard_map/all_to_all | solution.py:269
  224.8 2.7 %collective-permute-start.22 = (bf16[128,512]{1,0:T(8,128)(2,1)S(1)}, bf16[128,512]{1,0:T(8,128)(2,1)S(1)}, u32[]{:S(2)}, u32[]{:S(2)}) collective-permute-start(bf16[128,512]{1,0:T(8,128)(2,1)S(1)} %bitcast.37), channel_id=1, source_target_pairs={{0,24},{8,16},{16,8},{24,0},{1,25},{9,17},{17,9},{25,1},{2,26},{10... | collective-permute-start | bytes 393224 | tf_op jit(solution)/shard_map/ppermute | solution.py:283
  228.4 11.5 %collective-permute-done.22.refs_3_ = bf16[128,512]{1,0:T(8,128)(2,1)S(1)} collective-permute-done((bf16[128,512]{1,0:T(8,128)(2,1)S(1)}, bf16[128,512]{1,0:T(8,128)(2,1)S(1)}, u32[]{:S(2)}, u32[]{:S(2)}) %collective-permute-start.22) | collective-permute-done | bytes 131104 | tf_op jit(solution)/shard_map/ppermute | solution.py:283
  239.8 1.6 collective-permute-done.21.refs_2_
  242.8 1.8 unpack_owner.2
  244.7 1.5 final.1
  246.2 6.2 %all-to-all-done.6 = bf16[32,32,512]{2,1,0:T(8,128)(2,1)S(1)} async-done(((bf16[32,32,512]{2,1,0:T(8,128)(2,1)}), bf16[32,32,512]{2,1,0:T(8,128)(2,1)S(1)}, u32[]{:S(2)}, u32[]{:S(2)}) %all-to-all-start.6) | async-done | bytes 1048608 | tf_op jit(solution)/shard_map/all_to_all | solution.py:269
  252.4 1.8 unpack_owner.3
  (70 shorter events, 10.3 us)
Async XLA Ops:
  10.3 34.9 %all-to-all-start = ((bf16[32,32,512]{2,1,0:T(8,128)(2,1)}), bf16[32,32,512]{2,1,0:T(8,128)(2,1)S(1)}, u32[]{:S(2)}, u32[]{:S(2)}) async-start(bf16[32,32,512]{2,1,0:T(8,128)(2,1)} %bitcast.44), calls=%async_computation | async-start | bytes 2097152 | tf_op jit(solution)/shard_map/all_to_all | solution.py:269
  17.6 75.1 %all-gather.2.cloned.1.call-start = ((), (), s32[]{:S(2)}) async-start(), calls=%async_computation.8 | async-start | bytes 4718592 | tf_op jit(solution)/shard_map/all_gather | solution.py:347
  45.2 0.7 copy-start.3
  57.9 17.6 %all-to-all-start.1 = ((bf16[4,256,512]{2,1,0:T(8,128)(2,1)}), bf16[4,256,512]{2,1,0:T(8,128)(2,1)S(1)}, u32[]{:S(2)}, u32[]{:S(2)}) async-start(bf16[4,256,512]{2,1,0:T(8,128)(2,1)} %bitcast.46), calls=%async_computation.1 | async-start | bytes 2097152 | tf_op jit(solution)/shard_map/all_to_all | solution.py:273
  92.7 30.1 %all-to-all-start.3 = ((bf16[8,128,512]{2,1,0:T(8,128)(2,1)}), bf16[8,128,512]{2,1,0:T(8,128)(2,1)S(1)}, u32[]{:S(2)}, u32[]{:S(2)}) async-start(bf16[8,128,512]{2,1,0:T(8,128)(2,1)} %bitcast.14), calls=%async_computation.3 | async-start | bytes 2097152 | tf_op jit(solution)/shard_map/all_to_all | solution.py:277
  96.2 26.5 %copy-start.8 = (s32[8,512]{1,0:T(8,128)S(1)}, s32[8,512]{1,0:T(8,128)}, u32[]{:S(2)}) copy-start(s32[8,512]{1,0:T(8,128)} %get-tuple-element.88.row_ref) | copy-start | bytes 49156
  103.7 9.4 %collective-permute-start.1 = (bf16[256,512]{1,0:T(8,128)(2,1)}, bf16[256,512]{1,0:T(8,128)(2,1)S(1)}, u32[]{:S(2)}, u32[]{:S(2)}) collective-permute-start(bf16[256,512]{1,0:T(8,128)(2,1)} %get-tuple-element.80), channel_id=1, source_target_pairs={{0,16},{8,24},{16,0},{24,8},{1,17},{9,25},{17,1},{25,9},{2,18},{10... | collective-permute-start | bytes 786440 | tf_op jit(solution)/shard_map/ppermute | solution.py:283
  105.3 9.4 %collective-permute-start.2 = (bf16[256,512]{1,0:T(8,128)(2,1)}, bf16[256,512]{1,0:T(8,128)(2,1)S(1)}, u32[]{:S(2)}, u32[]{:S(2)}) collective-permute-start(bf16[256,512]{1,0:T(8,128)(2,1)} %get-tuple-element.81), channel_id=1, source_target_pairs={{0,8},{8,0},{16,24},{24,16},{1,9},{9,1},{17,25},{25,17},{2,10},{10... | collective-permute-start | bytes 786440 | tf_op jit(solution)/shard_map/ppermute | solution.py:283
  106.8 17.8 %collective-permute-start = (bf16[256,512]{1,0:T(8,128)(2,1)}, bf16[256,512]{1,0:T(8,128)(2,1)S(1)}, u32[]{:S(2)}, u32[]{:S(2)}) collective-permute-start(bf16[256,512]{1,0:T(8,128)(2,1)} %get-tuple-element.77), channel_id=1, source_target_pairs={{0,8},{8,0},{16,24},{24,16},{1,9},{9,1},{17,25},{25,17},{2,10},{10... | collective-permute-start | bytes 786440 | tf_op jit(solution)/shard_map/ppermute | solution.py:283
  107.3 17.3 %collective-permute-start.5 = (bf16[256,512]{1,0:T(8,128)(2,1)}, bf16[256,512]{1,0:T(8,128)(2,1)S(1)}, u32[]{:S(2)}, u32[]{:S(2)}) collective-permute-start(bf16[256,512]{1,0:T(8,128)(2,1)} %get-tuple-element.85), channel_id=1, source_target_pairs={{0,16},{8,24},{16,0},{24,8},{1,17},{9,25},{17,1},{25,9},{2,18},{10... | collective-permute-start | bytes 786440 | tf_op jit(solution)/shard_map/ppermute | solution.py:283
  113.1 1.5 copy-start.9
  114.6 0.7 copy-start.10
  117.4 7.2 %collective-permute-start.3 = (bf16[256,512]{1,0:T(8,128)(2,1)}, bf16[256,512]{1,0:T(8,128)(2,1)S(1)}, u32[]{:S(2)}, u32[]{:S(2)}) collective-permute-start(bf16[256,512]{1,0:T(8,128)(2,1)} %get-tuple-element.82), channel_id=1, source_target_pairs={{0,16},{8,24},{16,0},{24,8},{1,17},{9,25},{17,1},{25,9},{2,18},{10... | collective-permute-start | bytes 786440 | tf_op jit(solution)/shard_map/ppermute | solution.py:283
  117.9 7.3 %collective-permute-start.4 = (bf16[256,512]{1,0:T(8,128)(2,1)}, bf16[256,512]{1,0:T(8,128)(2,1)S(1)}, u32[]{:S(2)}, u32[]{:S(2)}) collective-permute-start(bf16[256,512]{1,0:T(8,128)(2,1)} %get-tuple-element.84), channel_id=1, source_target_pairs={{0,8},{8,0},{16,24},{24,16},{1,9},{9,1},{17,25},{25,17},{2,10},{10... | collective-permute-start | bytes 786440 | tf_op jit(solution)/shard_map/ppermute | solution.py:283
  123.8 0.8 copy-start.6
  124.6 0.7 copy-start.14
  124.6 0.8 copy-start.15
  124.6 0.9 copy-start.16
  125.2 0.7 copy-start.17
  130.0 13.3 %collective-permute-start.7 = (bf16[512,512]{1,0:T(8,128)(2,1)}, bf16[512,512]{1,0:T(8,128)(2,1)S(1)}, u32[]{:S(2)}, u32[]{:S(2)}) collective-permute-start(bf16[512,512]{1,0:T(8,128)(2,1)} %get-tuple-element.100.refs_0_), channel_id=1, source_target_pairs={{0,16},{8,24},{16,0},{24,8},{1,17},{9,25},{17,1},{25,9},{2,18},{10... | collective-permute-start | bytes 1572872 | tf_op jit(solution)/shard_map/ppermute | solution.py:283
  131.2 13.4 %collective-permute-start.6 = (bf16[512,512]{1,0:T(8,128)(2,1)}, bf16[512,512]{1,0:T(8,128)(2,1)S(1)}, u32[]{:S(2)}, u32[]{:S(2)}) collective-permute-start(bf16[512,512]{1,0:T(8,128)(2,1)} %get-tuple-element.100.refs_0_), channel_id=1, source_target_pairs={{0,8},{8,0},{16,24},{24,16},{1,9},{9,1},{17,25},{25,17},{2,10},{10... | collective-permute-start | bytes 1572872 | tf_op jit(solution)/shard_map/ppermute | solution.py:283
  135.4 31.5 %all-to-all-start.4 = ((bf16[8,128,512]{2,1,0:T(8,128)(2,1)}), bf16[8,128,512]{2,1,0:T(8,128)(2,1)S(1)}, u32[]{:S(2)}, u32[]{:S(2)}) async-start(bf16[8,128,512]{2,1,0:T(8,128)(2,1)} %bitcast.45), calls=%async_computation.4 | async-start | bytes 2097152 | tf_op jit(solution)/shard_map/all_to_all | solution.py:277
  140.3 78.3 %reduce-scatter.2.cloned.1.call-start = ((), (), s32[]{:S(2)}) async-start(), calls=%async_computation.9 | async-start | bytes 4718592 | tf_op jit(solution)/shard_map/reduce_scatter | solution.py:476
  143.4 9.2 %copy-start.11 = (bf16[512,512]{1,0:T(8,128)(2,1)}, bf16[512,512]{1,0:T(8,128)(2,1)S(1)}, u32[]{:S(2)}) copy-start(bf16[512,512]{1,0:T(8,128)(2,1)S(1)} %collective-permute-done.7.refs_2_) | copy-start | bytes 1572868
  144.6 8.0 %copy-start.12 = (bf16[512,512]{1,0:T(8,128)(2,1)}, bf16[512,512]{1,0:T(8,128)(2,1)S(1)}, u32[]{:S(2)}) copy-start(bf16[512,512]{1,0:T(8,128)(2,1)S(1)} %collective-permute-done.6.refs_1_) | copy-start | bytes 1572868
  144.6 6.7 %collective-permute-start.8 = (bf16[256,512]{1,0:T(8,128)(2,1)S(1)}, bf16[256,512]{1,0:T(8,128)(2,1)S(1)}, u32[]{:S(2)}, u32[]{:S(2)}) collective-permute-start(bf16[256,512]{1,0:T(8,128)(2,1)S(1)} %slice.6), channel_id=1, source_target_pairs={{0,8},{8,0},{16,24},{24,16},{1,9},{9,1},{17,25},{25,17},{2,10},{10... | collective-permute-start | bytes 786440 | tf_op jit(solution)/shard_map/ppermute | solution.py:283
  146.2 6.4 %collective-permute-start.9 = (bf16[256,512]{1,0:T(8,128)(2,1)S(1)}, bf16[256,512]{1,0:T(8,128)(2,1)S(1)}, u32[]{:S(2)}, u32[]{:S(2)}) collective-permute-start(bf16[256,512]{1,0:T(8,128)(2,1)S(1)} %slice.7), channel_id=1, source_target_pairs={{0,16},{8,24},{16,0},{24,8},{1,17},{9,25},{17,1},{25,9},{2,18},{10... | collective-permute-start | bytes 786440 | tf_op jit(solution)/shard_map/ppermute | solution.py:283
  151.4 1.2 copy-start.18
  152.5 0.7 copy-start.19
  166.9 4.8 %copy-start.13 = (bf16[512,512]{1,0:T(8,128)(2,1)S(1)}, bf16[512,512]{1,0:T(8,128)(2,1)}, u32[]{:S(2)}) copy-start(bf16[512,512]{1,0:T(8,128)(2,1)} %get-tuple-element.110) | copy-start | bytes 1572868
  166.9 6.8 %copy-start.2 = (bf16[512,512]{1,0:T(8,128)(2,1)S(1)}, bf16[512,512]{1,0:T(8,128)(2,1)}, u32[]{:S(2)}) copy-start(bf16[512,512]{1,0:T(8,128)(2,1)} %get-tuple-element.109.refs_0_) | copy-start | bytes 1572868
  166.9 6.8 %copy-start.5 = (s32[4]{0:T(128)S(1)}, s32[4]{0:T(128)}, u32[]{:S(2)}) copy-start(s32[4]{0:T(128)} %get-tuple-element.69.group_ref.index_ref) | copy-start | bytes 52
  166.9 51.7 %copy-start = (f32[512,512]{1,0:T(8,128)S(1)}, f32[512,512]{1,0:T(8,128)}, u32[]{:S(2)}) copy-start(f32[512,512]{1,0:T(8,128)} %get-tuple-element.119.own_ref) | copy-start | bytes 3145732
  166.9 51.7 %copy-start.4 = (s32[8,512]{1,0:T(8,128)S(1)}, s32[8,512]{1,0:T(8,128)}, u32[]{:S(2)}) copy-start(s32[8,512]{1,0:T(8,128)} %get-tuple-element.67.row_ref) | copy-start | bytes 49156
  168.0 53.4 %all-to-all-start.5 = ((bf16[4,256,512]{2,1,0:T(8,128)(2,1)}), bf16[4,256,512]{2,1,0:T(8,128)(2,1)S(1)}, u32[]{:S(2)}, u32[]{:S(2)}) async-start(bf16[4,256,512]{2,1,0:T(8,128)(2,1)} %bitcast.41), calls=%async_computation.5 | async-start | bytes 2097152 | tf_op jit(solution)/shard_map/all_to_all | solution.py:273
  171.7 71.1 %copy-start.7 = (s32[8,512]{1,0:T(8,128)S(1)}, s32[8,512]{1,0:T(8,128)}, u32[]{:S(2)}) copy-start(s32[8,512]{1,0:T(8,128)} %get-tuple-element.64.row_ref) | copy-start | bytes 49156
  171.7 2.0 collective-permute-start.10
  174.5 15.1 %collective-permute-start.11 = (bf16[128,512]{1,0:T(8,128)(2,1)S(1)}, bf16[128,512]{1,0:T(8,128)(2,1)S(1)}, u32[]{:S(2)}, u32[]{:S(2)}) collective-permute-start(bf16[128,512]{1,0:T(8,128)(2,1)S(1)} %get-tuple-element.112), channel_id=1, source_target_pairs={{0,8},{8,0},{16,24},{24,16},{1,9},{9,1},{17,25},{25,17},{2,10},{10... | collective-permute-start | bytes 393224 | tf_op jit(solution)/shard_map/ppermute | solution.py:283
  176.4 13.1 %collective-permute-start.12 = (bf16[128,512]{1,0:T(8,128)(2,1)S(1)}, bf16[128,512]{1,0:T(8,128)(2,1)S(1)}, u32[]{:S(2)}, u32[]{:S(2)}) collective-permute-start(bf16[128,512]{1,0:T(8,128)(2,1)S(1)} %get-tuple-element.113), channel_id=1, source_target_pairs={{0,16},{8,24},{16,0},{24,8},{1,17},{9,25},{17,1},{25,9},{2,18},{10... | collective-permute-start | bytes 393224 | tf_op jit(solution)/shard_map/ppermute | solution.py:283
  177.9 14.0 %collective-permute-start.13 = (bf16[128,512]{1,0:T(8,128)(2,1)S(1)}, bf16[128,512]{1,0:T(8,128)(2,1)S(1)}, u32[]{:S(2)}, u32[]{:S(2)}) collective-permute-start(bf16[128,512]{1,0:T(8,128)(2,1)S(1)} %get-tuple-element.114), channel_id=1, source_target_pairs={{0,24},{8,16},{16,8},{24,0},{1,25},{9,17},{17,9},{25,1},{2,26},{10... | collective-permute-start | bytes 393224 | tf_op jit(solution)/shard_map/ppermute | solution.py:283
  192.5 4.8 %collective-permute-start.14 = (bf16[32,512]{1,0:T(8,128)(2,1)S(1)}, bf16[32,512]{1,0:T(8,128)(2,1)S(1)}, u32[]{:S(2)}, u32[]{:S(2)}) collective-permute-start(bf16[32,512]{1,0:T(8,128)(2,1)S(1)} %get-tuple-element.116), channel_id=1, source_target_pairs={{0,2},{1,3},{2,0},{3,1},{4,6},{5,7},{6,4},{7,5},{8,10},{9,11},{10,... | collective-permute-start | bytes 98312 | tf_op jit(solution)/shard_map/ppermute | solution.py:286
  192.6 7.1 %collective-permute-start.15 = (bf16[32,512]{1,0:T(8,128)(2,1)S(1)}, bf16[32,512]{1,0:T(8,128)(2,1)S(1)}, u32[]{:S(2)}, u32[]{:S(2)}) collective-permute-start(bf16[32,512]{1,0:T(8,128)(2,1)S(1)} %get-tuple-element.117), channel_id=1, source_target_pairs={{0,4},{1,5},{2,6},{3,7},{4,0},{5,1},{6,2},{7,3},{8,12},{9,13},{10,... | collective-permute-start | bytes 98312 | tf_op jit(solution)/shard_map/ppermute | solution.py:286
  194.8 6.6 %collective-permute-start.16 = (bf16[32,512]{1,0:T(8,128)(2,1)S(1)}, bf16[32,512]{1,0:T(8,128)(2,1)S(1)}, u32[]{:S(2)}, u32[]{:S(2)}) collective-permute-start(bf16[32,512]{1,0:T(8,128)(2,1)S(1)} %get-tuple-element.118), channel_id=1, source_target_pairs={{0,6},{1,7},{2,4},{3,5},{4,2},{5,3},{6,0},{7,1},{8,14},{9,15},{10,... | collective-permute-start | bytes 98312 | tf_op jit(solution)/shard_map/ppermute | solution.py:286
  201.5 6.8 %collective-permute-start.19 = (bf16[32,512]{1,0:T(8,128)(2,1)S(1)}, bf16[32,512]{1,0:T(8,128)(2,1)S(1)}, u32[]{:S(2)}, u32[]{:S(2)}) collective-permute-start(bf16[32,512]{1,0:T(8,128)(2,1)S(1)} %split_sum.5.refs_0_), channel_id=1, source_target_pairs={{0,6},{1,7},{2,4},{3,5},{4,2},{5,3},{6,0},{7,1},{8,14},{9,15},{10,... | collective-permute-start | bytes 98312 | tf_op jit(solution)/shard_map/ppermute | solution.py:286
  203.7 6.3 %collective-permute-start.18 = (bf16[32,512]{1,0:T(8,128)(2,1)S(1)}, bf16[32,512]{1,0:T(8,128)(2,1)S(1)}, u32[]{:S(2)}, u32[]{:S(2)}) collective-permute-start(bf16[32,512]{1,0:T(8,128)(2,1)S(1)} %split_sum.5.refs_0_), channel_id=1, source_target_pairs={{0,4},{1,5},{2,6},{3,7},{4,0},{5,1},{6,2},{7,3},{8,12},{9,13},{10,... | collective-permute-start | bytes 98312 | tf_op jit(solution)/shard_map/ppermute | solution.py:286
  203.7 6.3 %collective-permute-start.17 = (bf16[32,512]{1,0:T(8,128)(2,1)S(1)}, bf16[32,512]{1,0:T(8,128)(2,1)S(1)}, u32[]{:S(2)}, u32[]{:S(2)}) collective-permute-start(bf16[32,512]{1,0:T(8,128)(2,1)S(1)} %split_sum.5.refs_0_), channel_id=1, source_target_pairs={{0,2},{1,3},{2,0},{3,1},{4,6},{5,7},{6,4},{7,5},{8,10},{9,11},{10,... | collective-permute-start | bytes 98312 | tf_op jit(solution)/shard_map/ppermute | solution.py:286
  218.6 1.0 copy-start.1
  221.4 31.0 %all-to-all-start.6 = ((bf16[32,32,512]{2,1,0:T(8,128)(2,1)}), bf16[32,32,512]{2,1,0:T(8,128)(2,1)S(1)}, u32[]{:S(2)}, u32[]{:S(2)}) async-start(bf16[32,32,512]{2,1,0:T(8,128)(2,1)} %bitcast.23), calls=%async_computation.7 | async-start | bytes 2097152 | tf_op jit(solution)/shard_map/all_to_all | solution.py:269
  224.8 15.0 %collective-permute-start.22 = (bf16[128,512]{1,0:T(8,128)(2,1)S(1)}, bf16[128,512]{1,0:T(8,128)(2,1)S(1)}, u32[]{:S(2)}, u32[]{:S(2)}) collective-permute-start(bf16[128,512]{1,0:T(8,128)(2,1)S(1)} %bitcast.37), channel_id=1, source_target_pairs={{0,24},{8,16},{16,8},{24,0},{1,25},{9,17},{17,9},{25,1},{2,26},{10... | collective-permute-start | bytes 393224 | tf_op jit(solution)/shard_map/ppermute | solution.py:283
  227.5 13.9 %collective-permute-start.21 = (bf16[128,512]{1,0:T(8,128)(2,1)S(1)}, bf16[128,512]{1,0:T(8,128)(2,1)S(1)}, u32[]{:S(2)}, u32[]{:S(2)}) collective-permute-start(bf16[128,512]{1,0:T(8,128)(2,1)S(1)} %bitcast.38), channel_id=1, source_target_pairs={{0,16},{8,24},{16,0},{24,8},{1,17},{9,25},{17,1},{25,9},{2,18},{10... | collective-permute-start | bytes 393224 | tf_op jit(solution)/shard_map/ppermute | solution.py:283
  228.1 14.1 %collective-permute-start.20 = (bf16[128,512]{1,0:T(8,128)(2,1)S(1)}, bf16[128,512]{1,0:T(8,128)(2,1)S(1)}, u32[]{:S(2)}, u32[]{:S(2)}) collective-permute-start(bf16[128,512]{1,0:T(8,128)(2,1)S(1)} %bitcast.39), channel_id=1, source_target_pairs={{0,8},{8,0},{16,24},{24,16},{1,9},{9,1},{17,25},{25,17},{2,10},{10... | collective-permute-start | bytes 393224 | tf_op jit(solution)/shard_map/ppermute | solution.py:283
  242.8 2.0 collective-permute-start.23
Sparse Core Ops, SparseCore 0:
  47.9 44.7 all-gather.1
  167.0 51.4 reduce-scatter.1
